TPU v7x, 32 devices: a whole 2x2x4 slice. The times are simulated.
32 devices in a mesh: group: 4 (over y, core), shard: 8 (over z, x).
Axes of the slice: x: 2, y: 2, z: 4, core: 2. Of those that a mesh axis runs over, the one named last changes fastest.
Arguments:
- edge_state: bfloat16 [32768, 128], P(('group', 'shard')), may hold values from -6 to 6
- atom_state: bfloat16 [2048, 256], P(('group', 'shard')), may hold values from -6 to 6
- radial_basis: bfloat16 [32768, 16], P(('group', 'shard')), may hold values from -6 to 6
- triplet_basis: bfloat16 [131072, 16], P(('group', 'shard')), may hold values from -6 to 6
- quad_basis: bfloat16 [131072, 16], P(('group', 'shard')), may hold values from -6 to 6
- dst_owner: int32 [32768, 1], P(('group', 'shard')), may hold values from 0 to 7; in each aligned block of 1024 rows (0 to 1023, 1024 to 2047, ...) at most 256 rows name the same one
- dst_local: int32 [32768], P(('group', 'shard')), may hold values from 0 to 63
- src_owner: int32 [32768, 1], P(('group', 'shard')), may hold values from 0 to 7; in each aligned block of 1024 rows (0 to 1023, 1024 to 2047, ...) at most 256 rows name the same one
- src_local: int32 [32768], P(('group', 'shard')), may hold values from 0 to 63
- triplet_in: int32 [131072], P(('group', 'shard')), may hold values from 0 to 1023
- triplet_out: int32 [131072], P(('group', 'shard')), may hold values from 0 to 1023
- quad_in: int32 [131072], P(('group', 'shard')), may hold values from 0 to 1023
- quad_out: int32 [131072], P(('group', 'shard')), may hold values from 0 to 1023
- fixed_atoms: int32 [2048], P(('group', 'shard')), may hold values 0 or 1
- edge_cotangent: bfloat16 [32768, 128], P(('group', 'shard')), may hold values from -6 to 6
- atom_cotangent: bfloat16 [2048, 256], P(('group', 'shard')), may hold values from -6 to 6
- weights: float32 [3000, 128], P(None, 'shard')
- first_moment: float32 [3000, 128], P(None, 'shard'), as said below
- second_moment: float32 [3000, 128], P(None, 'shard'), as said below
Outputs:
- edge_out: bfloat16 [32768, 128], P(('group', 'shard'))
- atom_out: bfloat16 [2048, 256], P(('group', 'shard'))
- edge_grad: float32 [32768, 128], P(('group', 'shard'))
- atom_grad: float32 [2048, 256], P(('group', 'shard'))
- weight_grad: float32 [3000, 128], P(None, 'shard')
- new_weights: float32 [3000, 128], P(None, 'shard')
- new_first: float32 [3000, 128], P(None, 'shard')
- new_second: float32 [3000, 128], P(None, 'shard')
- weights_low: bfloat16 [3000, 128], P(None, 'shard')
Inputs may be any that keep to these rules, and one draw needn't show every extreme that they name: `dst_owner`: in the rows of one device no owner is named by more than 256 edges; in the rows of some devices one owner is named by exactly 256. `src_owner`: in the rows of one device no owner is named by more than 256 edges; in the rows of some devices one owner is named by exactly 256. `first_moment`: state of earlier steps, of both signs. `second_moment`: state of earlier steps, positive.
All inputs are finite; a program needn't handle non-finite values. No bound on the sum of `fixed_atoms` on one device may be relied on, other than what follows from the above.
Results may differ from a plain program's by a relative error of at most 0.035.
Values may be sent and summed in bfloat16 or wider, within the bound.
No kernel may reach another device: no remote copies, remote signals or barrier semaphores. Data moves between devices by JAX's collectives and lax.ppermute only.
A program may use at most 128 MiB of HBM per device.

v0:
```python
import math

import jax
import jax.numpy as jnp
from jax import lax
from jax.sharding import PartitionSpec as P

D_EDGE = 128
D_ATOM = 256
D_TRI = 64
D_QUAD = 32
D_BASIS = 16
BLOCKS = 2


edge_scale = 0.25
pair_scale = 0.5
beta_one = 0.5
beta_two = 0.5
learn_rate = 0.1
decay_rate = 0.01
epsilon = 1e-08
adam_step = 4


def matrix_shapes():
    return [
        (D_EDGE, D_TRI),
        (D_BASIS, D_TRI),
        (D_TRI, D_EDGE),
        (D_EDGE, D_QUAD),
        (D_BASIS, D_QUAD),
        (D_QUAD, D_EDGE),
        (D_BASIS, D_EDGE),
        (D_EDGE, D_ATOM),
        (D_ATOM, D_ATOM),
        (D_ATOM, D_EDGE),
        (D_ATOM, D_EDGE),
    ]


def unpack(flat):
    result_list = []
    offset = 0
    for layer_index in range(BLOCKS):
        matrices = []
        for fan_in, width_out in matrix_shapes():
            row_total = fan_in * width_out // 128
            matrices.append(flat[offset : offset + row_total].reshape(fan_in, width_out))
            offset = offset + row_total
        result_list.append(matrices)
    return result_list


def silu_slope(preact):
    logistic = jax.nn.sigmoid(preact)
    return logistic * (1.0 + preact * (1.0 - logistic))


def matmul(left_side, right_side):
    return jnp.dot(left_side, right_side, preferred_element_type=jnp.float32)


def rows_inner(left_side, right_side):
    return lax.dot_general(
        left_side, right_side, (((0,), (0,)), ((), ())), preferred_element_type=jnp.float32
    )


def times_trans(left_side, right_side):
    return lax.dot_general(
        left_side, right_side, (((1,), (1,)), ((), ())), preferred_element_type=jnp.float32
    )


def split_pieces(values):
    if values.dtype == jnp.bfloat16:
        return (values,)
    upper = values.astype(jnp.bfloat16)
    remain = values - upper.astype(jnp.float32)
    middle_part = remain.astype(jnp.bfloat16)
    lower = (remain - middle_part.astype(jnp.float32)).astype(jnp.bfloat16)
    return (upper, middle_part, lower)


def pick_rows(table, indices):
    table_rows = table.shape[0]
    row_total = indices.shape[0]
    block_rows = math.gcd(row_total, 1024)
    pieces = split_pieces(table)
    columns = jnp.arange(table_rows, dtype=jnp.int32)

    def pick_block(block_index):
        onehot = (block_index[:, None] == columns[None, :]).astype(jnp.bfloat16)
        summed = matmul(onehot, pieces[0])
        for piece in pieces[1:]:
            summed = summed + matmul(onehot, piece)
        return summed

    picked = lax.map(pick_block, indices.reshape(row_total // block_rows, block_rows)).reshape(
        row_total, table.shape[1]
    )
    return picked.astype(table.dtype)


def add_rows(values, indices, table_rows):
    row_total = indices.shape[0]
    block_rows = math.gcd(row_total, 1024)
    block_count = row_total // block_rows
    width = values.shape[1]
    pieces = tuple(
        (piece.reshape(block_count, block_rows, width) for piece in split_pieces(values))
    )
    columns = jnp.arange(table_rows, dtype=jnp.int32)

    def add_block(carry, items):
        block_index, block_pieces = items
        onehot = (block_index[:, None] == columns[None, :]).astype(jnp.bfloat16)
        for piece in block_pieces:
            carry = carry + rows_inner(onehot, piece)
        return (carry, None)

    summed, unused = lax.scan(
        add_block,
        jnp.zeros((table_rows, width), jnp.float32),
        (indices.reshape(block_count, block_rows), pieces),
    )
    return summed


def slot_index(owner_col, capacity, owners):
    owner_ids = owner_col[:, 0]
    onehot = (owner_ids[:, None] == jnp.arange(owners, dtype=jnp.int32)[None, :]).astype(jnp.int32)
    before = jnp.cumsum(onehot, axis=0) - onehot
    return owner_ids * capacity + jnp.sum(before * onehot, axis=1)


def pair_forward(
    edge_low,
    basis_rows,
    source_edges,
    target_edges,
    down_weight,
    basis_weight,
    up_weight,
    edge_count,
):
    pre_in = matmul(edge_low, down_weight)
    activated = jax.nn.silu(pre_in)
    basis_out = matmul(basis_rows, basis_weight)
    products = pick_rows(activated, source_edges) * basis_out
    aggregate = (add_rows(products, target_edges, edge_count) * pair_scale).astype(jnp.bfloat16)
    pre_out = matmul(aggregate, up_weight)
    return (jax.nn.silu(pre_out), (pre_in, activated, basis_out, aggregate, pre_out))


def pair_backward(
    grad_result,
    kept_state,
    edge_low,
    basis_rows,
    source_edges,
    target_edges,
    down_weight,
    up_weight,
    edge_count,
):
    pre_in, activated, basis_out, aggregate, pre_out = kept_state
    grad_out = (grad_result * silu_slope(pre_out)).astype(jnp.bfloat16)
    grad_up = rows_inner(aggregate, grad_out)
    grad_aggregate = times_trans(grad_out, up_weight) * pair_scale
    grad_items = pick_rows(grad_aggregate, target_edges)
    grad_basis_out = (grad_items * pick_rows(activated, source_edges)).astype(jnp.bfloat16)
    grad_basis = rows_inner(basis_rows, grad_basis_out)
    grad_activated = add_rows(grad_items * basis_out, source_edges, edge_count)
    grad_in = (grad_activated * silu_slope(pre_in)).astype(jnp.bfloat16)
    grad_down = rows_inner(edge_low, grad_in)
    return (times_trans(grad_in, down_weight), grad_down, grad_basis, grad_up)


def per_device(
    edge_state,
    atom_state,
    radial_basis,
    triplet_basis,
    quad_basis,
    dst_owner,
    dst_local,
    src_owner,
    src_local,
    triplet_in,
    triplet_out,
    quad_in,
    quad_out,
    fixed_atoms,
    edge_cotangent,
    atom_cotangent,
    weights,
    first_moment,
    second_moment,
):
    owners = lax.axis_size("shard")
    edge_count = edge_state.shape[0]
    atom_count = atom_state.shape[0]
    capacity = 2 * edge_count // owners
    slot_count = owners * capacity
    dst_slot = slot_index(dst_owner, capacity, owners)
    src_slot = slot_index(src_owner, capacity, owners)
    dst_send = (
        jnp.full((slot_count,), atom_count, jnp.int32)
        .at[dst_slot]
        .set(dst_local)
        .reshape(owners, capacity)
    )
    src_send = (
        jnp.full((slot_count,), atom_count, jnp.int32)
        .at[src_slot]
        .set(src_local)
        .reshape(owners, capacity)
    )
    atom_ids = jnp.arange(atom_count, dtype=jnp.int32)[:, None]
    dst_global = dst_owner[:, 0] * atom_count + dst_local
    src_global = src_owner[:, 0] * atom_count + src_local
    recv_dst, recv_src = (
        lax.all_to_all(dst_send, "shard", split_axis=0, concat_axis=0, tiled=True),
        lax.all_to_all(src_send, "shard", split_axis=0, concat_axis=0, tiled=True),
    )
    src_pick = (atom_ids == recv_src.reshape(1, slot_count)).astype(jnp.bfloat16)
    dst_pick = (atom_ids == recv_dst.reshape(1, slot_count)).astype(jnp.bfloat16)
    free_rows = (1 - fixed_atoms).astype(jnp.float32)[:, None]
    gathered = lax.all_gather(weights.astype(jnp.bfloat16), "shard", axis=1, tiled=True)
    block_weights = unpack(gathered)
    state_edge = edge_state.astype(jnp.float32)
    state_atom = atom_state.astype(jnp.float32)
    kept_blocks = []
    for layer_index in range(BLOCKS):
        (
            down_trip,
            basis_trip,
            up_trip,
            down_quad,
            basis_quad,
            up_quad,
            radial_proj,
            atom_first,
            atom_second,
            src_proj,
            dst_proj,
        ) = block_weights[layer_index]
        edge_low = state_edge.astype(jnp.bfloat16)
        trip_value, trip_kept = pair_forward(
            edge_low,
            triplet_basis,
            triplet_in,
            triplet_out,
            down_trip,
            basis_trip,
            up_trip,
            edge_count,
        )
        quad_value, quad_kept = pair_forward(
            edge_low, quad_basis, quad_in, quad_out, down_quad, basis_quad, up_quad, edge_count
        )
        middle = state_edge + trip_value + quad_value
        radial = matmul(radial_basis, radial_proj)
        message = (middle * radial).astype(jnp.bfloat16)
        outgoing = (
            add_rows(message, dst_slot, slot_count)
            .astype(jnp.bfloat16)
            .reshape(owners, capacity, D_EDGE)
        )
        incoming = lax.all_to_all(outgoing, "shard", split_axis=0, concat_axis=0, tiled=True)
        atom_input = (matmul(dst_pick, incoming.reshape(slot_count, D_EDGE)) * edge_scale).astype(
            jnp.bfloat16
        )
        pre_atom = matmul(atom_input, atom_first)
        hidden = jax.nn.silu(pre_atom).astype(jnp.bfloat16)
        update = matmul(hidden, atom_second)
        new_atom = state_atom + free_rows * update
        atom_sent = new_atom.astype(jnp.bfloat16)
        rows_dst = (
            rows_inner(dst_pick, atom_sent).astype(jnp.bfloat16).reshape(owners, capacity, D_ATOM)
        )
        rows_src = (
            rows_inner(src_pick, atom_sent).astype(jnp.bfloat16).reshape(owners, capacity, D_ATOM)
        )
        back_dst, back_src = (
            lax.all_to_all(rows_dst, "shard", split_axis=0, concat_axis=0, tiled=True),
            lax.all_to_all(rows_src, "shard", split_axis=0, concat_axis=0, tiled=True),
        )
        edge_dst_rows = pick_rows(back_dst.reshape(slot_count, D_ATOM), dst_slot)
        edge_src_rows = pick_rows(back_src.reshape(slot_count, D_ATOM), src_slot)
        pre_edge = matmul(edge_src_rows, src_proj) + matmul(edge_dst_rows, dst_proj)
        kept_blocks.append(
            (
                edge_low,
                trip_kept,
                quad_kept,
                middle,
                radial,
                atom_input,
                pre_atom,
                hidden,
                edge_src_rows,
                edge_dst_rows,
                pre_edge,
            )
        )
        state_edge = middle + jax.nn.silu(pre_edge)
        state_atom = new_atom
    grad_edge = edge_cotangent.astype(jnp.float32)
    grad_atom = atom_cotangent.astype(jnp.float32)
    grad_blocks = [None] * BLOCKS
    for layer_index in reversed(range(BLOCKS)):
        (
            down_trip,
            basis_trip,
            up_trip,
            down_quad,
            basis_quad,
            up_quad,
            radial_proj,
            atom_first,
            atom_second,
            src_proj,
            dst_proj,
        ) = block_weights[layer_index]
        (
            edge_low,
            trip_kept,
            quad_kept,
            middle,
            radial,
            atom_input,
            pre_atom,
            hidden,
            edge_src_rows,
            edge_dst_rows,
            pre_edge,
        ) = kept_blocks[layer_index]
        grad_pre = (grad_edge * silu_slope(pre_edge)).astype(jnp.bfloat16)
        grad_src_proj = rows_inner(edge_src_rows, grad_pre)
        grad_dst_proj = rows_inner(edge_dst_rows, grad_pre)
        grad_src_rows = times_trans(grad_pre, src_proj)
        grad_dst_rows = times_trans(grad_pre, dst_proj)
        both_rows = jnp.concatenate([grad_dst_rows, grad_src_rows], axis=0)
        both_index = jnp.concatenate([dst_global, src_global], axis=0)
        table_grad = add_rows(both_rows, both_index, atom_count * owners)
        grad_new_atom = grad_atom + lax.psum_scatter(
            table_grad.astype(jnp.bfloat16), "shard", scatter_dimension=0, tiled=True
        ).astype(jnp.float32)
        grad_update = (grad_new_atom * free_rows).astype(jnp.bfloat16)
        grad_second = rows_inner(hidden, grad_update)
        grad_hidden = times_trans(grad_update, atom_second)
        grad_pre_atom = (grad_hidden * silu_slope(pre_atom)).astype(jnp.bfloat16)
        grad_first = rows_inner(atom_input, grad_pre_atom)
        grad_atom_input = times_trans(grad_pre_atom, atom_first).astype(jnp.bfloat16)
        to_slots = (
            rows_inner(dst_pick, grad_atom_input)
            .astype(jnp.bfloat16)
            .reshape(owners, capacity, D_EDGE)
        )
        from_atoms = lax.all_to_all(to_slots, "shard", split_axis=0, concat_axis=0, tiled=True)
        grad_message = (
            pick_rows(from_atoms.reshape(slot_count, D_EDGE), dst_slot).astype(jnp.float32)
            * edge_scale
        )
        grad_middle = grad_edge + grad_message * radial
        grad_radial = (grad_message * middle).astype(jnp.bfloat16)
        grad_radial_proj = rows_inner(radial_basis, grad_radial)
        trip_edge, grad_down_trip, grad_basis_trip, grad_up_trip = pair_backward(
            grad_middle,
            trip_kept,
            edge_low,
            triplet_basis,
            triplet_in,
            triplet_out,
            down_trip,
            up_trip,
            edge_count,
        )
        quad_edge, grad_down_quad, grad_basis_quad, grad_up_quad = pair_backward(
            grad_middle,
            quad_kept,
            edge_low,
            quad_basis,
            quad_in,
            quad_out,
            down_quad,
            up_quad,
            edge_count,
        )
        grad_edge = grad_middle + trip_edge + quad_edge
        grad_atom = grad_new_atom
        grad_blocks[layer_index] = [
            grad_down_trip,
            grad_basis_trip,
            grad_up_trip,
            grad_down_quad,
            grad_basis_quad,
            grad_up_quad,
            grad_radial_proj,
            grad_first,
            grad_second,
            grad_src_proj,
            grad_dst_proj,
        ]
    pieces = []
    for layer_index in range(BLOCKS):
        for matrix_grad in grad_blocks[layer_index]:
            pieces.append(matrix_grad.reshape(-1, 128))
    grad_flat = jnp.concatenate(pieces, axis=0)
    grad_local = lax.psum_scatter(
        grad_flat.astype(jnp.bfloat16), "shard", scatter_dimension=1, tiled=True
    )
    weight_grad = lax.psum(grad_local, "group").astype(jnp.float32)
    new_first = beta_one * first_moment + (1.0 - beta_one) * weight_grad
    new_second = beta_two * second_moment + (1.0 - beta_two) * weight_grad * weight_grad
    first_hat = new_first / (1.0 - beta_one**adam_step)
    second_hat = new_second / (1.0 - beta_two**adam_step)
    new_weights = weights - learn_rate * (
        first_hat / (jnp.sqrt(second_hat) + epsilon) + decay_rate * weights
    )
    return (
        state_edge.astype(jnp.bfloat16),
        state_atom.astype(jnp.bfloat16),
        grad_edge,
        grad_atom,
        weight_grad,
        new_weights,
        new_first,
        new_second,
        new_weights.astype(jnp.bfloat16),
    )


def solution(mesh):
    in_specs = (
        P(("group", "shard"), None),
        P(("group", "shard"), None),
        P(("group", "shard"), None),
        P(("group", "shard"), None),
        P(("group", "shard"), None),
        P(("group", "shard"), None),
        P(("group", "shard")),
        P(("group", "shard"), None),
        P(("group", "shard")),
        P(("group", "shard")),
        P(("group", "shard")),
        P(("group", "shard")),
        P(("group", "shard")),
        P(("group", "shard")),
        P(("group", "shard"), None),
        P(("group", "shard"), None),
        P(None, "shard"),
        P(None, "shard"),
        P(None, "shard"),
    )
    out_specs = (
        P(("group", "shard"), None),
        P(("group", "shard"), None),
        P(("group", "shard"), None),
        P(("group", "shard"), None),
        P(None, "shard"),
        P(None, "shard"),
        P(None, "shard"),
        P(None, "shard"),
        P(None, "shard"),
    )
    return jax.shard_map(
        per_device, mesh=mesh, in_specs=in_specs, out_specs=out_specs, check_vma=False
    )
```

profile of v0, /device:TPU:0, one launch (start us, length us, event | category | flops | bytes accessed | tf_op | source)
XLA Modules:
  0.0 1005.0 jit_solution(9715853465582967777)
XLA Ops:
  17.2 7.3 all-to-all-start.1
  25.4 32.6 %all_gather.3 = bf16[3000,128]{0,1:T(8,128)(2,1)S(1)} all-gather(bf16[3000,16]{0,1:T(8,128)(2,1)S(1)} %convert_element_type.558), channel_id=1, replica_groups=mesh['group'=4,'shard'=8] {'shard'}, dimensions={1}, use_global_device_ids=true | all-gather | bytes 864000 | tf_op jit(solution)/shard_map/all_gather | solution.py:231
  65.1 23.5 %while.246 = (s32[]{:T(128)}, f32[4,1024,64]{1,0,2:T(4,128)S(1)}, s32[4,1024]{1,0:T(4,128)S(1)}, bf16[1024,64]{1,0:T(8,128)(2,1)S(1)}, bf16[1024,64]{1,0:T(8,128...) while((s32[]{:T(128)}, f32[4,1024,64]{1,0,2:T(4,128)S(1)}, ...), condition=%wide.region_1.2_spmd.clone, body=%wide.region_0.0_spmd.clone.sunk | while | flops 405929984 | bytes 2773085 | solution.py:100
  95.4 19.3 %while.254 = (s32[]{:T(128)}, f32[1024,64]{0,1:T(8,128)S(1)}, s32[4,1024]{1,0:T(4,128)S(1)}, bf16[4,1024,64]{2,1,0:T(8,128)(2,1)}, bf16[4,1024,64]{2,1,0:T(8,128...) while((s32[]{:T(128)}, f32[1024,64]{0,1:T(8,128)S(1)}, ...), condition=%wide.region_3.4_spmd.clone, body=%wide.region_2.3_spmd.clone.sunk | while | flops 406061056 | bytes 2380903 | solution.py:123
  117.5 20.6 %while.247 = (s32[]{:T(128)}, f32[4,1024,32]{1,0,2:T(4,128)S(1)}, s32[4,1024]{1,0:T(4,128)S(1)}, bf16[1024,32]{1,0:T(8,128)(2,1)S(1)}, bf16[1024,32]{1,0:T(8,128...) while((s32[]{:T(128)}, f32[4,1024,32]{1,0,2:T(4,128)S(1)}, ...), condition=%wide.region_5.6_spmd.clone, body=%wide.region_4.5_spmd.clone.sunk | while | flops 204537856 | bytes 1396829 | solution.py:100
  143.9 22.8 %while.255 = (s32[]{:T(128)}, f32[1024,32]{0,1:T(8,128)S(1)}, s32[4,1024]{1,0:T(4,128)S(1)}, bf16[4,1024,32]{2,1,0:T(8,128)(2,1)}, bf16[4,1024,32]{2,1,0:T(8,128...) while((s32[]{:T(128)}, f32[1024,32]{0,1:T(8,128)S(1)}, s32[4,1024]{1,0:T(4,128)S(1)}, ...), condition=%wide.region_7.8_spmd.clone, body=%wide.region_6.7_spmd.clone.sunk | while | flops 204603392 | bytes 1594979 | solution.py:123
  205.7 15.8 %all-to-all-done.3 = bf16[8,256,256]{2,1,0:T(8,128)(2,1)S(1)} async-done(((bf16[8,256,256]{2,1,0:T(8,128)(2,1)}), bf16[8,256,256]{2,1,0:T(8,128)(2,1)S(1)}, u32[]{:S(2)}, u32[]{:S(2)}) %all-to-all-start.3) | async-done | bytes 1048608 | tf_op jit(solution)/shard_map/all_to_all | solution.py:289
  231.7 16.1 %all-to-all-done.4 = bf16[8,256,256]{2,1,0:T(8,128)(2,1)} async-done(((bf16[8,256,256]{2,1,0:T(8,128)(2,1)}), bf16[8,256,256]{2,1,0:T(8,128)(2,1)}, u32[]{:S(2)}, u32[]{:S(2)}) %all-to-all-start.4) | async-done | bytes 1048608 | tf_op jit(solution)/shard_map/all_to_all | solution.py:288
  253.3 16.6 %while.249 = (s32[]{:T(128)}, f32[4,1024,32]{1,0,2:T(4,128)S(1)}, s32[4,1024]{1,0:T(4,128)S(1)}, bf16[1024,32]{1,0:T(8,128)(2,1)S(1)}, bf16[1024,32]{1,0:T(8,128...) while((s32[]{:T(128)}, f32[4,1024,32]{1,0,2:T(4,128)S(1)}, ...), condition=%wide.region_21.22_spmd.clone, body=%wide.region_20.21_spmd.clone.sunk | while | flops 204537856 | bytes 1396829 | solution.py:100
  274.7 21.8 %while.257 = (s32[]{:T(128)}, f32[1024,32]{0,1:T(8,128)S(1)}, s32[4,1024]{1,0:T(4,128)}, bf16[4,1024,32]{2,1,0:T(8,128)(2,1)S(1)}, bf16[4,1024,32]{2,1,0:T(8,128...) while((s32[]{:T(128)}, f32[1024,32]{0,1:T(8,128)S(1)}, s32[4,1024]{1,0:T(4,128)}, ...), condition=%wide.region_23.24_spmd.clone, body=%wide.region_22.23_spmd.clone.sunk | while | flops 204603392 | bytes 1594471 | solution.py:123
  298.3 23.5 %while.248 = (s32[]{:T(128)}, f32[4,1024,64]{1,0,2:T(4,128)S(1)}, s32[4,1024]{1,0:T(4,128)S(1)}, bf16[1024,64]{1,0:T(8,128)(2,1)S(1)}, bf16[1024,64]{1,0:T(8,128...) while((s32[]{:T(128)}, f32[4,1024,64]{1,0,2:T(4,128)S(1)}, ...), condition=%wide.region_17.18_spmd.clone, body=%wide.region_16.17_spmd.clone.sunk | while | flops 405929984 | bytes 2773085 | solution.py:100
  328.1 22.1 %while.256 = (s32[]{:T(128)}, f32[1024,64]{0,1:T(8,128)S(1)}, s32[4,1024]{1,0:T(4,128)}, bf16[4,1024,64]{2,1,0:T(8,128)(2,1)}, bf16[4,1024,64]{2,1,0:T(8,128)(2,...) while((s32[]{:T(128)}, f32[1024,64]{0,1:T(8,128)S(1)}, s32[4,1024]{1,0:T(4,128)}, ...), condition=%wide.region_19.20_spmd.clone, body=%wide.region_18.19_spmd.clone.sunk | while | flops 406061056 | bytes 2380903 | solution.py:123
  360.6 12.7 %all-to-all-done.5 = bf16[8,256,128]{2,1,0:T(8,128)(2,1)S(1)} async-done(((bf16[8,256,128]{2,1,0:T(8,128)(2,1)}), bf16[8,256,128]{2,1,0:T(8,128)(2,1)S(1)}, u32[]{:S(2)}, u32[]{:S(2)}) %all-to-all-start.5) | async-done | bytes 524320 | tf_op jit(solution)/shard_map/all_to_all | solution.py:272
  382.4 22.9 %all-to-all-done.6 = bf16[8,256,256]{2,1,0:T(8,128)(2,1)S(1)} async-done(((bf16[8,256,256]{2,1,0:T(8,128)(2,1)}), bf16[8,256,256]{2,1,0:T(8,128)(2,1)S(1)}, u32[]{:S(2)}, u32[]{:S(2)}) %all-to-all-start.6) | async-done | bytes 1048608 | tf_op jit(solution)/shard_map/all_to_all | solution.py:289
  412.1 22.8 %all-to-all-done.7 = bf16[8,256,256]{2,1,0:T(8,128)(2,1)} async-done(((bf16[8,256,256]{2,1,0:T(8,128)(2,1)}), bf16[8,256,256]{2,1,0:T(8,128)(2,1)}, u32[]{:S(2)}, u32[]{:S(2)}) %all-to-all-start.7) | async-done | bytes 1048608 | tf_op jit(solution)/shard_map/all_to_all | solution.py:288
  442.0 12.9 %while.258 = (s32[]{:T(128)}, f32[512,256]{1,0:T(8,128)S(1)}, s32[2,1024]{1,0:T(2,128)}, bf16[2,1024,256]{2,1,0:T(8,128)(2,1)S(1)}, bf16[2,1024,256]{2,1,0:T(8,1...) while((s32[]{:T(128)}, f32[512,256]{1,0:T(8,128)S(1)}, ...), condition=%wide.region_25.26_spmd.clone, body=%wide.region_24.25_spmd.clone.sunk | while | flops 807403520 | bytes 4756611 | solution.py:123
  455.7 60.2 %reduce-scatter.4.cloned.1.call-done = bf16[64,256]{1,0:T(8,128)(2,1)} async-done(((bf16[512,256]{1,0:T(8,128)(2,1)}), bf16[64,256]{1,0:T(8,128)(2,1)}) %reduce-scatter.4.cloned.1.call-update) | async-done | bytes 32784 | tf_op jit(solution)/shard_map/reduce_scatter | solution.py:349
  527.2 8.6 all-to-all-done.8
  543.3 27.6 %while.251 = (s32[]{:T(128)}, f32[4,1024,32]{1,0,2:T(4,128)S(1)}, s32[4,1024]{1,0:T(4,128)}, bf16[1024,32]{1,0:T(8,128)(2,1)}, bf16[1024,32]{1,0:T(8,128)(2,1)},...) while((s32[]{:T(128)}, f32[4,1024,32]{1,0,2:T(4,128)S(1)}, s32[4,1024]{1,0:T(4,128)}, ...), condition=%wide.region_32.33_spmd.clone, body=%wide.region_31.32_spmd.clone.sunk | while | flops 204537856 | bytes 1659001 | solution.py:100
  578.2 25.6 %while.260 = (s32[]{:T(128)}, f32[1024,32]{0,1:T(8,128)S(1)}, s32[4,1024]{1,0:T(4,128)}, bf16[4,1024,32]{2,1,0:T(8,128)(2,1)}, bf16[4,1024,32]{2,1,0:T(8,128)(2,...) while((s32[]{:T(128)}, f32[1024,32]{0,1:T(8,128)S(1)}, s32[4,1024]{1,0:T(4,128)}, ...), condition=%wide.region_34.35_spmd.clone, body=%wide.region_33.34_spmd.clone.sunk | while | flops 204603392 | bytes 1594979 | solution.py:123
  606.3 41.2 %while.250 = (s32[]{:T(128)}, f32[4,1024,64]{1,0,2:T(4,128)}, s32[4,1024]{1,0:T(4,128)}, bf16[1024,64]{1,0:T(8,128)(2,1)S(1)}, bf16[1024,64]{1,0:T(8,128)(2,1)S(...) while((s32[]{:T(128)}, f32[4,1024,64]{1,0,2:T(4,128)}, s32[4,1024]{1,0:T(4,128)}, ...), condition=%wide.region_28.29_spmd.clone, body=%wide.region_27.28_spmd.clone.sunk | while | flops 405929984 | bytes 2773085 | solution.py:100
  610.7 5.8 dynamic_update_slice.64
  658.0 23.2 %while.259 = (s32[]{:T(128)}, f32[1024,64]{0,1:T(8,128)S(1)}, s32[4,1024]{1,0:T(4,128)S(1)}, bf16[4,1024,64]{2,1,0:T(8,128)(2,1)}, bf16[4,1024,64]{2,1,0:T(8,128...) while((s32[]{:T(128)}, f32[1024,64]{0,1:T(8,128)S(1)}, ...), condition=%wide.region_30.31_spmd.clone, body=%wide.region_29.30_spmd.clone.sunk | while | flops 406061056 | bytes 2381411 | solution.py:123
  688.8 11.6 %while.261 = (s32[]{:T(128)}, f32[512,256]{1,0:T(8,128)S(1)}, s32[2,1024]{1,0:T(2,128)}, bf16[2,1024,256]{2,1,0:T(8,128)(2,1)S(1)}, bf16[2,1024,256]{2,1,0:T(8,1...) while((s32[]{:T(128)}, f32[512,256]{1,0:T(8,128)S(1)}, ...), condition=%wide.region_36.37_spmd.clone, body=%wide.region_35.36_spmd.clone.sunk | while | flops 807403520 | bytes 4740199 | solution.py:123
  708.5 53.2 %reduce-scatter.6.cloned.1.call-done = bf16[64,256]{1,0:T(8,128)(2,1)} async-done(((bf16[512,256]{1,0:T(8,128)(2,1)}), bf16[64,256]{1,0:T(8,128)(2,1)}) %reduce-scatter.6.cloned.1.call-update) | async-done | bytes 32784 | tf_op jit(solution)/shard_map/reduce_scatter | solution.py:349
  774.5 8.3 all-to-all-done.9
  792.5 19.5 %while.253 = (s32[]{:T(128)}, f32[4,1024,32]{1,0,2:T(4,128)S(1)}, s32[4,1024]{1,0:T(4,128)}, bf16[1024,32]{1,0:T(8,128)(2,1)S(1)}, bf16[1024,32]{1,0:T(8,128)(2,...) while((s32[]{:T(128)}, f32[4,1024,32]{1,0,2:T(4,128)S(1)}, ...), condition=%wide.region_43.44_spmd.clone, body=%wide.region_42.43_spmd.clone.sunk | while | flops 204537856 | bytes 1396829 | solution.py:100
  815.8 18.0 %while.263 = (s32[]{:T(128)}, f32[1024,32]{0,1:T(8,128)S(1)}, s32[4,1024]{1,0:T(4,128)}, bf16[4,1024,32]{2,1,0:T(8,128)(2,1)S(1)}, bf16[4,1024,32]{2,1,0:T(8,128...) while((s32[]{:T(128)}, f32[1024,32]{0,1:T(8,128)S(1)}, ...), condition=%wide.region_45.46_spmd.clone, body=%wide.region_44.45_spmd.clone.sunk | while | flops 204603392 | bytes 1593963 | solution.py:123
  836.5 26.4 %while.252 = (s32[]{:T(128)}, f32[4,1024,64]{1,0,2:T(4,128)S(1)}, s32[4,1024]{1,0:T(4,128)}, bf16[1024,64]{1,0:T(8,128)(2,1)S(1)}, bf16[1024,64]{1,0:T(8,128)(2,...) while((s32[]{:T(128)}, f32[4,1024,64]{1,0,2:T(4,128)S(1)}, ...), condition=%wide.region_39.40_spmd.clone, body=%wide.region_38.39_spmd.clone.sunk | while | flops 405929984 | bytes 2773085 | solution.py:100
  869.7 28.3 %while.262 = (s32[]{:T(128)}, f32[1024,64]{0,1:T(8,128)}, s32[4,1024]{1,0:T(4,128)S(1)}, bf16[4,1024,64]{2,1,0:T(8,128)(2,1)S(1)}, bf16[4,1024,64]{2,1,0:T(8,128...) while((s32[]{:T(128)}, f32[1024,64]{0,1:T(8,128)}, ...), condition=%wide.region_41.42_spmd.clone, body=%wide.region_40.41_spmd.clone.sunk | while | flops 406061056 | bytes 4494015 | solution.py:123
  902.5 61.4 %reduce-scatter.8.cloned.1.call-done = bf16[3000,16]{0,1:T(8,128)(2,1)} async-done(((bf16[3000,128]{0,1:T(8,128)(2,1)}), bf16[3000,16]{0,1:T(8,128)(2,1)}) %reduce-scatter.8.cloned.1.call-update) | async-done | bytes 96016 | tf_op jit(solution)/shard_map/reduce_scatter | solution.py:413
  964.9 31.5 %all-reduce.2.cloned.1.call-done = bf16[3000,16]{0,1:T(8,128)(2,1)} async-done(((bf16[3000,16]{0,1:T(8,128)(2,1)}), bf16[3000,16]{0,1:T(8,128)(2,1)}) %all-reduce.2.cloned.1.call-update) | async-done | bytes 96016 | tf_op jit(solution)/shard_map/psum | solution.py:416
  (990 shorter events, 625.1 us)
Async XLA Ops:
  7.2 83.0 %copy-start = (bf16[4096,16]{0,1:T(8,128)(2,1)S(1)}, bf16[4096,16]{0,1:T(8,128)(2,1)}, u32[]{:S(2)}) copy-start(bf16[4096,16]{0,1:T(8,128)(2,1)} %param.58) | copy-start | bytes 393220
  17.2 155.1 %all-to-all-start.1 = ((s32[8,1,256]{2,1,0:T(1,128)}), s32[8,1,256]{2,1,0:T(1,128)}, u32[]{:S(2)}, u32[]{:S(2)}) async-start(s32[8,1,256]{2,1,0:T(1,128)} %bitcast.18), calls=%async_computation.1 | async-start | bytes 16384 | tf_op jit(solution)/shard_map/all_to_all | solution.py:225
  58.0 625.7 %copy-start.7 = (bf16[3000,128]{0,1:T(8,128)(2,1)}, bf16[3000,128]{0,1:T(8,128)(2,1)S(1)}, u32[]{:S(2)}) copy-start(bf16[3000,128]{0,1:T(8,128)(2,1)S(1)} %all_gather.3) | copy-start | bytes 2304004
  172.3 15.7 %all-to-all-start.2 = ((bf16[8,256,128]{2,1,0:T(8,128)(2,1)}), bf16[8,256,128]{2,1,0:T(8,128)(2,1)S(1)}, u32[]{:S(2)}, u32[]{:S(2)}) async-start(bf16[8,256,128]{2,1,0:T(8,128)(2,1)} %bitcast.20), calls=%async_computation.2 | async-start | bytes 1048576 | tf_op jit(solution)/shard_map/all_to_all | solution.py:272
  188.0 10.4 %all-to-all-start = ((s32[8,1,256]{2,1,0:T(1,128)}), s32[8,1,256]{2,1,0:T(1,128)S(1)}, u32[]{:S(2)}, u32[]{:S(2)}) async-start(s32[8,1,256]{2,1,0:T(1,128)} %bitcast.11), calls=%async_computation | async-start | bytes 16384 | tf_op jit(solution)/shard_map/all_to_all | solution.py:226
  199.9 21.6 %all-to-all-start.3 = ((bf16[8,256,256]{2,1,0:T(8,128)(2,1)}), bf16[8,256,256]{2,1,0:T(8,128)(2,1)S(1)}, u32[]{:S(2)}, u32[]{:S(2)}) async-start(bf16[8,256,256]{2,1,0:T(8,128)(2,1)} %bitcast.22), calls=%async_computation.3 | async-start | bytes 2097152 | tf_op jit(solution)/shard_map/all_to_all | solution.py:289
  221.5 26.3 %all-to-all-start.4 = ((bf16[8,256,256]{2,1,0:T(8,128)(2,1)}), bf16[8,256,256]{2,1,0:T(8,128)(2,1)}, u32[]{:S(2)}, u32[]{:S(2)}) async-start(bf16[8,256,256]{2,1,0:T(8,128)(2,1)} %bitcast.24), calls=%async_computation.4 | async-start | bytes 2097152 | tf_op jit(solution)/shard_map/all_to_all | solution.py:288
  227.9 68.6 %copy-start.118 = (bf16[128,64]{1,0:T(8,128)(2,1)}, bf16[128,64]{1,0:T(8,128)(2,1)S(1)}, u32[]{:S(2)}) copy-start(bf16[128,64]{1,0:T(8,128)(2,1)S(1)} %reshape.457) | copy-start | bytes 49156
  356.6 16.7 %all-to-all-start.5 = ((bf16[8,256,128]{2,1,0:T(8,128)(2,1)}), bf16[8,256,128]{2,1,0:T(8,128)(2,1)S(1)}, u32[]{:S(2)}, u32[]{:S(2)}) async-start(bf16[8,256,128]{2,1,0:T(8,128)(2,1)} %bitcast.32), calls=%async_computation.5 | async-start | bytes 1048576 | tf_op jit(solution)/shard_map/all_to_all | solution.py:272
  376.1 29.1 %all-to-all-start.6 = ((bf16[8,256,256]{2,1,0:T(8,128)(2,1)}), bf16[8,256,256]{2,1,0:T(8,128)(2,1)S(1)}, u32[]{:S(2)}, u32[]{:S(2)}) async-start(bf16[8,256,256]{2,1,0:T(8,128)(2,1)} %bitcast.34), calls=%async_computation.6 | async-start | bytes 2097152 | tf_op jit(solution)/shard_map/all_to_all | solution.py:289
  405.3 29.7 %all-to-all-start.7 = ((bf16[8,256,256]{2,1,0:T(8,128)(2,1)}), bf16[8,256,256]{2,1,0:T(8,128)(2,1)}, u32[]{:S(2)}, u32[]{:S(2)}) async-start(bf16[8,256,256]{2,1,0:T(8,128)(2,1)} %bitcast.36), calls=%async_computation.7 | async-start | bytes 2097152 | tf_op jit(solution)/shard_map/all_to_all | solution.py:288
  409.5 106.4 %reduce-scatter.4.cloned.1.call-start = ((), (), s32[]{:S(2)}) async-start(), calls=%async_computation.13 | async-start | bytes 294912 | tf_op jit(solution)/shard_map/reduce_scatter | solution.py:349
  454.9 68.1 %copy-start.15 = (bf16[1024,128]{1,0:T(8,128)(2,1)S(1)}, bf16[1024,128]{1,0:T(8,128)(2,1)}, u32[]{:S(2)}) copy-start(bf16[1024,128]{1,0:T(8,128)(2,1)} %copy-done.14) | copy-start | bytes 786436
  454.9 68.1 %copy-start.80 = (bf16[1024,256]{1,0:T(8,128)(2,1)S(1)}, bf16[1024,256]{1,0:T(8,128)(2,1)}, u32[]{:S(2)}) copy-start(bf16[1024,256]{1,0:T(8,128)(2,1)} %copy-done.79) | copy-start | bytes 1572868
  454.9 69.2 %copy-start.32 = (bf16[1024,256]{1,0:T(8,128)(2,1)S(1)}, bf16[1024,256]{1,0:T(8,128)(2,1)}, u32[]{:S(2)}) copy-start(bf16[1024,256]{1,0:T(8,128)(2,1)} %copy-done.31) | copy-start | bytes 1572868
  455.7 69.5 %copy-start.144 = (f32[64,256]{1,0:T(8,128)S(1)}, f32[64,256]{1,0:T(8,128)}, u32[]{:S(2)}) copy-start(f32[64,256]{1,0:T(8,128)} %copy-done.143) | copy-start | bytes 196612
  455.7 69.5 %copy-start.145 = (bf16[64,256]{1,0:T(8,128)(2,1)S(1)}, bf16[64,256]{1,0:T(8,128)(2,1)}, u32[]{:S(2)}) copy-start(bf16[64,256]{1,0:T(8,128)(2,1)} %param.70) | copy-start | bytes 98308
  455.7 69.5 %copy-start.170 = (f32[64]{0:T(128)S(1)}, f32[64]{0:T(128)}, u32[]{:S(2)}) copy-start(f32[64]{0:T(128)} %copy-done.168) | copy-start | bytes 772
  519.2 16.6 %all-to-all-start.8 = ((bf16[8,256,128]{2,1,0:T(8,128)(2,1)}), bf16[8,256,128]{2,1,0:T(8,128)(2,1)S(1)}, u32[]{:S(2)}, u32[]{:S(2)}) async-start(bf16[8,256,128]{2,1,0:T(8,128)(2,1)} %bitcast.39), calls=%async_computation.9 | async-start | bytes 1048576 | tf_op jit(solution)/shard_map/all_to_all | solution.py:363
  522.9 238.7 %reduce-scatter.6.cloned.1.call-start = ((), (), s32[]{:S(2)}) async-start(), calls=%async_computation.14 | async-start | bytes 294912 | tf_op jit(solution)/shard_map/reduce_scatter | solution.py:349
  540.4 63.5 %copy-start.22 = (f32[1024,128]{1,0:T(8,128)}, f32[1024,128]{1,0:T(8,128)S(1)}, u32[]{:S(2)}) copy-start(f32[1024,128]{1,0:T(8,128)S(1)} %get-tuple-element.1627) | copy-start | bytes 1572868
  702.9 67.3 %copy-start.38 = (bf16[1024,64]{0,1:T(8,128)(2,1)S(1)}, bf16[1024,64]{0,1:T(8,128)(2,1)}, u32[]{:S(2)}) copy-start(bf16[1024,64]{0,1:T(8,128)(2,1)} %copy-done.37) | copy-start | bytes 393220
  705.3 66.0 %copy-start.4 = (f32[8,8,4,1024]{3,1,2,0:T(8,128)S(1)}, f32[8,8,4,1024]{3,1,2,0:T(8,128)}, u32[]{:S(2)}) copy-start(f32[8,8,4,1024]{3,1,2,0:T(8,128)} %copy-done.3) | copy-start | bytes 3145732
  705.3 66.0 %copy-start.6 = (f32[8,8,4,1024]{3,1,2,0:T(8,128)S(1)}, f32[8,8,4,1024]{3,1,2,0:T(8,128)}, u32[]{:S(2)}) copy-start(f32[8,8,4,1024]{3,1,2,0:T(8,128)} %copy-done.5) | copy-start | bytes 3145732
  765.6 17.2 %all-to-all-start.9 = ((bf16[8,256,128]{2,1,0:T(8,128)(2,1)}), bf16[8,256,128]{2,1,0:T(8,128)(2,1)}, u32[]{:S(2)}, u32[]{:S(2)}) async-start(bf16[8,256,128]{2,1,0:T(8,128)(2,1)} %bitcast.48), calls=%async_computation.11 | async-start | bytes 1048576 | tf_op jit(solution)/shard_map/all_to_all | solution.py:363
  769.9 193.9 %reduce-scatter.8.cloned.1.call-start = ((), (), s32[]{:S(2)}) async-start(), calls=%async_computation.15 | async-start | bytes 884736 | tf_op jit(solution)/shard_map/reduce_scatter | solution.py:413
  899.3 64.6 %copy-start.57 = (bf16[1024,32]{0,1:T(8,128)(2,1)S(1)}, bf16[1024,32]{0,1:T(8,128)(2,1)}, u32[]{:S(2)}) copy-start(bf16[1024,32]{0,1:T(8,128)(2,1)} %copy-done.56) | copy-start | bytes 196612
  899.3 64.6 %copy-start.114 = (bf16[128,32]{1,0:T(8,128)(2,1)S(1)}, bf16[128,32]{1,0:T(8,128)(2,1)}, u32[]{:S(2)}) copy-start(bf16[128,32]{1,0:T(8,128)(2,1)} %copy-done.113) | copy-start | bytes 24580
  902.1 94.3 %copy-start.53 = (f32[3000,16]{0,1:T(8,128)S(1)}, f32[3000,16]{0,1:T(8,128)}, u32[]{:S(2)}) copy-start(f32[3000,16]{0,1:T(8,128)} %param.71) | copy-start | bytes 576004
  902.1 94.3 %copy-start.100 = (f32[3000,16]{0,1:T(8,128)S(1)}, f32[3000,16]{0,1:T(8,128)}, u32[]{:S(2)}) copy-start(f32[3000,16]{0,1:T(8,128)} %param.72) | copy-start | bytes 576004
  902.1 94.3 %copy-start.101 = (f32[3000,16]{0,1:T(8,128)S(1)}, f32[3000,16]{0,1:T(8,128)}, u32[]{:S(2)}) copy-start(f32[3000,16]{0,1:T(8,128)} %param.73) | copy-start | bytes 576004
  902.1 94.3 %all-reduce.2.cloned.1.call-start = ((), (), s32[]{:S(2)}) async-start(), calls=%async_computation.16 | async-start | bytes 196608 | tf_op jit(solution)/shard_map/psum | solution.py:416
  (168 other events, 1770.4 us)
Sparse Core Ops, SparseCore 0:
  455.8 60.0 reduce-scatter.3
  701.3 60.3 reduce-scatter.5
  902.3 61.5 reduce-scatter.7
  966.1 30.2 all-reduce.1
where the time goes:
time: 1010 us
  matrix products  371 us (37%)
  waiting for transfers between devices  321 us (32%)
  local copies, waits for them, and re-layouts  192 us (19%)
  starting transfers between devices  45 us (4%)
  blocking collectives  32.6 us (3%)
  other arithmetic  22.3 us (2%)
  between operations  16.6 us (2%)
    dot_general x138, matrix products, rows_inner(): lax.dot_general(left_side, right_side, (((0,), (0,)), ((), ())), preferre...  213 us
    dot_general x126, matrix products, matmul(): return jnp.dot(left_side, right_side, preferred_element_type=jnp.float32)  148 us
    reduce_scatter x2, waiting for transfers between devices, per_device(): lax.psum_scatter(table_grad.astype(jnp.bfloat16), 'shard', scatter_dimens...  113 us
    dynamic_update_slice x64, local copies, waits for them, and re-layouts, pick_rows(): lax.map(pick_block, indices.reshape(row_total // block_rows, block_rows))  72 us
    reduce_scatter x1, waiting for transfers between devices, per_device(): lax.psum_scatter(grad_flat.astype(jnp.bfloat16), 'shard', scatter_dimensi...  61.4 us
    unnamed x392, local copies, waits for them, and re-layouts  49.5 us
    all_to_all x2, waiting for transfers between devices, per_device(): lax.all_to_all(rows_dst, 'shard', split_axis=0, concat_axis=0, tiled=True)  38.9 us
    all_to_all x2, waiting for transfers between devices, per_device(): lax.all_to_all(rows_src, 'shard', split_axis=0, concat_axis=0, tiled=True)  38.7 us
  transfers between devices with their start and end apart: 14, of which 13 were waited for; matrix products, arithmetic and copies ran while one was open for 15% of the time, Pallas kernels for 0%

commit v1 on v0

v1 whole, which is shorter than its diff:
```python
import functools

import jax
import jax.numpy as jnp
from jax import lax
from jax.experimental import pallas as pl
from jax.experimental.pallas import tpu as pltpu
from jax.sharding import PartitionSpec as P

D_EDGE = 128
D_ATOM = 256
D_TRI = 64
D_QUAD = 32
D_BASIS = 16
BLOCKS = 2
FOLD = 256
CHUNK = 1024
SMALL = 220
BIG = 1280
PAD = 256

edge_scale = 0.25
pair_scale = 0.5
beta_one = 0.5
beta_two = 0.5
learn_rate = 0.1
decay_rate = 0.01
epsilon = 1e-08
adam_step = 4

OFF_DOWN = {D_TRI: 0, D_QUAD: 136}
OFF_BASIS = {D_TRI: 64, D_QUAD: 168}
OFF_UP = {D_TRI: 72, D_QUAD: 172}
OFF_RADIAL = 204

F32 = jnp.float32
BF16 = jnp.bfloat16


def sds(shape, dtype):
    return jax.ShapeDtypeStruct(shape, dtype)


def call(body, outs, args, flops=10**9, smem=0):
    space = [pltpu.SMEM] * smem + [pltpu.VMEM] * (len(args) - smem)
    return pl.pallas_call(
        body,
        out_shape=outs,
        in_specs=[pl.BlockSpec(memory_space=s) for s in space],
        out_specs=[pl.BlockSpec(memory_space=pltpu.VMEM)] * len(outs),
        compiler_params=pltpu.CompilerParams(vmem_limit_bytes=40 * 2**20),
        cost_estimate=pl.CostEstimate(flops=flops, bytes_accessed=4 * 2**20, transcendentals=0),
        name=body.func.__name__ if isinstance(body, functools.partial) else body.__name__,
    )(*args)


def dot(a, b):
    return jnp.dot(a, b, preferred_element_type=F32)


def dot_nt(a, b):
    return lax.dot_general(a, b, (((1,), (1,)), ((), ())), preferred_element_type=F32)


def low(v):
    return v.astype(BF16)


def iota(shape, axis):
    return lax.broadcasted_iota(jnp.int32, shape, axis)


def ones_where(mask):
    return jnp.where(mask, 1.0, 0.0).astype(BF16)


def onehot(count, row, first=0):
    return ones_where(iota((count, row.shape[1]), 0) + first == row)


def sigmoid(v):
    return 1.0 / (1.0 + jnp.exp(-v))


def silu_pair(v):
    s = sigmoid(v)
    return v * s, s * (1.0 + v * (1.0 - s))


def cut(value, width):
    count = FOLD // width
    length = value.shape[1] // count
    return jnp.concatenate([value[:, g * length : (g + 1) * length] for g in range(count)], axis=0)


def uncut(value, width):
    count = FOLD // width
    return jnp.concatenate([value[g * width : (g + 1) * width] for g in range(count)], axis=1)


def pick(folded, high, width):
    result = folded[:width]
    for g in range(1, FOLD // width):
        result = jnp.where(high == g, folded[g * width : (g + 1) * width], result)
    return result


def spread(value, high, width):
    return jnp.concatenate(
        [low(jnp.where(high == g, value, 0.0)) for g in range(FOLD // width)], axis=0
    )


def high_low(index, length):
    return index // length, index % length


def small_t(raw, offset, width, columns):
    count = 128 // width
    total = None
    for p in range(count):
        lane, d = iota((PAD, columns), 0), iota((PAD, columns), 1)
        sel = ones_where((d % count == p) & (lane == offset + d // count))
        part = dot(raw[p * width : (p + 1) * width], sel)
        total = part if total is None else total + part
    return low(total)


def small_plain(raw, offset, width, rows):
    count = 128 // width
    total = None
    for p in range(count):
        d, lane = iota((rows, PAD), 0), iota((rows, PAD), 1)
        sel = ones_where((d % count == p) & (lane == offset + d // count))
        part = dot_nt(sel, raw[p * width : (p + 1) * width])
        total = part if total is None else total + part
    return low(total)


def wide_t(raw, offset, rows):
    lane, d = iota((PAD, rows), 0), iota((PAD, rows), 1)
    return low(dot(raw, ones_where(lane == offset + d)))


def wide_plain(raw, offset, rows):
    d, lane = iota((rows, PAD), 0), iota((rows, PAD), 1)
    return low(dot_nt(ones_where(lane == offset + d), raw))


def double_plain(raw, rows):
    d, lane = iota((rows, 2 * rows), 0), iota((rows, 2 * rows), 1)
    return jnp.concatenate(
        [low(dot_nt(ones_where(lane == 2 * d + p), raw)) for p in range(2)], axis=1
    )


def put_small(grad_t, offset, width):
    count = 128 // width
    columns = grad_t.shape[1]
    value = low(grad_t)
    parts = []
    for p in range(count):
        d, lane = iota((columns, PAD), 0), iota((columns, PAD), 1)
        sel = ones_where((d % count == p) & (lane == offset + d // count))
        parts.append(dot(value, sel))
    return jnp.concatenate(parts, axis=0)


def put_wide(grad_t, offset):
    columns = grad_t.shape[1]
    d, lane = iota((columns, PAD), 0), iota((columns, PAD), 1)
    return dot(low(grad_t), ones_where(lane == offset + d))


def put_double(grad_t):
    rows = grad_t.shape[1]
    d, lane = iota((rows, 2 * rows), 0), iota((rows, 2 * rows), 1)
    value = low(grad_t)
    return low(
        dot(value[:128], ones_where(lane == 2 * d)) + dot(value[128:], ones_where(lane == 2 * d + 1))
    )


def pair_forward(edge_t, basis_ref, in_ref, out_ref, raw, width, xg_ref, bt_ref, kept_row):
    edges = edge_t.shape[1]
    length = edges * width // FOLD
    down_t = small_t(raw, OFF_DOWN[width], width, D_EDGE)
    basis_t = small_t(raw, OFF_BASIS[width], width, D_BASIS)
    up_t = wide_t(raw, OFF_UP[width], width)
    act, slope_in = silu_pair(dot(down_t, edge_t))
    table = cut(low(act), width)
    total = jnp.zeros((FOLD, length), F32)
    rows = pl.ds(kept_row, width)
    items = in_ref.shape[1]
    chunk = min(CHUNK, items)
    for start in range(0, items, chunk):
        cols = pl.ds(start, chunk)
        in_high, in_low = high_low(in_ref[:, cols], length)
        out_high, out_low = high_low(out_ref[:, cols], length)
        xg = pick(dot(table, onehot(length, in_low)), in_high, width)
        bt = dot(basis_t, basis_ref[:, cols])
        xg_ref[rows, cols] = low(xg)
        bt_ref[rows, cols] = low(bt)
        total = total + dot_nt(spread(xg * bt, out_high, width), onehot(length, out_low))
    agg_t = low(uncut(total, width) * pair_scale)
    value, slope_out = silu_pair(dot(up_t, agg_t))
    return value, slope_in, agg_t, slope_out


def pair_backward(
    grad_mid, edge_t, basis_ref, in_ref, out_ref, raw, width, xg_ref, bt_ref, kept_row,
    slope_in, agg_t, slope_out,
):
    edges = edge_t.shape[1]
    length = edges * width // FOLD
    up = wide_plain(raw, OFF_UP[width], width)
    down = small_plain(raw, OFF_DOWN[width], width, D_EDGE)
    grad_out = low(grad_mid * slope_out)
    grad_up_t = dot_nt(grad_out, agg_t)
    table = cut(low(dot(up, grad_out) * pair_scale), width)
    total = jnp.zeros((FOLD, length), F32)
    grad_basis_t = jnp.zeros((width, D_BASIS), F32)
    rows = pl.ds(kept_row, width)
    items = in_ref.shape[1]
    chunk = min(CHUNK, items)
    for start in range(0, items, chunk):
        cols = pl.ds(start, chunk)
        in_high, in_low = high_low(in_ref[:, cols], length)
        out_high, out_low = high_low(out_ref[:, cols], length)
        gy = pick(dot(table, onehot(length, out_low)), out_high, width)
        grad_bt = low(gy * xg_ref[rows, cols].astype(F32))
        grad_basis_t = grad_basis_t + dot_nt(grad_bt, basis_ref[:, cols])
        moved = gy * bt_ref[rows, cols].astype(F32)
        total = total + dot_nt(spread(moved, in_high, width), onehot(length, in_low))
    grad_in = low(uncut(total, width) * slope_in)
    grad_down_t = dot_nt(grad_in, edge_t)
    small = (
        put_small(grad_down_t, OFF_DOWN[width], width)
        + put_small(grad_basis_t, OFF_BASIS[width], width)
        + put_wide(grad_up_t, OFF_UP[width])
    )
    return dot(down, grad_in), small


def block_forward(
    state_t, raw, radial_basis, tri_basis, quad_basis, tri_in, tri_out, quad_in, quad_out, dst_row,
    atoms, out_refs,
):
    edge_ref, mid_ref, slope_in_ref, agg_ref, slope_out_ref, xg_ref, bt_ref, table_ref = out_refs
    edge_t = low(state_t)
    edge_ref[...] = edge_t
    tri, s_in, agg, s_out = pair_forward(
        edge_t, tri_basis, tri_in, tri_out, raw, D_TRI, xg_ref, bt_ref, 0
    )
    slope_in_ref[:D_TRI] = low(s_in)
    agg_ref[:D_TRI] = agg
    slope_out_ref[:D_EDGE] = low(s_out)
    quad, s_in, agg, s_out = pair_forward(
        edge_t, quad_basis, quad_in, quad_out, raw, D_QUAD, xg_ref, bt_ref, D_TRI
    )
    slope_in_ref[D_TRI:] = low(s_in)
    agg_ref[D_TRI:] = agg
    slope_out_ref[D_EDGE:] = low(s_out)
    mid = state_t + tri + quad
    mid_ref[...] = mid
    radial = dot(wide_t(raw, OFF_RADIAL, D_BASIS), radial_basis[...])
    message = low(mid * radial)
    step = min(512, atoms)
    for start in range(0, atoms, step):
        table_ref[pl.ds(start, step)] = low(
            dot_nt(onehot(step, dst_row[...], start), message)
        )


def kept_shapes(edges, items, atoms):
    return [
        sds((D_EDGE, edges), BF16),
        sds((D_EDGE, edges), F32),
        sds((D_TRI + D_QUAD, edges), BF16),
        sds((D_TRI + D_QUAD, edges), BF16),
        sds((2 * D_EDGE, edges), BF16),
        sds((D_TRI + D_QUAD, items), BF16),
        sds((D_TRI + D_QUAD, items), BF16),
        sds((atoms, D_EDGE), BF16),
    ]


def first_half(
    edge_state, raw, radial_basis, tri_basis, quad_basis, tri_in, tri_out, quad_in, quad_out, dst_row,
    *out_refs,
):
    eye = ones_where(iota((D_EDGE, D_EDGE), 0) == iota((D_EDGE, D_EDGE), 1))
    state_t = dot_nt(eye, edge_state[...])
    atoms = out_refs[-1].shape[0]
    block_forward(
        state_t, raw[...], radial_basis, tri_basis, quad_basis, tri_in, tri_out, quad_in, quad_out,
        dst_row, atoms, out_refs,
    )


def atom_forward(near, far, state, free, big):
    atom_in = low((near[...].astype(F32) + far[...].astype(F32)) * edge_scale)
    first = double_plain(big[:, :256], D_EDGE)
    second = double_plain(big[:, 256:768], D_ATOM)
    act, slope = silu_pair(dot(atom_in, first))
    hidden = low(act)
    new_state = state + free * dot(hidden, second)
    return atom_in, hidden, slope, new_state


def edge_pre(sent, big, src_row, dst_row):
    src_t = low(dot_nt(big[:, 768:1024], sent))
    dst_t = low(dot_nt(big[:, 1024:1280], sent))
    atoms = sent.shape[0]
    step = min(512, atoms)
    total = None
    for start in range(0, atoms, step):
        part = dot(src_t[:, start : start + step], onehot(step, src_row[...], start))
        part = part + dot(dst_t[:, start : start + step], onehot(step, dst_row[...], start))
        total = part if total is None else total + part
    return total


def middle_half(
    near, far, atom_pack, big, mid_in, raw, radial_basis, tri_basis, quad_basis, tri_in, tri_out,
    quad_in, quad_out, src_row, dst_row,
    atom_in_ref, hidden_ref, slope_atom_ref, state_ref, free_ref, slope_edge_ref, *out_refs,
):
    owners = atom_pack.shape[0]
    count = state_ref.shape[0] // owners
    eye = iota((count, count), 0) == iota((count, count), 1)
    for s in range(owners):
        rows = pl.ds(s * count, count)
        state_ref[rows] = atom_pack[s, :count].astype(F32)
        flag = atom_pack[s, count : count + 1, :count].astype(F32)
        column = jnp.sum(jnp.where(eye, flag, 0.0), axis=1, keepdims=True)
        free_ref[rows] = low(jnp.broadcast_to(column, (count, D_ATOM)))
    atom_in, hidden, slope, state = atom_forward(
        near, far, state_ref[...], free_ref[...].astype(F32), big[...]
    )
    atom_in_ref[...] = atom_in
    hidden_ref[...] = hidden
    slope_atom_ref[...] = low(slope)
    state_ref[...] = state
    act, slope_edge = silu_pair(edge_pre(low(state), big[...], src_row, dst_row))
    slope_edge_ref[...] = low(slope_edge)
    block_forward(
        mid_in[...] + act, raw[...], radial_basis, tri_basis, quad_basis, tri_in, tri_out, quad_in,
        quad_out, dst_row, state.shape[0], out_refs,
    )


def edge_tables(
    grad_pre, sent, big, src_row, dst_row, free, slope_atom, own, own_row,
    part_ref, gain_ref, grad_proj_ref, scratch,
):
    atoms = sent.shape[0]
    count = own.shape[0]
    step = min(512, atoms)
    src_t, dst_t = big[:, 768:1024], big[:, 1024:1280]
    grad_src = jnp.zeros((D_EDGE, D_ATOM), F32)
    grad_dst = jnp.zeros((D_EDGE, D_ATOM), F32)
    for start in range(0, atoms, step):
        rows = pl.ds(start, step)
        pick_src = onehot(step, src_row[...], start)
        pick_dst = onehot(step, dst_row[...], start)
        sent_here = sent[start : start + step]
        grad_src = grad_src + dot(low(dot_nt(grad_pre, pick_src)), sent_here)
        grad_dst = grad_dst + dot(low(dot_nt(grad_pre, pick_dst)), sent_here)
        part = dot(low(dot_nt(pick_src, grad_pre)), src_t) + dot(low(dot_nt(pick_dst, grad_pre)), dst_t)
        part_ref[rows] = low(part)
        scratch[rows] = part
    grad_proj_ref[:, :D_ATOM] = low(grad_src)
    grad_proj_ref[:, D_ATOM:] = low(grad_dst)
    mine = pl.ds(pl.multiple_of(own_row, count), count)
    scratch[mine] = scratch[mine] + own
    first = double_plain(big[:, :256], D_EDGE)
    second = double_plain(big[:, 256:768], D_ATOM)
    pushed = dot_nt(low(scratch[...] * free), second) * slope_atom
    gain_ref[...] = low(dot_nt(first, low(pushed)))


def turn(
    me, near, far, state_in, free_ref, big, mid_in, src_row, dst_row, edge_cotangent, own,
    atom_in_ref, hidden_ref, slope_atom_ref, edge_out_ref, atom_out_ref, grad_ref, part_ref,
    gain_ref, grad_proj_ref, scratch, hold,
):
    free = free_ref[...].astype(F32)
    atom_in, hidden, slope, state = atom_forward(near, far, state_in[...], free, big[...])
    atom_in_ref[...] = atom_in
    hidden_ref[...] = hidden
    slope_atom_ref[...] = low(slope)
    sent = low(state)
    hold[...] = state
    count = atom_out_ref.shape[0]
    own_row = me[0] * count
    atom_out_ref[...] = low(hold[pl.ds(pl.multiple_of(own_row, count), count)])
    act, slope_edge = silu_pair(edge_pre(sent, big[...], src_row, dst_row))
    edge_out_ref[...] = low(jnp.transpose(mid_in[...] + act))
    eye = ones_where(iota((D_EDGE, D_EDGE), 0) == iota((D_EDGE, D_EDGE), 1))
    grad = dot_nt(eye, edge_cotangent[...])
    grad_ref[...] = grad
    edge_tables(
        low(grad * slope_edge), sent, big[...], src_row, dst_row, free, slope,
        own[...].astype(F32), own_row, part_ref, gain_ref, grad_proj_ref, scratch,
    )


def block_backward(
    near, far, grad_in, mid, raw, radial_basis, tri_basis, quad_basis, tri_in, tri_out, quad_in,
    quad_out, dst_row, edge_t, slope_in, agg, slope_out, xg_ref, bt_ref, small_ref,
):
    gain_t = low(near[...].astype(F32) + far[...].astype(F32))
    atoms = gain_t.shape[1]
    step = min(512, atoms)
    grad_message = None
    for start in range(0, atoms, step):
        part = dot(gain_t[:, start : start + step], onehot(step, dst_row[...], start))
        grad_message = part if grad_message is None else grad_message + part
    grad_message = grad_message * edge_scale
    weights = raw[...]
    radial = dot(wide_t(weights, OFF_RADIAL, D_BASIS), radial_basis[...])
    grad_mid = grad_in[...] + grad_message * radial
    grad_radial = low(grad_message * mid[...])
    small = put_wide(dot_nt(grad_radial, radial_basis[...]), OFF_RADIAL)
    tri, more = pair_backward(
        grad_mid, edge_t[...], tri_basis, tri_in, tri_out, weights, D_TRI, xg_ref, bt_ref, 0,
        slope_in[:D_TRI].astype(F32), agg[:D_TRI], slope_out[:D_EDGE].astype(F32),
    )
    small = small + more
    quad, more = pair_backward(
        grad_mid, edge_t[...], quad_basis, quad_in, quad_out, weights, D_QUAD, xg_ref, bt_ref, D_TRI,
        slope_in[D_TRI:].astype(F32), agg[D_TRI:], slope_out[D_EDGE:].astype(F32),
    )
    small_ref[...] = low(small + more)
    return grad_mid + tri + quad


def back_pairs(*refs):
    *rest, small_ref, grad_ref = refs
    grad_ref[...] = block_backward(*rest, small_ref)


def back_last(*refs):
    *rest, small_ref, grad_ref = refs
    grad_ref[...] = jnp.transpose(block_backward(*rest, small_ref))


def atom_sums(me, arrived, own, free, hidden, slope_atom, atom_in, grad_proj, big, grad_ref, out_ref):
    owners, count, width = arrived.shape
    total = own[...].astype(F32)
    for s in range(owners):
        total = total + arrived[s].astype(F32)
    grad_ref[...] = total
    mine = pl.ds(pl.multiple_of(me[0] * count, count), count)
    update = total * free[mine].astype(F32)
    second = double_plain(big[:, 256:768], D_ATOM)
    pushed = dot_nt(low(update), second) * slope_atom[mine].astype(F32)
    grad_second_t = dot(low(jnp.transpose(update)), hidden[mine])
    grad_first_t = dot(low(jnp.transpose(pushed)), atom_in[mine])
    out_ref[:, :256] = put_double(grad_first_t)
    out_ref[:, 256:768] = put_double(grad_second_t)
    out_ref[:, 768:] = grad_proj[...]


def back_tables(
    me, grad, slope_edge, state, big, src_row, dst_row, free_ref, slope_atom, own,
    part_ref, gain_ref, grad_proj_ref, scratch,
):
    grad_pre = low(grad[...] * slope_edge[...].astype(F32))
    edge_tables(
        grad_pre, low(state[...]), big[...], src_row, dst_row, free_ref[...].astype(F32),
        slope_atom[...].astype(F32), own[...], me[0] * own.shape[0], part_ref, gain_ref, grad_proj_ref,
        scratch,
    )


def shard_sum(arrived, out_ref):
    total = arrived[0].astype(F32)
    for s in range(1, arrived.shape[0]):
        total = total + arrived[s].astype(F32)
    out_ref[...] = low(total)


def adam(arrived, weights, first, second, grad_ref, weights_ref, first_ref, second_ref, low_ref):
    total = arrived[0].astype(F32)
    for s in range(1, arrived.shape[0]):
        total = total + arrived[s].astype(F32)
    grad = jnp.concatenate(
        [
            total[:, :SMALL],
            total[:, PAD : PAD + BIG],
            total[:, PAD + BIG : PAD + BIG + SMALL],
            total[:, 2 * PAD + BIG :],
        ],
        axis=1,
    )
    grad_ref[...] = grad
    old = weights[...]
    new_first = beta_one * first[...] + (1.0 - beta_one) * grad
    new_second = beta_two * second[...] + (1.0 - beta_two) * grad * grad
    first_ref[...] = new_first
    second_ref[...] = new_second
    first_hat = new_first / (1.0 - beta_one**adam_step)
    second_hat = new_second / (1.0 - beta_two**adam_step)
    new = old - learn_rate * (first_hat / (jnp.sqrt(second_hat) + epsilon) + decay_rate * old)
    weights_ref[...] = new
    low_ref[...] = low(new)


def call_scratch(body, outs, args, scratch, flops=10**9):
    return pl.pallas_call(
        body,
        out_shape=outs,
        in_specs=[pl.BlockSpec(memory_space=pltpu.SMEM)]
        + [pl.BlockSpec(memory_space=pltpu.VMEM)] * (len(args) - 1),
        out_specs=[pl.BlockSpec(memory_space=pltpu.VMEM)] * len(outs),
        scratch_shapes=[pltpu.VMEM(s, F32) for s in scratch],
        compiler_params=pltpu.CompilerParams(vmem_limit_bytes=40 * 2**20),
        cost_estimate=pl.CostEstimate(flops=flops, bytes_accessed=4 * 2**20, transcendentals=0),
        name=body.__name__,
    )(*args)


def to_all(value, owners):
    return lax.all_to_all(
        jnp.broadcast_to(value[None], (owners,) + value.shape), "shard", split_axis=0, concat_axis=0
    )


def sum_pair(table, owners):
    far = None
    step = 1
    while step < owners:
        if far is not None:
            table = table + far
        far = lax.ppermute(table, "shard", [(i, i ^ step) for i in range(owners)])
        step = 2 * step
    return table, far


def per_device(
    edge_state, atom_state, radial_basis, triplet_basis, quad_basis, dst_owner, dst_local, src_owner,
    src_local, triplet_in, triplet_out, quad_in, quad_out, fixed_atoms, edge_cotangent,
    atom_cotangent, weights, first_moment, second_moment,
):
    owners = lax.axis_size("shard")
    edges = edge_state.shape[0]
    count = atom_state.shape[0]
    atoms = count * owners
    items = triplet_in.shape[0]
    me = lax.axis_index("shard").astype(jnp.int32).reshape(1)
    weights_t = jnp.transpose(weights)
    low_t = weights_t.astype(BF16)
    cols = low_t.shape[0]
    half = SMALL + BIG
    gap = ((0, 0), (0, PAD - SMALL))
    small_one = jnp.pad(low_t[:, :SMALL], gap)
    rest = jnp.concatenate(
        [low_t[:, SMALL:half], jnp.pad(low_t[:, half : half + SMALL], gap), low_t[:, half + SMALL :]],
        axis=1,
    )
    raw_one = to_all(small_one, owners).reshape(owners * cols, PAD)
    rest = to_all(rest, owners).reshape(owners * cols, 2 * BIG + PAD)
    big_one, raw_two, big_two = rest[:, :BIG], rest[:, BIG : BIG + PAD], rest[:, BIG + PAD :]
    flag = jnp.zeros((16, D_ATOM), BF16).at[0, :count].set((1 - fixed_atoms).astype(BF16))
    atom_pack = to_all(jnp.concatenate([atom_state, flag], axis=0), owners)

    dst_row = (dst_owner[:, 0] * count + dst_local).reshape(1, edges)
    src_row = (src_owner[:, 0] * count + src_local).reshape(1, edges)
    graph = [
        jnp.transpose(radial_basis),
        jnp.transpose(triplet_basis),
        jnp.transpose(quad_basis),
        triplet_in.reshape(1, items),
        triplet_out.reshape(1, items),
        quad_in.reshape(1, items),
        quad_out.reshape(1, items),
    ]
    kept = kept_shapes(edges, items, atoms)
    edge_shape = sds((D_EDGE, edges), BF16)
    atom_shapes = [
        sds((atoms, D_EDGE), BF16),
        sds((atoms, D_ATOM), BF16),
        sds((atoms, D_ATOM), BF16),
    ]
    *kept_one, table = call(
        first_half, kept, [edge_state, raw_one] + graph + [dst_row], flops=8 * 10**9
    )
    near, far = sum_pair(table, owners)
    atom_in_one, hidden_one, slope_one, state_one, free, slope_edge_one, *kept_two, table = call(
        middle_half,
        atom_shapes + [sds((atoms, D_ATOM), F32), sds((atoms, D_ATOM), BF16), edge_shape] + kept,
        [near, far, atom_pack, big_one, kept_one[1], raw_two] + graph + [src_row, dst_row],
        flops=10 * 10**9,
    )
    near, far = sum_pair(table, owners)
    tables_shape = [
        sds((atoms, D_ATOM), BF16),
        sds((D_EDGE, atoms), BF16),
        sds((D_EDGE, 2 * D_ATOM), BF16),
    ]
    (
        atom_in_two, hidden_two, slope_two, edge_out, atom_out, grad_t, part, gain, grad_proj_two,
    ) = call_scratch(
        turn,
        atom_shapes
        + [sds((edges, D_EDGE), BF16), sds((count, D_ATOM), BF16), sds((D_EDGE, edges), F32)]
        + tables_shape,
        [me, near, far, state_one, free, big_two, kept_two[1], src_row, dst_row, edge_cotangent,
         atom_cotangent],
        [(atoms, D_ATOM), (atoms, D_ATOM)],
        flops=2 * 10**9,
    )

    def summed(part):
        return lax.all_to_all(
            part.reshape(owners, count, D_ATOM), "shard", split_axis=0, concat_axis=0
        )

    def backward(body, near, far, grad_t, kept, raw, out):
        edge_t, mid, slope_in, agg, slope_out, xg, bt = kept
        return call(
            body,
            [sds((D_EDGE, PAD), BF16), out],
            [near, far, grad_t, mid, raw]
            + graph
            + [dst_row, edge_t, slope_in, agg, slope_out, xg, bt],
            flops=10 * 10**9,
        )

    def sums(part, own, hidden, slope, atom_in, grad_proj, big):
        return call(
            atom_sums,
            [sds((count, D_ATOM), F32), sds((D_EDGE, BIG), BF16)],
            [me, summed(part), own, free, hidden, slope, atom_in, grad_proj, big],
            flops=10**9,
            smem=1,
        )

    near, far = sum_pair(gain, owners)
    grad_atom, grad_big_two = sums(
        part, atom_cotangent, hidden_two, slope_two, atom_in_two, grad_proj_two, big_two
    )
    grad_small_two, grad_t = backward(
        back_pairs, near, far, grad_t, kept_two, raw_two, sds((D_EDGE, edges), F32)
    )
    part, gain, grad_proj_one = call_scratch(
        back_tables,
        tables_shape,
        [me, grad_t, slope_edge_one, state_one, big_one, src_row, dst_row, free, slope_one, grad_atom],
        [(atoms, D_ATOM)],
        flops=2 * 10**9,
    )
    near, far = sum_pair(gain, owners)
    grad_atom, grad_big_one = sums(
        part, grad_atom, hidden_one, slope_one, atom_in_one, grad_proj_one, big_one
    )
    grad_small_one, grad_edge = backward(
        back_last, near, far, grad_t, kept_one, raw_one, sds((edges, D_EDGE), F32)
    )
    grads = jnp.concatenate([grad_small_one, grad_big_one, grad_small_two, grad_big_two], axis=1)
    grads = lax.all_to_all(
        grads.reshape(owners, cols, 2 * (PAD + BIG)), "shard", split_axis=0, concat_axis=0
    )
    [grads] = call(shard_sum, [sds((cols, 2 * (PAD + BIG)), BF16)], [grads], flops=10**8)
    grads = lax.all_gather(grads, "group", axis=0)
    rows = weights.shape[0]
    results = call(
        adam,
        [sds((cols, rows), F32)] * 4 + [sds((cols, rows), BF16)],
        [grads, weights_t, jnp.transpose(first_moment), jnp.transpose(second_moment)],
        flops=10**8,
    )
    return (edge_out, atom_out, grad_edge, grad_atom) + tuple(jnp.transpose(r) for r in results)


def solution(mesh):
    both = P(("group", "shard"), None)
    line = P(("group", "shard"))
    flat = P(None, "shard")
    in_specs = (both,) * 6 + (line, both) + (line,) * 6 + (both, both) + (flat,) * 3
    out_specs = (both,) * 4 + (flat,) * 5
    return jax.shard_map(
        per_device, mesh=mesh, in_specs=in_specs, out_specs=out_specs, check_vma=False
    )
```

time: 1010 us -> 192 us (0.19)
  matrix products: 371 us -> 0 us
  waiting for transfers between devices: 321 us -> 59.2 us
  local copies, waits for them, and re-layouts: 192 us -> 32.4 us
  Pallas kernels: 0 us -> 33.8 us
  other arithmetic: 22.3 us -> 2.01 us
  between operations: 16.6 us -> 1.11 us
    dot_general x278 -> x0, matrix products: 371 us -> none  [the longest x138 213 us: rows_inner(): lax.dot_general(left_side, right_side, (((0,), (0,)), ((), ())), preferre...]
    reduce_scatter x3 -> x0, waiting for transfers between devices: 175 us -> none  [the longest x2 113 us: per_device(): lax.psum_scatter(table_grad.astype(jnp.bfloat16), 'shard', scatter_dimens...]
    all_to_all x10 -> x5, waiting for transfers between devices: 115 us -> 7.75 us  [the longest x3 7.75 us: to_all(): lax.all_to_all(jnp.broadcast_to(value[None], (owners,) + value.shape), 's...]
    dynamic_update_slice x64 -> x0, local copies, waits for them, and re-layouts: 72 us -> none  [pick_rows(): lax.map(pick_block, indices.reshape(row_total // block_rows, block_rows))]
    ppermute x0 -> x12, waiting for transfers between devices: none -> 51.4 us  [sum_pair(): far = lax.ppermute(table, 'shard', [(i, i ^ step) for i in range(owners)])]
    pallas_call x0 -> x10, Pallas kernels: none -> 33.8 us  [the longest x8 26.5 us: call(): pl.pallas_call(body, out_shape=outs, in_specs=[pl.BlockSpec(memory_space=...]
    psum x1 -> x0, waiting for transfers between devices: 31.5 us -> none  [per_device(): weight_grad = lax.psum(grad_local, 'group').astype(jnp.float32)]
    dynamic_slice x68 -> x0, local copies, waits for them, and re-layouts: 26.8 us -> none  [the longest x64 24 us: pick_rows(): lax.map(pick_block, indices.reshape(row_total // block_rows, block_rows))]
  transfers between devices with their start and end apart: 14 -> 17, of which waited for: 13 -> 13; matrix products, arithmetic and copies ran while one was open for 15% -> 1% of each run, Pallas kernels for 0% -> 9%
where the time goes in v1:
time: 192 us; the launch traced here: 190 us
  waiting for transfers between devices  59.2 us (31%)
  starting transfers between devices  37.4 us (19%)
  Pallas kernels  33.8 us (18%)
  local copies, waits for them, and re-layouts  32.4 us (17%)
  blocking collectives  24.4 us (13%)
  other arithmetic  2.01 us (1%)
    ppermute x12, waiting for transfers between devices, sum_pair(): far = lax.ppermute(table, 'shard', [(i, i ^ step) for i in range(owners)])  51.4 us
    unnamed x118, local copies, waits for them, and re-layouts  29.9 us
    pallas_call x8, Pallas kernels, call(): pl.pallas_call(body, out_shape=outs, in_specs=[pl.BlockSpec(memory_space=...  26.5 us
    all_to_all x1, blocking collectives, per_device(): lax.all_to_all(grads.reshape(owners, cols, 2 * (PAD + BIG)), 'shard', spl...  17.7 us
    all_to_all x3, starting transfers between devices, to_all(): lax.all_to_all(jnp.broadcast_to(value[None], (owners,) + value.shape), 's...  15 us
    ppermute x12, starting transfers between devices, sum_pair(): far = lax.ppermute(table, 'shard', [(i, i ^ step) for i in range(owners)])  13.6 us
    all_to_all x2, starting transfers between devices, summed(): lax.all_to_all(part.reshape(owners, count, D_ATOM), 'shard', split_axis=0...  8.81 us
    all_to_all x3, waiting for transfers between devices, to_all(): lax.all_to_all(jnp.broadcast_to(value[None], (owners,) + value.shape), 's...  7.75 us
  transfers between devices with their start and end apart: 17, of which 13 were waited for; matrix products, arithmetic and copies ran while one was open for 1% of the time, Pallas kernels for 9%

profile of v1, /device:TPU:0, one launch (start us, length us, event | category | flops | bytes accessed | tf_op | source)
XLA Modules:
  0.0 190.2 jit_solution(16205647731815740962)
XLA Ops:
  2.9 7.3 %all-to-all-start = ((bf16[8,16,256]{2,1,0:T(8,128)(2,1)}), bf16[8,16,256]{2,1,0:T(8,128)(2,1)S(1)}, u32[]{:S(2)}, u32[]{:S(2)}) async-start(bf16[8,16,256]{2,1,0:T(8,128)(2,1)} %broadcast_in_dim.6), calls=%async_computation | async-start | bytes 131072 | tf_op jit(solution)/shard_map/all_to_all | solution.py:526
  10.3 6.7 %all-to-all-done = bf16[8,16,256]{2,1,0:T(8,128)(2,1)S(1)} async-done(((bf16[8,16,256]{2,1,0:T(8,128)(2,1)}), bf16[8,16,256]{2,1,0:T(8,128)(2,1)S(1)}, u32[]{:S(2)}, u32[]{:S(2)}) %all-to-all-start) | async-done | bytes 65568 | tf_op jit(solution)/shard_map/all_to_all | solution.py:526
  18.0 3.7 %all-to-all-start.2 = ((bf16[8,16,2816]{2,1,0:T(8,128)(2,1)}), bf16[8,16,2816]{2,1,0:T(8,128)(2,1)S(1)}, u32[]{:S(2)}, u32[]{:S(2)}) async-start(bf16[8,16,2816]{2,1,0:T(8,128)(2,1)} %broadcast_in_dim.8), calls=%async_computation.2 | async-start | bytes 1441792 | tf_op jit(solution)/shard_map/all_to_all | solution.py:526
  21.9 5.3 %first_half.1 = (bf16[128,1024]{1,0:T(8,128)(2,1)S(1)}, f32[128,1024]{1,0:T(8,128)S(1)}, bf16[96,1024]{1,0:T(8,128)(2,1)S(1)}, bf16[96,1024]{1,0:T(8,128)(2,1)S(...) custom-call(bf16[1024,128]{1,0:T(8,128)(2,1)S(1)} %copy-done.3, ...), custom_call_target="tpu_custom_call" | custom-call | flops 8000000000 | bytes 4194304 | tf_op jit(solution)/shard_map/first_half/pallas_call | solution.py:46
  31.3 2.0 %collective-permute-start = (bf16[512,128]{1,0:T(8,128)(2,1)S(1)}, bf16[512,128]{1,0:T(8,128)(2,1)S(1)}, u32[]{:S(2)}, u32[]{:S(2)}) collective-permute-start(bf16[512,128]{1,0:T(8,128)(2,1)S(1)} %get-tuple-element.68), channel_id=1, source_target_pairs={{0,1},{1,0},{2,3},{3,2},{4,5},{5,4},{6,7},{7,6},{8,9},{9,8},{10,11... | collective-permute-start | bytes 393224 | tf_op jit(solution)/shard_map/ppermute | solution.py:537
  33.3 4.0 %collective-permute-done = bf16[512,128]{1,0:T(8,128)(2,1)S(1)} collective-permute-done((bf16[512,128]{1,0:T(8,128)(2,1)S(1)}, bf16[512,128]{1,0:T(8,128)(2,1)S(1)}, u32[]{:S(2)}, u32[]{:S(2)}) %collective-permute-start) | collective-permute-done | bytes 131104 | tf_op jit(solution)/shard_map/ppermute | solution.py:537
  40.1 4.0 %all-to-all-start.1 = ((bf16[8,80,256]{2,1,0:T(8,128)(2,1)}), bf16[8,80,256]{2,1,0:T(8,128)(2,1)S(1)}, u32[]{:S(2)}, u32[]{:S(2)}) async-start(bf16[8,80,256]{2,1,0:T(8,128)(2,1)} %broadcast_in_dim.7), calls=%async_computation.1 | async-start | bytes 655360 | tf_op jit(solution)/shard_map/all_to_all | solution.py:526
  44.3 3.0 %collective-permute-start.2 = (bf16[512,128]{1,0:T(8,128)(2,1)S(1)}, bf16[512,128]{1,0:T(8,128)(2,1)S(1)}, u32[]{:S(2)}, u32[]{:S(2)}) collective-permute-start(bf16[512,128]{1,0:T(8,128)(2,1)S(1)} %add.38.near), channel_id=1, source_target_pairs={{0,4},{1,5},{2,6},{3,7},{4,0},{5,1},{6,2},{7,3},{8,12},{9,13},{10,... | collective-permute-start | bytes 393224 | tf_op jit(solution)/shard_map/ppermute | solution.py:537
  47.3 11.8 %collective-permute-done.2.far = bf16[512,128]{1,0:T(8,128)(2,1)S(1)} collective-permute-done((bf16[512,128]{1,0:T(8,128)(2,1)S(1)}, bf16[512,128]{1,0:T(8,128)(2,1)S(1)}, u32[]{:S(2)}, u32[]{:S(2)}) %collective-permute-start.2) | collective-permute-done | bytes 131104 | tf_op jit(solution)/shard_map/ppermute | solution.py:537
  60.2 6.6 %middle_half.1 = (bf16[512,128]{1,0:T(8,128)(2,1)S(1)}, bf16[512,256]{1,0:T(8,128)(2,1)S(1)}, bf16[512,256]{1,0:T(8,128)(2,1)S(1)}, f32[512,256]{1,0:T(8,128)S(1...) custom-call(bf16[512,128]{1,0:T(8,128)(2,1)S(1)} %add.38.near, ...), custom_call_target="tpu_custom_call" | custom-call | flops 10000000000 | bytes 4194304 | tf_op jit(solution)/shard_map/middle_half/pallas_call | solution.py:46
  72.9 1.5 collective-permute-start.3
  74.4 3.5 %collective-permute-done.3 = bf16[512,128]{1,0:T(8,128)(2,1)S(1)} collective-permute-done((bf16[512,128]{1,0:T(8,128)(2,1)S(1)}, bf16[512,128]{1,0:T(8,128)(2,1)S(1)}, u32[]{:S(2)}, u32[]{:S(2)}) %collective-permute-start.3) | collective-permute-done | bytes 131104 | tf_op jit(solution)/shard_map/ppermute | solution.py:537
  78.0 5.0 %collective-permute-done.4 = bf16[512,128]{1,0:T(8,128)(2,1)S(1)} collective-permute-done((bf16[512,128]{1,0:T(8,128)(2,1)S(1)}, bf16[512,128]{1,0:T(8,128)(2,1)S(1)}, u32[]{:S(2)}, u32[]{:S(2)}) %collective-permute-start.4) | collective-permute-done | bytes 131104 | tf_op jit(solution)/shard_map/ppermute | solution.py:537
  83.1 7.1 %collective-permute-done.5.far = bf16[512,128]{1,0:T(8,128)(2,1)S(1)} collective-permute-done((bf16[512,128]{1,0:T(8,128)(2,1)S(1)}, bf16[512,128]{1,0:T(8,128)(2,1)S(1)}, u32[]{:S(2)}, u32[]{:S(2)}) %collective-permute-start.5) | collective-permute-done | bytes 131104 | tf_op jit(solution)/shard_map/ppermute | solution.py:537
  92.3 4.6 %turn.1 = (bf16[512,128]{1,0:T(8,128)(2,1)S(1)}, bf16[512,256]{1,0:T(8,128)(2,1)S(1)}, bf16[512,256]{1,0:T(8,128)(2,1)S(1)}, bf16[1024,128]{1,0:T(8,128)(2,1)}, ...) custom-call(s32[1]{0:T(128)} %bitcast.me, ...), custom_call_target="tpu_custom_call" | custom-call | flops 2000000000 | bytes 4194304 | tf_op jit(solution)/shard_map/turn/pallas_call | solution.py:512
  97.7 1.2 collective-permute-start.6
  99.0 3.7 %collective-permute-done.6 = bf16[128,512]{1,0:T(8,128)(2,1)S(1)} collective-permute-done((bf16[128,512]{1,0:T(8,128)(2,1)S(1)}, bf16[128,512]{1,0:T(8,128)(2,1)S(1)}, u32[]{:S(2)}, u32[]{:S(2)}) %collective-permute-start.6) | collective-permute-done | bytes 131104 | tf_op jit(solution)/shard_map/ppermute | solution.py:537
  102.8 5.2 %collective-permute-done.7 = bf16[128,512]{1,0:T(8,128)(2,1)S(1)} collective-permute-done((bf16[128,512]{1,0:T(8,128)(2,1)S(1)}, bf16[128,512]{1,0:T(8,128)(2,1)S(1)}, u32[]{:S(2)}, u32[]{:S(2)}) %collective-permute-start.7) | collective-permute-done | bytes 131104 | tf_op jit(solution)/shard_map/ppermute | solution.py:537
  108.3 5.4 %all-to-all-start.3 = ((bf16[8,64,256]{2,1,0:T(8,128)(2,1)}), bf16[8,64,256]{2,1,0:T(8,128)(2,1)S(1)}, u32[]{:S(2)}, u32[]{:S(2)}) async-start(bf16[8,64,256]{2,1,0:T(8,128)(2,1)} %bitcast.16), calls=%async_computation.3 | async-start | bytes 524288 | tf_op jit(solution)/shard_map/all_to_all | solution.py:617
  116.8 1.1 copy-done.31
  122.9 5.1 %back_pairs.1 = (bf16[128,256]{1,0:T(8,128)(2,1)S(1)}, f32[128,1024]{1,0:T(8,128)S(1)}) custom-call(bf16[128,512]{1,0:T(8,128)(2,1)S(1)} %add.43.refs_0_, bf16[128,512]{1,0:T(8,128)(2,1)S(1)} %collective-permute-done.8.refs_1_, f32[128,1024]{1,0:T(8,128)S(1)} %copy-done.23, f32[128,1024]{1,0:T(8,128)S(1)} %copy-done.21, ...), custom_call_target="tpu_custom_call" | custom-call | flops 10000000000 | bytes 4194304 | tf_op jit(solution)/shard_map/back_pairs/pallas_call | solution.py:46
  130.1 2.7 %back_tables.1 = (bf16[512,256]{1,0:T(8,128)(2,1)}, bf16[128,512]{1,0:T(8,128)(2,1)S(1)}, bf16[128,512]{1,0:T(8,128)(2,1)S(1)}) custom-call(s32[1]{0:T(128)} %bitcast.me, f32[128,1024]{1,0:T(8,128)S(1)} %copy-done.17, bf16[128,1024]{1,0:T(8,128)(2,1)S(1)} %copy-done.25, f32[512,256]{1,0:T(8,128)S(1)} %copy-done.15, ...), custom_call_target="tpu_custom_call" | custom-call | flops 2000000000 | bytes 4194304 | tf_op jit(solution)/shard_map/back_tables/pallas_call | solution.py:512
  132.8 1.6 collective-permute-start.9
  134.4 3.4 %collective-permute-done.9 = bf16[128,512]{1,0:T(8,128)(2,1)S(1)} collective-permute-done((bf16[128,512]{1,0:T(8,128)(2,1)S(1)}, bf16[128,512]{1,0:T(8,128)(2,1)S(1)}, u32[]{:S(2)}, u32[]{:S(2)}) %collective-permute-start.9) | collective-permute-done | bytes 131104 | tf_op jit(solution)/shard_map/ppermute | solution.py:537
  138.9 5.4 %collective-permute-done.10 = bf16[128,512]{1,0:T(8,128)(2,1)S(1)} collective-permute-done((bf16[128,512]{1,0:T(8,128)(2,1)S(1)}, bf16[128,512]{1,0:T(8,128)(2,1)S(1)}, u32[]{:S(2)}, u32[]{:S(2)}) %collective-permute-start.10) | collective-permute-done | bytes 131104 | tf_op jit(solution)/shard_map/ppermute | solution.py:537
  144.3 1.7 collective-permute-start.11
  146.1 3.4 %all-to-all-start.4 = ((bf16[8,64,256]{2,1,0:T(8,128)(2,1)}), bf16[8,64,256]{2,1,0:T(8,128)(2,1)S(1)}, u32[]{:S(2)}, u32[]{:S(2)}) async-start(bf16[8,64,256]{2,1,0:T(8,128)(2,1)} %bitcast.17), calls=%async_computation.4 | async-start | bytes 524288 | tf_op jit(solution)/shard_map/all_to_all | solution.py:617
  149.5 1.4 collective-permute-done.11.refs_1_
  157.2 6.0 %back_last.1 = (bf16[128,256]{1,0:T(8,128)(2,1)S(1)}, f32[1024,128]{1,0:T(8,128)}) custom-call(bf16[128,512]{1,0:T(8,128)(2,1)S(1)} %add.45.refs_0_, bf16[128,512]{1,0:T(8,128)(2,1)S(1)} %collective-permute-done.11.refs_1_, f32[128,1024]{1,0:T(8,128)S(1)} %copy-done.18, f32[128,1024]{1,0:T(8,128)S(1)} %copy-done.36, bf16[128,256]{1,0:T(8,128)(2,1)S(1)} %bitcast.34, ...), custom_call_target="tpu_custom_call" | custom-call | flops 10000000000 | bytes 4194304 | tf_op jit(solution)/shard_map/back_last/pallas_call | solution.py:46
  163.2 1.4 atom_sums.3
  164.6 17.7 %all_to_all.30.arrived = bf16[8,16,3072]{2,1,0:T(8,128)(2,1)S(1)} all-to-all(bf16[8,16,3072]{2,1,0:T(8,128)(2,1)S(1)} %bitcast.72), channel_id=1, replica_groups=mesh['group'=4,'shard'=8] {'shard'}, dimensions={0} | all-to-all | bytes 1572864 | tf_op jit(solution)/shard_map/all_to_all | solution.py:663
  182.4 6.7 %all-gather = bf16[64,3072]{1,0:T(8,128)(2,1)S(1)} all-gather(bf16[16,3072]{1,0:T(8,128)(2,1)S(1)} %shard_sum.1), channel_id=2, replica_groups=mesh['group'=4,'shard'=8] {'group'}, dimensions={0}, use_global_device_ids=true | all-gather | bytes 491520 | tf_op jit(solution)/shard_map/all_gather | solution.py:667
  (157 shorter events, 40.0 us)
Async XLA Ops:
  2.9 14.2 %all-to-all-start = ((bf16[8,16,256]{2,1,0:T(8,128)(2,1)}), bf16[8,16,256]{2,1,0:T(8,128)(2,1)S(1)}, u32[]{:S(2)}, u32[]{:S(2)}) async-start(bf16[8,16,256]{2,1,0:T(8,128)(2,1)} %broadcast_in_dim.6), calls=%async_computation | async-start | bytes 131072 | tf_op jit(solution)/shard_map/all_to_all | solution.py:526
  18.0 3.8 %copy-start.6 = (bf16[4096,16]{0,1:T(8,128)(2,1)S(1)}, bf16[4096,16]{0,1:T(8,128)(2,1)}, u32[]{:S(2)}) copy-start(bf16[4096,16]{0,1:T(8,128)(2,1)} %param.25) | copy-start | bytes 393220
  18.0 21.3 %all-to-all-start.2 = ((bf16[8,16,2816]{2,1,0:T(8,128)(2,1)}), bf16[8,16,2816]{2,1,0:T(8,128)(2,1)S(1)}, u32[]{:S(2)}, u32[]{:S(2)}) async-start(bf16[8,16,2816]{2,1,0:T(8,128)(2,1)} %broadcast_in_dim.8), calls=%async_computation.2 | async-start | bytes 1441792 | tf_op jit(solution)/shard_map/all_to_all | solution.py:526
  21.9 11.4 %copy-start.58 = (s32[64]{0:T(128)S(1)}, s32[64]{0:T(128)}, u32[]{:S(2)}) copy-start(s32[64]{0:T(128)} %param.34) | copy-start | bytes 772
  21.9 11.4 %copy-start.53 = (bf16[64,256]{1,0:T(8,128)(2,1)S(1)}, bf16[64,256]{1,0:T(8,128)(2,1)}, u32[]{:S(2)}) copy-start(bf16[64,256]{1,0:T(8,128)(2,1)} %param.22) | copy-start | bytes 98308
  31.2 6.1 %copy-start.41 = (bf16[128,1024]{1,0:T(8,128)(2,1)}, bf16[128,1024]{1,0:T(8,128)(2,1)S(1)}, u32[]{:S(2)}) copy-start(bf16[128,1024]{1,0:T(8,128)(2,1)S(1)} %get-tuple-element.94.refs_13_) | copy-start | bytes 786436
  31.2 6.1 %copy-start.45 = (bf16[96,1024]{1,0:T(8,128)(2,1)}, bf16[96,1024]{1,0:T(8,128)(2,1)S(1)}, u32[]{:S(2)}) copy-start(bf16[96,1024]{1,0:T(8,128)(2,1)S(1)} %get-tuple-element.95.refs_14_) | copy-start | bytes 589828
  31.2 12.9 %copy-start.57 = (s32[1024,1]{0,1:T(1,128)S(1)}, s32[1024,1]{0,1:T(1,128)}, u32[]{:S(2)}) copy-start(s32[1024,1]{0,1:T(1,128)} %param.28) | copy-start | bytes 12292
  31.3 12.9 %copy-start.55 = (s32[1024]{0:T(1024)S(1)}, s32[1024]{0:T(1024)}, u32[]{:S(2)}) copy-start(s32[1024]{0:T(1024)} %param.29) | copy-start | bytes 12292
  31.3 6.0 %collective-permute-start = (bf16[512,128]{1,0:T(8,128)(2,1)S(1)}, bf16[512,128]{1,0:T(8,128)(2,1)S(1)}, u32[]{:S(2)}, u32[]{:S(2)}) collective-permute-start(bf16[512,128]{1,0:T(8,128)(2,1)S(1)} %get-tuple-element.68), channel_id=1, source_target_pairs={{0,1},{1,0},{2,3},{3,2},{4,5},{5,4},{6,7},{7,6},{8,9},{9,8},{10,11... | collective-permute-start | bytes 393224 | tf_op jit(solution)/shard_map/ppermute | solution.py:537
  37.3 6.9 %collective-permute-start.1 = (bf16[512,128]{1,0:T(8,128)(2,1)S(1)}, bf16[512,128]{1,0:T(8,128)(2,1)S(1)}, u32[]{:S(2)}, u32[]{:S(2)}) collective-permute-start(bf16[512,128]{1,0:T(8,128)(2,1)S(1)} %add.37), channel_id=1, source_target_pairs={{0,2},{1,3},{2,0},{3,1},{4,6},{5,7},{6,4},{7,5},{8,10},{9,11},{10,... | collective-permute-start | bytes 393224 | tf_op jit(solution)/shard_map/ppermute | solution.py:537
  40.1 19.0 %all-to-all-start.1 = ((bf16[8,80,256]{2,1,0:T(8,128)(2,1)}), bf16[8,80,256]{2,1,0:T(8,128)(2,1)S(1)}, u32[]{:S(2)}, u32[]{:S(2)}) async-start(bf16[8,80,256]{2,1,0:T(8,128)(2,1)} %broadcast_in_dim.7), calls=%async_computation.1 | async-start | bytes 655360 | tf_op jit(solution)/shard_map/all_to_all | solution.py:526
  44.3 14.9 %collective-permute-start.2 = (bf16[512,128]{1,0:T(8,128)(2,1)S(1)}, bf16[512,128]{1,0:T(8,128)(2,1)S(1)}, u32[]{:S(2)}, u32[]{:S(2)}) collective-permute-start(bf16[512,128]{1,0:T(8,128)(2,1)S(1)} %add.38.near), channel_id=1, source_target_pairs={{0,4},{1,5},{2,6},{3,7},{4,0},{5,1},{6,2},{7,3},{8,12},{9,13},{10,... | collective-permute-start | bytes 393224 | tf_op jit(solution)/shard_map/ppermute | solution.py:537
  72.9 17.3 %copy-start.13 = (f32[512,256]{1,0:T(8,128)}, f32[512,256]{1,0:T(8,128)S(1)}, u32[]{:S(2)}) copy-start(f32[512,256]{1,0:T(8,128)S(1)} %get-tuple-element.71.state_in.state) | copy-start | bytes 1572868
  72.9 17.3 %copy-start.4 = (bf16[1024,128]{1,0:T(8,128)(2,1)S(1)}, bf16[1024,128]{1,0:T(8,128)(2,1)}, u32[]{:S(2)}) copy-start(bf16[1024,128]{1,0:T(8,128)(2,1)} %edge_cotangent.1) | copy-start | bytes 786436
  72.9 17.3 %copy-start.7 = (bf16[64,256]{1,0:T(8,128)(2,1)S(1)}, bf16[64,256]{1,0:T(8,128)(2,1)}, u32[]{:S(2)}) copy-start(bf16[64,256]{1,0:T(8,128)(2,1)} %own.3) | copy-start | bytes 98308
  72.9 5.0 %collective-permute-start.3 = (bf16[512,128]{1,0:T(8,128)(2,1)S(1)}, bf16[512,128]{1,0:T(8,128)(2,1)S(1)}, u32[]{:S(2)}, u32[]{:S(2)}) collective-permute-start(bf16[512,128]{1,0:T(8,128)(2,1)S(1)} %get-tuple-element.70), channel_id=1, source_target_pairs={{0,1},{1,0},{2,3},{3,2},{4,5},{5,4},{6,7},{7,6},{8,9},{9,8},{10,11... | collective-permute-start | bytes 393224 | tf_op jit(solution)/shard_map/ppermute | solution.py:537
  77.9 5.1 %collective-permute-start.4 = (bf16[512,128]{1,0:T(8,128)(2,1)S(1)}, bf16[512,128]{1,0:T(8,128)(2,1)S(1)}, u32[]{:S(2)}, u32[]{:S(2)}) collective-permute-start(bf16[512,128]{1,0:T(8,128)(2,1)S(1)} %add.40), channel_id=1, source_target_pairs={{0,2},{1,3},{2,0},{3,1},{4,6},{5,7},{6,4},{7,5},{8,10},{9,11},{10,... | collective-permute-start | bytes 393224 | tf_op jit(solution)/shard_map/ppermute | solution.py:537
  83.0 7.2 %collective-permute-start.5 = (bf16[512,128]{1,0:T(8,128)(2,1)S(1)}, bf16[512,128]{1,0:T(8,128)(2,1)S(1)}, u32[]{:S(2)}, u32[]{:S(2)}) collective-permute-start(bf16[512,128]{1,0:T(8,128)(2,1)S(1)} %add.41.near), channel_id=1, source_target_pairs={{0,4},{1,5},{2,6},{3,7},{4,0},{5,1},{6,2},{7,3},{8,12},{9,13},{10,... | collective-permute-start | bytes 393224 | tf_op jit(solution)/shard_map/ppermute | solution.py:537
  97.7 5.0 %collective-permute-start.6 = (bf16[128,512]{1,0:T(8,128)(2,1)S(1)}, bf16[128,512]{1,0:T(8,128)(2,1)S(1)}, u32[]{:S(2)}, u32[]{:S(2)}) collective-permute-start(bf16[128,512]{1,0:T(8,128)(2,1)S(1)} %get-tuple-element.76), channel_id=1, source_target_pairs={{0,1},{1,0},{2,3},{3,2},{4,5},{5,4},{6,7},{7,6},{8,9},{9,8},{10,11... | collective-permute-start | bytes 393224 | tf_op jit(solution)/shard_map/ppermute | solution.py:537
  102.7 5.3 %collective-permute-start.7 = (bf16[128,512]{1,0:T(8,128)(2,1)S(1)}, bf16[128,512]{1,0:T(8,128)(2,1)S(1)}, u32[]{:S(2)}, u32[]{:S(2)}) collective-permute-start(bf16[128,512]{1,0:T(8,128)(2,1)S(1)} %add.42), channel_id=1, source_target_pairs={{0,2},{1,3},{2,0},{3,1},{4,6},{5,7},{6,4},{7,5},{8,10},{9,11},{10,... | collective-permute-start | bytes 393224 | tf_op jit(solution)/shard_map/ppermute | solution.py:537
  108.1 6.7 %collective-permute-start.8 = (bf16[128,512]{1,0:T(8,128)(2,1)S(1)}, bf16[128,512]{1,0:T(8,128)(2,1)S(1)}, u32[]{:S(2)}, u32[]{:S(2)}) collective-permute-start(bf16[128,512]{1,0:T(8,128)(2,1)S(1)} %add.43.refs_0_), channel_id=1, source_target_pairs={{0,4},{1,5},{2,6},{3,7},{4,0},{5,1},{6,2},{7,3},{8,12},{9,13},{10,... | collective-permute-start | bytes 393224 | tf_op jit(solution)/shard_map/ppermute | solution.py:537
  108.3 20.5 %all-to-all-start.3 = ((bf16[8,64,256]{2,1,0:T(8,128)(2,1)}), bf16[8,64,256]{2,1,0:T(8,128)(2,1)S(1)}, u32[]{:S(2)}, u32[]{:S(2)}) async-start(bf16[8,64,256]{2,1,0:T(8,128)(2,1)} %bitcast.16), calls=%async_computation.3 | async-start | bytes 524288 | tf_op jit(solution)/shard_map/all_to_all | solution.py:617
  132.8 18.0 %copy-start.42 = (bf16[128,1024]{1,0:T(8,128)(2,1)S(1)}, bf16[128,1024]{1,0:T(8,128)(2,1)}, u32[]{:S(2)}) copy-start(bf16[128,1024]{1,0:T(8,128)(2,1)} %copy-done.41) | copy-start | bytes 786436
  132.8 18.0 %copy-start.46 = (bf16[96,1024]{1,0:T(8,128)(2,1)S(1)}, bf16[96,1024]{1,0:T(8,128)(2,1)}, u32[]{:S(2)}) copy-start(bf16[96,1024]{1,0:T(8,128)(2,1)} %copy-done.45) | copy-start | bytes 589828
  132.8 5.0 %collective-permute-start.9 = (bf16[128,512]{1,0:T(8,128)(2,1)S(1)}, bf16[128,512]{1,0:T(8,128)(2,1)S(1)}, u32[]{:S(2)}, u32[]{:S(2)}) collective-permute-start(bf16[128,512]{1,0:T(8,128)(2,1)S(1)} %get-tuple-element.93), channel_id=1, source_target_pairs={{0,1},{1,0},{2,3},{3,2},{4,5},{5,4},{6,7},{7,6},{8,9},{9,8},{10,11... | collective-permute-start | bytes 393224 | tf_op jit(solution)/shard_map/ppermute | solution.py:537
  137.8 6.4 %collective-permute-start.10 = (bf16[128,512]{1,0:T(8,128)(2,1)S(1)}, bf16[128,512]{1,0:T(8,128)(2,1)S(1)}, u32[]{:S(2)}, u32[]{:S(2)}) collective-permute-start(bf16[128,512]{1,0:T(8,128)(2,1)S(1)} %add.44), channel_id=1, source_target_pairs={{0,2},{1,3},{2,0},{3,1},{4,6},{5,7},{6,4},{7,5},{8,10},{9,11},{10,... | collective-permute-start | bytes 393224 | tf_op jit(solution)/shard_map/ppermute | solution.py:537
  144.3 6.5 %collective-permute-start.11 = (bf16[128,512]{1,0:T(8,128)(2,1)S(1)}, bf16[128,512]{1,0:T(8,128)(2,1)S(1)}, u32[]{:S(2)}, u32[]{:S(2)}) collective-permute-start(bf16[128,512]{1,0:T(8,128)(2,1)S(1)} %add.45.refs_0_), channel_id=1, source_target_pairs={{0,4},{1,5},{2,6},{3,7},{4,0},{5,1},{6,2},{7,3},{8,12},{9,13},{10,... | collective-permute-start | bytes 393224 | tf_op jit(solution)/shard_map/ppermute | solution.py:537
  146.1 17.1 %all-to-all-start.4 = ((bf16[8,64,256]{2,1,0:T(8,128)(2,1)}), bf16[8,64,256]{2,1,0:T(8,128)(2,1)S(1)}, u32[]{:S(2)}, u32[]{:S(2)}) async-start(bf16[8,64,256]{2,1,0:T(8,128)(2,1)} %bitcast.17), calls=%async_computation.4 | async-start | bytes 524288 | tf_op jit(solution)/shard_map/all_to_all | solution.py:617
  182.3 6.8 %copy-start = (f32[3000,16]{0,1:T(8,128)S(1)}, f32[3000,16]{0,1:T(8,128)}, u32[]{:S(2)}) copy-start(f32[3000,16]{0,1:T(8,128)} %param.37) | copy-start | bytes 576004
  182.3 6.8 %copy-start.1 = (f32[3000,16]{0,1:T(8,128)S(1)}, f32[3000,16]{0,1:T(8,128)}, u32[]{:S(2)}) copy-start(f32[3000,16]{0,1:T(8,128)} %param.38) | copy-start | bytes 576004
  182.3 6.8 %copy-start.2 = (f32[3000,16]{0,1:T(8,128)S(1)}, f32[3000,16]{0,1:T(8,128)}, u32[]{:S(2)}) copy-start(f32[3000,16]{0,1:T(8,128)} %param.39) | copy-start | bytes 576004
  (44 other events, 67.3 us)

commit v2 on v1

v2 whole, which is shorter than its diff:
```python
import jax
import jax.numpy as jnp
from jax import lax
from jax.experimental import pallas as pl
from jax.experimental.pallas import tpu as pltpu
from jax.sharding import PartitionSpec as P

D_EDGE = 128
D_ATOM = 256
D_TRI = 64
D_QUAD = 32
D_BASIS = 16
BLOCKS = 2
FOLD = 256
CHUNK = 1024
SMALL = 220
BIG = 1280
PAD = 256
ROWS = 16

edge_scale = 0.25
pair_scale = 0.5
beta_one = 0.5
beta_two = 0.5
learn_rate = 0.1
decay_rate = 0.01
epsilon = 1e-08
adam_step = 4

OFF_DOWN = {D_TRI: 0, D_QUAD: 136}
OFF_BASIS = {D_TRI: 64, D_QUAD: 168}
OFF_UP = {D_TRI: 72, D_QUAD: 172}
OFF_RADIAL = 204

F32 = jnp.float32
BF16 = jnp.bfloat16


def sds(shape, dtype):
    return jax.ShapeDtypeStruct(shape, dtype)


class Late:
    def __init__(self, source, ref, sem):
        self.ref, self.copy, self.here = ref, pltpu.make_async_copy(source, ref, sem), False
        self.shape = ref.shape
        self.copy.start()

    def wait(self):
        if not self.here:
            self.copy.wait()
            self.here = True

    def __getitem__(self, index):
        self.wait()
        return self.ref[index]


class Kept:
    def __init__(self, target, ref, sem):
        self.ref, self.copy, self.sent = ref, pltpu.make_async_copy(ref, target, sem), False
        self.shape, self.dtype = ref.shape, ref.dtype

    def __getitem__(self, index):
        return self.ref[index]

    def __setitem__(self, index, value):
        self.ref[index] = value

    def send(self):
        if not self.sent:
            self.copy.start()
            self.sent = True


def send(*refs):
    for ref in refs:
        if isinstance(ref, Kept):
            ref.send()


def call(body, outs, args, flops=10**9, late=(), kept=(), smem=0, scratch=()):
    moved = [args[i] for i in late] + [outs[i] for i in kept]

    def kernel(*refs):
        refs = list(refs)
        ins, rest = refs[: len(args)], refs[len(args) :]
        results, rest = rest[: len(outs)], rest[len(outs) :]
        extra, rest = rest[: len(scratch)], rest[len(scratch) :]
        buffers, sems = rest[: len(moved)], rest[len(moved) :]
        for k, i in enumerate(late):
            ins[i] = Late(ins[i], buffers[k], sems[k])
        for k, i in enumerate(kept, len(late)):
            results[i] = Kept(results[i], buffers[k], sems[k])
        body(*ins, *results, *extra)
        for i in late:
            ins[i].wait()
        for i in kept:
            results[i].send()
        for i in kept:
            results[i].copy.wait()

    args = [pltpu.with_memory_space_constraint(x, pltpu.HBM) if i in late else x for i, x in enumerate(args)]
    outs = [pltpu.HBM(x.shape, x.dtype) if i in kept else x for i, x in enumerate(outs)]
    space = [pltpu.SMEM] * smem + [pltpu.VMEM] * (len(args) - smem)
    for i in late:
        space[i] = pltpu.HBM
    return pl.pallas_call(
        kernel,
        out_shape=outs,
        in_specs=[pl.BlockSpec(memory_space=s) for s in space],
        out_specs=[
            pl.BlockSpec(memory_space=pltpu.HBM if i in kept else pltpu.VMEM)
            for i in range(len(outs))
        ],
        scratch_shapes=[pltpu.VMEM(shape, F32) for shape in scratch]
        + [pltpu.VMEM(m.shape, m.dtype) for m in moved]
        + [pltpu.SemaphoreType.DMA] * len(moved),
        compiler_params=pltpu.CompilerParams(vmem_limit_bytes=40 * 2**20),
        cost_estimate=pl.CostEstimate(flops=flops, bytes_accessed=2**20, transcendentals=0),
        name=body.__name__,
    )(*args)


def dot(a, b):
    return jnp.dot(a, b, preferred_element_type=F32)


def dot_nt(a, b):
    return lax.dot_general(a, b, (((1,), (1,)), ((), ())), preferred_element_type=F32)


def low(v):
    return v.astype(BF16)


def iota(shape, axis):
    return lax.broadcasted_iota(jnp.int32, shape, axis)


def ones_where(mask):
    return jnp.where(mask, 1.0, 0.0).astype(BF16)


def onehot(count, row, first=0):
    return ones_where(iota((count, row.shape[1]), 0) + first == row)


def sigmoid(v):
    return 1.0 / (1.0 + jnp.exp(-v))


def silu_pair(v):
    s = sigmoid(v)
    return v * s, s * (1.0 + v * (1.0 - s))


def cut(value, width):
    count = FOLD // width
    length = value.shape[1] // count
    return jnp.concatenate([value[:, g * length : (g + 1) * length] for g in range(count)], axis=0)


def uncut(value, width):
    count = FOLD // width
    return jnp.concatenate([value[g * width : (g + 1) * width] for g in range(count)], axis=1)


def pick(folded, high, width):
    result = folded[:width]
    for g in range(1, FOLD // width):
        result = jnp.where(high == g, folded[g * width : (g + 1) * width], result)
    return result


def spread(value, high, width):
    return jnp.concatenate(
        [low(jnp.where(high == g, value, 0.0)) for g in range(FOLD // width)], axis=0
    )


def high_low(index, length):
    return index // length, index % length


def small_t(raw, offset, width, columns):
    count = 128 // width
    total = None
    for p in range(count):
        lane, d = iota((PAD, columns), 0), iota((PAD, columns), 1)
        sel = ones_where((d % count == p) & (lane == offset + d // count))
        part = dot(raw[p * width : (p + 1) * width], sel)
        total = part if total is None else total + part
    return low(total)


def small_plain(raw, offset, width, rows):
    count = 128 // width
    total = None
    for p in range(count):
        d, lane = iota((rows, PAD), 0), iota((rows, PAD), 1)
        sel = ones_where((d % count == p) & (lane == offset + d // count))
        part = dot_nt(sel, raw[p * width : (p + 1) * width])
        total = part if total is None else total + part
    return low(total)


def wide_t(raw, offset, rows):
    lane, d = iota((PAD, rows), 0), iota((PAD, rows), 1)
    return low(dot(raw, ones_where(lane == offset + d)))


def wide_plain(raw, offset, rows):
    d, lane = iota((rows, PAD), 0), iota((rows, PAD), 1)
    return low(dot_nt(ones_where(lane == offset + d), raw))


def double_plain(raw, rows):
    d, lane = iota((rows, 2 * rows), 0), iota((rows, 2 * rows), 1)
    return jnp.concatenate(
        [low(dot_nt(ones_where(lane == 2 * d + p), raw)) for p in range(2)], axis=1
    )


def put_small(grad_t, offset, width):
    count = 128 // width
    columns = grad_t.shape[1]
    value = low(grad_t)
    parts = []
    for p in range(count):
        d, lane = iota((columns, PAD), 0), iota((columns, PAD), 1)
        sel = ones_where((d % count == p) & (lane == offset + d // count))
        parts.append(dot(value, sel))
    return jnp.concatenate(parts, axis=0)


def put_wide(grad_t, offset):
    columns = grad_t.shape[1]
    d, lane = iota((columns, PAD), 0), iota((columns, PAD), 1)
    return dot(low(grad_t), ones_where(lane == offset + d))


def put_double(grad_t):
    rows = grad_t.shape[1]
    d, lane = iota((rows, 2 * rows), 0), iota((rows, 2 * rows), 1)
    value = low(grad_t)
    return low(
        dot(value[:128], ones_where(lane == 2 * d)) + dot(value[128:], ones_where(lane == 2 * d + 1))
    )


def small_matrices(raw):
    return (
        [small_t(raw, OFF_DOWN[w], w, D_EDGE) for w in (D_TRI, D_QUAD)]
        + [small_t(raw, OFF_BASIS[w], w, D_BASIS) for w in (D_TRI, D_QUAD)]
        + [wide_t(raw, OFF_UP[w], w) for w in (D_TRI, D_QUAD)]
        + [wide_t(raw, OFF_RADIAL, D_BASIS)]
    )


def back_matrices(raw):
    return [wide_plain(raw, OFF_UP[w], w) for w in (D_TRI, D_QUAD)] + [
        small_plain(raw, OFF_DOWN[w], w, D_EDGE) for w in (D_TRI, D_QUAD)
    ]


SMALL_SHAPES = [
    (D_TRI, D_EDGE), (D_QUAD, D_EDGE), (D_TRI, D_BASIS), (D_QUAD, D_BASIS), (D_EDGE, D_TRI),
    (D_EDGE, D_QUAD), (D_EDGE, D_BASIS),
]
BACK_SHAPES = [(D_TRI, D_EDGE), (D_QUAD, D_EDGE), (D_EDGE, D_TRI), (D_EDGE, D_QUAD)]


def slots(width):
    return -(-width // PAD)


def padded(value, rows, lanes):
    have, wide = value.shape
    if wide < lanes:
        value = jnp.concatenate([value, jnp.zeros((have, lanes - wide), value.dtype)], axis=1)
    if have < rows:
        value = jnp.concatenate([value, jnp.zeros((rows - have, lanes), value.dtype)], axis=0)
    return value


def pack_first(weights, out_ref):
    head = low(padded(weights[:, :SMALL], ROWS, PAD))
    for s in range(out_ref.shape[0]):
        out_ref[s] = head


def pack_cargo(me, weights, state, fixed, out_ref, hold):
    count = state.shape[0]
    free = (1 - fixed[...]).astype(F32)
    out_ref[0, :count] = state[...]
    out_ref[0, count : count + ROWS] = low(padded(free, ROWS, PAD))
    values = weights[...]
    half = SMALL + BIG
    gap = jnp.zeros((values.shape[0], PAD - SMALL), F32)
    one = jnp.concatenate([values[:, SMALL : half + SMALL], gap], axis=1)
    two = padded(values[:, half + SMALL :], values.shape[0], BIG + PAD)
    groups, _, width = hold.shape
    base = count + ROWS
    for side in (one, two):
        for g in range(groups):
            hold[g] = side[:, g * width : (g + 1) * width]
        mine = padded(hold[me[1]], ROWS, slots(width) * PAD)
        for k in range(slots(width)):
            out_ref[0, base : base + ROWS] = low(mine[:, k * PAD : (k + 1) * PAD])
            base = base + ROWS


def order_of(owners):
    order, step = [0], owners // 2
    while step:
        order = order + [k ^ step for k in order]
        step = step // 2
    return order


def collect(me, *refs):
    *cargo, one_ref, two_ref = refs
    rows = cargo[0].shape[1]
    owners = sum(c.shape[0] for c in cargo)
    full, width = one_ref.shape
    cols = full // owners
    count = slots(width)
    base = rows - 2 * count * ROWS
    order = order_of(owners)
    shape = (full, owners * ROWS)
    row, col = iota(shape, 0), iota(shape, 1)
    owner, inside = row // cols, row % cols
    sel = None
    for position, k in enumerate(order):
        hit = (col == position * ROWS + inside) & (owner == (me[0] ^ k))
        sel = hit if sel is None else sel | hit
    sel = ones_where(sel)
    for side, ref in ((0, one_ref), (1, two_ref)):
        for k in range(count):
            start = base + (side * count + k) * ROWS
            values = jnp.concatenate(
                [c[i, start : start + ROWS] for c in cargo for i in range(c.shape[0])], axis=0
            )
            lanes = min(PAD, width - k * PAD)
            ref[:, k * PAD : k * PAD + lanes] = low(dot(sel, values))[:, :lanes]


def joined(me, pieces, hold):
    for k, piece in enumerate(pieces):
        hold[me[1] ^ k] = piece[...].astype(F32)
    return low(jnp.concatenate([hold[g] for g in range(len(pieces))], axis=1))


def small_rows(pack, cols):
    owners = pack.shape[0]
    value = pack[...].reshape(owners * ROWS, PAD)
    if cols == ROWS:
        return value
    c, row = iota((owners * cols, owners * ROWS), 0), iota((owners * cols, owners * ROWS), 1)
    return low(dot(ones_where(row == c // cols * ROWS + c % cols), value))


def prepare_one(me, pack, *refs):
    *rest, hold = refs
    groups = hold.shape[0]
    wide = joined(me, rest[:groups], hold)
    raw_one = small_rows(pack, D_EDGE // pack.shape[0])
    raw_two = wide[:, BIG:]
    values = back_matrices(raw_one) + [wide_t(raw_one, OFF_RADIAL, D_BASIS)]
    values = values + small_matrices(raw_two) + back_matrices(raw_two)
    values = values + [double_plain(wide[:, :256], D_EDGE), double_plain(wide[:, 256:768], D_ATOM)]
    for ref, value in zip(rest[groups:], values + [wide[:, :BIG]]):
        ref[...] = value


def prepare_two(me, *refs):
    *rest, hold = refs
    groups = hold.shape[0]
    big = joined(me, rest[:groups], hold)
    first_ref, second_ref, big_ref = rest[groups:]
    first_ref[...] = double_plain(big[:, :256], D_EDGE)
    second_ref[...] = double_plain(big[:, 256:768], D_ATOM)
    big_ref[...] = big[:, :BIG]


LARGE_SHAPES = [(D_EDGE, D_ATOM), (D_ATOM, D_ATOM), (D_EDGE, BIG)]
PREPARED = BACK_SHAPES + [(D_EDGE, D_BASIS)] + SMALL_SHAPES + BACK_SHAPES + LARGE_SHAPES


def pair_forward(edge_t, basis_ref, in_ref, out_ref, down_t, basis_t, up_t, xg_ref, bt_ref):
    width, edges = down_t.shape[0], edge_t.shape[1]
    length = edges * width // FOLD
    act, slope_in = silu_pair(dot(down_t, edge_t))
    table = cut(low(act), width)
    total = jnp.zeros((FOLD, length), F32)
    items = in_ref.shape[1]
    chunk = min(CHUNK, items)
    for start in range(0, items, chunk):
        cols = slice(start, start + chunk)
        in_high, in_low = high_low(in_ref[:, cols], length)
        out_high, out_low = high_low(out_ref[:, cols], length)
        xg = pick(dot(table, onehot(length, in_low)), in_high, width)
        bt = dot(basis_t, basis_ref[:, cols])
        xg_ref[:, cols] = low(xg)
        bt_ref[:, cols] = low(bt)
        total = total + dot_nt(spread(xg * bt, out_high, width), onehot(length, out_low))
    send(xg_ref, bt_ref)
    agg_t = low(uncut(total, width) * pair_scale)
    value, slope_out = silu_pair(dot(up_t, agg_t))
    return value, slope_in, agg_t, slope_out


def pair_backward(
    grad_mid, edge_t, basis_ref, in_ref, out_ref, up, down, slope_out, agg_t, xg_ref, bt_ref, slope_in,
):
    width, edges = up.shape[0], slope_in.shape[1]
    length = edges * width // FOLD
    grad_out = low(grad_mid * slope_out[...].astype(F32))
    grad_up_t = dot_nt(grad_out, agg_t[...])
    table = cut(low(dot(up, grad_out) * pair_scale), width)
    total = jnp.zeros((FOLD, length), F32)
    grad_basis_t = jnp.zeros((width, D_BASIS), F32)
    items = in_ref.shape[1]
    chunk = min(CHUNK, items)
    for start in range(0, items, chunk):
        cols = slice(start, start + chunk)
        in_high, in_low = high_low(in_ref[:, cols], length)
        out_high, out_low = high_low(out_ref[:, cols], length)
        gy = pick(dot(table, onehot(length, out_low)), out_high, width)
        grad_bt = low(gy * xg_ref[:, cols].astype(F32))
        grad_basis_t = grad_basis_t + dot_nt(grad_bt, basis_ref[:, cols])
        moved = gy * bt_ref[:, cols].astype(F32)
        total = total + dot_nt(spread(moved, in_high, width), onehot(length, in_low))
    grad_in = low(uncut(total, width) * slope_in[...].astype(F32))
    grad_down_t = dot_nt(grad_in, edge_t[...])
    small = (
        put_small(grad_down_t, OFF_DOWN[width], width)
        + put_small(grad_basis_t, OFF_BASIS[width], width)
        + put_wide(grad_up_t, OFF_UP[width])
    )
    return dot(down, grad_in), small


def block_forward(state_t, matrices, graph, dst_row, out_refs):
    radial_basis, tri_basis, quad_basis, tri_in, tri_out, quad_in, quad_out = graph
    down_tri, down_quad, basis_tri, basis_quad, up_tri, up_quad, radial_t = matrices
    mid_ref, mid_low_ref = out_refs[:2]
    tri_refs, edge_ref, quad_refs, table_ref = out_refs[2:7], out_refs[7], out_refs[8:13], out_refs[13]
    edge_t = low(state_t)
    edge_ref[...] = edge_t
    send(edge_ref)
    mid = state_t
    for refs, basis, inner, outer, down, basis_t, up in (
        (tri_refs, tri_basis, tri_in, tri_out, down_tri, basis_tri, up_tri),
        (quad_refs, quad_basis, quad_in, quad_out, down_quad, basis_quad, up_quad),
    ):
        slope_out_ref, agg_ref, xg_ref, bt_ref, slope_in_ref = refs
        value, slope_in, agg, slope_out = pair_forward(
            edge_t, basis, inner, outer, down, basis_t, up, xg_ref, bt_ref
        )
        slope_in_ref[...] = low(slope_in)
        agg_ref[...] = agg
        slope_out_ref[...] = low(slope_out)
        send(slope_in_ref, agg_ref, slope_out_ref)
        mid = mid + value
    mid_ref[...] = mid
    mid_low_ref[...] = low(mid)
    send(mid_ref, mid_low_ref)
    message = low(mid * dot(radial_t, radial_basis[...]))
    atoms = table_ref.shape[0]
    step = min(512, atoms)
    for start in range(0, atoms, step):
        rows = slice(start, start + step)
        table_ref[rows] = low(dot_nt(onehot(step, dst_row[...], start), message))


def kept_shapes(edges, items):
    edge = ((D_EDGE, edges), BF16)
    tri, quad = [
        [edge, ((w, edges), BF16), ((w, items), BF16), ((w, items), BF16), ((w, edges), BF16)]
        for w in (D_TRI, D_QUAD)
    ]
    return [sds(*x) for x in [((D_EDGE, edges), F32), edge] + tri + [edge] + quad]


KEPT = 13


def first_half(edge_state, pack, *refs):
    graph, dst_row, out_refs = refs[:7], refs[7], refs[8:]
    eye = ones_where(iota((D_EDGE, D_EDGE), 0) == iota((D_EDGE, D_EDGE), 1))
    state_t = dot_nt(eye, edge_state[...])
    raw = small_rows(pack, D_EDGE // pack.shape[0])
    block_forward(state_t, small_matrices(raw), graph, dst_row, out_refs)


def atom_forward(near, far, state, free, first, second):
    atom_in = low((near[...].astype(F32) + far[...].astype(F32)) * edge_scale)
    act, slope = silu_pair(dot(atom_in, first[...]))
    hidden = low(act)
    new_state = state + free * dot(hidden, second[...])
    return atom_in, hidden, slope, new_state


def edge_pre(sent, big, src_row, dst_row):
    src_t = low(dot_nt(big[:, 768:1024], sent))
    dst_t = low(dot_nt(big[:, 1024:1280], sent))
    atoms = sent.shape[0]
    step = min(512, atoms)
    total = None
    for start in range(0, atoms, step):
        part = dot(src_t[:, start : start + step], onehot(step, src_row[...], start))
        part = part + dot(dst_t[:, start : start + step], onehot(step, dst_row[...], start))
        total = part if total is None else total + part
    return total


def middle_half(me, near, far, big, first, second, mid_in, *refs):
    matrices, graph, src_row, dst_row = refs[:7], refs[7:14], refs[14], refs[15]
    atoms = near.shape[0]
    cargo, refs = refs[16:], None
    split = 0
    owners = 0
    while len(cargo[split].shape) == 3:
        owners = owners + cargo[split].shape[0]
        split = split + 1
    cargo, rest = cargo[:split], cargo[split:]
    atom_in_ref, hidden_ref, slope_atom_ref, state_ref, sent_ref, free_ref, slope_edge_ref = rest[:7]
    *out_refs, free_wide = rest[7:]
    count = atoms // owners
    eye = iota((count, count), 0) == iota((count, count), 1)
    order = order_of(owners)
    position = 0
    for pieces in cargo:
        for i in range(pieces.shape[0]):
            rows = pl.ds(pl.multiple_of((me[0] ^ order[position]) * count, count), count)
            state_ref.ref[rows] = pieces[i, :count].astype(F32)
            flag = pieces[i, count : count + 1, :count].astype(F32)
            column = jnp.sum(jnp.where(eye, flag, 0.0), axis=1, keepdims=True)
            free_wide[rows] = jnp.broadcast_to(column, (count, D_ATOM))
            position = position + 1
    free_ref[...] = low(free_wide[...])
    send(free_ref)
    atom_in, hidden, slope, state = atom_forward(
        near, far, state_ref[...], free_wide[...], first, second
    )
    atom_in_ref[...] = atom_in
    hidden_ref[...] = hidden
    slope_atom_ref[...] = low(slope)
    state_ref[...] = state
    sent = low(state)
    sent_ref[...] = sent
    send(atom_in_ref, hidden_ref, slope_atom_ref, state_ref, sent_ref)
    act, slope_edge = silu_pair(edge_pre(sent, big, src_row, dst_row))
    slope_edge_ref[...] = low(slope_edge)
    send(slope_edge_ref)
    block_forward(mid_in[...] + act, [m[...] for m in matrices], graph, dst_row, out_refs)


def edge_tables(
    grad_pre, big, first, second, src_row, dst_row, free, slope_atom, grad_atoms, gain_ref, update_ref,
    pushed_ref,
):
    atoms = free.shape[0]
    step = min(512, atoms)
    src_t, dst_t = big[:, 768:1024], big[:, 1024:1280]
    for start in range(0, atoms, step):
        rows = slice(start, start + step)
        pick_src = onehot(step, src_row[...], start)
        pick_dst = onehot(step, dst_row[...], start)
        part = dot(low(dot_nt(pick_src, grad_pre)), src_t) + dot(low(dot_nt(pick_dst, grad_pre)), dst_t)
        grad_atoms[rows] = grad_atoms[rows] + part
    update = low(grad_atoms[...] * free)
    update_ref[...] = update
    send(update_ref)
    pushed = low(dot_nt(update, second[...]) * slope_atom)
    pushed_ref[...] = pushed
    send(pushed_ref)
    gain_ref[...] = low(dot_nt(first[...], pushed))


def turn(
    me, near, far, big, first, second, src_row, dst_row, edge_cotangent, own, state_in, free_ref, mid_in,
    atom_in_ref, hidden_ref, sent_ref, edge_ref, atom_out_ref, cotangent_ref, grad_pre_ref, atoms_ref,
    gain_ref, update_ref, pushed_ref, hold,
):
    free = free_ref[...].astype(F32)
    atom_in, hidden, slope, state = atom_forward(near, far, state_in[...], free, first, second)
    atom_in_ref[...] = atom_in
    hidden_ref[...] = hidden
    sent = low(state)
    sent_ref[...] = sent
    send(atom_in_ref, hidden_ref, sent_ref)
    hold[...] = state
    count = atom_out_ref.shape[0]
    mine = pl.ds(pl.multiple_of(me[0] * count, count), count)
    atom_out_ref[...] = low(hold[mine])
    act, slope_edge = silu_pair(edge_pre(sent, big, src_row, dst_row))
    edge_ref[...] = mid_in[...] + act
    send(edge_ref, atom_out_ref)
    eye = ones_where(iota((D_EDGE, D_EDGE), 0) == iota((D_EDGE, D_EDGE), 1))
    cotangent = dot_nt(eye, edge_cotangent[...])
    cotangent_ref[...] = cotangent
    grad_pre = low(cotangent * slope_edge)
    grad_pre_ref[...] = grad_pre
    send(cotangent_ref, grad_pre_ref)
    atoms_ref[...] = jnp.zeros(atoms_ref.shape, F32)
    atoms_ref.ref[mine] = own[...].astype(F32)
    edge_tables(
        grad_pre, big, first, second, src_row, dst_row, free, slope, atoms_ref, gain_ref, update_ref,
        pushed_ref,
    )


def large_grads(me, update, pushed, atom_in, hidden, sent, grad_pre, src_row, dst_row, small, out_ref, hold):
    atoms = sent.shape[0]
    step = min(512, atoms)
    grad_src = jnp.zeros((D_EDGE, D_ATOM), F32)
    grad_dst = jnp.zeros((D_EDGE, D_ATOM), F32)
    for start in range(0, atoms, step):
        rows = slice(start, start + step)
        grads = grad_pre[...]
        grad_src = grad_src + dot(low(dot_nt(grads, onehot(step, src_row[...], start))), sent[rows])
        grad_dst = grad_dst + dot(low(dot_nt(grads, onehot(step, dst_row[...], start))), sent[rows])
    grad_second_t = dot(low(jnp.transpose(update[...].astype(F32))), hidden[...])
    grad_first_t = dot(low(jnp.transpose(pushed[...].astype(F32))), atom_in[...])
    hold[:, :256] = small[...].astype(F32)
    hold[:, 256:512] = put_double(grad_first_t).astype(F32)
    hold[:, 512:1024] = put_double(grad_second_t).astype(F32)
    hold[:, 1024:1280] = grad_src
    hold[:, 1280:1536] = grad_dst
    pieces, _, width = out_ref.shape
    for g in range(pieces):
        out_ref[g ^ me[1]] = low(hold[:, g * width : (g + 1) * width])


def turned(value_ref, out_ref):
    out_ref[...] = jnp.transpose(value_ref[...]).astype(out_ref.dtype)


def block_backward(near, far, grad_in, *refs):
    mid, tri_refs, edge_ref, quad_refs = refs[0], refs[1:6], refs[6], refs[7:12]
    up_tri, up_quad, down_tri, down_quad, radial_t = refs[12:17]
    radial_basis, tri_basis, quad_basis, tri_in, tri_out, quad_in, quad_out = refs[17:24]
    dst_row, small_ref = refs[24], refs[25]
    gain_t = low(near[...].astype(F32) + far[...].astype(F32))
    atoms = gain_t.shape[1]
    step = min(512, atoms)
    grad_message = None
    for start in range(0, atoms, step):
        part = dot(gain_t[:, start : start + step], onehot(step, dst_row[...], start))
        grad_message = part if grad_message is None else grad_message + part
    grad_message = grad_message * edge_scale
    radial = dot(radial_t[...], radial_basis[...])
    grad_mid = grad_in[...] + grad_message * radial
    grad_radial = low(grad_message * mid[...].astype(F32))
    small = put_wide(dot_nt(grad_radial, radial_basis[...]), OFF_RADIAL)
    total = grad_mid
    for kept, basis, inner, outer, up, down in (
        (tri_refs, tri_basis, tri_in, tri_out, up_tri, down_tri),
        (quad_refs, quad_basis, quad_in, quad_out, up_quad, down_quad),
    ):
        value, more = pair_backward(grad_mid, edge_ref, basis, inner, outer, up[...], down[...], *kept)
        total = total + value
        small = small + more
    small_ref[...] = jnp.broadcast_to(low(small), small_ref.shape)
    send(small_ref)
    return total


BACK = 28


def back_last(*refs):
    refs[-1][...] = block_backward(*refs[:-1])


def back_middle(me, *refs):
    back, refs = refs[:BACK], refs[BACK:]
    big, first, second, src_row, slope_edge, free_ref, slope_atom, held = refs[:8]
    small_ref, gain_ref, update_ref, pushed_ref, grad_pre_ref, grad_ref, high_ref, low_ref, grad_atoms = refs[8:]
    grad = block_backward(*back, small_ref)
    grad_ref[...] = grad
    grad_pre = low(grad * slope_edge[...].astype(F32))
    grad_pre_ref[...] = grad_pre
    send(grad_ref, grad_pre_ref)
    grad_atoms[...] = held[...]
    edge_tables(
        grad_pre, big, first, second, src_row, back[-1], free_ref[...].astype(F32),
        slope_atom[...].astype(F32), grad_atoms, gain_ref, update_ref, pushed_ref,
    )
    half, count, _ = low_ref.shape
    for k in range(half):
        for ref, step in ((low_ref, k), (high_ref, half + k)):
            rows = pl.ds(pl.multiple_of((me[0] ^ step) * count, count), count)
            ref[k] = low(grad_atoms[rows])


def total_of(arrived):
    total = arrived[0].astype(F32)
    for s in range(1, arrived.shape[0]):
        total = total + arrived[s].astype(F32)
    return total


def sum_parts(arrived, out_ref):
    out_ref[...] = low(total_of(arrived))


def sum_pieces(*refs):
    *pieces, out_ref = refs
    count = len(pieces) // 2
    width = pieces[0].shape[1]
    for side in range(2):
        total = pieces[side * count][...].astype(F32)
        for piece in pieces[side * count + 1 : (side + 1) * count]:
            total = total + piece[...].astype(F32)
        out_ref[:, side * width : (side + 1) * width] = low(total)


def adam(me, last, weights, first, second, *refs):
    *pieces, grad_ref, weights_ref, first_ref, second_ref, low_ref, hold = refs
    width = pieces[0].shape[1] // 2
    for k, piece in enumerate(pieces):
        hold[me[1] ^ k] = piece[...].astype(F32)
    two, one = [
        jnp.concatenate([hold[g, :, side * width : (side + 1) * width] for g in range(len(pieces))], axis=1)
        for side in range(2)
    ]
    grad = jnp.concatenate(
        [total_of(last)[:, :SMALL], one[:, PAD:], one[:, :SMALL], two[:, PAD:]], axis=1
    )
    grad_ref[...] = grad
    old = weights[...]
    new_first = beta_one * first[...] + (1.0 - beta_one) * grad
    new_second = beta_two * second[...] + (1.0 - beta_two) * grad * grad
    first_ref[...] = new_first
    second_ref[...] = new_second
    first_hat = new_first / (1.0 - beta_one**adam_step)
    second_hat = new_second / (1.0 - beta_two**adam_step)
    new = old - learn_rate * (first_hat / (jnp.sqrt(second_hat) + epsilon) + decay_rate * old)
    weights_ref[...] = new
    low_ref[...] = low(new)


def exchange(pieces):
    return lax.all_to_all(pieces, "shard", split_axis=0, concat_axis=0)


def sum_pair(table, owners):
    rounds = []
    step = 1
    while step < owners:
        rounds.append([step])
        step = 2 * step
    if len(rounds) > 2:
        rounds = [[1, 2, 3]] + rounds[2:]
    for steps in rounds[:-1]:
        total = table.astype(F32)
        for k in steps:
            total = total + moved(table, k, owners).astype(F32)
        table = total.astype(BF16)
    return table, moved(table, rounds[-1][0], owners)


def moved(table, step, owners, axis="shard"):
    return lax.ppermute(table, axis, [(i, i ^ step) for i in range(owners)])


def per_device(
    edge_state, atom_state, radial_basis, triplet_basis, quad_basis, dst_owner, dst_local, src_owner,
    src_local, triplet_in, triplet_out, quad_in, quad_out, fixed_atoms, edge_cotangent,
    atom_cotangent, weights, first_moment, second_moment,
):
    owners = lax.axis_size("shard")
    groups = lax.axis_size("group")
    edges = edge_state.shape[0]
    count = atom_state.shape[0]
    atoms = count * owners
    items = triplet_in.shape[0]
    me = jnp.stack([lax.axis_index("shard"), lax.axis_index("group")]).astype(jnp.int32)
    weights_t = jnp.transpose(weights)
    cols = weights_t.shape[0]
    lanes = (BIG + PAD) // groups
    [pack] = call(pack_first, [sds((owners, ROWS, PAD), BF16)], [weights_t], flops=10**7)
    pack = exchange(pack)
    [cargo] = call(
        pack_cargo,
        [sds((1, count + ROWS * (1 + 2 * slots(lanes)), D_ATOM), BF16)],
        [me, weights_t, atom_state, fixed_atoms.reshape(1, count)],
        flops=10**7,
        smem=1,
        scratch=[(groups, cols, lanes)],
    )
    cargo = [cargo]
    step = owners // 2
    while step:
        cargo.append(moved(cargo[0] if len(cargo) == 1 else jnp.concatenate(cargo, axis=0), step, owners))
        step = step // 2
    lanes_shape = sds((D_EDGE, lanes), BF16)
    wide, big_two = call(collect, [lanes_shape, lanes_shape], [me] + cargo, flops=10**7, smem=1)
    dst_row = (dst_owner[:, 0] * count + dst_local).reshape(1, edges)
    src_row = (src_owner[:, 0] * count + src_local).reshape(1, edges)
    graph = [
        jnp.transpose(radial_basis),
        jnp.transpose(triplet_basis),
        jnp.transpose(quad_basis),
        triplet_in.reshape(1, items),
        triplet_out.reshape(1, items),
        quad_in.reshape(1, items),
        quad_out.reshape(1, items),
    ]
    kept = kept_shapes(edges, items)
    table_shape = sds((atoms, D_EDGE), BF16)
    edge_shape = sds((D_EDGE, edges), BF16)
    edge_wide = sds((D_EDGE, edges), F32)
    atom_shape = sds((atoms, D_ATOM), BF16)
    atom_wide = sds((atoms, D_ATOM), F32)
    gain_shape = sds((D_EDGE, atoms), BF16)
    *kept_one, table = call(
        first_half,
        kept + [table_shape],
        [edge_state, pack] + graph + [dst_row],
        flops=8 * 10**9,
        kept=range(KEPT),
    )
    near, far = sum_pair(table, owners)

    def everywhere(piece):
        return [piece] + [moved(piece, k, groups, "group") for k in range(1, groups)]

    prepared = list(
        call(
            prepare_one,
            [sds(s, BF16) for s in PREPARED],
            [me, pack] + everywhere(wide),
            flops=10**9,
            smem=1,
            scratch=[(groups, D_EDGE, lanes)],
        )
    )
    back_one, small_two, back_two = prepared[:5], prepared[5:12], prepared[12:16] + [prepared[11]]
    first_one, second_one, big_one = prepared[16:]
    (
        atom_in_one, hidden_one, slope_one, state_one, sent_one, free, slope_edge_one, *kept_two, table,
    ) = call(
        middle_half,
        [table_shape, atom_shape, atom_shape, atom_wide, atom_shape, atom_shape, edge_shape]
        + kept
        + [table_shape],
        [me, near, far, big_one, first_one, second_one, kept_one[0]]
        + small_two
        + graph
        + [src_row, dst_row]
        + cargo,
        flops=10 * 10**9,
        late=[6],
        kept=range(7 + KEPT),
        smem=1,
        scratch=[(atoms, D_ATOM)],
    )
    near, far = sum_pair(table, owners)
    first_two, second_two, big_two = call(
        prepare_two,
        [sds(s, BF16) for s in LARGE_SHAPES],
        [me] + everywhere(big_two),
        flops=10**9,
        smem=1,
        scratch=[(groups, D_EDGE, lanes)],
    )
    (
        atom_in_two, hidden_two, sent_two, edge_out_t, atom_out, grad_t, grad_pre, grad_atoms, gain, update,
        pushed,
    ) = call(
        turn,
        [table_shape, atom_shape, atom_shape, edge_wide, sds((count, D_ATOM), BF16), edge_wide, edge_shape,
         atom_wide, gain_shape, atom_shape, atom_shape],
        [me, near, far, big_two, first_two, second_two, src_row, dst_row, edge_cotangent,
         atom_cotangent, state_one, free, kept_two[0]],
        flops=2 * 10**9,
        late=[10, 11, 12],
        kept=[0, 1, 2, 3, 4, 5, 6, 7, 9, 10],
        smem=1,
        scratch=[(atoms, D_ATOM)],
    )

    def rows_first(value_t, dtype):
        return call(turned, [sds((edges, D_EDGE), dtype)], [value_t], flops=10**8, late=[0])[0]

    def large(update, pushed, atom_in, hidden, sent, grad_pre, small):
        [pieces] = call(
            large_grads,
            [sds((groups, D_EDGE, (PAD + BIG) // groups), BF16)],
            [me, update, pushed, atom_in, hidden, sent, grad_pre, src_row, dst_row, small],
            flops=10**9,
            late=[1, 2, 3, 4, 5, 6],
            smem=1,
            scratch=[(D_EDGE, PAD + BIG)],
        )
        return pieces

    def traded(pieces):
        return [pieces[0]] + [moved(pieces[k], k, groups, "group") for k in range(1, groups)]

    near, far = sum_pair(gain, owners)
    edge_out = rows_first(edge_out_t, BF16)
    pieces_two = large(
        update, pushed, atom_in_two, hidden_two, sent_two, grad_pre, jnp.zeros((D_EDGE, PAD), BF16)
    )
    near, pieces_two = lax.optimization_barrier((near, pieces_two))
    pieces_two = traded(pieces_two)
    half = owners // 2
    half_shape = sds((half, count, D_ATOM), BF16)
    grad_small_two, gain, update, pushed, grad_pre, grad_t, high, lower = call(
        back_middle,
        [sds((D_EDGE, PAD), BF16), gain_shape, atom_shape, atom_shape, edge_shape, edge_wide, half_shape,
         half_shape],
        [me, near, far, grad_t]
        + kept_two[1:]
        + back_two
        + graph
        + [dst_row, big_one, first_one, second_one, src_row, slope_edge_one, free, slope_one, grad_atoms],
        flops=10 * 10**9,
        late=list(range(3, 3 + KEPT)) + list(range(BACK + 5, BACK + 9)),
        kept=[0, 2, 3, 4, 5, 6, 7],
        smem=1,
        scratch=[(atoms, D_ATOM)],
    )
    near, far = sum_pair(gain, owners)
    pieces_one = traded(
        large(update, pushed, atom_in_one, hidden_one, sent_one, grad_pre, grad_small_two)
    )
    width = pieces_one[0].shape[1]
    [spreads] = call(
        sum_pieces, [sds((D_EDGE, 2 * width), BF16)], pieces_two + pieces_one, flops=10**7
    )
    arrived = exchange(spreads.reshape(owners, cols, 2 * width))
    [owned] = call(sum_parts, [sds((cols, 2 * width), BF16)], [arrived], flops=10**7)
    owned = [owned] + [moved(owned, k, groups, "group") for k in range(1, groups)]
    near, far, high = lax.optimization_barrier((near, far, high))
    while half > 1:
        lower = (lower.astype(F32) + moved(high, half, owners).astype(F32)).astype(BF16)
        half = half // 2
        high, lower = lower[half:], lower[:half]
    grad_atom = lower[0].astype(F32) + moved(high[0], 1, owners).astype(F32)
    grad_small_one, grad_edge_t = call(
        back_last,
        [sds((groups, D_EDGE, PAD), BF16), edge_wide],
        [near, far, grad_t] + kept_one[1:] + back_one + graph + [dst_row],
        flops=10 * 10**9,
        late=range(2, 2 + KEPT),
        kept=[0, 1],
    )
    grad_edge = rows_first(grad_edge_t, F32)
    last = lax.all_to_all(
        grad_small_one.reshape(groups * owners, cols, PAD), ("group", "shard"), split_axis=0, concat_axis=0
    )
    rows = weights.shape[0]
    results = call(
        adam,
        [sds((cols, rows), F32)] * 4 + [sds((cols, rows), BF16)],
        [me, last, weights_t, jnp.transpose(first_moment), jnp.transpose(second_moment)] + owned,
        flops=10**8,
        smem=1,
        scratch=[(groups, cols, 2 * width)],
    )
    return (edge_out, atom_out, grad_edge, grad_atom) + tuple(jnp.transpose(r) for r in results)


def solution(mesh):
    both = P(("group", "shard"), None)
    line = P(("group", "shard"))
    flat = P(None, "shard")
    in_specs = (both,) * 6 + (line, both) + (line,) * 6 + (both, both) + (flat,) * 3
    out_specs = (both,) * 4 + (flat,) * 5
    return jax.shard_map(
        per_device, mesh=mesh, in_specs=in_specs, out_specs=out_specs, check_vma=False
    )
```

time: 192 us -> 163 us (0.85)
  local copies, waits for them, and re-layouts: 32.4 us -> 2.54 us
  blocking collectives: 24.4 us -> 0 us
  Pallas kernels: 33.8 us -> 56.7 us
  starting transfers between devices: 37.4 us -> 50.5 us
  waiting for transfers between devices: 59.2 us -> 50.5 us
    unnamed x118 -> x46, local copies, waits for them, and re-layouts: 29.9 us -> 2.44 us
    ppermute x12 -> x37, starting transfers between devices: 13.6 us -> 38.4 us  [moved(): return lax.ppermute(table, axis, [(i, i ^ step) for i in range(owners)])]
    pallas_call x10 -> x17, Pallas kernels: 33.8 us -> 56.7 us  [call(): pl.pallas_call(kernel, out_shape=outs, in_specs=[pl.BlockSpec(memory_spac...]
    all_to_all x1 -> x0, blocking collectives: 17.7 us -> none  [per_device(): lax.all_to_all(grads.reshape(owners, cols, 2 * (PAD + BIG)), 'shard', spl...]
    all_to_all x5 -> x3, starting transfers between devices: 23.8 us -> 12.1 us  [the longest x2 7.44 us: exchange(): return lax.all_to_all(pieces, 'shard', split_axis=0, concat_axis=0)]
    all_gather x1 -> x0, blocking collectives: 6.65 us -> none  [per_device(): grads = lax.all_gather(grads, 'group', axis=0)]
    ppermute x12 -> x37, waiting for transfers between devices: 51.4 us -> 45.4 us  [moved(): return lax.ppermute(table, axis, [(i, i ^ step) for i in range(owners)])]
    all_to_all x5 -> x3, waiting for transfers between devices: 7.75 us -> 5.12 us  [the longest x2 5.12 us: exchange(): return lax.all_to_all(pieces, 'shard', split_axis=0, concat_axis=0)]
  transfers between devices with their start and end apart: 17 -> 40, of which waited for: 13 -> 21; matrix products, arithmetic and copies ran while one was open for 1% -> 1% of each run, Pallas kernels for 9% -> 19%
where the time goes in v2:
time: 163 us
  Pallas kernels  56.7 us (35%)
  starting transfers between devices  50.5 us (31%)
  waiting for transfers between devices  50.5 us (31%)
  local copies, waits for them, and re-layouts  2.54 us (2%)
    pallas_call x17, Pallas kernels, call(): pl.pallas_call(kernel, out_shape=outs, in_specs=[pl.BlockSpec(memory_spac...  56.7 us
    ppermute x37, waiting for transfers between devices, moved(): return lax.ppermute(table, axis, [(i, i ^ step) for i in range(owners)])  45.4 us
    ppermute x37, starting transfers between devices, moved(): return lax.ppermute(table, axis, [(i, i ^ step) for i in range(owners)])  38.4 us
    all_to_all x2, starting transfers between devices, exchange(): return lax.all_to_all(pieces, 'shard', split_axis=0, concat_axis=0)  7.44 us
    all_to_all x2, waiting for transfers between devices, exchange(): return lax.all_to_all(pieces, 'shard', split_axis=0, concat_axis=0)  5.12 us
    all_to_all x1, starting transfers between devices, per_device(): lax.all_to_all(grad_small_one.reshape(groups * owners, cols, PAD), ('grou...  4.62 us
  transfers between devices with their start and end apart: 40, of which 21 were waited for; matrix products, arithmetic and copies ran while one was open for 1% of the time, Pallas kernels for 19%

profile of v2, /device:TPU:0, one launch (start us, length us, event | category | flops | bytes accessed | tf_op | source)
XLA Modules:
  0.0 162.6 jit_solution(14010775666974789924)
XLA Ops:
  3.7 4.1 %collective-permute-start.4 = (bf16[1,144,256]{2,1,0:T(8,128)(2,1)S(1)}, bf16[1,144,256]{2,1,0:T(8,128)(2,1)S(1)}, u32[]{:S(2)}, u32[]{:S(2)}) collective-permute-start(bf16[1,144,256]{2,1,0:T(8,128)(2,1)S(1)} %pack_cargo.1.refs_1_.refs_23_), channel_id=1, source_target_pairs={{0,4},{1,5},{2,6},{3,7},{4,0},{5,1},{6,2},{7,3},{8,12},{9,13},{10,... | collective-permute-start | bytes 221192 | tf_op jit(solution)/shard_map/ppermute | solution.py:768
  8.5 3.9 %all-to-all-start = ((bf16[8,16,256]{2,1,0:T(8,128)(2,1)}), bf16[8,16,256]{2,1,0:T(8,128)(2,1)S(1)}, u32[]{:S(2)}, u32[]{:S(2)}) async-start(bf16[8,16,256]{2,1,0:T(8,128)(2,1)} %pack_first.1), calls=%async_computation | async-start | bytes 131072 | tf_op jit(solution)/shard_map/all_to_all | solution.py:748
  12.5 2.1 %collective-permute-start.5 = (bf16[2,144,256]{2,1,0:T(8,128)(2,1)S(1)}, bf16[2,144,256]{2,1,0:T(8,128)(2,1)S(1)}, u32[]{:S(2)}, u32[]{:S(2)}) collective-permute-start(bf16[2,144,256]{2,1,0:T(8,128)(2,1)S(1)} %pad_maximum_fusion.1), channel_id=1, source_target_pairs={{0,2},{1,3},{2,0},{3,1},{4,6},{5,7},{6,4},{7,5},{8,10},{9,11},{10,... | collective-permute-start | bytes 442376 | tf_op jit(solution)/shard_map/ppermute | solution.py:768
  14.6 5.1 %all-to-all-done.refs_1_ = bf16[8,16,256]{2,1,0:T(8,128)(2,1)S(1)} async-done(((bf16[8,16,256]{2,1,0:T(8,128)(2,1)}), bf16[8,16,256]{2,1,0:T(8,128)(2,1)S(1)}, u32[]{:S(2)}, u32[]{:S(2)}) %all-to-all-start) | async-done | bytes 65568 | tf_op jit(solution)/shard_map/all_to_all | solution.py:748
  19.8 6.0 %first_half.1 = (f32[128,1024]{1,0:T(8,128)}, bf16[128,1024]{1,0:T(8,128)(2,1)}, bf16[128,1024]{1,0:T(8,128)(2,1)}, bf16[64,1024]{1,0:T(8,128)(2,1)}, bf16[64,40...) custom-call(bf16[1024,128]{1,0:T(8,128)(2,1)S(1)} %copy-done.6, ...), custom_call_target="tpu_custom_call" | custom-call | flops 8000000000 | bytes 1048576 | tf_op jit(solution)/shard_map/first_half/pallas_call | solution.py:108
  27.1 2.3 %collective-permute-start.2 = (bf16[512,128]{1,0:T(8,128)(2,1)S(1)}, bf16[512,128]{1,0:T(8,128)(2,1)S(1)}, u32[]{:S(2)}, u32[]{:S(2)}) collective-permute-start(bf16[512,128]{1,0:T(8,128)(2,1)S(1)} %get-tuple-element.99), channel_id=1, source_target_pairs={{0,3},{1,2},{2,1},{3,0},{4,7},{5,6},{6,5},{7,4},{8,11},{9,10},{10,... | collective-permute-start | bytes 393224 | tf_op jit(solution)/shard_map/ppermute | solution.py:768
  29.7 4.7 %collective-permute-done = bf16[512,128]{1,0:T(8,128)(2,1)S(1)} collective-permute-done((bf16[512,128]{1,0:T(8,128)(2,1)S(1)}, bf16[512,128]{1,0:T(8,128)(2,1)S(1)}, u32[]{:S(2)}, u32[]{:S(2)}) %collective-permute-start) | collective-permute-done | bytes 131104 | tf_op jit(solution)/shard_map/ppermute | solution.py:768
  35.3 4.0 %collective-permute-done.6.refs_4_.refs_26_ = bf16[4,144,256]{2,1,0:T(8,128)(2,1)S(1)} collective-permute-done((bf16[4,144,256]{2,1,0:T(8,128)(2,1)S(1)}, bf16[4,144,256]{2,1,0:T(8,128)(2,1)S(1)}, u32[]{:S(2)}, u32[]{:S(2)}) %collective-permute-start.6) | collective-permute-done | bytes 294944 | tf_op jit(solution)/shard_map/ppermute | solution.py:768
  42.1 3.8 %collective-permute-done.8.refs_4_ = bf16[128,384]{1,0:T(8,128)(2,1)S(1)} collective-permute-done((bf16[128,384]{1,0:T(8,128)(2,1)S(1)}, bf16[128,384]{1,0:T(8,128)(2,1)S(1)}, u32[]{:S(2)}, u32[]{:S(2)}) %collective-permute-start.8) | collective-permute-done | bytes 98336 | tf_op jit(solution)/shard_map/ppermute | solution.py:768
  48.5 8.5 %middle_half.1 = (bf16[512,128]{1,0:T(8,128)(2,1)}, bf16[512,256]{1,0:T(8,128)(2,1)}, bf16[512,256]{1,0:T(8,128)(2,1)}, f32[512,256]{1,0:T(8,128)}, bf16[512,256...) custom-call(s32[2]{0:T(128)S(1)} %pad_add_fusion.refs_0_, ...), custom_call_target="tpu_custom_call" | custom-call | flops 10000000000 | bytes 1048576 | tf_op jit(solution)/shard_map/middle_half/pallas_call | solution.py:108
  58.3 2.1 %collective-permute-start.12 = (bf16[512,128]{1,0:T(8,128)(2,1)S(1)}, bf16[512,128]{1,0:T(8,128)(2,1)S(1)}, u32[]{:S(2)}, u32[]{:S(2)}) collective-permute-start(bf16[512,128]{1,0:T(8,128)(2,1)S(1)} %get-tuple-element.112), channel_id=1, source_target_pairs={{0,3},{1,2},{2,1},{3,0},{4,7},{5,6},{6,5},{7,4},{8,11},{9,10},{10,... | collective-permute-start | bytes 393224 | tf_op jit(solution)/shard_map/ppermute | solution.py:768
  63.8 2.8 %collective-permute-done.12 = bf16[512,128]{1,0:T(8,128)(2,1)S(1)} collective-permute-done((bf16[512,128]{1,0:T(8,128)(2,1)S(1)}, bf16[512,128]{1,0:T(8,128)(2,1)S(1)}, u32[]{:S(2)}, u32[]{:S(2)}) %collective-permute-start.12) | collective-permute-done | bytes 131104 | tf_op jit(solution)/shard_map/ppermute | solution.py:768
  68.7 6.1 %collective-permute-done.13.refs_2_ = bf16[512,128]{1,0:T(8,128)(2,1)S(1)} collective-permute-done((bf16[512,128]{1,0:T(8,128)(2,1)S(1)}, bf16[512,128]{1,0:T(8,128)(2,1)S(1)}, u32[]{:S(2)}, u32[]{:S(2)}) %collective-permute-start.13) | collective-permute-done | bytes 131104 | tf_op jit(solution)/shard_map/ppermute | solution.py:768
  74.8 5.4 %turn.1 = (bf16[512,128]{1,0:T(8,128)(2,1)}, bf16[512,256]{1,0:T(8,128)(2,1)}, bf16[512,256]{1,0:T(8,128)(2,1)}, f32[128,1024]{1,0:T(8,128)}, bf16[64,256]{1,0:T...) custom-call(s32[2]{0:T(128)S(1)} %pad_add_fusion.refs_0_, ...), custom_call_target="tpu_custom_call" | custom-call | flops 2000000000 | bytes 1048576 | tf_op jit(solution)/shard_map/turn/pallas_call | solution.py:108
  81.0 2.7 %collective-permute-start.19 = (bf16[128,512]{1,0:T(8,128)(2,1)S(1)}, bf16[128,512]{1,0:T(8,128)(2,1)S(1)}, u32[]{:S(2)}, u32[]{:S(2)}) collective-permute-start(bf16[128,512]{1,0:T(8,128)(2,1)S(1)} %get-tuple-element.122), channel_id=1, source_target_pairs={{0,3},{1,2},{2,1},{3,0},{4,7},{5,6},{6,5},{7,4},{8,11},{9,10},{10,... | collective-permute-start | bytes 393224 | tf_op jit(solution)/shard_map/ppermute | solution.py:768
  83.7 2.0 %collective-permute-done.17 = bf16[128,512]{1,0:T(8,128)(2,1)S(1)} collective-permute-done((bf16[128,512]{1,0:T(8,128)(2,1)S(1)}, bf16[128,512]{1,0:T(8,128)(2,1)S(1)}, u32[]{:S(2)}, u32[]{:S(2)}) %collective-permute-start.17) | collective-permute-done | bytes 131104 | tf_op jit(solution)/shard_map/ppermute | solution.py:768
  87.2 2.1 %collective-permute-done.19 = bf16[128,512]{1,0:T(8,128)(2,1)S(1)} collective-permute-done((bf16[128,512]{1,0:T(8,128)(2,1)S(1)}, bf16[128,512]{1,0:T(8,128)(2,1)S(1)}, u32[]{:S(2)}, u32[]{:S(2)}) %collective-permute-start.19) | collective-permute-done | bytes 131104 | tf_op jit(solution)/shard_map/ppermute | solution.py:768
  89.4 4.1 %large_grads.2 = bf16[4,128,384]{2,1,0:T(8,128)(2,1)S(1)} custom-call(s32[2]{0:T(128)S(1)} %pad_add_fusion.refs_0_, bf16[512,256]{1,0:T(8,128)(2,1)} %get-tuple-element.123.refs_1_, bf16[512,256]{1,0:T(8,128)(2,1)} %get-tuple-element.124.refs_2_, bf16[512,128]{1,0:T(8,128)(2,1)} %get-tuple-element.125.refs_3_, bf16[512,256]{1,0:T(8,128)(2,1)} %get-tuple-element.126.refs_4_, ...), custom_call_target="tpu_custom_call" | custom-call | flops 1000000000 | bytes 1048576 | tf_op jit(solution)/shard_map/large_grads/pallas_call | solution.py:108
  93.5 3.1 %collective-permute-done.20.refs_2_ = bf16[128,512]{1,0:T(8,128)(2,1)S(1)} collective-permute-done((bf16[128,512]{1,0:T(8,128)(2,1)S(1)}, bf16[128,512]{1,0:T(8,128)(2,1)S(1)}, u32[]{:S(2)}, u32[]{:S(2)}) %collective-permute-start.20) | collective-permute-done | bytes 131104 | tf_op jit(solution)/shard_map/ppermute | solution.py:768
  96.6 10.0 %back_middle.1 = (bf16[128,256]{1,0:T(8,128)(2,1)}, bf16[128,512]{1,0:T(8,128)(2,1)S(1)}, bf16[512,256]{1,0:T(8,128)(2,1)}, bf16[512,256]{1,0:T(8,128)(2,1)}, bf...) custom-call(s32[2]{0:T(128)S(1)} %pad_add_fusion.refs_0_, ...), custom_call_target="tpu_custom_call" | custom-call | flops 10000000000 | bytes 1048576 | tf_op jit(solution)/shard_map/back_middle/pallas_call | solution.py:108
  107.5 2.7 %collective-permute-start.23 = (bf16[128,512]{1,0:T(8,128)(2,1)S(1)}, bf16[128,512]{1,0:T(8,128)(2,1)S(1)}, u32[]{:S(2)}, u32[]{:S(2)}) collective-permute-start(bf16[128,512]{1,0:T(8,128)(2,1)S(1)} %get-tuple-element.150), channel_id=1, source_target_pairs={{0,3},{1,2},{2,1},{3,0},{4,7},{5,6},{6,5},{7,4},{8,11},{9,10},{10,... | collective-permute-start | bytes 393224 | tf_op jit(solution)/shard_map/ppermute | solution.py:768
  110.2 2.9 %collective-permute-done.21 = bf16[128,512]{1,0:T(8,128)(2,1)S(1)} collective-permute-done((bf16[128,512]{1,0:T(8,128)(2,1)S(1)}, bf16[128,512]{1,0:T(8,128)(2,1)S(1)}, u32[]{:S(2)}, u32[]{:S(2)}) %collective-permute-start.21) | collective-permute-done | bytes 131104 | tf_op jit(solution)/shard_map/ppermute | solution.py:768
  113.1 1.9 %collective-permute-done.23 = bf16[128,512]{1,0:T(8,128)(2,1)S(1)} collective-permute-done((bf16[128,512]{1,0:T(8,128)(2,1)S(1)}, bf16[128,512]{1,0:T(8,128)(2,1)S(1)}, u32[]{:S(2)}, u32[]{:S(2)}) %collective-permute-start.23) | collective-permute-done | bytes 131104 | tf_op jit(solution)/shard_map/ppermute | solution.py:768
  117.2 4.3 %large_grads.3 = bf16[4,128,384]{2,1,0:T(8,128)(2,1)S(1)} custom-call(s32[2]{0:T(128)S(1)} %pad_add_fusion.refs_0_, bf16[512,256]{1,0:T(8,128)(2,1)} %get-tuple-element.177.refs_1_, bf16[512,256]{1,0:T(8,128)(2,1)} %get-tuple-element.178.refs_2_, bf16[512,128]{1,0:T(8,128)(2,1)} %get-tuple-element.179.refs_3_, bf16[512,256]{1,0:T(8,128)(2,1)} %get-tuple-element.180.refs_4_, ...), custom_call_target="tpu_custom_call" | custom-call | flops 1000000000 | bytes 1048576 | tf_op jit(solution)/shard_map/large_grads/pallas_call | solution.py:108
  122.3 2.1 %collective-permute-start.25 = (bf16[4,64,256]{2,1,0:T(8,128)(2,1)S(1)}, bf16[4,64,256]{2,1,0:T(8,128)(2,1)S(1)}, u32[]{:S(2)}, u32[]{:S(2)}) collective-permute-start(bf16[4,64,256]{2,1,0:T(8,128)(2,1)S(1)} %copy-done.22), channel_id=1, source_target_pairs={{0,4},{1,5},{2,6},{3,7},{4,0},{5,1},{6,2},{7,3},{8,12},{9,13},{10,... | collective-permute-start | bytes 393224 | tf_op jit(solution)/shard_map/ppermute | solution.py:768
  126.4 3.8 %collective-permute-done.32.refs_6_ = bf16[128,384]{1,0:T(8,128)(2,1)S(1)} collective-permute-done((bf16[128,384]{1,0:T(8,128)(2,1)S(1)}, bf16[128,384]{1,0:T(8,128)(2,1)S(1)}, u32[]{:S(2)}, u32[]{:S(2)}) %collective-permute-start.32) | collective-permute-done | bytes 98336 | tf_op jit(solution)/shard_map/ppermute | solution.py:768
  132.2 3.5 %all-to-all-start.2 = ((bf16[8,16,768]{2,1,0:T(8,128)(2,1)}), bf16[8,16,768]{2,1,0:T(8,128)(2,1)S(1)}, u32[]{:S(2)}, u32[]{:S(2)}) async-start(bf16[8,16,768]{2,1,0:T(8,128)(2,1)} %bitcast.28), calls=%async_computation.2 | async-start | bytes 393216 | tf_op jit(solution)/shard_map/all_to_all | solution.py:748
  135.8 2.0 %collective-permute-start.26 = (bf16[2,64,256]{2,1,0:T(8,128)(2,1)S(1)}, bf16[2,64,256]{2,1,0:T(8,128)(2,1)S(1)}, u32[]{:S(2)}, u32[]{:S(2)}) collective-permute-start(bf16[2,64,256]{2,1,0:T(8,128)(2,1)S(1)} %slice.49), channel_id=1, source_target_pairs={{0,2},{1,3},{2,0},{3,1},{4,6},{5,7},{6,4},{7,5},{8,10},{9,11},{10,... | collective-permute-start | bytes 196616 | tf_op jit(solution)/shard_map/ppermute | solution.py:768
  137.7 7.7 %back_last.1 = (bf16[4,128,256]{2,1,0:T(8,128)(2,1)}, f32[128,1024]{1,0:T(8,128)}) custom-call(bf16[128,512]{1,0:T(8,128)(2,1)S(1)} %add_convert_fusion.1.refs_0_, bf16[128,512]{1,0:T(8,128)(2,1)S(1)} %collective-permute-done.24.refs_1_, f32[128,1024]{1,0:T(8,128)} %get-tuple-element.154.refs_2_, bf16[128,1024]{1,0:T(8,128)(2,1)} %get-tuple-element.155.refs_3_, ...), custom_call_target="tpu_custom_call" | custom-call | flops 10000000000 | bytes 1048576 | tf_op jit(solution)/shard_map/back_last/pallas_call | solution.py:108
  145.4 4.6 %all-to-all-start.1 = ((bf16[32,16,256]{2,1,0:T(8,128)(2,1)}), bf16[32,16,256]{2,1,0:T(8,128)(2,1)S(1)}, u32[]{:S(2)}, u32[]{:S(2)}) async-start(bf16[32,16,256]{2,1,0:T(8,128)(2,1)} %bitcast.93), calls=%async_computation.1 | async-start | bytes 524288 | tf_op jit(solution)/shard_map/all_to_all | solution.py:956
  151.9 1.9 %turned.2 = bf16[1024,128]{1,0:T(8,128)(2,1)} custom-call(f32[128,1024]{1,0:T(8,128)} %get-tuple-element.120.refs_0_), custom_call_target="tpu_custom_call" | custom-call | flops 100000000 | bytes 1048576 | tf_op jit(solution)/shard_map/turned/pallas_call | solution.py:108
  153.9 2.1 %turned.3 = f32[1024,128]{1,0:T(8,128)} custom-call(f32[128,1024]{1,0:T(8,128)} %get-tuple-element.172.refs_0_), custom_call_target="tpu_custom_call" | custom-call | flops 100000000 | bytes 1048576 | tf_op jit(solution)/shard_map/turned/pallas_call | solution.py:108
  (130 shorter events, 37.1 us)
Async XLA Ops:
  3.7 8.8 %collective-permute-start.4 = (bf16[1,144,256]{2,1,0:T(8,128)(2,1)S(1)}, bf16[1,144,256]{2,1,0:T(8,128)(2,1)S(1)}, u32[]{:S(2)}, u32[]{:S(2)}) collective-permute-start(bf16[1,144,256]{2,1,0:T(8,128)(2,1)S(1)} %pack_cargo.1.refs_1_.refs_23_), channel_id=1, source_target_pairs={{0,4},{1,5},{2,6},{3,7},{4,0},{5,1},{6,2},{7,3},{8,12},{9,13},{10,... | collective-permute-start | bytes 221192 | tf_op jit(solution)/shard_map/ppermute | solution.py:768
  8.5 11.2 %all-to-all-start = ((bf16[8,16,256]{2,1,0:T(8,128)(2,1)}), bf16[8,16,256]{2,1,0:T(8,128)(2,1)S(1)}, u32[]{:S(2)}, u32[]{:S(2)}) async-start(bf16[8,16,256]{2,1,0:T(8,128)(2,1)} %pack_first.1), calls=%async_computation | async-start | bytes 131072 | tf_op jit(solution)/shard_map/all_to_all | solution.py:748
  12.5 16.8 %collective-permute-start.5 = (bf16[2,144,256]{2,1,0:T(8,128)(2,1)S(1)}, bf16[2,144,256]{2,1,0:T(8,128)(2,1)S(1)}, u32[]{:S(2)}, u32[]{:S(2)}) collective-permute-start(bf16[2,144,256]{2,1,0:T(8,128)(2,1)S(1)} %pad_maximum_fusion.1), channel_id=1, source_target_pairs={{0,2},{1,3},{2,0},{3,1},{4,6},{5,7},{6,4},{7,5},{8,10},{9,11},{10,... | collective-permute-start | bytes 442376 | tf_op jit(solution)/shard_map/ppermute | solution.py:768
  25.8 8.6 %collective-permute-start = (bf16[512,128]{1,0:T(8,128)(2,1)S(1)}, bf16[512,128]{1,0:T(8,128)(2,1)S(1)}, u32[]{:S(2)}, u32[]{:S(2)}) collective-permute-start(bf16[512,128]{1,0:T(8,128)(2,1)S(1)} %get-tuple-element.99), channel_id=1, source_target_pairs={{0,1},{1,0},{2,3},{3,2},{4,5},{5,4},{6,7},{7,6},{8,9},{9,8},{10,11... | collective-permute-start | bytes 393224 | tf_op jit(solution)/shard_map/ppermute | solution.py:768
  26.2 8.3 %collective-permute-start.1 = (bf16[512,128]{1,0:T(8,128)(2,1)S(1)}, bf16[512,128]{1,0:T(8,128)(2,1)S(1)}, u32[]{:S(2)}, u32[]{:S(2)}) collective-permute-start(bf16[512,128]{1,0:T(8,128)(2,1)S(1)} %get-tuple-element.99), channel_id=1, source_target_pairs={{0,2},{1,3},{2,0},{3,1},{4,6},{5,7},{6,4},{7,5},{8,10},{9,11},{10,... | collective-permute-start | bytes 393224 | tf_op jit(solution)/shard_map/ppermute | solution.py:768
  27.1 7.4 %collective-permute-start.2 = (bf16[512,128]{1,0:T(8,128)(2,1)S(1)}, bf16[512,128]{1,0:T(8,128)(2,1)S(1)}, u32[]{:S(2)}, u32[]{:S(2)}) collective-permute-start(bf16[512,128]{1,0:T(8,128)(2,1)S(1)} %get-tuple-element.99), channel_id=1, source_target_pairs={{0,3},{1,2},{2,1},{3,0},{4,7},{5,6},{6,5},{7,4},{8,11},{9,10},{10,... | collective-permute-start | bytes 393224 | tf_op jit(solution)/shard_map/ppermute | solution.py:768
  29.4 9.9 %collective-permute-start.6 = (bf16[4,144,256]{2,1,0:T(8,128)(2,1)S(1)}, bf16[4,144,256]{2,1,0:T(8,128)(2,1)S(1)}, u32[]{:S(2)}, u32[]{:S(2)}) collective-permute-start(bf16[4,144,256]{2,1,0:T(8,128)(2,1)S(1)} %pad_maximum_fusion), channel_id=1, source_target_pairs={{0,1},{1,0},{2,3},{3,2},{4,5},{5,4},{6,7},{7,6},{8,9},{9,8},{10,11... | collective-permute-start | bytes 884744 | tf_op jit(solution)/shard_map/ppermute | solution.py:768
  34.5 13.9 %collective-permute-start.3 = (bf16[512,128]{1,0:T(8,128)(2,1)S(1)}, bf16[512,128]{1,0:T(8,128)(2,1)S(1)}, u32[]{:S(2)}, u32[]{:S(2)}) collective-permute-start(bf16[512,128]{1,0:T(8,128)(2,1)S(1)} %add_convert_fusion.4.refs_1_), channel_id=1, source_target_pairs={{0,4},{1,5},{2,6},{3,7},{4,0},{5,1},{6,2},{7,3},{8,12},{9,13},{10,... | collective-permute-start | bytes 393224 | tf_op jit(solution)/shard_map/ppermute | solution.py:768
  40.2 5.7 %collective-permute-start.8 = (bf16[128,384]{1,0:T(8,128)(2,1)S(1)}, bf16[128,384]{1,0:T(8,128)(2,1)S(1)}, u32[]{:S(2)}, u32[]{:S(2)}) collective-permute-start(bf16[128,384]{1,0:T(8,128)(2,1)S(1)} %get-tuple-element.100.refs_2_), channel_id=1, source_target_pairs={{0,16},{8,24},{16,0},{24,8},{1,17},{9,25},{17,1},{25,9},{2,18},{10... | collective-permute-start | bytes 294920 | tf_op jit(solution)/shard_map/ppermute | solution.py:768
  56.9 5.7 %collective-permute-start.10 = (bf16[512,128]{1,0:T(8,128)(2,1)S(1)}, bf16[512,128]{1,0:T(8,128)(2,1)S(1)}, u32[]{:S(2)}, u32[]{:S(2)}) collective-permute-start(bf16[512,128]{1,0:T(8,128)(2,1)S(1)} %get-tuple-element.112), channel_id=1, source_target_pairs={{0,1},{1,0},{2,3},{3,2},{4,5},{5,4},{6,7},{7,6},{8,9},{9,8},{10,11... | collective-permute-start | bytes 393224 | tf_op jit(solution)/shard_map/ppermute | solution.py:768
  57.5 6.4 %collective-permute-start.11 = (bf16[512,128]{1,0:T(8,128)(2,1)S(1)}, bf16[512,128]{1,0:T(8,128)(2,1)S(1)}, u32[]{:S(2)}, u32[]{:S(2)}) collective-permute-start(bf16[512,128]{1,0:T(8,128)(2,1)S(1)} %get-tuple-element.112), channel_id=1, source_target_pairs={{0,2},{1,3},{2,0},{3,1},{4,6},{5,7},{6,4},{7,5},{8,10},{9,11},{10,... | collective-permute-start | bytes 393224 | tf_op jit(solution)/shard_map/ppermute | solution.py:768
  58.3 8.3 %collective-permute-start.12 = (bf16[512,128]{1,0:T(8,128)(2,1)S(1)}, bf16[512,128]{1,0:T(8,128)(2,1)S(1)}, u32[]{:S(2)}, u32[]{:S(2)}) collective-permute-start(bf16[512,128]{1,0:T(8,128)(2,1)S(1)} %get-tuple-element.112), channel_id=1, source_target_pairs={{0,3},{1,2},{2,1},{3,0},{4,7},{5,6},{6,5},{7,4},{8,11},{9,10},{10,... | collective-permute-start | bytes 393224 | tf_op jit(solution)/shard_map/ppermute | solution.py:768
  60.5 7.1 %collective-permute-start.14 = (bf16[128,384]{1,0:T(8,128)(2,1)S(1)}, bf16[128,384]{1,0:T(8,128)(2,1)S(1)}, u32[]{:S(2)}, u32[]{:S(2)}) collective-permute-start(bf16[128,384]{1,0:T(8,128)(2,1)S(1)} %get-tuple-element.113.refs_1_), channel_id=1, source_target_pairs={{0,8},{8,0},{16,24},{24,16},{1,9},{9,1},{17,25},{25,17},{2,10},{10... | collective-permute-start | bytes 294920 | tf_op jit(solution)/shard_map/ppermute | solution.py:768
  60.5 7.1 %collective-permute-start.15 = (bf16[128,384]{1,0:T(8,128)(2,1)S(1)}, bf16[128,384]{1,0:T(8,128)(2,1)S(1)}, u32[]{:S(2)}, u32[]{:S(2)}) collective-permute-start(bf16[128,384]{1,0:T(8,128)(2,1)S(1)} %get-tuple-element.113.refs_1_), channel_id=1, source_target_pairs={{0,16},{8,24},{16,0},{24,8},{1,17},{9,25},{17,1},{25,9},{2,18},{10... | collective-permute-start | bytes 294920 | tf_op jit(solution)/shard_map/ppermute | solution.py:768
  66.7 8.0 %collective-permute-start.13 = (bf16[512,128]{1,0:T(8,128)(2,1)S(1)}, bf16[512,128]{1,0:T(8,128)(2,1)S(1)}, u32[]{:S(2)}, u32[]{:S(2)}) collective-permute-start(bf16[512,128]{1,0:T(8,128)(2,1)S(1)} %add_convert_fusion.3.refs_1_), channel_id=1, source_target_pairs={{0,4},{1,5},{2,6},{3,7},{4,0},{5,1},{6,2},{7,3},{8,12},{9,13},{10,... | collective-permute-start | bytes 393224 | tf_op jit(solution)/shard_map/ppermute | solution.py:768
  80.2 5.6 %collective-permute-start.17 = (bf16[128,512]{1,0:T(8,128)(2,1)S(1)}, bf16[128,512]{1,0:T(8,128)(2,1)S(1)}, u32[]{:S(2)}, u32[]{:S(2)}) collective-permute-start(bf16[128,512]{1,0:T(8,128)(2,1)S(1)} %get-tuple-element.122), channel_id=1, source_target_pairs={{0,1},{1,0},{2,3},{3,2},{4,5},{5,4},{6,7},{7,6},{8,9},{9,8},{10,11... | collective-permute-start | bytes 393224 | tf_op jit(solution)/shard_map/ppermute | solution.py:768
  81.0 6.1 %collective-permute-start.18 = (bf16[128,512]{1,0:T(8,128)(2,1)S(1)}, bf16[128,512]{1,0:T(8,128)(2,1)S(1)}, u32[]{:S(2)}, u32[]{:S(2)}) collective-permute-start(bf16[128,512]{1,0:T(8,128)(2,1)S(1)} %get-tuple-element.122), channel_id=1, source_target_pairs={{0,2},{1,3},{2,0},{3,1},{4,6},{5,7},{6,4},{7,5},{8,10},{9,11},{10,... | collective-permute-start | bytes 393224 | tf_op jit(solution)/shard_map/ppermute | solution.py:768
  81.0 8.3 %collective-permute-start.19 = (bf16[128,512]{1,0:T(8,128)(2,1)S(1)}, bf16[128,512]{1,0:T(8,128)(2,1)S(1)}, u32[]{:S(2)}, u32[]{:S(2)}) collective-permute-start(bf16[128,512]{1,0:T(8,128)(2,1)S(1)} %get-tuple-element.122), channel_id=1, source_target_pairs={{0,3},{1,2},{2,1},{3,0},{4,7},{5,6},{6,5},{7,4},{8,11},{9,10},{10,... | collective-permute-start | bytes 393224 | tf_op jit(solution)/shard_map/ppermute | solution.py:768
  89.3 7.3 %collective-permute-start.20 = (bf16[128,512]{1,0:T(8,128)(2,1)S(1)}, bf16[128,512]{1,0:T(8,128)(2,1)S(1)}, u32[]{:S(2)}, u32[]{:S(2)}) collective-permute-start(bf16[128,512]{1,0:T(8,128)(2,1)S(1)} %add_convert_fusion.2.refs_1_), channel_id=1, source_target_pairs={{0,4},{1,5},{2,6},{3,7},{4,0},{5,1},{6,2},{7,3},{8,12},{9,13},{10,... | collective-permute-start | bytes 393224 | tf_op jit(solution)/shard_map/ppermute | solution.py:768
  106.6 6.4 %collective-permute-start.21 = (bf16[128,512]{1,0:T(8,128)(2,1)S(1)}, bf16[128,512]{1,0:T(8,128)(2,1)S(1)}, u32[]{:S(2)}, u32[]{:S(2)}) collective-permute-start(bf16[128,512]{1,0:T(8,128)(2,1)S(1)} %get-tuple-element.150), channel_id=1, source_target_pairs={{0,1},{1,0},{2,3},{3,2},{4,5},{5,4},{6,7},{7,6},{8,9},{9,8},{10,11... | collective-permute-start | bytes 393224 | tf_op jit(solution)/shard_map/ppermute | solution.py:768
  107.5 5.6 %collective-permute-start.22 = (bf16[128,512]{1,0:T(8,128)(2,1)S(1)}, bf16[128,512]{1,0:T(8,128)(2,1)S(1)}, u32[]{:S(2)}, u32[]{:S(2)}) collective-permute-start(bf16[128,512]{1,0:T(8,128)(2,1)S(1)} %get-tuple-element.150), channel_id=1, source_target_pairs={{0,2},{1,3},{2,0},{3,1},{4,6},{5,7},{6,4},{7,5},{8,10},{9,11},{10,... | collective-permute-start | bytes 393224 | tf_op jit(solution)/shard_map/ppermute | solution.py:768
  107.5 7.5 %collective-permute-start.23 = (bf16[128,512]{1,0:T(8,128)(2,1)S(1)}, bf16[128,512]{1,0:T(8,128)(2,1)S(1)}, u32[]{:S(2)}, u32[]{:S(2)}) collective-permute-start(bf16[128,512]{1,0:T(8,128)(2,1)S(1)} %get-tuple-element.150), channel_id=1, source_target_pairs={{0,3},{1,2},{2,1},{3,0},{4,7},{5,6},{6,5},{7,4},{8,11},{9,10},{10,... | collective-permute-start | bytes 393224 | tf_op jit(solution)/shard_map/ppermute | solution.py:768
  115.0 7.3 %collective-permute-start.24 = (bf16[128,512]{1,0:T(8,128)(2,1)S(1)}, bf16[128,512]{1,0:T(8,128)(2,1)S(1)}, u32[]{:S(2)}, u32[]{:S(2)}) collective-permute-start(bf16[128,512]{1,0:T(8,128)(2,1)S(1)} %add_convert_fusion.1.refs_0_), channel_id=1, source_target_pairs={{0,4},{1,5},{2,6},{3,7},{4,0},{5,1},{6,2},{7,3},{8,12},{9,13},{10,... | collective-permute-start | bytes 393224 | tf_op jit(solution)/shard_map/ppermute | solution.py:768
  115.3 9.3 %collective-permute-start.28 = (bf16[128,384]{1,0:T(8,128)(2,1)S(1)}, bf16[128,384]{1,0:T(8,128)(2,1)S(1)}, u32[]{:S(2)}, u32[]{:S(2)}) collective-permute-start(bf16[128,384]{1,0:T(8,128)(2,1)S(1)} %get-tuple-element.195), channel_id=1, source_target_pairs={{0,8},{8,0},{16,24},{24,16},{1,9},{9,1},{17,25},{25,17},{2,10},{10... | collective-permute-start | bytes 294920 | tf_op jit(solution)/shard_map/ppermute | solution.py:768
  115.4 10.7 %collective-permute-start.29 = (bf16[128,384]{1,0:T(8,128)(2,1)S(1)}, bf16[128,384]{1,0:T(8,128)(2,1)S(1)}, u32[]{:S(2)}, u32[]{:S(2)}) collective-permute-start(bf16[128,384]{1,0:T(8,128)(2,1)S(1)} %get-tuple-element.194), channel_id=1, source_target_pairs={{0,16},{8,24},{16,0},{24,8},{1,17},{9,25},{17,1},{25,9},{2,18},{10... | collective-permute-start | bytes 294920 | tf_op jit(solution)/shard_map/ppermute | solution.py:768
  116.8 9.6 %collective-permute-start.30 = (bf16[128,384]{1,0:T(8,128)(2,1)S(1)}, bf16[128,384]{1,0:T(8,128)(2,1)S(1)}, u32[]{:S(2)}, u32[]{:S(2)}) collective-permute-start(bf16[128,384]{1,0:T(8,128)(2,1)S(1)} %get-tuple-element.193), channel_id=1, source_target_pairs={{0,24},{8,16},{16,8},{24,0},{1,25},{9,17},{17,9},{25,1},{2,26},{10... | collective-permute-start | bytes 294920 | tf_op jit(solution)/shard_map/ppermute | solution.py:768
  122.3 13.4 %collective-permute-start.25 = (bf16[4,64,256]{2,1,0:T(8,128)(2,1)S(1)}, bf16[4,64,256]{2,1,0:T(8,128)(2,1)S(1)}, u32[]{:S(2)}, u32[]{:S(2)}) collective-permute-start(bf16[4,64,256]{2,1,0:T(8,128)(2,1)S(1)} %copy-done.22), channel_id=1, source_target_pairs={{0,4},{1,5},{2,6},{3,7},{4,0},{5,1},{6,2},{7,3},{8,12},{9,13},{10,... | collective-permute-start | bytes 393224 | tf_op jit(solution)/shard_map/ppermute | solution.py:768
  124.6 5.6 %collective-permute-start.32 = (bf16[128,384]{1,0:T(8,128)(2,1)S(1)}, bf16[128,384]{1,0:T(8,128)(2,1)S(1)}, u32[]{:S(2)}, u32[]{:S(2)}) collective-permute-start(bf16[128,384]{1,0:T(8,128)(2,1)S(1)} %get-tuple-element.190), channel_id=1, source_target_pairs={{0,16},{8,24},{16,0},{24,8},{1,17},{9,25},{17,1},{25,9},{2,18},{10... | collective-permute-start | bytes 294920 | tf_op jit(solution)/shard_map/ppermute | solution.py:768
  132.2 13.3 %all-to-all-start.2 = ((bf16[8,16,768]{2,1,0:T(8,128)(2,1)}), bf16[8,16,768]{2,1,0:T(8,128)(2,1)S(1)}, u32[]{:S(2)}, u32[]{:S(2)}) async-start(bf16[8,16,768]{2,1,0:T(8,128)(2,1)} %bitcast.28), calls=%async_computation.2 | async-start | bytes 393216 | tf_op jit(solution)/shard_map/all_to_all | solution.py:748
  135.8 14.3 %collective-permute-start.26 = (bf16[2,64,256]{2,1,0:T(8,128)(2,1)S(1)}, bf16[2,64,256]{2,1,0:T(8,128)(2,1)S(1)}, u32[]{:S(2)}, u32[]{:S(2)}) collective-permute-start(bf16[2,64,256]{2,1,0:T(8,128)(2,1)S(1)} %slice.49), channel_id=1, source_target_pairs={{0,2},{1,3},{2,0},{3,1},{4,6},{5,7},{6,4},{7,5},{8,10},{9,11},{10,... | collective-permute-start | bytes 196616 | tf_op jit(solution)/shard_map/ppermute | solution.py:768
  145.4 15.5 %all-to-all-start.1 = ((bf16[32,16,256]{2,1,0:T(8,128)(2,1)}), bf16[32,16,256]{2,1,0:T(8,128)(2,1)S(1)}, u32[]{:S(2)}, u32[]{:S(2)}) async-start(bf16[32,16,256]{2,1,0:T(8,128)(2,1)} %bitcast.93), calls=%async_computation.1 | async-start | bytes 524288 | tf_op jit(solution)/shard_map/all_to_all | solution.py:956
  150.1 7.8 %collective-permute-start.27 = (bf16[64,256]{1,0:T(8,128)(2,1)S(1)}, bf16[64,256]{1,0:T(8,128)(2,1)S(1)}, u32[]{:S(2)}, u32[]{:S(2)}) collective-permute-start(bf16[64,256]{1,0:T(8,128)(2,1)S(1)} %slice_bitcast_fusion.8), channel_id=1, source_target_pairs={{0,1},{1,0},{2,3},{3,2},{4,5},{5,4},{6,7},{7,6},{8,9},{9,8},{10,11... | collective-permute-start | bytes 98312 | tf_op jit(solution)/shard_map/ppermute | solution.py:768
  (31 other events, 167.7 us)

commit v3 on v2

--- a/solution.py
+++ b/solution.py
@@ -42,12 +42,17 @@
 
 class Late:
     def __init__(self, source, ref, sem):
-        self.ref, self.copy, self.here = ref, pltpu.make_async_copy(source, ref, sem), False
-        self.shape = ref.shape
-        self.copy.start()
+        self.ref, self.copy = ref, pltpu.make_async_copy(source, ref, sem)
+        self.shape, self.begun, self.here = ref.shape, False, False
+
+    def start(self):
+        if not self.begun:
+            self.copy.start()
+            self.begun = True
 
     def wait(self):
         if not self.here:
+            self.start()
             self.copy.wait()
             self.here = True
 
@@ -73,14 +78,28 @@
             self.sent = True
 
 
+def begin(*refs):
+    for ref in refs:
+        if isinstance(ref, Late):
+            ref.start()
+
+
+def arrive(*refs):
+    for ref in refs:
+        if isinstance(ref, Late):
+            ref.wait()
+
+
 def send(*refs):
     for ref in refs:
         if isinstance(ref, Kept):
             ref.send()
 
 
-def call(body, outs, args, flops=10**9, late=(), kept=(), smem=0, scratch=()):
-    moved = [args[i] for i in late] + [outs[i] for i in kept]
+def call(body, outs, args, flops=10**9, late=(), kept=(), smem=0, scratch=(), early=None, alias=None):
+    alias = alias or {}
+    held = [i for i in kept if i not in alias.values()]
+    moved = [args[i] for i in late] + [outs[i] for i in held]
 
     def kernel(*refs):
         refs = list(refs)
@@ -90,20 +109,21 @@
         buffers, sems = rest[: len(moved)], rest[len(moved) :]
         for k, i in enumerate(late):
             ins[i] = Late(ins[i], buffers[k], sems[k])
-        for k, i in enumerate(kept, len(late)):
+        begin(*[ins[i] for i in (late if early is None else early)])
+        for k, i in enumerate(held, len(late)):
             results[i] = Kept(results[i], buffers[k], sems[k])
         body(*ins, *results, *extra)
         for i in late:
             ins[i].wait()
-        for i in kept:
+        for i in held:
             results[i].send()
-        for i in kept:
+        for i in held:
             results[i].copy.wait()
 
-    args = [pltpu.with_memory_space_constraint(x, pltpu.HBM) if i in late else x for i, x in enumerate(args)]
+    args = [pltpu.with_memory_space_constraint(x, pltpu.HBM) if i in late or i in alias else x for i, x in enumerate(args)]
     outs = [pltpu.HBM(x.shape, x.dtype) if i in kept else x for i, x in enumerate(outs)]
     space = [pltpu.SMEM] * smem + [pltpu.VMEM] * (len(args) - smem)
-    for i in late:
+    for i in [*late, *alias]:
         space[i] = pltpu.HBM
     return pl.pallas_call(
         kernel,
@@ -113,15 +133,41 @@
             pl.BlockSpec(memory_space=pltpu.HBM if i in kept else pltpu.VMEM)
             for i in range(len(outs))
         ],
-        scratch_shapes=[pltpu.VMEM(shape, F32) for shape in scratch]
+        scratch_shapes=[pltpu.VMEM(x, F32) if isinstance(x, tuple) else x for x in scratch]
         + [pltpu.VMEM(m.shape, m.dtype) for m in moved]
         + [pltpu.SemaphoreType.DMA] * len(moved),
-        compiler_params=pltpu.CompilerParams(vmem_limit_bytes=40 * 2**20),
+        input_output_aliases=alias,
+        compiler_params=pltpu.CompilerParams(vmem_limit_bytes=24 * 2**20),
         cost_estimate=pl.CostEstimate(flops=flops, bytes_accessed=2**20, transcendentals=0),
         name=body.__name__,
     )(*args)
 
 
+def fetch(arrays):
+    count = len(arrays)
+
+    def kernel(*refs):
+        copies = [
+            pltpu.make_async_copy(refs[i], refs[count + i], refs[2 * count + i]) for i in range(count)
+        ]
+        for copy in copies:
+            copy.start()
+        for copy in copies:
+            copy.wait()
+
+    results = pl.pallas_call(
+        kernel,
+        out_shape=[sds(x.shape, x.dtype) for x in arrays],
+        in_specs=[pl.BlockSpec(memory_space=pltpu.HBM)] * count,
+        out_specs=[pl.BlockSpec(memory_space=pltpu.VMEM)] * count,
+        scratch_shapes=[pltpu.SemaphoreType.DMA] * count,
+        compiler_params=pltpu.CompilerParams(vmem_limit_bytes=2**20 * 20),
+        cost_estimate=pl.CostEstimate(flops=10**9, bytes_accessed=2**20, transcendentals=0),
+        name="fetch",
+    )(*[pltpu.with_memory_space_constraint(x, pltpu.HBM) for x in arrays])
+    return list(results)
+
+
 def dot(a, b):
     return jnp.dot(a, b, preferred_element_type=F32)
 
@@ -143,7 +189,13 @@
 
 
 def onehot(count, row, first=0):
-    return ones_where(iota((count, row.shape[1]), 0) + first == row)
+    parts = []
+    for start in range(0, count, 256):
+        size = min(256, count - start)
+        ids = iota((size, row.shape[1]), 0).astype(F32).astype(BF16)
+        mask = ids == (row - (first + start)).astype(F32).astype(BF16)
+        parts.append(jnp.where(mask, jnp.ones((), BF16), jnp.zeros((), BF16)))
+    return parts[0] if len(parts) == 1 else jnp.concatenate(parts, axis=0)
 
 
 def sigmoid(v):
@@ -174,8 +226,10 @@
 
 
 def spread(value, high, width):
+    value = low(value)
+    high = high.astype(F32).astype(BF16)
     return jnp.concatenate(
-        [low(jnp.where(high == g, value, 0.0)) for g in range(FOLD // width)], axis=0
+        [jnp.where(high == g, value, jnp.zeros((), BF16)) for g in range(FOLD // width)], axis=0
     )
 
 
@@ -312,11 +366,26 @@
 
 
 def order_of(owners):
+    order = [0]
+    for steps in gather_rounds(owners):
+        order = order + [k ^ step for step in steps for k in order]
+    return order
+
+
+def gather_rounds(owners):
+    rounds, step = [], owners // 2
+    while step > 2:
+        rounds.append([step])
+        step = step // 2
+    return rounds + ([[1, 2, 3]] if owners > 2 else [[1]])
+
+
+def scatter_order(owners):
     order, step = [0], owners // 2
-    while step:
+    while step > 2:
         order = order + [k ^ step for k in order]
         step = step // 2
-    return order
+    return [k ^ low_bits for low_bits in range(4) for k in order]
 
 
 def collect(me, *refs):
@@ -413,12 +482,16 @@
 
 def pair_backward(
     grad_mid, edge_t, basis_ref, in_ref, out_ref, up, down, slope_out, agg_t, xg_ref, bt_ref, slope_in,
+    following,
 ):
     width, edges = up.shape[0], slope_in.shape[1]
     length = edges * width // FOLD
     grad_out = low(grad_mid * slope_out[...].astype(F32))
     grad_up_t = dot_nt(grad_out, agg_t[...])
     table = cut(low(dot(up, grad_out) * pair_scale), width)
+    begin(xg_ref, bt_ref)
+    arrive(xg_ref, bt_ref)
+    begin(*following)
     total = jnp.zeros((FOLD, length), F32)
     grad_basis_t = jnp.zeros((width, D_BASIS), F32)
     items = in_ref.shape[1]
@@ -586,6 +659,7 @@
     gain_ref, update_ref, pushed_ref, hold,
 ):
     free = free_ref[...].astype(F32)
+    begin(mid_in)
     atom_in, hidden, slope, state = atom_forward(near, far, state_in[...], free, first, second)
     atom_in_ref[...] = atom_in
     hidden_ref[...] = hidden
@@ -613,37 +687,48 @@
     )
 
 
-def large_grads(me, update, pushed, atom_in, hidden, sent, grad_pre, src_row, dst_row, small, out_ref, hold):
+def large_grads(update, pushed, grad_pre, src_row, dst_row, atom_in, hidden, sent, *refs):
+    *small, out_ref = refs
+    base = 2 * PAD * len(small)
+    for ref in small:
+        out_ref[:, PAD : 2 * PAD] = ref[...]
+    for lanes, value in large_values(update, pushed, grad_pre, src_row, dst_row, atom_in, hidden, sent):
+        out_ref[:, base + lanes.start : base + lanes.stop] = value
+    send(out_ref)
+
+
+def large_values(update, pushed, grad_pre, src_row, dst_row, atom_in, hidden, sent):
     atoms = sent.shape[0]
     step = min(512, atoms)
+    grads = grad_pre[...]
+    update_t = low(jnp.transpose(update[...].astype(F32)))
+    pushed_t = low(jnp.transpose(pushed[...].astype(F32)))
     grad_src = jnp.zeros((D_EDGE, D_ATOM), F32)
     grad_dst = jnp.zeros((D_EDGE, D_ATOM), F32)
     for start in range(0, atoms, step):
         rows = slice(start, start + step)
-        grads = grad_pre[...]
-        grad_src = grad_src + dot(low(dot_nt(grads, onehot(step, src_row[...], start))), sent[rows])
-        grad_dst = grad_dst + dot(low(dot_nt(grads, onehot(step, dst_row[...], start))), sent[rows])
-    grad_second_t = dot(low(jnp.transpose(update[...].astype(F32))), hidden[...])
-    grad_first_t = dot(low(jnp.transpose(pushed[...].astype(F32))), atom_in[...])
-    hold[:, :256] = small[...].astype(F32)
-    hold[:, 256:512] = put_double(grad_first_t).astype(F32)
-    hold[:, 512:1024] = put_double(grad_second_t).astype(F32)
-    hold[:, 1024:1280] = grad_src
-    hold[:, 1280:1536] = grad_dst
-    pieces, _, width = out_ref.shape
-    for g in range(pieces):
-        out_ref[g ^ me[1]] = low(hold[:, g * width : (g + 1) * width])
+        sums = [low(dot_nt(grads, onehot(step, row[...], start))) for row in (src_row, dst_row)]
+        grad_src = grad_src + dot(sums[0], sent[rows])
+        grad_dst = grad_dst + dot(sums[1], sent[rows])
+    grad_second_t = dot(update_t, hidden[...])
+    grad_first_t = dot(pushed_t, atom_in[...])
+    return [
+        (slice(0, 256), put_double(grad_first_t)),
+        (slice(256, 768), put_double(grad_second_t)),
+        (slice(768, 1024), low(grad_src)),
+        (slice(1024, 1280), low(grad_dst)),
+    ]
 
 
 def turned(value_ref, out_ref):
     out_ref[...] = jnp.transpose(value_ref[...]).astype(out_ref.dtype)
 
 
-def block_backward(near, far, grad_in, *refs):
+def block_backward(near, far, grad_in, *refs, more_refs=()):
     mid, tri_refs, edge_ref, quad_refs = refs[0], refs[1:6], refs[6], refs[7:12]
     up_tri, up_quad, down_tri, down_quad, radial_t = refs[12:17]
     radial_basis, tri_basis, quad_basis, tri_in, tri_out, quad_in, quad_out = refs[17:24]
-    dst_row, small_ref = refs[24], refs[25]
+    dst_row = refs[24]
     gain_t = low(near[...].astype(F32) + far[...].astype(F32))
     atoms = gain_t.shape[1]
     step = min(512, atoms)
@@ -655,32 +740,41 @@
     radial = dot(radial_t[...], radial_basis[...])
     grad_mid = grad_in[...] + grad_message * radial
     grad_radial = low(grad_message * mid[...].astype(F32))
+    begin(*tri_refs[2:], edge_ref)
     small = put_wide(dot_nt(grad_radial, radial_basis[...]), OFF_RADIAL)
     total = grad_mid
-    for kept, basis, inner, outer, up, down in (
-        (tri_refs, tri_basis, tri_in, tri_out, up_tri, down_tri),
-        (quad_refs, quad_basis, quad_in, quad_out, up_quad, down_quad),
+    for kept, basis, inner, outer, up, down, following in (
+        (tri_refs, tri_basis, tri_in, tri_out, up_tri, down_tri, quad_refs),
+        (quad_refs, quad_basis, quad_in, quad_out, up_quad, down_quad, more_refs),
     ):
-        value, more = pair_backward(grad_mid, edge_ref, basis, inner, outer, up[...], down[...], *kept)
+        value, more = pair_backward(
+            grad_mid, edge_ref, basis, inner, outer, up[...], down[...], *kept, following
+        )
         total = total + value
         small = small + more
-    small_ref[...] = jnp.broadcast_to(low(small), small_ref.shape)
-    send(small_ref)
-    return total
+    return total, low(small)
 
 
 BACK = 28
 
 
 def back_last(*refs):
-    refs[-1][...] = block_backward(*refs[:-1])
+    _, grad_ref, all_ref, hold, sem = refs[BACK:]
+    grad, small = block_backward(*refs[:BACK])
+    hold[...] = small
+    copy = pltpu.make_async_copy(hold, all_ref.at[:, :PAD], sem)
+    copy.start()
+    grad_ref[...] = grad
+    copy.wait()
 
 
 def back_middle(me, *refs):
     back, refs = refs[:BACK], refs[BACK:]
     big, first, second, src_row, slope_edge, free_ref, slope_atom, held = refs[:8]
-    small_ref, gain_ref, update_ref, pushed_ref, grad_pre_ref, grad_ref, high_ref, low_ref, grad_atoms = refs[8:]
-    grad = block_backward(*back, small_ref)
+    small_ref, gain_ref, update_ref, pushed_ref, grad_pre_ref, grad_ref = refs[8:14]
+    *parts, grad_atoms = refs[14:]
+    grad, small = block_backward(*back, more_refs=(slope_edge, free_ref, slope_atom, held))
+    small_ref[...] = small
     grad_ref[...] = grad
     grad_pre = low(grad * slope_edge[...].astype(F32))
     grad_pre_ref[...] = grad_pre
@@ -690,11 +784,10 @@
         grad_pre, big, first, second, src_row, back[-1], free_ref[...].astype(F32),
         slope_atom[...].astype(F32), grad_atoms, gain_ref, update_ref, pushed_ref,
     )
-    half, count, _ = low_ref.shape
-    for k in range(half):
-        for ref, step in ((low_ref, k), (high_ref, half + k)):
-            rows = pl.ds(pl.multiple_of((me[0] ^ step) * count, count), count)
-            ref[k] = low(grad_atoms[rows])
+    quarter, count, _ = parts[0].shape
+    for k, step in enumerate(scatter_order(4 * quarter)):
+        rows = pl.ds(pl.multiple_of((me[0] ^ step) * count, count), count)
+        parts[k // quarter][k % quarter] = low(grad_atoms[rows])
 
 
 def total_of(arrived):
@@ -704,32 +797,30 @@
     return total
 
 
-def sum_parts(arrived, out_ref):
-    out_ref[...] = low(total_of(arrived))
-
-
-def sum_pieces(*refs):
-    *pieces, out_ref = refs
-    count = len(pieces) // 2
-    width = pieces[0].shape[1]
-    for side in range(2):
-        total = pieces[side * count][...].astype(F32)
-        for piece in pieces[side * count + 1 : (side + 1) * count]:
-            total = total + piece[...].astype(F32)
-        out_ref[:, side * width : (side + 1) * width] = low(total)
-
-
-def adam(me, last, weights, first, second, *refs):
-    *pieces, grad_ref, weights_ref, first_ref, second_ref, low_ref, hold = refs
-    width = pieces[0].shape[1] // 2
-    for k, piece in enumerate(pieces):
-        hold[me[1] ^ k] = piece[...].astype(F32)
-    two, one = [
-        jnp.concatenate([hold[g, :, side * width : (side + 1) * width] for g in range(len(pieces))], axis=1)
-        for side in range(2)
-    ]
+def sum_list(pieces):
+    total = pieces[0][...].astype(F32)
+    for piece in pieces[1:]:
+        total = total + piece[...].astype(F32)
+    return total
+
+
+def sum_parts(one, two, out_ref):
+    width = one.shape[2]
+    out_ref[:, :width] = low(total_of(one))
+    out_ref[:, width:] = low(total_of(two))
+
+
+def adam(weights, first, second, *refs):
+    *pieces, grad_ref, weights_ref, first_ref, second_ref, low_ref = refs
+    total = sum_list(pieces)
     grad = jnp.concatenate(
-        [total_of(last)[:, :SMALL], one[:, PAD:], one[:, :SMALL], two[:, PAD:]], axis=1
+        [
+            total[:, :SMALL],
+            total[:, 2 * PAD : 2 * PAD + BIG],
+            total[:, PAD : PAD + SMALL],
+            total[:, 2 * PAD + BIG :],
+        ],
+        axis=1,
     )
     grad_ref[...] = grad
     old = weights[...]
@@ -748,7 +839,7 @@
     return lax.all_to_all(pieces, "shard", split_axis=0, concat_axis=0)
 
 
-def sum_pair(table, owners):
+def sum_pair(table, owners, beside=None):
     rounds = []
     step = 1
     while step < owners:
@@ -757,11 +848,14 @@
     if len(rounds) > 2:
         rounds = [[1, 2, 3]] + rounds[2:]
     for steps in rounds[:-1]:
+        others = [moved(table, k, owners) for k in steps]
+        if beside is not None:
+            table, beside = lax.optimization_barrier((table, beside))
         total = table.astype(F32)
-        for k in steps:
-            total = total + moved(table, k, owners).astype(F32)
+        for other in others:
+            total = total + other.astype(F32)
         table = total.astype(BF16)
-    return table, moved(table, rounds[-1][0], owners)
+    return table, moved(table, rounds[-1][0], owners), beside
 
 
 def moved(table, step, owners, axis="shard"):
@@ -783,21 +877,22 @@
     weights_t = jnp.transpose(weights)
     cols = weights_t.shape[0]
     lanes = (BIG + PAD) // groups
-    [pack] = call(pack_first, [sds((owners, ROWS, PAD), BF16)], [weights_t], flops=10**7)
+    [pack] = call(pack_first, [sds((owners, ROWS, PAD), BF16)], [weights_t], flops=10**7, late=[0])
+    pack, state = lax.optimization_barrier((pack, atom_state))
     pack = exchange(pack)
     [cargo] = call(
         pack_cargo,
         [sds((1, count + ROWS * (1 + 2 * slots(lanes)), D_ATOM), BF16)],
-        [me, weights_t, atom_state, fixed_atoms.reshape(1, count)],
+        [me, weights_t, state, fixed_atoms.reshape(1, count)],
         flops=10**7,
+        late=[1, 2],
         smem=1,
         scratch=[(groups, cols, lanes)],
     )
     cargo = [cargo]
-    step = owners // 2
-    while step:
-        cargo.append(moved(cargo[0] if len(cargo) == 1 else jnp.concatenate(cargo, axis=0), step, owners))
-        step = step // 2
+    for steps in gather_rounds(owners):
+        held = cargo[0] if len(cargo) == 1 else jnp.concatenate(cargo, axis=0)
+        cargo = cargo + [moved(held, step, owners) for step in steps]
     lanes_shape = sds((D_EDGE, lanes), BF16)
     wide, big_two = call(collect, [lanes_shape, lanes_shape], [me] + cargo, flops=10**7, smem=1)
     dst_row = (dst_owner[:, 0] * count + dst_local).reshape(1, edges)
@@ -825,7 +920,7 @@
         flops=8 * 10**9,
         kept=range(KEPT),
     )
-    near, far = sum_pair(table, owners)
+    near, far, _ = sum_pair(table, owners)
 
     def everywhere(piece):
         return [piece] + [moved(piece, k, groups, "group") for k in range(1, groups)]
@@ -860,7 +955,7 @@
         smem=1,
         scratch=[(atoms, D_ATOM)],
     )
-    near, far = sum_pair(table, owners)
+    near, far, _ = sum_pair(table, owners)
     first_two, second_two, big_two = call(
         prepare_two,
         [sds(s, BF16) for s in LARGE_SHAPES],
@@ -880,90 +975,85 @@
          atom_cotangent, state_one, free, kept_two[0]],
         flops=2 * 10**9,
         late=[10, 11, 12],
-        kept=[0, 1, 2, 3, 4, 5, 6, 7, 9, 10],
+        early=[10, 11],
+        kept=[4, 5, 7],
         smem=1,
         scratch=[(atoms, D_ATOM)],
     )
 
     def rows_first(value_t, dtype):
-        return call(turned, [sds((edges, D_EDGE), dtype)], [value_t], flops=10**8, late=[0])[0]
-
-    def large(update, pushed, atom_in, hidden, sent, grad_pre, small):
-        [pieces] = call(
+        return call(turned, [sds((edges, D_EDGE), dtype)], [value_t], flops=10**8)[0]
+
+    near, far, grads_two = sum_pair(
+        gain,
+        owners,
+        call(
             large_grads,
-            [sds((groups, D_EDGE, (PAD + BIG) // groups), BF16)],
-            [me, update, pushed, atom_in, hidden, sent, grad_pre, src_row, dst_row, small],
+            [sds((D_EDGE, BIG), BF16)],
+            [update, pushed, grad_pre, src_row, dst_row, atom_in_two, hidden_two, sent_two],
             flops=10**9,
-            late=[1, 2, 3, 4, 5, 6],
-            smem=1,
-            scratch=[(D_EDGE, PAD + BIG)],
-        )
-        return pieces
-
-    def traded(pieces):
-        return [pieces[0]] + [moved(pieces[k], k, groups, "group") for k in range(1, groups)]
-
-    near, far = sum_pair(gain, owners)
+        )[0],
+    )
+    arrived_two = exchange(grads_two.reshape(owners, cols, BIG))
     edge_out = rows_first(edge_out_t, BF16)
-    pieces_two = large(
-        update, pushed, atom_in_two, hidden_two, sent_two, grad_pre, jnp.zeros((D_EDGE, PAD), BF16)
-    )
-    near, pieces_two = lax.optimization_barrier((near, pieces_two))
-    pieces_two = traded(pieces_two)
-    half = owners // 2
-    half_shape = sds((half, count, D_ATOM), BF16)
-    grad_small_two, gain, update, pushed, grad_pre, grad_t, high, lower = call(
+    near, edge_out = lax.optimization_barrier((near, edge_out))
+    fetched = fetch([grad_t] + kept_two[1:] + [slope_edge_one, free, slope_one, grad_atoms])
+    half = owners // 4
+    grad_small_two, gain, update, pushed, grad_pre, grad_t, *parts = call(
         back_middle,
-        [sds((D_EDGE, PAD), BF16), gain_shape, atom_shape, atom_shape, edge_shape, edge_wide, half_shape,
-         half_shape],
-        [me, near, far, grad_t]
-        + kept_two[1:]
+        [sds((D_EDGE, PAD), BF16), gain_shape, atom_shape, atom_shape, edge_shape, edge_wide,
+         *[sds((half, count, D_ATOM), BF16)] * 4],
+        [me, near, far]
+        + fetched[:KEPT]
         + back_two
         + graph
-        + [dst_row, big_one, first_one, second_one, src_row, slope_edge_one, free, slope_one, grad_atoms],
+        + [dst_row, big_one, first_one, second_one, src_row]
+        + fetched[KEPT:],
         flops=10 * 10**9,
-        late=list(range(3, 3 + KEPT)) + list(range(BACK + 5, BACK + 9)),
-        kept=[0, 2, 3, 4, 5, 6, 7],
+        kept=[5],
         smem=1,
         scratch=[(atoms, D_ATOM)],
     )
-    near, far = sum_pair(gain, owners)
-    pieces_one = traded(
-        large(update, pushed, atom_in_one, hidden_one, sent_one, grad_pre, grad_small_two)
-    )
-    width = pieces_one[0].shape[1]
-    [spreads] = call(
-        sum_pieces, [sds((D_EDGE, 2 * width), BF16)], pieces_two + pieces_one, flops=10**7
-    )
-    arrived = exchange(spreads.reshape(owners, cols, 2 * width))
-    [owned] = call(sum_parts, [sds((cols, 2 * width), BF16)], [arrived], flops=10**7)
+    [grads_one] = call(
+        large_grads,
+        [sds((D_EDGE, 2 * PAD + BIG), BF16)],
+        [update, pushed, grad_pre, src_row, dst_row, atom_in_one, hidden_one, sent_one, grad_small_two],
+        flops=10**9,
+        late=[5, 6, 7],
+        kept=[0],
+    )
+    near, far, (grads_one, arrived_two) = sum_pair(gain, owners, (grads_one, arrived_two))
+    mine = parts[0].astype(F32)
+    for k in range(1, 4):
+        mine = mine + moved(parts[k], k, owners).astype(F32)
+    near, mine, grad_t = lax.optimization_barrier((near, mine.astype(BF16), grad_t))
+    step = 4
+    while half > 2:
+        high, mine = mine[half // 2 :], mine[: half // 2]
+        mine = (mine.astype(F32) + moved(high, step, owners).astype(F32)).astype(BF16)
+        half, step = half // 2, 2 * step
+    grad_atom = mine[0].astype(F32) + moved(mine[1], step, owners).astype(F32)
+    grad_edge_t, grads_one = call(
+        back_last,
+        [edge_wide, sds((D_EDGE, 2 * PAD + BIG), BF16)],
+        [near, far] + fetch([grad_t] + kept_one[1:]) + back_one + graph + [dst_row, grads_one],
+        flops=10 * 10**9,
+        kept=[1],
+        alias={BACK: 1},
+        scratch=[pltpu.VMEM((D_EDGE, PAD), BF16), pltpu.SemaphoreType.DMA],
+    )
+    grad_edge = rows_first(grad_edge_t, F32)
+    arrived_one = exchange(grads_one.reshape(owners, cols, 2 * PAD + BIG))
+    [owned] = call(
+        sum_parts, [sds((cols, 2 * (PAD + BIG)), BF16)], [arrived_one, arrived_two], flops=10**7
+    )
     owned = [owned] + [moved(owned, k, groups, "group") for k in range(1, groups)]
-    near, far, high = lax.optimization_barrier((near, far, high))
-    while half > 1:
-        lower = (lower.astype(F32) + moved(high, half, owners).astype(F32)).astype(BF16)
-        half = half // 2
-        high, lower = lower[half:], lower[:half]
-    grad_atom = lower[0].astype(F32) + moved(high[0], 1, owners).astype(F32)
-    grad_small_one, grad_edge_t = call(
-        back_last,
-        [sds((groups, D_EDGE, PAD), BF16), edge_wide],
-        [near, far, grad_t] + kept_one[1:] + back_one + graph + [dst_row],
-        flops=10 * 10**9,
-        late=range(2, 2 + KEPT),
-        kept=[0, 1],
-    )
-    grad_edge = rows_first(grad_edge_t, F32)
-    last = lax.all_to_all(
-        grad_small_one.reshape(groups * owners, cols, PAD), ("group", "shard"), split_axis=0, concat_axis=0
-    )
     rows = weights.shape[0]
     results = call(
         adam,
         [sds((cols, rows), F32)] * 4 + [sds((cols, rows), BF16)],
-        [me, last, weights_t, jnp.transpose(first_moment), jnp.transpose(second_moment)] + owned,
+        [weights_t, jnp.transpose(first_moment), jnp.transpose(second_moment)] + owned,
         flops=10**8,
-        smem=1,
-        scratch=[(groups, cols, 2 * width)],
     )
     return (edge_out, atom_out, grad_edge, grad_atom) + tuple(jnp.transpose(r) for r in results)
 

time: 163 us -> 150 us (0.920)
  waiting for transfers between devices: 50.5 us -> 35.2 us
  starting transfers between devices: 50.5 us -> 60.9 us
  Pallas kernels: 56.7 us -> 50.4 us
  local copies, waits for them, and re-layouts: 2.54 us -> 0.74 us
    ppermute x37 -> x33, waiting for transfers between devices: 45.4 us -> 24.9 us  [moved(): return lax.ppermute(table, axis, [(i, i ^ step) for i in range(owners)])]
    pallas_call x17 -> x16, Pallas kernels: 56.7 us -> 45.9 us  [call(): pl.pallas_call(kernel, out_shape=outs, in_specs=[pl.BlockSpec(memory_spac...]
    all_to_all x2 -> x3, starting transfers between devices: 7.44 us -> 15.8 us  [exchange(): return lax.all_to_all(pieces, 'shard', split_axis=0, concat_axis=0)]
    ppermute x37 -> x33, starting transfers between devices: 38.4 us -> 45.1 us  [moved(): return lax.ppermute(table, axis, [(i, i ^ step) for i in range(owners)])]
    all_to_all x2 -> x3, waiting for transfers between devices: 5.12 us -> 10.3 us  [exchange(): return lax.all_to_all(pieces, 'shard', split_axis=0, concat_axis=0)]
    all_to_all x1 -> x0, starting transfers between devices: 4.62 us -> none  [per_device(): lax.all_to_all(grad_small_one.reshape(groups * owners, cols, PAD), ('grou...]
    pallas_call x0 -> x2, Pallas kernels: none -> 4.54 us  [fetch(): pl.pallas_call(kernel, out_shape=[sds(x.shape, x.dtype) for x in arrays],...]
    unnamed x46 -> x36, local copies, waits for them, and re-layouts: 2.44 us -> 0.74 us
  transfers between devices with their start and end apart: 40 -> 36, of which waited for: 21 -> 16; matrix products, arithmetic and copies ran while one was open for 1% -> 1% of each run, Pallas kernels for 19% -> 20%
where the time goes in v3:
time: 150 us; the launch traced here: 149 us
  starting transfers between devices  60.9 us (41%)
  Pallas kernels  50.4 us (34%)
  waiting for transfers between devices  35.2 us (23%)
    pallas_call x16, Pallas kernels, call(): pl.pallas_call(kernel, out_shape=outs, in_specs=[pl.BlockSpec(memory_spac...  45.9 us
    ppermute x33, starting transfers between devices, moved(): return lax.ppermute(table, axis, [(i, i ^ step) for i in range(owners)])  45.1 us
    ppermute x33, waiting for transfers between devices, moved(): return lax.ppermute(table, axis, [(i, i ^ step) for i in range(owners)])  24.9 us
    all_to_all x3, starting transfers between devices, exchange(): return lax.all_to_all(pieces, 'shard', split_axis=0, concat_axis=0)  15.8 us
    all_to_all x3, waiting for transfers between devices, exchange(): return lax.all_to_all(pieces, 'shard', split_axis=0, concat_axis=0)  10.3 us
    pallas_call x2, Pallas kernels, fetch(): pl.pallas_call(kernel, out_shape=[sds(x.shape, x.dtype) for x in arrays],...  4.54 us
  transfers between devices with their start and end apart: 36, of which 16 were waited for; matrix products, arithmetic and copies ran while one was open for 1% of the time, Pallas kernels for 20%

profile of v3, /device:TPU:0, one launch (start us, length us, event | category | flops | bytes accessed | tf_op | source)
XLA Modules:
  0.0 149.3 jit_solution(14914241376063002953)
XLA Ops:
  0.6 1.6 %pack_first.1 = bf16[8,16,256]{2,1,0:T(8,128)(2,1)} custom-call(f32[16,3000]{1,0:T(8,128)} %bitcast.29), custom_call_target="tpu_custom_call" | custom-call | flops 10000000 | bytes 1048576 | tf_op jit(solution)/shard_map/pack_first/pallas_call | solution.py:128
  2.2 7.3 %all-to-all-start = ((bf16[8,16,256]{2,1,0:T(8,128)(2,1)}), bf16[8,16,256]{2,1,0:T(8,128)(2,1)S(1)}, u32[]{:S(2)}, u32[]{:S(2)}) async-start(bf16[8,16,256]{2,1,0:T(8,128)(2,1)} %pack_first.1), calls=%async_computation | async-start | bytes 131072 | tf_op jit(solution)/shard_map/all_to_all | solution.py:839
  10.2 1.6 %pack_cargo.1.refs_1_.refs_23_ = bf16[1,144,256]{2,1,0:T(8,128)(2,1)S(1)} custom-call(s32[2]{0:T(128)S(1)} %pad_add_fusion.refs_0_, f32[16,3000]{1,0:T(8,128)} %bitcast.30, bf16[64,256]{1,0:T(8,128)(2,1)} %refs_2_, s32[1,64]{1,0:T(1,128)S(1)} %bitcast.46), custom_call_target="tpu_custom_call" | custom-call | flops 10000000 | bytes 1048576 | tf_op jit(solution)/shard_map/pack_cargo/pallas_call | solution.py:128
  11.8 3.0 %collective-permute-start.4 = (bf16[1,144,256]{2,1,0:T(8,128)(2,1)S(1)}, bf16[1,144,256]{2,1,0:T(8,128)(2,1)S(1)}, u32[]{:S(2)}, u32[]{:S(2)}) collective-permute-start(bf16[1,144,256]{2,1,0:T(8,128)(2,1)S(1)} %pack_cargo.1.refs_1_.refs_23_), channel_id=1, source_target_pairs={{0,4},{1,5},{2,6},{3,7},{4,0},{5,1},{6,2},{7,3},{8,12},{9,13},{10,... | collective-permute-start | bytes 221192 | tf_op jit(solution)/shard_map/ppermute | solution.py:862
  14.9 2.8 %collective-permute-done.4.refs_2_.refs_24_ = bf16[1,144,256]{2,1,0:T(8,128)(2,1)S(1)} collective-permute-done((bf16[1,144,256]{2,1,0:T(8,128)(2,1)S(1)}, bf16[1,144,256]{2,1,0:T(8,128)(2,1)S(1)}, u32[]{:S(2)}, u32[]{:S(2)}) %collective-permute-start.4) | collective-permute-done | bytes 73760 | tf_op jit(solution)/shard_map/ppermute | solution.py:862
  17.7 2.5 %collective-permute-start.7 = (bf16[2,144,256]{2,1,0:T(8,128)(2,1)S(1)}, bf16[2,144,256]{2,1,0:T(8,128)(2,1)S(1)}, u32[]{:S(2)}, u32[]{:S(2)}) collective-permute-start(bf16[2,144,256]{2,1,0:T(8,128)(2,1)S(1)} %pad_maximum_fusion), channel_id=1, source_target_pairs={{0,3},{1,2},{2,1},{3,0},{4,7},{5,6},{6,5},{7,4},{8,11},{9,10},{10,... | collective-permute-start | bytes 442376 | tf_op jit(solution)/shard_map/ppermute | solution.py:862
  21.4 5.9 %first_half.1 = (f32[128,1024]{1,0:T(8,128)}, bf16[128,1024]{1,0:T(8,128)(2,1)}, bf16[128,1024]{1,0:T(8,128)(2,1)}, bf16[64,1024]{1,0:T(8,128)(2,1)}, bf16[64,40...) custom-call(bf16[1024,128]{1,0:T(8,128)(2,1)S(1)} %copy-done.4, ...), custom_call_target="tpu_custom_call" | custom-call | flops 8000000000 | bytes 1048576 | tf_op jit(solution)/shard_map/first_half/pallas_call | solution.py:128
  27.2 2.5 %collective-permute-start.2 = (bf16[512,128]{1,0:T(8,128)(2,1)S(1)}, bf16[512,128]{1,0:T(8,128)(2,1)S(1)}, u32[]{:S(2)}, u32[]{:S(2)}) collective-permute-start(bf16[512,128]{1,0:T(8,128)(2,1)S(1)} %get-tuple-element.139), channel_id=1, source_target_pairs={{0,3},{1,2},{2,1},{3,0},{4,7},{5,6},{6,5},{7,4},{8,11},{9,10},{10,... | collective-permute-start | bytes 393224 | tf_op jit(solution)/shard_map/ppermute | solution.py:862
  31.7 1.6 %collective-permute-start.9 = (bf16[128,384]{1,0:T(8,128)(2,1)S(1)}, bf16[128,384]{1,0:T(8,128)(2,1)S(1)}, u32[]{:S(2)}, u32[]{:S(2)}) collective-permute-start(bf16[128,384]{1,0:T(8,128)(2,1)S(1)} %get-tuple-element.141.refs_2_), channel_id=1, source_target_pairs={{0,16},{8,24},{16,0},{24,8},{1,17},{9,25},{17,1},{25,9},{2,18},{10... | collective-permute-start | bytes 294920 | tf_op jit(solution)/shard_map/ppermute | solution.py:862
  35.5 2.5 %collective-permute-start.3 = (bf16[512,128]{1,0:T(8,128)(2,1)S(1)}, bf16[512,128]{1,0:T(8,128)(2,1)S(1)}, u32[]{:S(2)}, u32[]{:S(2)}) collective-permute-start(bf16[512,128]{1,0:T(8,128)(2,1)S(1)} %add_convert_fusion.3.refs_1_), channel_id=1, source_target_pairs={{0,4},{1,5},{2,6},{3,7},{4,0},{5,1},{6,2},{7,3},{8,12},{9,13},{10,... | collective-permute-start | bytes 393224 | tf_op jit(solution)/shard_map/ppermute | solution.py:862
  40.3 2.9 %collective-permute-done.3.refs_2_ = bf16[512,128]{1,0:T(8,128)(2,1)S(1)} collective-permute-done((bf16[512,128]{1,0:T(8,128)(2,1)S(1)}, bf16[512,128]{1,0:T(8,128)(2,1)S(1)}, u32[]{:S(2)}, u32[]{:S(2)}) %collective-permute-start.3) | collective-permute-done | bytes 131104 | tf_op jit(solution)/shard_map/ppermute | solution.py:862
  43.1 8.0 %middle_half.1 = (bf16[512,128]{1,0:T(8,128)(2,1)}, bf16[512,256]{1,0:T(8,128)(2,1)}, bf16[512,256]{1,0:T(8,128)(2,1)}, f32[512,256]{1,0:T(8,128)}, bf16[512,256...) custom-call(s32[2]{0:T(128)S(1)} %pad_add_fusion.refs_0_, ...), custom_call_target="tpu_custom_call" | custom-call | flops 10000000000 | bytes 1048576 | tf_op jit(solution)/shard_map/middle_half/pallas_call | solution.py:128
  51.2 1.6 %collective-permute-start.13 = (bf16[512,128]{1,0:T(8,128)(2,1)S(1)}, bf16[512,128]{1,0:T(8,128)(2,1)S(1)}, u32[]{:S(2)}, u32[]{:S(2)}) collective-permute-start(bf16[512,128]{1,0:T(8,128)(2,1)S(1)} %get-tuple-element.153), channel_id=1, source_target_pairs={{0,3},{1,2},{2,1},{3,0},{4,7},{5,6},{6,5},{7,4},{8,11},{9,10},{10,... | collective-permute-start | bytes 393224 | tf_op jit(solution)/shard_map/ppermute | solution.py:862
  59.3 3.3 %collective-permute-start.14 = (bf16[512,128]{1,0:T(8,128)(2,1)S(1)}, bf16[512,128]{1,0:T(8,128)(2,1)S(1)}, u32[]{:S(2)}, u32[]{:S(2)}) collective-permute-start(bf16[512,128]{1,0:T(8,128)(2,1)S(1)} %add_convert_fusion.2.refs_1_), channel_id=1, source_target_pairs={{0,4},{1,5},{2,6},{3,7},{4,0},{5,1},{6,2},{7,3},{8,12},{9,13},{10,... | collective-permute-start | bytes 393224 | tf_op jit(solution)/shard_map/ppermute | solution.py:862
  63.6 5.1 %collective-permute-done.14.refs_2_ = bf16[512,128]{1,0:T(8,128)(2,1)S(1)} collective-permute-done((bf16[512,128]{1,0:T(8,128)(2,1)S(1)}, bf16[512,128]{1,0:T(8,128)(2,1)S(1)}, u32[]{:S(2)}, u32[]{:S(2)}) %collective-permute-start.14) | collective-permute-done | bytes 131104 | tf_op jit(solution)/shard_map/ppermute | solution.py:862
  68.7 4.9 %turn.1 = (bf16[512,128]{1,0:T(8,128)(2,1)S(1)}, bf16[512,256]{1,0:T(8,128)(2,1)S(1)}, bf16[512,256]{1,0:T(8,128)(2,1)S(1)}, f32[128,1024]{1,0:T(8,128)S(1)}, bf...) custom-call(s32[2]{0:T(128)S(1)} %pad_add_fusion.refs_0_, ...), custom_call_target="tpu_custom_call" | custom-call | flops 2000000000 | bytes 1048576 | tf_op jit(solution)/shard_map/turn/pallas_call | solution.py:128
  74.2 1.6 %collective-permute-start.19 = (bf16[128,512]{1,0:T(8,128)(2,1)S(1)}, bf16[128,512]{1,0:T(8,128)(2,1)S(1)}, u32[]{:S(2)}, u32[]{:S(2)}) collective-permute-start(bf16[128,512]{1,0:T(8,128)(2,1)S(1)} %get-tuple-element.168), channel_id=1, source_target_pairs={{0,2},{1,3},{2,0},{3,1},{4,6},{5,7},{6,4},{7,5},{8,10},{9,11},{10,... | collective-permute-start | bytes 393224 | tf_op jit(solution)/shard_map/ppermute | solution.py:862
  77.1 2.1 %large_grads.2 = bf16[128,1280]{1,0:T(8,128)(2,1)} custom-call(bf16[512,256]{1,0:T(8,128)(2,1)S(1)} %get-tuple-element.162.refs_0_, bf16[512,256]{1,0:T(8,128)(2,1)S(1)} %get-tuple-element.163.refs_1_, bf16[128,1024]{1,0:T(8,128)(2,1)S(1)} %get-tuple-element.164.refs_2_, s32[1,1024]{1,0:T(1,128)S(1)} %bitcast.43, s32[1,1024]{1,0:T(1,128)S(1)} %bitcast.37, ...), custom_call_target="tpu_custom_call" | custom-call | flops 1000000000 | bytes 1048576 | tf_op jit(solution)/shard_map/large_grads/pallas_call | solution.py:128
  82.1 2.0 %collective-permute-start.21 = (bf16[128,512]{1,0:T(8,128)(2,1)S(1)}, bf16[128,512]{1,0:T(8,128)(2,1)S(1)}, u32[]{:S(2)}, u32[]{:S(2)}) collective-permute-start(bf16[128,512]{1,0:T(8,128)(2,1)S(1)} %add_convert_fusion.1.refs_1_), channel_id=1, source_target_pairs={{0,4},{1,5},{2,6},{3,7},{4,0},{5,1},{6,2},{7,3},{8,12},{9,13},{10,... | collective-permute-start | bytes 393224 | tf_op jit(solution)/shard_map/ppermute | solution.py:862
  84.1 3.9 %all-to-all-start.1 = ((bf16[8,16,1280]{2,1,0:T(8,128)(2,1)}), bf16[8,16,1280]{2,1,0:T(8,128)(2,1)S(1)}, u32[]{:S(2)}, u32[]{:S(2)}) async-start(bf16[8,16,1280]{2,1,0:T(8,128)(2,1)} %bitcast.15), calls=%async_computation.1 | async-start | bytes 655360 | tf_op jit(solution)/shard_map/all_to_all | solution.py:839
  88.9 2.5 %fetch.2 = (f32[128,1024]{1,0:T(8,128)S(1)}, bf16[128,1024]{1,0:T(8,128)(2,1)S(1)}, bf16[128,1024]{1,0:T(8,128)(2,1)S(1)}, bf16[64,1024]{1,0:T(8,128)(2,1)S(1)},...) custom-call(f32[128,1024]{1,0:T(8,128)} %get-tuple-element.173.refs_, ...), custom_call_target="tpu_custom_call" | custom-call | flops 1000000000 | bytes 1048576 | tf_op jit(solution)/shard_map/fetch/pallas_call | solution.py:158
  91.4 7.2 %back_middle.1 = (bf16[128,256]{1,0:T(8,128)(2,1)S(1)}, bf16[128,512]{1,0:T(8,128)(2,1)S(1)}, bf16[512,256]{1,0:T(8,128)(2,1)S(1)}, bf16[512,256]{1,0:T(8,128)(2...) custom-call(s32[2]{0:T(128)S(1)} %pad_add_fusion.refs_0_, ...), custom_call_target="tpu_custom_call" | custom-call | flops 10000000000 | bytes 1048576 | tf_op jit(solution)/shard_map/back_middle/pallas_call | solution.py:128
  98.7 3.0 %collective-permute-start.24 = (bf16[128,512]{1,0:T(8,128)(2,1)S(1)}, bf16[128,512]{1,0:T(8,128)(2,1)S(1)}, u32[]{:S(2)}, u32[]{:S(2)}) collective-permute-start(bf16[128,512]{1,0:T(8,128)(2,1)S(1)} %get-tuple-element.219), channel_id=1, source_target_pairs={{0,3},{1,2},{2,1},{3,0},{4,7},{5,6},{6,5},{7,4},{8,11},{9,10},{10,... | collective-permute-start | bytes 393224 | tf_op jit(solution)/shard_map/ppermute | solution.py:862
  105.7 3.0 %large_grads.3.refs_28_ = bf16[128,1792]{1,0:T(8,128)(2,1)} custom-call(bf16[512,256]{1,0:T(8,128)(2,1)S(1)} %get-tuple-element.211.refs_0_, bf16[512,256]{1,0:T(8,128)(2,1)S(1)} %get-tuple-element.212.refs_1_, bf16[128,1024]{1,0:T(8,128)(2,1)S(1)} %get-tuple-element.213.refs_2_, s32[1,1024]{1,0:T(1,128)S(1)} %bitcast.45, s32[1,1024]{1,0:T(1,128)S(1)} %bitcast.39, ...), custom_call_target="tpu_custom_call" | custom-call | flops 1000000000 | bytes 1048576 | tf_op jit(solution)/shard_map/large_grads/pallas_call | solution.py:128
  110.2 3.5 %collective-permute-start.28 = (bf16[128,512]{1,0:T(8,128)(2,1)S(1)}, bf16[128,512]{1,0:T(8,128)(2,1)S(1)}, u32[]{:S(2)}, u32[]{:S(2)}) collective-permute-start(bf16[128,512]{1,0:T(8,128)(2,1)S(1)} %add_convert_fusion.refs_0_), channel_id=1, source_target_pairs={{0,4},{1,5},{2,6},{3,7},{4,0},{5,1},{6,2},{7,3},{8,12},{9,13},{10,... | collective-permute-start | bytes 393224 | tf_op jit(solution)/shard_map/ppermute | solution.py:862
  115.2 2.0 %fetch.3 = (f32[128,1024]{1,0:T(8,128)S(1)}, bf16[128,1024]{1,0:T(8,128)(2,1)S(1)}, bf16[128,1024]{1,0:T(8,128)(2,1)S(1)}, bf16[64,1024]{1,0:T(8,128)(2,1)S(1)},...) custom-call(f32[128,1024]{1,0:T(8,128)} %get-tuple-element.226.refs_, ...), custom_call_target="tpu_custom_call" | custom-call | flops 1000000000 | bytes 1048576 | tf_op jit(solution)/shard_map/fetch/pallas_call | solution.py:158
  117.2 1.7 %collective-permute-done.28.refs_1_ = bf16[128,512]{1,0:T(8,128)(2,1)S(1)} collective-permute-done((bf16[128,512]{1,0:T(8,128)(2,1)S(1)}, bf16[128,512]{1,0:T(8,128)(2,1)S(1)}, u32[]{:S(2)}, u32[]{:S(2)}) %collective-permute-start.28) | collective-permute-done | bytes 131104 | tf_op jit(solution)/shard_map/ppermute | solution.py:862
  119.0 5.4 %back_last.1 = (f32[128,1024]{1,0:T(8,128)S(1)}, bf16[128,1792]{1,0:T(8,128)(2,1)}) custom-call(bf16[128,512]{1,0:T(8,128)(2,1)S(1)} %add_convert_fusion.refs_0_, bf16[128,512]{1,0:T(8,128)(2,1)S(1)} %collective-permute-done.28.refs_1_, f32[128,1024]{1,0:T(8,128)S(1)} %get-tuple-element.239.refs_2_, ...), custom_call_target="tpu_custom_call", output_to_operand_aliasing={{1}: (28, {})} | custom-call | flops 10000000000 | bytes 1048576 | tf_op jit(solution)/shard_map/back_last/pallas_call | solution.py:128
  124.4 4.6 %all-to-all-start.2 = ((bf16[8,16,1792]{2,1,0:T(8,128)(2,1)}), bf16[8,16,1792]{2,1,0:T(8,128)(2,1)S(1)}, u32[]{:S(2)}, u32[]{:S(2)}) async-start(bf16[8,16,1792]{2,1,0:T(8,128)(2,1)} %bitcast.75), calls=%async_computation.2 | async-start | bytes 917504 | tf_op jit(solution)/shard_map/all_to_all | solution.py:839
  129.1 2.9 %collective-permute-start.29 = (bf16[64,256]{1,0:T(8,128)(2,1)S(1)}, bf16[64,256]{1,0:T(8,128)(2,1)S(1)}, u32[]{:S(2)}, u32[]{:S(2)}) collective-permute-start(bf16[64,256]{1,0:T(8,128)(2,1)S(1)} %slice_bitcast_fusion), channel_id=1, source_target_pairs={{0,4},{1,5},{2,6},{3,7},{4,0},{5,1},{6,2},{7,3},{8,12},{9,13},{10,... | collective-permute-start | bytes 98312 | tf_op jit(solution)/shard_map/ppermute | solution.py:862
  132.0 10.3 %all-to-all-done.2.refs_0_ = bf16[8,16,1792]{2,1,0:T(8,128)(2,1)S(1)} async-done(((bf16[8,16,1792]{2,1,0:T(8,128)(2,1)}), bf16[8,16,1792]{2,1,0:T(8,128)(2,1)S(1)}, u32[]{:S(2)}, u32[]{:S(2)}) %all-to-all-start.2) | async-done | bytes 458784 | tf_op jit(solution)/shard_map/all_to_all | solution.py:839
  142.6 1.8 %collective-permute-start.30 = (bf16[16,3072]{1,0:T(8,128)(2,1)S(1)}, bf16[16,3072]{1,0:T(8,128)(2,1)S(1)}, u32[]{:S(2)}, u32[]{:S(2)}) collective-permute-start(bf16[16,3072]{1,0:T(8,128)(2,1)S(1)} %sum_parts.1.refs_3_), channel_id=1, source_target_pairs={{0,8},{8,0},{16,24},{24,16},{1,9},{9,1},{17,25},{25,17},{2,10},{10... | collective-permute-start | bytes 294920 | tf_op jit(solution)/shard_map/ppermute | solution.py:862
  (107 shorter events, 33.7 us)
Async XLA Ops:
  2.2 19.1 %all-to-all-start = ((bf16[8,16,256]{2,1,0:T(8,128)(2,1)}), bf16[8,16,256]{2,1,0:T(8,128)(2,1)S(1)}, u32[]{:S(2)}, u32[]{:S(2)}) async-start(bf16[8,16,256]{2,1,0:T(8,128)(2,1)} %pack_first.1), calls=%async_computation | async-start | bytes 131072 | tf_op jit(solution)/shard_map/all_to_all | solution.py:839
  11.8 5.9 %collective-permute-start.4 = (bf16[1,144,256]{2,1,0:T(8,128)(2,1)S(1)}, bf16[1,144,256]{2,1,0:T(8,128)(2,1)S(1)}, u32[]{:S(2)}, u32[]{:S(2)}) collective-permute-start(bf16[1,144,256]{2,1,0:T(8,128)(2,1)S(1)} %pack_cargo.1.refs_1_.refs_23_), channel_id=1, source_target_pairs={{0,4},{1,5},{2,6},{3,7},{4,0},{5,1},{6,2},{7,3},{8,12},{9,13},{10,... | collective-permute-start | bytes 221192 | tf_op jit(solution)/shard_map/ppermute | solution.py:862
  17.7 12.7 %collective-permute-start.7 = (bf16[2,144,256]{2,1,0:T(8,128)(2,1)S(1)}, bf16[2,144,256]{2,1,0:T(8,128)(2,1)S(1)}, u32[]{:S(2)}, u32[]{:S(2)}) collective-permute-start(bf16[2,144,256]{2,1,0:T(8,128)(2,1)S(1)} %pad_maximum_fusion), channel_id=1, source_target_pairs={{0,3},{1,2},{2,1},{3,0},{4,7},{5,6},{6,5},{7,4},{8,11},{9,10},{10,... | collective-permute-start | bytes 442376 | tf_op jit(solution)/shard_map/ppermute | solution.py:862
  20.2 10.6 %collective-permute-start.6 = (bf16[2,144,256]{2,1,0:T(8,128)(2,1)S(1)}, bf16[2,144,256]{2,1,0:T(8,128)(2,1)S(1)}, u32[]{:S(2)}, u32[]{:S(2)}) collective-permute-start(bf16[2,144,256]{2,1,0:T(8,128)(2,1)S(1)} %pad_maximum_fusion), channel_id=1, source_target_pairs={{0,2},{1,3},{2,0},{3,1},{4,6},{5,7},{6,4},{7,5},{8,10},{9,11},{10,... | collective-permute-start | bytes 442376 | tf_op jit(solution)/shard_map/ppermute | solution.py:862
  20.9 9.9 %collective-permute-start.5 = (bf16[2,144,256]{2,1,0:T(8,128)(2,1)S(1)}, bf16[2,144,256]{2,1,0:T(8,128)(2,1)S(1)}, u32[]{:S(2)}, u32[]{:S(2)}) collective-permute-start(bf16[2,144,256]{2,1,0:T(8,128)(2,1)S(1)} %pad_maximum_fusion), channel_id=1, source_target_pairs={{0,1},{1,0},{2,3},{3,2},{4,5},{5,4},{6,7},{7,6},{8,9},{9,8},{10,11... | collective-permute-start | bytes 442376 | tf_op jit(solution)/shard_map/ppermute | solution.py:862
  27.2 6.1 %collective-permute-start.2 = (bf16[512,128]{1,0:T(8,128)(2,1)S(1)}, bf16[512,128]{1,0:T(8,128)(2,1)S(1)}, u32[]{:S(2)}, u32[]{:S(2)}) collective-permute-start(bf16[512,128]{1,0:T(8,128)(2,1)S(1)} %get-tuple-element.139), channel_id=1, source_target_pairs={{0,3},{1,2},{2,1},{3,0},{4,7},{5,6},{6,5},{7,4},{8,11},{9,10},{10,... | collective-permute-start | bytes 393224 | tf_op jit(solution)/shard_map/ppermute | solution.py:862
  29.7 5.0 %collective-permute-start.1 = (bf16[512,128]{1,0:T(8,128)(2,1)S(1)}, bf16[512,128]{1,0:T(8,128)(2,1)S(1)}, u32[]{:S(2)}, u32[]{:S(2)}) collective-permute-start(bf16[512,128]{1,0:T(8,128)(2,1)S(1)} %get-tuple-element.139), channel_id=1, source_target_pairs={{0,2},{1,3},{2,0},{3,1},{4,6},{5,7},{6,4},{7,5},{8,10},{9,11},{10,... | collective-permute-start | bytes 393224 | tf_op jit(solution)/shard_map/ppermute | solution.py:862
  31.7 6.3 %collective-permute-start.10 = (bf16[128,384]{1,0:T(8,128)(2,1)S(1)}, bf16[128,384]{1,0:T(8,128)(2,1)S(1)}, u32[]{:S(2)}, u32[]{:S(2)}) collective-permute-start(bf16[128,384]{1,0:T(8,128)(2,1)S(1)} %get-tuple-element.141.refs_2_), channel_id=1, source_target_pairs={{0,24},{8,16},{16,8},{24,0},{1,25},{9,17},{17,9},{25,1},{2,26},{10... | collective-permute-start | bytes 294920 | tf_op jit(solution)/shard_map/ppermute | solution.py:862
  31.7 7.2 %collective-permute-start.9 = (bf16[128,384]{1,0:T(8,128)(2,1)S(1)}, bf16[128,384]{1,0:T(8,128)(2,1)S(1)}, u32[]{:S(2)}, u32[]{:S(2)}) collective-permute-start(bf16[128,384]{1,0:T(8,128)(2,1)S(1)} %get-tuple-element.141.refs_2_), channel_id=1, source_target_pairs={{0,16},{8,24},{16,0},{24,8},{1,17},{9,25},{17,1},{25,9},{2,18},{10... | collective-permute-start | bytes 294920 | tf_op jit(solution)/shard_map/ppermute | solution.py:862
  33.3 5.6 %collective-permute-start.8 = (bf16[128,384]{1,0:T(8,128)(2,1)S(1)}, bf16[128,384]{1,0:T(8,128)(2,1)S(1)}, u32[]{:S(2)}, u32[]{:S(2)}) collective-permute-start(bf16[128,384]{1,0:T(8,128)(2,1)S(1)} %get-tuple-element.141.refs_2_), channel_id=1, source_target_pairs={{0,8},{8,0},{16,24},{24,16},{1,9},{9,1},{17,25},{25,17},{2,10},{10... | collective-permute-start | bytes 294920 | tf_op jit(solution)/shard_map/ppermute | solution.py:862
  35.5 7.7 %collective-permute-start.3 = (bf16[512,128]{1,0:T(8,128)(2,1)S(1)}, bf16[512,128]{1,0:T(8,128)(2,1)S(1)}, u32[]{:S(2)}, u32[]{:S(2)}) collective-permute-start(bf16[512,128]{1,0:T(8,128)(2,1)S(1)} %add_convert_fusion.3.refs_1_), channel_id=1, source_target_pairs={{0,4},{1,5},{2,6},{3,7},{4,0},{5,1},{6,2},{7,3},{8,12},{9,13},{10,... | collective-permute-start | bytes 393224 | tf_op jit(solution)/shard_map/ppermute | solution.py:862
  51.2 6.6 %collective-permute-start.13 = (bf16[512,128]{1,0:T(8,128)(2,1)S(1)}, bf16[512,128]{1,0:T(8,128)(2,1)S(1)}, u32[]{:S(2)}, u32[]{:S(2)}) collective-permute-start(bf16[512,128]{1,0:T(8,128)(2,1)S(1)} %get-tuple-element.153), channel_id=1, source_target_pairs={{0,3},{1,2},{2,1},{3,0},{4,7},{5,6},{6,5},{7,4},{8,11},{9,10},{10,... | collective-permute-start | bytes 393224 | tf_op jit(solution)/shard_map/ppermute | solution.py:862
  52.8 6.3 %collective-permute-start.12 = (bf16[512,128]{1,0:T(8,128)(2,1)S(1)}, bf16[512,128]{1,0:T(8,128)(2,1)S(1)}, u32[]{:S(2)}, u32[]{:S(2)}) collective-permute-start(bf16[512,128]{1,0:T(8,128)(2,1)S(1)} %get-tuple-element.153), channel_id=1, source_target_pairs={{0,2},{1,3},{2,0},{3,1},{4,6},{5,7},{6,4},{7,5},{8,10},{9,11},{10,... | collective-permute-start | bytes 393224 | tf_op jit(solution)/shard_map/ppermute | solution.py:862
  54.7 7.9 %collective-permute-start.17 = (bf16[128,384]{1,0:T(8,128)(2,1)S(1)}, bf16[128,384]{1,0:T(8,128)(2,1)S(1)}, u32[]{:S(2)}, u32[]{:S(2)}) collective-permute-start(bf16[128,384]{1,0:T(8,128)(2,1)S(1)} %get-tuple-element.154.refs_1_), channel_id=1, source_target_pairs={{0,24},{8,16},{16,8},{24,0},{1,25},{9,17},{17,9},{25,1},{2,26},{10... | collective-permute-start | bytes 294920 | tf_op jit(solution)/shard_map/ppermute | solution.py:862
  54.7 7.9 %collective-permute-start.16 = (bf16[128,384]{1,0:T(8,128)(2,1)S(1)}, bf16[128,384]{1,0:T(8,128)(2,1)S(1)}, u32[]{:S(2)}, u32[]{:S(2)}) collective-permute-start(bf16[128,384]{1,0:T(8,128)(2,1)S(1)} %get-tuple-element.154.refs_1_), channel_id=1, source_target_pairs={{0,16},{8,24},{16,0},{24,8},{1,17},{9,25},{17,1},{25,9},{2,18},{10... | collective-permute-start | bytes 294920 | tf_op jit(solution)/shard_map/ppermute | solution.py:862
  59.3 9.3 %collective-permute-start.14 = (bf16[512,128]{1,0:T(8,128)(2,1)S(1)}, bf16[512,128]{1,0:T(8,128)(2,1)S(1)}, u32[]{:S(2)}, u32[]{:S(2)}) collective-permute-start(bf16[512,128]{1,0:T(8,128)(2,1)S(1)} %add_convert_fusion.2.refs_1_), channel_id=1, source_target_pairs={{0,4},{1,5},{2,6},{3,7},{4,0},{5,1},{6,2},{7,3},{8,12},{9,13},{10,... | collective-permute-start | bytes 393224 | tf_op jit(solution)/shard_map/ppermute | solution.py:862
  73.6 7.1 %collective-permute-start.20 = (bf16[128,512]{1,0:T(8,128)(2,1)S(1)}, bf16[128,512]{1,0:T(8,128)(2,1)S(1)}, u32[]{:S(2)}, u32[]{:S(2)}) collective-permute-start(bf16[128,512]{1,0:T(8,128)(2,1)S(1)} %get-tuple-element.168), channel_id=1, source_target_pairs={{0,3},{1,2},{2,1},{3,0},{4,7},{5,6},{6,5},{7,4},{8,11},{9,10},{10,... | collective-permute-start | bytes 393224 | tf_op jit(solution)/shard_map/ppermute | solution.py:862
  74.2 6.5 %collective-permute-start.19 = (bf16[128,512]{1,0:T(8,128)(2,1)S(1)}, bf16[128,512]{1,0:T(8,128)(2,1)S(1)}, u32[]{:S(2)}, u32[]{:S(2)}) collective-permute-start(bf16[128,512]{1,0:T(8,128)(2,1)S(1)} %get-tuple-element.168), channel_id=1, source_target_pairs={{0,2},{1,3},{2,0},{3,1},{4,6},{5,7},{6,4},{7,5},{8,10},{9,11},{10,... | collective-permute-start | bytes 393224 | tf_op jit(solution)/shard_map/ppermute | solution.py:862
  75.9 6.2 %collective-permute-start.18 = (bf16[128,512]{1,0:T(8,128)(2,1)S(1)}, bf16[128,512]{1,0:T(8,128)(2,1)S(1)}, u32[]{:S(2)}, u32[]{:S(2)}) collective-permute-start(bf16[128,512]{1,0:T(8,128)(2,1)S(1)} %get-tuple-element.168), channel_id=1, source_target_pairs={{0,1},{1,0},{2,3},{3,2},{4,5},{5,4},{6,7},{7,6},{8,9},{9,8},{10,11... | collective-permute-start | bytes 393224 | tf_op jit(solution)/shard_map/ppermute | solution.py:862
  82.1 9.3 %collective-permute-start.21 = (bf16[128,512]{1,0:T(8,128)(2,1)S(1)}, bf16[128,512]{1,0:T(8,128)(2,1)S(1)}, u32[]{:S(2)}, u32[]{:S(2)}) collective-permute-start(bf16[128,512]{1,0:T(8,128)(2,1)S(1)} %add_convert_fusion.1.refs_1_), channel_id=1, source_target_pairs={{0,4},{1,5},{2,6},{3,7},{4,0},{5,1},{6,2},{7,3},{8,12},{9,13},{10,... | collective-permute-start | bytes 393224 | tf_op jit(solution)/shard_map/ppermute | solution.py:862
  84.1 24.6 %all-to-all-start.1 = ((bf16[8,16,1280]{2,1,0:T(8,128)(2,1)}), bf16[8,16,1280]{2,1,0:T(8,128)(2,1)S(1)}, u32[]{:S(2)}, u32[]{:S(2)}) async-start(bf16[8,16,1280]{2,1,0:T(8,128)(2,1)} %bitcast.15), calls=%async_computation.1 | async-start | bytes 655360 | tf_op jit(solution)/shard_map/all_to_all | solution.py:839
  98.7 10.1 %collective-permute-start.24 = (bf16[128,512]{1,0:T(8,128)(2,1)S(1)}, bf16[128,512]{1,0:T(8,128)(2,1)S(1)}, u32[]{:S(2)}, u32[]{:S(2)}) collective-permute-start(bf16[128,512]{1,0:T(8,128)(2,1)S(1)} %get-tuple-element.219), channel_id=1, source_target_pairs={{0,3},{1,2},{2,1},{3,0},{4,7},{5,6},{6,5},{7,4},{8,11},{9,10},{10,... | collective-permute-start | bytes 393224 | tf_op jit(solution)/shard_map/ppermute | solution.py:862
  101.6 8.4 %collective-permute-start.23 = (bf16[128,512]{1,0:T(8,128)(2,1)S(1)}, bf16[128,512]{1,0:T(8,128)(2,1)S(1)}, u32[]{:S(2)}, u32[]{:S(2)}) collective-permute-start(bf16[128,512]{1,0:T(8,128)(2,1)S(1)} %get-tuple-element.219), channel_id=1, source_target_pairs={{0,2},{1,3},{2,0},{3,1},{4,6},{5,7},{6,4},{7,5},{8,10},{9,11},{10,... | collective-permute-start | bytes 393224 | tf_op jit(solution)/shard_map/ppermute | solution.py:862
  102.2 7.9 %collective-permute-start.22 = (bf16[128,512]{1,0:T(8,128)(2,1)S(1)}, bf16[128,512]{1,0:T(8,128)(2,1)S(1)}, u32[]{:S(2)}, u32[]{:S(2)}) collective-permute-start(bf16[128,512]{1,0:T(8,128)(2,1)S(1)} %get-tuple-element.219), channel_id=1, source_target_pairs={{0,1},{1,0},{2,3},{3,2},{4,5},{5,4},{6,7},{7,6},{8,9},{9,8},{10,11... | collective-permute-start | bytes 393224 | tf_op jit(solution)/shard_map/ppermute | solution.py:862
  103.5 10.2 %collective-permute-start.25 = (bf16[2,64,256]{2,1,0:T(8,128)(2,1)S(1)}, bf16[2,64,256]{2,1,0:T(8,128)(2,1)S(1)}, u32[]{:S(2)}, u32[]{:S(2)}) collective-permute-start(bf16[2,64,256]{2,1,0:T(8,128)(2,1)S(1)} %get-tuple-element.221), channel_id=1, source_target_pairs={{0,1},{1,0},{2,3},{3,2},{4,5},{5,4},{6,7},{7,6},{8,9},{9,8},{10,11... | collective-permute-start | bytes 196616 | tf_op jit(solution)/shard_map/ppermute | solution.py:862
  104.2 9.4 %collective-permute-start.26 = (bf16[2,64,256]{2,1,0:T(8,128)(2,1)S(1)}, bf16[2,64,256]{2,1,0:T(8,128)(2,1)S(1)}, u32[]{:S(2)}, u32[]{:S(2)}) collective-permute-start(bf16[2,64,256]{2,1,0:T(8,128)(2,1)S(1)} %get-tuple-element.222), channel_id=1, source_target_pairs={{0,2},{1,3},{2,0},{3,1},{4,6},{5,7},{6,4},{7,5},{8,10},{9,11},{10,... | collective-permute-start | bytes 196616 | tf_op jit(solution)/shard_map/ppermute | solution.py:862
  108.8 6.4 %collective-permute-start.27 = (bf16[2,64,256]{2,1,0:T(8,128)(2,1)S(1)}, bf16[2,64,256]{2,1,0:T(8,128)(2,1)S(1)}, u32[]{:S(2)}, u32[]{:S(2)}) collective-permute-start(bf16[2,64,256]{2,1,0:T(8,128)(2,1)S(1)} %get-tuple-element.223), channel_id=1, source_target_pairs={{0,3},{1,2},{2,1},{3,0},{4,7},{5,6},{6,5},{7,4},{8,11},{9,10},{10,... | collective-permute-start | bytes 196616 | tf_op jit(solution)/shard_map/ppermute | solution.py:862
  110.2 8.8 %collective-permute-start.28 = (bf16[128,512]{1,0:T(8,128)(2,1)S(1)}, bf16[128,512]{1,0:T(8,128)(2,1)S(1)}, u32[]{:S(2)}, u32[]{:S(2)}) collective-permute-start(bf16[128,512]{1,0:T(8,128)(2,1)S(1)} %add_convert_fusion.refs_0_), channel_id=1, source_target_pairs={{0,4},{1,5},{2,6},{3,7},{4,0},{5,1},{6,2},{7,3},{8,12},{9,13},{10,... | collective-permute-start | bytes 393224 | tf_op jit(solution)/shard_map/ppermute | solution.py:862
  124.4 17.9 %all-to-all-start.2 = ((bf16[8,16,1792]{2,1,0:T(8,128)(2,1)}), bf16[8,16,1792]{2,1,0:T(8,128)(2,1)S(1)}, u32[]{:S(2)}, u32[]{:S(2)}) async-start(bf16[8,16,1792]{2,1,0:T(8,128)(2,1)} %bitcast.75), calls=%async_computation.2 | async-start | bytes 917504 | tf_op jit(solution)/shard_map/all_to_all | solution.py:839
  129.1 15.3 %collective-permute-start.29 = (bf16[64,256]{1,0:T(8,128)(2,1)S(1)}, bf16[64,256]{1,0:T(8,128)(2,1)S(1)}, u32[]{:S(2)}, u32[]{:S(2)}) collective-permute-start(bf16[64,256]{1,0:T(8,128)(2,1)S(1)} %slice_bitcast_fusion), channel_id=1, source_target_pairs={{0,4},{1,5},{2,6},{3,7},{4,0},{5,1},{6,2},{7,3},{8,12},{9,13},{10,... | collective-permute-start | bytes 98312 | tf_op jit(solution)/shard_map/ppermute | solution.py:862
  142.5 5.7 %collective-permute-start.31 = (bf16[16,3072]{1,0:T(8,128)(2,1)S(1)}, bf16[16,3072]{1,0:T(8,128)(2,1)S(1)}, u32[]{:S(2)}, u32[]{:S(2)}) collective-permute-start(bf16[16,3072]{1,0:T(8,128)(2,1)S(1)} %sum_parts.1.refs_3_), channel_id=1, source_target_pairs={{0,16},{8,24},{16,0},{24,8},{1,17},{9,25},{17,1},{25,9},{2,18},{10... | collective-permute-start | bytes 294920 | tf_op jit(solution)/shard_map/ppermute | solution.py:862
  142.6 5.6 %collective-permute-start.30 = (bf16[16,3072]{1,0:T(8,128)(2,1)S(1)}, bf16[16,3072]{1,0:T(8,128)(2,1)S(1)}, u32[]{:S(2)}, u32[]{:S(2)}) collective-permute-start(bf16[16,3072]{1,0:T(8,128)(2,1)S(1)} %sum_parts.1.refs_3_), channel_id=1, source_target_pairs={{0,8},{8,0},{16,24},{24,16},{1,9},{9,1},{17,25},{25,17},{2,10},{10... | collective-permute-start | bytes 294920 | tf_op jit(solution)/shard_map/ppermute | solution.py:862
  (22 other events, 138.0 us)

commit v4 on v3

--- a/solution.py
+++ b/solution.py
@@ -96,7 +96,7 @@
             ref.send()
 
 
-def call(body, outs, args, flops=10**9, late=(), kept=(), smem=0, scratch=(), early=None, alias=None):
+def call(body, outs, args, flops=10**9, late=(), kept=(), smem=0, scratch=(), early=None, alias=None, raw=()):
     alias = alias or {}
     held = [i for i in kept if i not in alias.values()]
     moved = [args[i] for i in late] + [outs[i] for i in held]
@@ -120,10 +120,10 @@
         for i in held:
             results[i].copy.wait()
 
-    args = [pltpu.with_memory_space_constraint(x, pltpu.HBM) if i in late or i in alias else x for i, x in enumerate(args)]
+    args = [pltpu.with_memory_space_constraint(x, pltpu.HBM) if i in late or i in alias or i in raw else x for i, x in enumerate(args)]
     outs = [pltpu.HBM(x.shape, x.dtype) if i in kept else x for i, x in enumerate(outs)]
     space = [pltpu.SMEM] * smem + [pltpu.VMEM] * (len(args) - smem)
-    for i in [*late, *alias]:
+    for i in [*late, *alias, *raw]:
         space[i] = pltpu.HBM
     return pl.pallas_call(
         kernel,
@@ -199,7 +199,7 @@
 
 
 def sigmoid(v):
-    return 1.0 / (1.0 + jnp.exp(-v))
+    return 0.5 + 0.5 * jnp.tanh(0.5 * v)
 
 
 def silu_pair(v):
@@ -234,7 +234,7 @@
 
 
 def high_low(index, length):
-    return index // length, index % length
+    return index >> (length.bit_length() - 1), index & (length - 1)
 
 
 def small_t(raw, offset, width, columns):
@@ -242,7 +242,8 @@
     total = None
     for p in range(count):
         lane, d = iota((PAD, columns), 0), iota((PAD, columns), 1)
-        sel = ones_where((d % count == p) & (lane == offset + d // count))
+        high, rest = high_low(d, count)
+        sel = ones_where((rest == p) & (lane == offset + high))
         part = dot(raw[p * width : (p + 1) * width], sel)
         total = part if total is None else total + part
     return low(total)
@@ -253,7 +254,8 @@
     total = None
     for p in range(count):
         d, lane = iota((rows, PAD), 0), iota((rows, PAD), 1)
-        sel = ones_where((d % count == p) & (lane == offset + d // count))
+        high, rest = high_low(d, count)
+        sel = ones_where((rest == p) & (lane == offset + high))
         part = dot_nt(sel, raw[p * width : (p + 1) * width])
         total = part if total is None else total + part
     return low(total)
@@ -283,7 +285,8 @@
     parts = []
     for p in range(count):
         d, lane = iota((columns, PAD), 0), iota((columns, PAD), 1)
-        sel = ones_where((d % count == p) & (lane == offset + d // count))
+        high, rest = high_low(d, count)
+        sel = ones_where((rest == p) & (lane == offset + high))
         parts.append(dot(value, sel))
     return jnp.concatenate(parts, axis=0)
 
@@ -338,8 +341,11 @@
     return value
 
 
-def pack_first(weights, out_ref):
-    head = low(padded(weights[:, :SMALL], ROWS, PAD))
+def pack_first(weights, out_ref, hold, sem):
+    copy = pltpu.make_async_copy(weights.at[:, :PAD], hold, sem)
+    copy.start()
+    copy.wait()
+    head = low(padded(hold[...], ROWS, PAD))
     for s in range(out_ref.shape[0]):
         out_ref[s] = head
 
@@ -687,14 +693,20 @@
     )
 
 
-def large_grads(update, pushed, grad_pre, src_row, dst_row, atom_in, hidden, sent, *refs):
-    *small, out_ref = refs
-    base = 2 * PAD * len(small)
-    for ref in small:
-        out_ref[:, PAD : 2 * PAD] = ref[...]
+def large_grads(update, pushed, grad_pre, src_row, dst_row, atom_in, hidden, sent, out_ref):
     for lanes, value in large_values(update, pushed, grad_pre, src_row, dst_row, atom_in, hidden, sent):
-        out_ref[:, base + lanes.start : base + lanes.stop] = value
-    send(out_ref)
+        out_ref[:, lanes] = value
+
+
+def large_pieces(
+    me, update, pushed, grad_pre, src_row, dst_row, atom_in, hidden, sent, small, out_ref, hold
+):
+    hold[:, :PAD] = small[...].astype(F32)
+    for lanes, value in large_values(update, pushed, grad_pre, src_row, dst_row, atom_in, hidden, sent):
+        hold[:, PAD + lanes.start : PAD + lanes.stop] = value.astype(F32)
+    groups, _, width = out_ref.shape
+    for g in range(groups):
+        out_ref[g ^ me[1]] = low(hold[:, g * width : (g + 1) * width])
 
 
 def large_values(update, pushed, grad_pre, src_row, dst_row, atom_in, hidden, sent):
@@ -804,23 +816,28 @@
     return total
 
 
+def sum_pieces(*refs):
+    *pieces, out_ref = refs
+    out_ref[:, :PAD] = jnp.zeros((out_ref.shape[0], PAD), BF16)
+    out_ref[:, PAD:] = low(sum_list(pieces))
+    send(out_ref)
+
+
 def sum_parts(one, two, out_ref):
     width = one.shape[2]
     out_ref[:, :width] = low(total_of(one))
     out_ref[:, width:] = low(total_of(two))
 
 
-def adam(weights, first, second, *refs):
-    *pieces, grad_ref, weights_ref, first_ref, second_ref, low_ref = refs
+def adam(me, weights, first, second, *refs):
+    *pieces, grad_ref, weights_ref, first_ref, second_ref, low_ref, hold = refs
+    groups, _, lanes = hold.shape
     total = sum_list(pieces)
+    for k, piece in enumerate(pieces):
+        hold[me[1] ^ k] = piece[:, PAD : PAD + lanes].astype(F32)
+    joint = jnp.concatenate([hold[g] for g in range(groups)], axis=1)
     grad = jnp.concatenate(
-        [
-            total[:, :SMALL],
-            total[:, 2 * PAD : 2 * PAD + BIG],
-            total[:, PAD : PAD + SMALL],
-            total[:, 2 * PAD + BIG :],
-        ],
-        axis=1,
+        [total[:, :SMALL], joint[:, PAD:], joint[:, :SMALL], total[:, PAD + lanes :]], axis=1
     )
     grad_ref[...] = grad
     old = weights[...]
@@ -877,7 +894,14 @@
     weights_t = jnp.transpose(weights)
     cols = weights_t.shape[0]
     lanes = (BIG + PAD) // groups
-    [pack] = call(pack_first, [sds((owners, ROWS, PAD), BF16)], [weights_t], flops=10**7, late=[0])
+    [pack] = call(
+        pack_first,
+        [sds((owners, ROWS, PAD), BF16)],
+        [weights_t],
+        flops=10**7,
+        raw=[0],
+        scratch=[pltpu.VMEM((cols, PAD), F32), pltpu.SemaphoreType.DMA],
+    )
     pack, state = lax.optimization_barrier((pack, atom_state))
     pack = exchange(pack)
     [cargo] = call(
@@ -885,7 +909,7 @@
         [sds((1, count + ROWS * (1 + 2 * slots(lanes)), D_ATOM), BF16)],
         [me, weights_t, state, fixed_atoms.reshape(1, count)],
         flops=10**7,
-        late=[1, 2],
+        late=[1, 2, 3],
         smem=1,
         scratch=[(groups, cols, lanes)],
     )
@@ -956,6 +980,7 @@
         scratch=[(atoms, D_ATOM)],
     )
     near, far, _ = sum_pair(table, owners)
+    near, state_one, kept_two[0] = lax.optimization_barrier((near, state_one, kept_two[0]))
     first_two, second_two, big_two = call(
         prepare_two,
         [sds(s, BF16) for s in LARGE_SHAPES],
@@ -972,10 +997,8 @@
         [table_shape, atom_shape, atom_shape, edge_wide, sds((count, D_ATOM), BF16), edge_wide, edge_shape,
          atom_wide, gain_shape, atom_shape, atom_shape],
         [me, near, far, big_two, first_two, second_two, src_row, dst_row, edge_cotangent,
-         atom_cotangent, state_one, free, kept_two[0]],
+         atom_cotangent] + fetch([state_one, free, kept_two[0]]),
         flops=2 * 10**9,
-        late=[10, 11, 12],
-        early=[10, 11],
         kept=[4, 5, 7],
         smem=1,
         scratch=[(atoms, D_ATOM)],
@@ -984,19 +1007,18 @@
     def rows_first(value_t, dtype):
         return call(turned, [sds((edges, D_EDGE), dtype)], [value_t], flops=10**8)[0]
 
-    near, far, grads_two = sum_pair(
+    edge_out = rows_first(edge_out_t, BF16)
+    near, far, (grads_two, edge_out) = sum_pair(
         gain,
         owners,
-        call(
+        (call(
             large_grads,
             [sds((D_EDGE, BIG), BF16)],
             [update, pushed, grad_pre, src_row, dst_row, atom_in_two, hidden_two, sent_two],
             flops=10**9,
-        )[0],
+        )[0], edge_out),
     )
     arrived_two = exchange(grads_two.reshape(owners, cols, BIG))
-    edge_out = rows_first(edge_out_t, BF16)
-    near, edge_out = lax.optimization_barrier((near, edge_out))
     fetched = fetch([grad_t] + kept_two[1:] + [slope_edge_one, free, slope_one, grad_atoms])
     half = owners // 4
     grad_small_two, gain, update, pushed, grad_pre, grad_t, *parts = call(
@@ -1014,19 +1036,23 @@
         smem=1,
         scratch=[(atoms, D_ATOM)],
     )
-    [grads_one] = call(
-        large_grads,
-        [sds((D_EDGE, 2 * PAD + BIG), BF16)],
-        [update, pushed, grad_pre, src_row, dst_row, atom_in_one, hidden_one, sent_one, grad_small_two],
+    [pieces] = call(
+        large_pieces,
+        [sds((groups, D_EDGE, lanes), BF16)],
+        [me, update, pushed, grad_pre, src_row, dst_row, atom_in_one, hidden_one, sent_one, grad_small_two],
         flops=10**9,
-        late=[5, 6, 7],
-        kept=[0],
-    )
-    near, far, (grads_one, arrived_two) = sum_pair(gain, owners, (grads_one, arrived_two))
+        late=[6, 7, 8],
+        smem=1,
+        scratch=[(D_EDGE, PAD + BIG)],
+    )
+    near, far, (pieces, arrived_two) = sum_pair(gain, owners, (pieces, arrived_two))
+    pieces = [pieces[0]] + [moved(pieces[k], k, groups, "group") for k in range(1, groups)]
+    [grads_one] = call(sum_pieces, [sds((D_EDGE, PAD + lanes), BF16)], pieces, flops=10**7, kept=[0])
+    grads_one, grad_t = lax.optimization_barrier((grads_one, grad_t))
     mine = parts[0].astype(F32)
     for k in range(1, 4):
         mine = mine + moved(parts[k], k, owners).astype(F32)
-    near, mine, grad_t = lax.optimization_barrier((near, mine.astype(BF16), grad_t))
+    mine = mine.astype(BF16)
     step = 4
     while half > 2:
         high, mine = mine[half // 2 :], mine[: half // 2]
@@ -1035,7 +1061,7 @@
     grad_atom = mine[0].astype(F32) + moved(mine[1], step, owners).astype(F32)
     grad_edge_t, grads_one = call(
         back_last,
-        [edge_wide, sds((D_EDGE, 2 * PAD + BIG), BF16)],
+        [edge_wide, sds((D_EDGE, PAD + lanes), BF16)],
         [near, far] + fetch([grad_t] + kept_one[1:]) + back_one + graph + [dst_row, grads_one],
         flops=10 * 10**9,
         kept=[1],
@@ -1043,17 +1069,19 @@
         scratch=[pltpu.VMEM((D_EDGE, PAD), BF16), pltpu.SemaphoreType.DMA],
     )
     grad_edge = rows_first(grad_edge_t, F32)
-    arrived_one = exchange(grads_one.reshape(owners, cols, 2 * PAD + BIG))
+    arrived_one = exchange(grads_one.reshape(owners, cols, PAD + lanes))
     [owned] = call(
-        sum_parts, [sds((cols, 2 * (PAD + BIG)), BF16)], [arrived_one, arrived_two], flops=10**7
+        sum_parts, [sds((cols, PAD + lanes + BIG), BF16)], [arrived_one, arrived_two], flops=10**7
     )
     owned = [owned] + [moved(owned, k, groups, "group") for k in range(1, groups)]
     rows = weights.shape[0]
     results = call(
         adam,
         [sds((cols, rows), F32)] * 4 + [sds((cols, rows), BF16)],
-        [weights_t, jnp.transpose(first_moment), jnp.transpose(second_moment)] + owned,
+        [me, weights_t, jnp.transpose(first_moment), jnp.transpose(second_moment)] + owned,
         flops=10**8,
+        smem=1,
+        scratch=[(groups, cols, lanes)],
     )
     return (edge_out, atom_out, grad_edge, grad_atom) + tuple(jnp.transpose(r) for r in results)
 

time: 150 us -> 141 us (0.940)
  waiting for transfers between devices: 35.2 us -> 28.7 us
  starting transfers between devices: 60.9 us -> 58.6 us
    all_to_all x3, waiting for transfers between devices: 10.3 us -> 4.97 us  [exchange(): return lax.all_to_all(pieces, 'shard', split_axis=0, concat_axis=0)]
    ppermute x33 -> x36, starting transfers between devices: 45.1 us -> 41.7 us  [moved(): return lax.ppermute(table, axis, [(i, i ^ step) for i in range(owners)])]
    pallas_call x2 -> x3, Pallas kernels: 4.54 us -> 5.89 us  [fetch(): pl.pallas_call(kernel, out_shape=[sds(x.shape, x.dtype) for x in arrays],...]
    ppermute x33 -> x36, waiting for transfers between devices: 24.9 us -> 23.7 us  [moved(): return lax.ppermute(table, axis, [(i, i ^ step) for i in range(owners)])]
    pallas_call x16 -> x17, Pallas kernels: 45.9 us -> 45 us  [call(): pl.pallas_call(kernel, out_shape=outs, in_specs=[pl.BlockSpec(memory_spac...]
  transfers between devices with their start and end apart: 36 -> 39, of which waited for: 16 -> 16; matrix products, arithmetic and copies ran while one was open for 1% -> 1% of each run, Pallas kernels for 20% -> 26%
where the time goes in v4:
time: 141 us
  starting transfers between devices  58.6 us (42%)
  Pallas kernels  50.9 us (36%)
  waiting for transfers between devices  28.7 us (20%)
    pallas_call x17, Pallas kernels, call(): pl.pallas_call(kernel, out_shape=outs, in_specs=[pl.BlockSpec(memory_spac...  45 us
    ppermute x36, starting transfers between devices, moved(): return lax.ppermute(table, axis, [(i, i ^ step) for i in range(owners)])  41.7 us
    ppermute x36, waiting for transfers between devices, moved(): return lax.ppermute(table, axis, [(i, i ^ step) for i in range(owners)])  23.7 us
    all_to_all x3, starting transfers between devices, exchange(): return lax.all_to_all(pieces, 'shard', split_axis=0, concat_axis=0)  17 us
    pallas_call x3, Pallas kernels, fetch(): pl.pallas_call(kernel, out_shape=[sds(x.shape, x.dtype) for x in arrays],...  5.89 us
    all_to_all x3, waiting for transfers between devices, exchange(): return lax.all_to_all(pieces, 'shard', split_axis=0, concat_axis=0)  4.97 us
  transfers between devices with their start and end apart: 39, of which 16 were waited for; matrix products, arithmetic and copies ran while one was open for 1% of the time, Pallas kernels for 26%

profile of v4, /device:TPU:0, one launch (start us, length us, event | category | flops | bytes accessed | tf_op | source)
XLA Modules:
  0.0 140.7 jit_solution(5629407040476879980)
XLA Ops:
  2.0 7.3 %all-to-all-start = ((bf16[8,16,256]{2,1,0:T(8,128)(2,1)}), bf16[8,16,256]{2,1,0:T(8,128)(2,1)S(1)}, u32[]{:S(2)}, u32[]{:S(2)}) async-start(bf16[8,16,256]{2,1,0:T(8,128)(2,1)} %pack_first.1), calls=%async_computation | async-start | bytes 131072 | tf_op jit(solution)/shard_map/all_to_all | solution.py:856
  9.4 1.6 %pack_cargo.1.refs_1_.refs_23_ = bf16[1,144,256]{2,1,0:T(8,128)(2,1)S(1)} custom-call(s32[2]{0:T(128)S(1)} %pad_add_fusion.refs_0_, f32[16,3000]{1,0:T(8,128)} %bitcast.40, bf16[64,256]{1,0:T(8,128)(2,1)} %refs_2_, s32[1,64]{1,0:T(1,128)} %bitcast.87), custom_call_target="tpu_custom_call" | custom-call | flops 10000000 | bytes 1048576 | tf_op jit(solution)/shard_map/pack_cargo/pallas_call | solution.py:128
  11.0 3.0 %collective-permute-start.4 = (bf16[1,144,256]{2,1,0:T(8,128)(2,1)S(1)}, bf16[1,144,256]{2,1,0:T(8,128)(2,1)S(1)}, u32[]{:S(2)}, u32[]{:S(2)}) collective-permute-start(bf16[1,144,256]{2,1,0:T(8,128)(2,1)S(1)} %pack_cargo.1.refs_1_.refs_23_), channel_id=1, source_target_pairs={{0,4},{1,5},{2,6},{3,7},{4,0},{5,1},{6,2},{7,3},{8,12},{9,13},{10,... | collective-permute-start | bytes 221192 | tf_op jit(solution)/shard_map/ppermute | solution.py:879
  14.1 3.0 %collective-permute-done.4.refs_2_.refs_24_ = bf16[1,144,256]{2,1,0:T(8,128)(2,1)S(1)} collective-permute-done((bf16[1,144,256]{2,1,0:T(8,128)(2,1)S(1)}, bf16[1,144,256]{2,1,0:T(8,128)(2,1)S(1)}, u32[]{:S(2)}, u32[]{:S(2)}) %collective-permute-start.4) | collective-permute-done | bytes 73760 | tf_op jit(solution)/shard_map/ppermute | solution.py:879
  17.1 2.4 %collective-permute-start.7 = (bf16[2,144,256]{2,1,0:T(8,128)(2,1)S(1)}, bf16[2,144,256]{2,1,0:T(8,128)(2,1)S(1)}, u32[]{:S(2)}, u32[]{:S(2)}) collective-permute-start(bf16[2,144,256]{2,1,0:T(8,128)(2,1)S(1)} %pad_maximum_fusion), channel_id=1, source_target_pairs={{0,3},{1,2},{2,1},{3,0},{4,7},{5,6},{6,5},{7,4},{8,11},{9,10},{10,... | collective-permute-start | bytes 442376 | tf_op jit(solution)/shard_map/ppermute | solution.py:879
  21.0 5.8 %first_half.1 = (f32[128,1024]{1,0:T(8,128)}, bf16[128,1024]{1,0:T(8,128)(2,1)}, bf16[128,1024]{1,0:T(8,128)(2,1)}, bf16[64,1024]{1,0:T(8,128)(2,1)}, bf16[64,40...) custom-call(bf16[1024,128]{1,0:T(8,128)(2,1)S(1)} %copy-done.3, ...), custom_call_target="tpu_custom_call" | custom-call | flops 8000000000 | bytes 1048576 | tf_op jit(solution)/shard_map/first_half/pallas_call | solution.py:128
  26.8 2.1 %collective-permute-start.2 = (bf16[512,128]{1,0:T(8,128)(2,1)S(1)}, bf16[512,128]{1,0:T(8,128)(2,1)S(1)}, u32[]{:S(2)}, u32[]{:S(2)}) collective-permute-start(bf16[512,128]{1,0:T(8,128)(2,1)S(1)} %get-tuple-element.143), channel_id=1, source_target_pairs={{0,3},{1,2},{2,1},{3,0},{4,7},{5,6},{6,5},{7,4},{8,11},{9,10},{10,... | collective-permute-start | bytes 393224 | tf_op jit(solution)/shard_map/ppermute | solution.py:879
  31.3 1.6 %collective-permute-start.9 = (bf16[128,384]{1,0:T(8,128)(2,1)S(1)}, bf16[128,384]{1,0:T(8,128)(2,1)S(1)}, u32[]{:S(2)}, u32[]{:S(2)}) collective-permute-start(bf16[128,384]{1,0:T(8,128)(2,1)S(1)} %get-tuple-element.145.refs_2_), channel_id=1, source_target_pairs={{0,16},{8,24},{16,0},{24,8},{1,17},{9,25},{17,1},{25,9},{2,18},{10... | collective-permute-start | bytes 294920 | tf_op jit(solution)/shard_map/ppermute | solution.py:879
  35.4 1.6 %collective-permute-start.3 = (bf16[512,128]{1,0:T(8,128)(2,1)S(1)}, bf16[512,128]{1,0:T(8,128)(2,1)S(1)}, u32[]{:S(2)}, u32[]{:S(2)}) collective-permute-start(bf16[512,128]{1,0:T(8,128)(2,1)S(1)} %add_convert_fusion.3.refs_1_), channel_id=1, source_target_pairs={{0,4},{1,5},{2,6},{3,7},{4,0},{5,1},{6,2},{7,3},{8,12},{9,13},{10,... | collective-permute-start | bytes 393224 | tf_op jit(solution)/shard_map/ppermute | solution.py:879
  39.9 2.9 %collective-permute-done.3.refs_2_ = bf16[512,128]{1,0:T(8,128)(2,1)S(1)} collective-permute-done((bf16[512,128]{1,0:T(8,128)(2,1)S(1)}, bf16[512,128]{1,0:T(8,128)(2,1)S(1)}, u32[]{:S(2)}, u32[]{:S(2)}) %collective-permute-start.3) | collective-permute-done | bytes 131104 | tf_op jit(solution)/shard_map/ppermute | solution.py:879
  42.8 8.0 %middle_half.1 = (bf16[512,128]{1,0:T(8,128)(2,1)}, bf16[512,256]{1,0:T(8,128)(2,1)}, bf16[512,256]{1,0:T(8,128)(2,1)}, f32[512,256]{1,0:T(8,128)}, bf16[512,256...) custom-call(s32[2]{0:T(128)S(1)} %pad_add_fusion.refs_0_, ...), custom_call_target="tpu_custom_call" | custom-call | flops 10000000000 | bytes 1048576 | tf_op jit(solution)/shard_map/middle_half/pallas_call | solution.py:128
  51.9 2.4 %collective-permute-start.12 = (bf16[512,128]{1,0:T(8,128)(2,1)S(1)}, bf16[512,128]{1,0:T(8,128)(2,1)S(1)}, u32[]{:S(2)}, u32[]{:S(2)}) collective-permute-start(bf16[512,128]{1,0:T(8,128)(2,1)S(1)} %get-tuple-element.157), channel_id=1, source_target_pairs={{0,2},{1,3},{2,0},{3,1},{4,6},{5,7},{6,4},{7,5},{8,10},{9,11},{10,... | collective-permute-start | bytes 393224 | tf_op jit(solution)/shard_map/ppermute | solution.py:879
  57.4 2.6 %collective-permute-done.12 = bf16[512,128]{1,0:T(8,128)(2,1)S(1)} collective-permute-done((bf16[512,128]{1,0:T(8,128)(2,1)S(1)}, bf16[512,128]{1,0:T(8,128)(2,1)S(1)}, u32[]{:S(2)}, u32[]{:S(2)}) %collective-permute-start.12) | collective-permute-done | bytes 131104 | tf_op jit(solution)/shard_map/ppermute | solution.py:879
  60.3 1.6 %collective-permute-start.14 = (bf16[512,128]{1,0:T(8,128)(2,1)S(1)}, bf16[512,128]{1,0:T(8,128)(2,1)S(1)}, u32[]{:S(2)}, u32[]{:S(2)}) collective-permute-start(bf16[512,128]{1,0:T(8,128)(2,1)S(1)} %add_convert_fusion.2.refs_1_), channel_id=1, source_target_pairs={{0,4},{1,5},{2,6},{3,7},{4,0},{5,1},{6,2},{7,3},{8,12},{9,13},{10,... | collective-permute-start | bytes 393224 | tf_op jit(solution)/shard_map/ppermute | solution.py:879
  64.2 4.2 %collective-permute-done.14.refs_2_ = bf16[512,128]{1,0:T(8,128)(2,1)S(1)} collective-permute-done((bf16[512,128]{1,0:T(8,128)(2,1)S(1)}, bf16[512,128]{1,0:T(8,128)(2,1)S(1)}, u32[]{:S(2)}, u32[]{:S(2)}) %collective-permute-start.14) | collective-permute-done | bytes 131104 | tf_op jit(solution)/shard_map/ppermute | solution.py:879
  68.4 3.4 %turn.1 = (bf16[512,128]{1,0:T(8,128)(2,1)S(1)}, bf16[512,256]{1,0:T(8,128)(2,1)S(1)}, bf16[512,256]{1,0:T(8,128)(2,1)S(1)}, f32[128,1024]{1,0:T(8,128)S(1)}, bf...) custom-call(s32[2]{0:T(128)S(1)} %pad_add_fusion.refs_0_, ...), custom_call_target="tpu_custom_call" | custom-call | flops 2000000000 | bytes 1048576 | tf_op jit(solution)/shard_map/turn/pallas_call | solution.py:128
  72.1 3.5 %collective-permute-start.19 = (bf16[128,512]{1,0:T(8,128)(2,1)S(1)}, bf16[128,512]{1,0:T(8,128)(2,1)S(1)}, u32[]{:S(2)}, u32[]{:S(2)}) collective-permute-start(bf16[128,512]{1,0:T(8,128)(2,1)S(1)} %get-tuple-element.181), channel_id=1, source_target_pairs={{0,2},{1,3},{2,0},{3,1},{4,6},{5,7},{6,4},{7,5},{8,10},{9,11},{10,... | collective-permute-start | bytes 393224 | tf_op jit(solution)/shard_map/ppermute | solution.py:879
  76.4 2.1 %large_grads.1 = bf16[128,1280]{1,0:T(8,128)(2,1)} custom-call(bf16[512,256]{1,0:T(8,128)(2,1)S(1)} %get-tuple-element.172.refs_0_, bf16[512,256]{1,0:T(8,128)(2,1)S(1)} %get-tuple-element.173.refs_1_, bf16[128,1024]{1,0:T(8,128)(2,1)S(1)} %get-tuple-element.174.refs_2_, s32[1,1024]{1,0:T(1,128)S(1)} %bitcast.53, s32[1,1024]{1,0:T(1,128)S(1)} %bitcast.47, ...), custom_call_target="tpu_custom_call" | custom-call | flops 1000000000 | bytes 1048576 | tf_op jit(solution)/shard_map/large_grads/pallas_call | solution.py:128
  79.2 2.4 %collective-permute-done.19 = bf16[128,512]{1,0:T(8,128)(2,1)S(1)} collective-permute-done((bf16[128,512]{1,0:T(8,128)(2,1)S(1)}, bf16[128,512]{1,0:T(8,128)(2,1)S(1)}, u32[]{:S(2)}, u32[]{:S(2)}) %collective-permute-start.19) | collective-permute-done | bytes 131104 | tf_op jit(solution)/shard_map/ppermute | solution.py:879
  82.0 4.9 %all-to-all-start.1 = ((bf16[8,16,1280]{2,1,0:T(8,128)(2,1)}), bf16[8,16,1280]{2,1,0:T(8,128)(2,1)S(1)}, u32[]{:S(2)}, u32[]{:S(2)}) async-start(bf16[8,16,1280]{2,1,0:T(8,128)(2,1)} %bitcast.15), calls=%async_computation.1 | async-start | bytes 655360 | tf_op jit(solution)/shard_map/all_to_all | solution.py:856
  86.9 2.5 %fetch.4 = (f32[128,1024]{1,0:T(8,128)S(1)}, bf16[128,1024]{1,0:T(8,128)(2,1)S(1)}, bf16[128,1024]{1,0:T(8,128)(2,1)S(1)}, bf16[64,1024]{1,0:T(8,128)(2,1)S(1)},...) custom-call(f32[128,1024]{1,0:T(8,128)} %get-tuple-element.182.refs_, ...), custom_call_target="tpu_custom_call" | custom-call | flops 1000000000 | bytes 1048576 | tf_op jit(solution)/shard_map/fetch/pallas_call | solution.py:158
  90.0 7.2 %back_middle.1 = (bf16[128,256]{1,0:T(8,128)(2,1)S(1)}, bf16[128,512]{1,0:T(8,128)(2,1)S(1)}, bf16[512,256]{1,0:T(8,128)(2,1)S(1)}, bf16[512,256]{1,0:T(8,128)(2...) custom-call(s32[2]{0:T(128)S(1)} %pad_add_fusion.refs_0_, ...), custom_call_target="tpu_custom_call" | custom-call | flops 10000000000 | bytes 1048576 | tf_op jit(solution)/shard_map/back_middle/pallas_call | solution.py:128
  97.2 2.4 %collective-permute-start.24 = (bf16[128,512]{1,0:T(8,128)(2,1)S(1)}, bf16[128,512]{1,0:T(8,128)(2,1)S(1)}, u32[]{:S(2)}, u32[]{:S(2)}) collective-permute-start(bf16[128,512]{1,0:T(8,128)(2,1)S(1)} %get-tuple-element.228), channel_id=1, source_target_pairs={{0,3},{1,2},{2,1},{3,0},{4,7},{5,6},{6,5},{7,4},{8,11},{9,10},{10,... | collective-permute-start | bytes 393224 | tf_op jit(solution)/shard_map/ppermute | solution.py:879
  100.8 2.7 %large_pieces.1 = bf16[4,128,384]{2,1,0:T(8,128)(2,1)S(1)} custom-call(s32[2]{0:T(128)S(1)} %pad_add_fusion.refs_0_, bf16[512,256]{1,0:T(8,128)(2,1)S(1)} %get-tuple-element.220.refs_1_, bf16[512,256]{1,0:T(8,128)(2,1)S(1)} %get-tuple-element.221.refs_2_, bf16[128,1024]{1,0:T(8,128)(2,1)S(1)} %get-tuple-element.222.refs_3_, s32[1,1024]{1,0:T(1,128)S(1)} %bitcast.55, ...), custom_call_target="tpu_custom_call" | custom-call | flops 1000000000 | bytes 1048576 | tf_op jit(solution)/shard_map/large_pieces/pallas_call | solution.py:128
  105.9 2.2 %collective-permute-start.25 = (bf16[128,512]{1,0:T(8,128)(2,1)S(1)}, bf16[128,512]{1,0:T(8,128)(2,1)S(1)}, u32[]{:S(2)}, u32[]{:S(2)}) collective-permute-start(bf16[128,512]{1,0:T(8,128)(2,1)S(1)} %add_convert_fusion.refs_0_), channel_id=1, source_target_pairs={{0,4},{1,5},{2,6},{3,7},{4,0},{5,1},{6,2},{7,3},{8,12},{9,13},{10,... | collective-permute-start | bytes 393224 | tf_op jit(solution)/shard_map/ppermute | solution.py:879
  111.0 1.6 %collective-permute-start.31 = (bf16[2,64,256]{2,1,0:T(8,128)(2,1)S(1)}, bf16[2,64,256]{2,1,0:T(8,128)(2,1)S(1)}, u32[]{:S(2)}, u32[]{:S(2)}) collective-permute-start(bf16[2,64,256]{2,1,0:T(8,128)(2,1)S(1)} %get-tuple-element.267), channel_id=1, source_target_pairs={{0,3},{1,2},{2,1},{3,0},{4,7},{5,6},{6,5},{7,4},{8,11},{9,10},{10,... | collective-permute-start | bytes 196616 | tf_op jit(solution)/shard_map/ppermute | solution.py:879
  113.4 2.0 %fetch.5 = (f32[128,1024]{1,0:T(8,128)S(1)}, bf16[128,1024]{1,0:T(8,128)(2,1)S(1)}, bf16[128,1024]{1,0:T(8,128)(2,1)S(1)}, bf16[64,1024]{1,0:T(8,128)(2,1)S(1)},...) custom-call(f32[128,1024]{1,0:T(8,128)} %get-tuple-element.231.refs_, ...), custom_call_target="tpu_custom_call" | custom-call | flops 1000000000 | bytes 1048576 | tf_op jit(solution)/shard_map/fetch/pallas_call | solution.py:158
  115.4 5.4 %back_last.1 = (f32[128,1024]{1,0:T(8,128)S(1)}, bf16[128,640]{1,0:T(8,128)(2,1)}) custom-call(bf16[128,512]{1,0:T(8,128)(2,1)S(1)} %add_convert_fusion.refs_0_, bf16[128,512]{1,0:T(8,128)(2,1)S(1)} %collective-permute-done.25.refs_1_, f32[128,1024]{1,0:T(8,128)S(1)} %get-tuple-element.244.refs_2_, ...), custom_call_target="tpu_custom_call", output_to_operand_aliasing={{1}: (28, {})} | custom-call | flops 10000000000 | bytes 1048576 | tf_op jit(solution)/shard_map/back_last/pallas_call | solution.py:128
  120.9 4.8 %all-to-all-start.2 = ((bf16[8,16,640]{2,1,0:T(8,128)(2,1)}), bf16[8,16,640]{2,1,0:T(8,128)(2,1)S(1)}, u32[]{:S(2)}, u32[]{:S(2)}) async-start(bf16[8,16,640]{2,1,0:T(8,128)(2,1)} %bitcast.84), calls=%async_computation.2 | async-start | bytes 327680 | tf_op jit(solution)/shard_map/all_to_all | solution.py:856
  125.8 3.0 %collective-permute-start.32 = (bf16[64,256]{1,0:T(8,128)(2,1)S(1)}, bf16[64,256]{1,0:T(8,128)(2,1)S(1)}, u32[]{:S(2)}, u32[]{:S(2)}) collective-permute-start(bf16[64,256]{1,0:T(8,128)(2,1)S(1)} %slice_bitcast_fusion.4), channel_id=1, source_target_pairs={{0,4},{1,5},{2,6},{3,7},{4,0},{5,1},{6,2},{7,3},{8,12},{9,13},{10,... | collective-permute-start | bytes 98312 | tf_op jit(solution)/shard_map/ppermute | solution.py:879
  128.7 5.0 %all-to-all-done.2.refs_0_ = bf16[8,16,640]{2,1,0:T(8,128)(2,1)S(1)} async-done(((bf16[8,16,640]{2,1,0:T(8,128)(2,1)}), bf16[8,16,640]{2,1,0:T(8,128)(2,1)S(1)}, u32[]{:S(2)}, u32[]{:S(2)}) %all-to-all-start.2) | async-done | bytes 163872 | tf_op jit(solution)/shard_map/all_to_all | solution.py:856
  139.0 1.7 %adam.1 = (f32[16,3000]{1,0:T(8,128)}, f32[16,3000]{1,0:T(8,128)}, f32[16,3000]{1,0:T(8,128)}, f32[16,3000]{1,0:T(8,128)}, bf16[16,3000]{1,0:T(8,128)(2,1)}) custom-call(s32[2]{0:T(128)S(1)} %pad_add_fusion.refs_0_, f32[16,3000]{1,0:T(8,128)S(1)} %bitcast.41, f32[16,3000]{1,0:T(8,128)S(1)} %bitcast.42, f32[16,3000]{1,0:T(8,128)S(1)} %bitcast.43, ...), custom_call_target="tpu_custom_call" | custom-call | flops 100000000 | bytes 1048576 | tf_op jit(solution)/shard_map/adam/pallas_call | solution.py:128
  (114 shorter events, 32.7 us)
Async XLA Ops:
  2.0 18.9 %all-to-all-start = ((bf16[8,16,256]{2,1,0:T(8,128)(2,1)}), bf16[8,16,256]{2,1,0:T(8,128)(2,1)S(1)}, u32[]{:S(2)}, u32[]{:S(2)}) async-start(bf16[8,16,256]{2,1,0:T(8,128)(2,1)} %pack_first.1), calls=%async_computation | async-start | bytes 131072 | tf_op jit(solution)/shard_map/all_to_all | solution.py:856
  11.0 6.0 %collective-permute-start.4 = (bf16[1,144,256]{2,1,0:T(8,128)(2,1)S(1)}, bf16[1,144,256]{2,1,0:T(8,128)(2,1)S(1)}, u32[]{:S(2)}, u32[]{:S(2)}) collective-permute-start(bf16[1,144,256]{2,1,0:T(8,128)(2,1)S(1)} %pack_cargo.1.refs_1_.refs_23_), channel_id=1, source_target_pairs={{0,4},{1,5},{2,6},{3,7},{4,0},{5,1},{6,2},{7,3},{8,12},{9,13},{10,... | collective-permute-start | bytes 221192 | tf_op jit(solution)/shard_map/ppermute | solution.py:879
  17.1 13.3 %collective-permute-start.7 = (bf16[2,144,256]{2,1,0:T(8,128)(2,1)S(1)}, bf16[2,144,256]{2,1,0:T(8,128)(2,1)S(1)}, u32[]{:S(2)}, u32[]{:S(2)}) collective-permute-start(bf16[2,144,256]{2,1,0:T(8,128)(2,1)S(1)} %pad_maximum_fusion), channel_id=1, source_target_pairs={{0,3},{1,2},{2,1},{3,0},{4,7},{5,6},{6,5},{7,4},{8,11},{9,10},{10,... | collective-permute-start | bytes 442376 | tf_op jit(solution)/shard_map/ppermute | solution.py:879
  19.4 11.0 %collective-permute-start.6 = (bf16[2,144,256]{2,1,0:T(8,128)(2,1)S(1)}, bf16[2,144,256]{2,1,0:T(8,128)(2,1)S(1)}, u32[]{:S(2)}, u32[]{:S(2)}) collective-permute-start(bf16[2,144,256]{2,1,0:T(8,128)(2,1)S(1)} %pad_maximum_fusion), channel_id=1, source_target_pairs={{0,2},{1,3},{2,0},{3,1},{4,6},{5,7},{6,4},{7,5},{8,10},{9,11},{10,... | collective-permute-start | bytes 442376 | tf_op jit(solution)/shard_map/ppermute | solution.py:879
  20.9 9.5 %collective-permute-start.5 = (bf16[2,144,256]{2,1,0:T(8,128)(2,1)S(1)}, bf16[2,144,256]{2,1,0:T(8,128)(2,1)S(1)}, u32[]{:S(2)}, u32[]{:S(2)}) collective-permute-start(bf16[2,144,256]{2,1,0:T(8,128)(2,1)S(1)} %pad_maximum_fusion), channel_id=1, source_target_pairs={{0,1},{1,0},{2,3},{3,2},{4,5},{5,4},{6,7},{7,6},{8,9},{9,8},{10,11... | collective-permute-start | bytes 442376 | tf_op jit(solution)/shard_map/ppermute | solution.py:879
  26.8 6.1 %collective-permute-start.2 = (bf16[512,128]{1,0:T(8,128)(2,1)S(1)}, bf16[512,128]{1,0:T(8,128)(2,1)S(1)}, u32[]{:S(2)}, u32[]{:S(2)}) collective-permute-start(bf16[512,128]{1,0:T(8,128)(2,1)S(1)} %get-tuple-element.143), channel_id=1, source_target_pairs={{0,3},{1,2},{2,1},{3,0},{4,7},{5,6},{6,5},{7,4},{8,11},{9,10},{10,... | collective-permute-start | bytes 393224 | tf_op jit(solution)/shard_map/ppermute | solution.py:879
  28.9 5.8 %collective-permute-start.1 = (bf16[512,128]{1,0:T(8,128)(2,1)S(1)}, bf16[512,128]{1,0:T(8,128)(2,1)S(1)}, u32[]{:S(2)}, u32[]{:S(2)}) collective-permute-start(bf16[512,128]{1,0:T(8,128)(2,1)S(1)} %get-tuple-element.143), channel_id=1, source_target_pairs={{0,2},{1,3},{2,0},{3,1},{4,6},{5,7},{6,4},{7,5},{8,10},{9,11},{10,... | collective-permute-start | bytes 393224 | tf_op jit(solution)/shard_map/ppermute | solution.py:879
  31.3 5.9 %collective-permute-start.10 = (bf16[128,384]{1,0:T(8,128)(2,1)S(1)}, bf16[128,384]{1,0:T(8,128)(2,1)S(1)}, u32[]{:S(2)}, u32[]{:S(2)}) collective-permute-start(bf16[128,384]{1,0:T(8,128)(2,1)S(1)} %get-tuple-element.145.refs_2_), channel_id=1, source_target_pairs={{0,24},{8,16},{16,8},{24,0},{1,25},{9,17},{17,9},{25,1},{2,26},{10... | collective-permute-start | bytes 294920 | tf_op jit(solution)/shard_map/ppermute | solution.py:879
  31.3 7.2 %collective-permute-start.9 = (bf16[128,384]{1,0:T(8,128)(2,1)S(1)}, bf16[128,384]{1,0:T(8,128)(2,1)S(1)}, u32[]{:S(2)}, u32[]{:S(2)}) collective-permute-start(bf16[128,384]{1,0:T(8,128)(2,1)S(1)} %get-tuple-element.145.refs_2_), channel_id=1, source_target_pairs={{0,16},{8,24},{16,0},{24,8},{1,17},{9,25},{17,1},{25,9},{2,18},{10... | collective-permute-start | bytes 294920 | tf_op jit(solution)/shard_map/ppermute | solution.py:879
  35.4 7.3 %collective-permute-start.3 = (bf16[512,128]{1,0:T(8,128)(2,1)S(1)}, bf16[512,128]{1,0:T(8,128)(2,1)S(1)}, u32[]{:S(2)}, u32[]{:S(2)}) collective-permute-start(bf16[512,128]{1,0:T(8,128)(2,1)S(1)} %add_convert_fusion.3.refs_1_), channel_id=1, source_target_pairs={{0,4},{1,5},{2,6},{3,7},{4,0},{5,1},{6,2},{7,3},{8,12},{9,13},{10,... | collective-permute-start | bytes 393224 | tf_op jit(solution)/shard_map/ppermute | solution.py:879
  50.8 6.6 %collective-permute-start.13 = (bf16[512,128]{1,0:T(8,128)(2,1)S(1)}, bf16[512,128]{1,0:T(8,128)(2,1)S(1)}, u32[]{:S(2)}, u32[]{:S(2)}) collective-permute-start(bf16[512,128]{1,0:T(8,128)(2,1)S(1)} %get-tuple-element.157), channel_id=1, source_target_pairs={{0,3},{1,2},{2,1},{3,0},{4,7},{5,6},{6,5},{7,4},{8,11},{9,10},{10,... | collective-permute-start | bytes 393224 | tf_op jit(solution)/shard_map/ppermute | solution.py:879
  51.9 8.1 %collective-permute-start.12 = (bf16[512,128]{1,0:T(8,128)(2,1)S(1)}, bf16[512,128]{1,0:T(8,128)(2,1)S(1)}, u32[]{:S(2)}, u32[]{:S(2)}) collective-permute-start(bf16[512,128]{1,0:T(8,128)(2,1)S(1)} %get-tuple-element.157), channel_id=1, source_target_pairs={{0,2},{1,3},{2,0},{3,1},{4,6},{5,7},{6,4},{7,5},{8,10},{9,11},{10,... | collective-permute-start | bytes 393224 | tf_op jit(solution)/shard_map/ppermute | solution.py:879
  54.3 5.7 %collective-permute-start.11 = (bf16[512,128]{1,0:T(8,128)(2,1)S(1)}, bf16[512,128]{1,0:T(8,128)(2,1)S(1)}, u32[]{:S(2)}, u32[]{:S(2)}) collective-permute-start(bf16[512,128]{1,0:T(8,128)(2,1)S(1)} %get-tuple-element.157), channel_id=1, source_target_pairs={{0,1},{1,0},{2,3},{3,2},{4,5},{5,4},{6,7},{7,6},{8,9},{9,8},{10,11... | collective-permute-start | bytes 393224 | tf_op jit(solution)/shard_map/ppermute | solution.py:879
  54.4 7.6 %collective-permute-start.17 = (bf16[128,384]{1,0:T(8,128)(2,1)S(1)}, bf16[128,384]{1,0:T(8,128)(2,1)S(1)}, u32[]{:S(2)}, u32[]{:S(2)}) collective-permute-start(bf16[128,384]{1,0:T(8,128)(2,1)S(1)} %get-tuple-element.161.refs_1_), channel_id=1, source_target_pairs={{0,24},{8,16},{16,8},{24,0},{1,25},{9,17},{17,9},{25,1},{2,26},{10... | collective-permute-start | bytes 294920 | tf_op jit(solution)/shard_map/ppermute | solution.py:879
  54.4 7.5 %collective-permute-start.16 = (bf16[128,384]{1,0:T(8,128)(2,1)S(1)}, bf16[128,384]{1,0:T(8,128)(2,1)S(1)}, u32[]{:S(2)}, u32[]{:S(2)}) collective-permute-start(bf16[128,384]{1,0:T(8,128)(2,1)S(1)} %get-tuple-element.161.refs_1_), channel_id=1, source_target_pairs={{0,16},{8,24},{16,0},{24,8},{1,17},{9,25},{17,1},{25,9},{2,18},{10... | collective-permute-start | bytes 294920 | tf_op jit(solution)/shard_map/ppermute | solution.py:879
  60.3 8.2 %collective-permute-start.14 = (bf16[512,128]{1,0:T(8,128)(2,1)S(1)}, bf16[512,128]{1,0:T(8,128)(2,1)S(1)}, u32[]{:S(2)}, u32[]{:S(2)}) collective-permute-start(bf16[512,128]{1,0:T(8,128)(2,1)S(1)} %add_convert_fusion.2.refs_1_), channel_id=1, source_target_pairs={{0,4},{1,5},{2,6},{3,7},{4,0},{5,1},{6,2},{7,3},{8,12},{9,13},{10,... | collective-permute-start | bytes 393224 | tf_op jit(solution)/shard_map/ppermute | solution.py:879
  71.9 7.4 %collective-permute-start.20 = (bf16[128,512]{1,0:T(8,128)(2,1)S(1)}, bf16[128,512]{1,0:T(8,128)(2,1)S(1)}, u32[]{:S(2)}, u32[]{:S(2)}) collective-permute-start(bf16[128,512]{1,0:T(8,128)(2,1)S(1)} %get-tuple-element.181), channel_id=1, source_target_pairs={{0,3},{1,2},{2,1},{3,0},{4,7},{5,6},{6,5},{7,4},{8,11},{9,10},{10,... | collective-permute-start | bytes 393224 | tf_op jit(solution)/shard_map/ppermute | solution.py:879
  72.1 9.6 %collective-permute-start.19 = (bf16[128,512]{1,0:T(8,128)(2,1)S(1)}, bf16[128,512]{1,0:T(8,128)(2,1)S(1)}, u32[]{:S(2)}, u32[]{:S(2)}) collective-permute-start(bf16[128,512]{1,0:T(8,128)(2,1)S(1)} %get-tuple-element.181), channel_id=1, source_target_pairs={{0,2},{1,3},{2,0},{3,1},{4,6},{5,7},{6,4},{7,5},{8,10},{9,11},{10,... | collective-permute-start | bytes 393224 | tf_op jit(solution)/shard_map/ppermute | solution.py:879
  75.6 6.1 %collective-permute-start.18 = (bf16[128,512]{1,0:T(8,128)(2,1)S(1)}, bf16[128,512]{1,0:T(8,128)(2,1)S(1)}, u32[]{:S(2)}, u32[]{:S(2)}) collective-permute-start(bf16[128,512]{1,0:T(8,128)(2,1)S(1)} %get-tuple-element.181), channel_id=1, source_target_pairs={{0,1},{1,0},{2,3},{3,2},{4,5},{5,4},{6,7},{7,6},{8,9},{9,8},{10,11... | collective-permute-start | bytes 393224 | tf_op jit(solution)/shard_map/ppermute | solution.py:879
  81.7 8.3 %collective-permute-start.21 = (bf16[128,512]{1,0:T(8,128)(2,1)S(1)}, bf16[128,512]{1,0:T(8,128)(2,1)S(1)}, u32[]{:S(2)}, u32[]{:S(2)}) collective-permute-start(bf16[128,512]{1,0:T(8,128)(2,1)S(1)} %add_convert_fusion.1.refs_1_), channel_id=1, source_target_pairs={{0,4},{1,5},{2,6},{3,7},{4,0},{5,1},{6,2},{7,3},{8,12},{9,13},{10,... | collective-permute-start | bytes 393224 | tf_op jit(solution)/shard_map/ppermute | solution.py:879
  82.0 21.5 %all-to-all-start.1 = ((bf16[8,16,1280]{2,1,0:T(8,128)(2,1)}), bf16[8,16,1280]{2,1,0:T(8,128)(2,1)S(1)}, u32[]{:S(2)}, u32[]{:S(2)}) async-start(bf16[8,16,1280]{2,1,0:T(8,128)(2,1)} %bitcast.15), calls=%async_computation.1 | async-start | bytes 655360 | tf_op jit(solution)/shard_map/all_to_all | solution.py:856
  97.2 7.8 %collective-permute-start.24 = (bf16[128,512]{1,0:T(8,128)(2,1)S(1)}, bf16[128,512]{1,0:T(8,128)(2,1)S(1)}, u32[]{:S(2)}, u32[]{:S(2)}) collective-permute-start(bf16[128,512]{1,0:T(8,128)(2,1)S(1)} %get-tuple-element.228), channel_id=1, source_target_pairs={{0,3},{1,2},{2,1},{3,0},{4,7},{5,6},{6,5},{7,4},{8,11},{9,10},{10,... | collective-permute-start | bytes 393224 | tf_op jit(solution)/shard_map/ppermute | solution.py:879
  99.6 6.0 %collective-permute-start.23 = (bf16[128,512]{1,0:T(8,128)(2,1)S(1)}, bf16[128,512]{1,0:T(8,128)(2,1)S(1)}, u32[]{:S(2)}, u32[]{:S(2)}) collective-permute-start(bf16[128,512]{1,0:T(8,128)(2,1)S(1)} %get-tuple-element.228), channel_id=1, source_target_pairs={{0,2},{1,3},{2,0},{3,1},{4,6},{5,7},{6,4},{7,5},{8,10},{9,11},{10,... | collective-permute-start | bytes 393224 | tf_op jit(solution)/shard_map/ppermute | solution.py:879
  103.5 6.0 %collective-permute-start.28 = (bf16[128,384]{1,0:T(8,128)(2,1)S(1)}, bf16[128,384]{1,0:T(8,128)(2,1)S(1)}, u32[]{:S(2)}, u32[]{:S(2)}) collective-permute-start(bf16[128,384]{1,0:T(8,128)(2,1)S(1)} %get-tuple-element.275), channel_id=1, source_target_pairs={{0,24},{8,16},{16,8},{24,0},{1,25},{9,17},{17,9},{25,1},{2,26},{10... | collective-permute-start | bytes 294920 | tf_op jit(solution)/shard_map/ppermute | solution.py:879
  103.6 7.4 %collective-permute-start.27 = (bf16[128,384]{1,0:T(8,128)(2,1)S(1)}, bf16[128,384]{1,0:T(8,128)(2,1)S(1)}, u32[]{:S(2)}, u32[]{:S(2)}) collective-permute-start(bf16[128,384]{1,0:T(8,128)(2,1)S(1)} %get-tuple-element.276), channel_id=1, source_target_pairs={{0,16},{8,24},{16,0},{24,8},{1,17},{9,25},{17,1},{25,9},{2,18},{10... | collective-permute-start | bytes 294920 | tf_op jit(solution)/shard_map/ppermute | solution.py:879
  105.0 7.6 %collective-permute-start.26 = (bf16[128,384]{1,0:T(8,128)(2,1)S(1)}, bf16[128,384]{1,0:T(8,128)(2,1)S(1)}, u32[]{:S(2)}, u32[]{:S(2)}) collective-permute-start(bf16[128,384]{1,0:T(8,128)(2,1)S(1)} %get-tuple-element.277), channel_id=1, source_target_pairs={{0,8},{8,0},{16,24},{24,16},{1,9},{9,1},{17,25},{25,17},{2,10},{10... | collective-permute-start | bytes 294920 | tf_op jit(solution)/shard_map/ppermute | solution.py:879
  105.9 9.5 %collective-permute-start.25 = (bf16[128,512]{1,0:T(8,128)(2,1)S(1)}, bf16[128,512]{1,0:T(8,128)(2,1)S(1)}, u32[]{:S(2)}, u32[]{:S(2)}) collective-permute-start(bf16[128,512]{1,0:T(8,128)(2,1)S(1)} %add_convert_fusion.refs_0_), channel_id=1, source_target_pairs={{0,4},{1,5},{2,6},{3,7},{4,0},{5,1},{6,2},{7,3},{8,12},{9,13},{10,... | collective-permute-start | bytes 393224 | tf_op jit(solution)/shard_map/ppermute | solution.py:879
  108.1 17.6 %collective-permute-start.29 = (bf16[2,64,256]{2,1,0:T(8,128)(2,1)S(1)}, bf16[2,64,256]{2,1,0:T(8,128)(2,1)S(1)}, u32[]{:S(2)}, u32[]{:S(2)}) collective-permute-start(bf16[2,64,256]{2,1,0:T(8,128)(2,1)S(1)} %get-tuple-element.265), channel_id=1, source_target_pairs={{0,1},{1,0},{2,3},{3,2},{4,5},{5,4},{6,7},{7,6},{8,9},{9,8},{10,11... | collective-permute-start | bytes 196616 | tf_op jit(solution)/shard_map/ppermute | solution.py:879
  109.5 16.2 %collective-permute-start.30 = (bf16[2,64,256]{2,1,0:T(8,128)(2,1)S(1)}, bf16[2,64,256]{2,1,0:T(8,128)(2,1)S(1)}, u32[]{:S(2)}, u32[]{:S(2)}) collective-permute-start(bf16[2,64,256]{2,1,0:T(8,128)(2,1)S(1)} %get-tuple-element.266), channel_id=1, source_target_pairs={{0,2},{1,3},{2,0},{3,1},{4,6},{5,7},{6,4},{7,5},{8,10},{9,11},{10,... | collective-permute-start | bytes 196616 | tf_op jit(solution)/shard_map/ppermute | solution.py:879
  111.0 14.7 %collective-permute-start.31 = (bf16[2,64,256]{2,1,0:T(8,128)(2,1)S(1)}, bf16[2,64,256]{2,1,0:T(8,128)(2,1)S(1)}, u32[]{:S(2)}, u32[]{:S(2)}) collective-permute-start(bf16[2,64,256]{2,1,0:T(8,128)(2,1)S(1)} %get-tuple-element.267), channel_id=1, source_target_pairs={{0,3},{1,2},{2,1},{3,0},{4,7},{5,6},{6,5},{7,4},{8,11},{9,10},{10,... | collective-permute-start | bytes 196616 | tf_op jit(solution)/shard_map/ppermute | solution.py:879
  120.9 12.8 %all-to-all-start.2 = ((bf16[8,16,640]{2,1,0:T(8,128)(2,1)}), bf16[8,16,640]{2,1,0:T(8,128)(2,1)S(1)}, u32[]{:S(2)}, u32[]{:S(2)}) async-start(bf16[8,16,640]{2,1,0:T(8,128)(2,1)} %bitcast.84), calls=%async_computation.2 | async-start | bytes 327680 | tf_op jit(solution)/shard_map/all_to_all | solution.py:856
  125.8 9.9 %collective-permute-start.32 = (bf16[64,256]{1,0:T(8,128)(2,1)S(1)}, bf16[64,256]{1,0:T(8,128)(2,1)S(1)}, u32[]{:S(2)}, u32[]{:S(2)}) collective-permute-start(bf16[64,256]{1,0:T(8,128)(2,1)S(1)} %slice_bitcast_fusion.4), channel_id=1, source_target_pairs={{0,4},{1,5},{2,6},{3,7},{4,0},{5,1},{6,2},{7,3},{8,12},{9,13},{10,... | collective-permute-start | bytes 98312 | tf_op jit(solution)/shard_map/ppermute | solution.py:879
  (24 other events, 144.1 us)

commit v5 on v4

--- a/solution.py
+++ b/solution.py
@@ -345,9 +345,7 @@
     copy = pltpu.make_async_copy(weights.at[:, :PAD], hold, sem)
     copy.start()
     copy.wait()
-    head = low(padded(hold[...], ROWS, PAD))
-    for s in range(out_ref.shape[0]):
-        out_ref[s] = head
+    out_ref[0] = low(padded(hold[...], ROWS, PAD))
 
 
 def pack_cargo(me, weights, state, fixed, out_ref, hold):
@@ -394,31 +392,40 @@
     return [k ^ low_bits for low_bits in range(4) for k in order]
 
 
+def arrivals(pieces):
+    return [piece[i] for piece in pieces for i in range(piece.shape[0])]
+
+
+def arrival_pick(me, order, cols):
+    col = iota((1, len(order) * ROWS), 1)
+    block, inside = high_low(col, ROWS)
+    owner = jnp.zeros(col.shape, jnp.int32)
+    for position, k in enumerate(order):
+        owner = jnp.where(block == position, me ^ k, owner)
+    return onehot(len(order) * cols, jnp.where(inside < cols, owner * cols + inside, -1))
+
+
 def collect(me, *refs):
-    *cargo, one_ref, two_ref = refs
-    rows = cargo[0].shape[1]
-    owners = sum(c.shape[0] for c in cargo)
+    *cargo, one_ref, two_ref, state_ref, free_ref = refs
+    cargo = arrivals(cargo)
+    owners = len(cargo)
     full, width = one_ref.shape
-    cols = full // owners
-    count = slots(width)
-    base = rows - 2 * count * ROWS
+    count = state_ref.shape[0] // owners
     order = order_of(owners)
-    shape = (full, owners * ROWS)
-    row, col = iota(shape, 0), iota(shape, 1)
-    owner, inside = row // cols, row % cols
-    sel = None
-    for position, k in enumerate(order):
-        hit = (col == position * ROWS + inside) & (owner == (me[0] ^ k))
-        sel = hit if sel is None else sel | hit
-    sel = ones_where(sel)
+    sel = arrival_pick(me[0], order, full // owners)
     for side, ref in ((0, one_ref), (1, two_ref)):
-        for k in range(count):
-            start = base + (side * count + k) * ROWS
-            values = jnp.concatenate(
-                [c[i, start : start + ROWS] for c in cargo for i in range(c.shape[0])], axis=0
-            )
+        for k in range(slots(width)):
+            start = count + ROWS * (1 + side * slots(width) + k)
+            values = jnp.concatenate([c[start : start + ROWS] for c in cargo], axis=0)
             lanes = min(PAD, width - k * PAD)
             ref[:, k * PAD : k * PAD + lanes] = low(dot(sel, values))[:, :lanes]
+    eye = iota((count, count), 0) == iota((count, count), 1)
+    for piece, k in zip(cargo, order):
+        rows = pl.ds(pl.multiple_of((me[0] ^ k) * count, count), count)
+        state_ref[rows] = piece[:count]
+        flag = piece[count : count + 1, :count].astype(F32)
+        column = jnp.sum(jnp.where(eye, flag, 0.0), axis=1, keepdims=True)
+        free_ref[rows] = low(jnp.broadcast_to(column, (count, D_ATOM)))
 
 
 def joined(me, pieces, hold):
@@ -427,20 +434,11 @@
     return low(jnp.concatenate([hold[g] for g in range(len(pieces))], axis=1))
 
 
-def small_rows(pack, cols):
-    owners = pack.shape[0]
-    value = pack[...].reshape(owners * ROWS, PAD)
-    if cols == ROWS:
-        return value
-    c, row = iota((owners * cols, owners * ROWS), 0), iota((owners * cols, owners * ROWS), 1)
-    return low(dot(ones_where(row == c // cols * ROWS + c % cols), value))
-
-
-def prepare_one(me, pack, *refs):
+def prepare_one(me, raw, *refs):
     *rest, hold = refs
     groups = hold.shape[0]
     wide = joined(me, rest[:groups], hold)
-    raw_one = small_rows(pack, D_EDGE // pack.shape[0])
+    raw_one = raw[...]
     raw_two = wide[:, BIG:]
     values = back_matrices(raw_one) + [wide_t(raw_one, OFF_RADIAL, D_BASIS)]
     values = values + small_matrices(raw_two) + back_matrices(raw_two)
@@ -566,11 +564,17 @@
 KEPT = 13
 
 
-def first_half(edge_state, pack, *refs):
-    graph, dst_row, out_refs = refs[:7], refs[7], refs[8:]
+def first_half(me, edge_state, *refs):
+    graph, dst_row, rest = refs[:7], refs[7], refs[8:]
+    pack = [ref for ref in rest if len(ref.shape) == 3]
+    raw_ref, *out_refs = rest[len(pack) :]
+    blocks = arrivals(pack)
+    owners = len(blocks)
+    sel = arrival_pick(me[0], order_of(owners), D_EDGE // owners)
+    raw = low(dot(sel, jnp.concatenate(blocks, axis=0)))
+    raw_ref[...] = raw
     eye = ones_where(iota((D_EDGE, D_EDGE), 0) == iota((D_EDGE, D_EDGE), 1))
     state_t = dot_nt(eye, edge_state[...])
-    raw = small_rows(pack, D_EDGE // pack.shape[0])
     block_forward(state_t, small_matrices(raw), graph, dst_row, out_refs)
 
 
@@ -595,34 +599,16 @@
     return total
 
 
-def middle_half(me, near, far, big, first, second, mid_in, *refs):
+def middle_half(near, far, big, first, second, mid_in, *refs):
     matrices, graph, src_row, dst_row = refs[:7], refs[7:14], refs[14], refs[15]
-    atoms = near.shape[0]
-    cargo, refs = refs[16:], None
-    split = 0
-    owners = 0
-    while len(cargo[split].shape) == 3:
-        owners = owners + cargo[split].shape[0]
-        split = split + 1
-    cargo, rest = cargo[:split], cargo[split:]
-    atom_in_ref, hidden_ref, slope_atom_ref, state_ref, sent_ref, free_ref, slope_edge_ref = rest[:7]
-    *out_refs, free_wide = rest[7:]
-    count = atoms // owners
-    eye = iota((count, count), 0) == iota((count, count), 1)
-    order = order_of(owners)
-    position = 0
-    for pieces in cargo:
-        for i in range(pieces.shape[0]):
-            rows = pl.ds(pl.multiple_of((me[0] ^ order[position]) * count, count), count)
-            state_ref.ref[rows] = pieces[i, :count].astype(F32)
-            flag = pieces[i, count : count + 1, :count].astype(F32)
-            column = jnp.sum(jnp.where(eye, flag, 0.0), axis=1, keepdims=True)
-            free_wide[rows] = jnp.broadcast_to(column, (count, D_ATOM))
-            position = position + 1
-    free_ref[...] = low(free_wide[...])
+    old_state, old_free = refs[16:18]
+    atom_in_ref, hidden_ref, slope_atom_ref, state_ref, sent_ref, free_ref, slope_edge_ref = refs[18:25]
+    out_refs = refs[25:]
+    free = old_free[...]
+    free_ref[...] = free
     send(free_ref)
     atom_in, hidden, slope, state = atom_forward(
-        near, far, state_ref[...], free_wide[...], first, second
+        near, far, old_state[...].astype(F32), free.astype(F32), first, second
     )
     atom_in_ref[...] = atom_in
     hidden_ref[...] = hidden
@@ -894,16 +880,23 @@
     weights_t = jnp.transpose(weights)
     cols = weights_t.shape[0]
     lanes = (BIG + PAD) // groups
+    def gathered(piece):
+        arrays = [piece]
+        for steps in gather_rounds(owners):
+            held = arrays[0] if len(arrays) == 1 else jnp.concatenate(arrays, axis=0)
+            arrays = arrays + [moved(held, step, owners) for step in steps]
+        return arrays
+
     [pack] = call(
         pack_first,
-        [sds((owners, ROWS, PAD), BF16)],
+        [sds((1, ROWS, PAD), BF16)],
         [weights_t],
         flops=10**7,
         raw=[0],
         scratch=[pltpu.VMEM((cols, PAD), F32), pltpu.SemaphoreType.DMA],
     )
     pack, state = lax.optimization_barrier((pack, atom_state))
-    pack = exchange(pack)
+    pack = gathered(pack)
     [cargo] = call(
         pack_cargo,
         [sds((1, count + ROWS * (1 + 2 * slots(lanes)), D_ATOM), BF16)],
@@ -913,12 +906,7 @@
         smem=1,
         scratch=[(groups, cols, lanes)],
     )
-    cargo = [cargo]
-    for steps in gather_rounds(owners):
-        held = cargo[0] if len(cargo) == 1 else jnp.concatenate(cargo, axis=0)
-        cargo = cargo + [moved(held, step, owners) for step in steps]
-    lanes_shape = sds((D_EDGE, lanes), BF16)
-    wide, big_two = call(collect, [lanes_shape, lanes_shape], [me] + cargo, flops=10**7, smem=1)
+    cargo = gathered(cargo)
     dst_row = (dst_owner[:, 0] * count + dst_local).reshape(1, edges)
     src_row = (src_owner[:, 0] * count + src_local).reshape(1, edges)
     graph = [
@@ -937,12 +925,22 @@
     atom_shape = sds((atoms, D_ATOM), BF16)
     atom_wide = sds((atoms, D_ATOM), F32)
     gain_shape = sds((D_EDGE, atoms), BF16)
-    *kept_one, table = call(
+    raw_one, *kept_one, table = call(
         first_half,
-        kept + [table_shape],
-        [edge_state, pack] + graph + [dst_row],
+        [sds((D_EDGE, PAD), BF16)] + kept + [table_shape],
+        [me, edge_state] + graph + [dst_row] + pack,
         flops=8 * 10**9,
-        kept=range(KEPT),
+        kept=range(1, 1 + KEPT),
+        smem=1,
+    )
+    table, cargo = lax.optimization_barrier((table, cargo))
+    lanes_shape = sds((D_EDGE, lanes), BF16)
+    wide, big_two, old_state, old_free = call(
+        collect,
+        [lanes_shape, lanes_shape] + [sds((atoms, D_ATOM), BF16)] * 2,
+        [me] + cargo,
+        flops=10**7,
+        smem=1,
     )
     near, far, _ = sum_pair(table, owners)
 
@@ -953,7 +951,7 @@
         call(
             prepare_one,
             [sds(s, BF16) for s in PREPARED],
-            [me, pack] + everywhere(wide),
+            [me, raw_one] + everywhere(wide),
             flops=10**9,
             smem=1,
             scratch=[(groups, D_EDGE, lanes)],
@@ -968,16 +966,13 @@
         [table_shape, atom_shape, atom_shape, atom_wide, atom_shape, atom_shape, edge_shape]
         + kept
         + [table_shape],
-        [me, near, far, big_one, first_one, second_one, kept_one[0]]
+        [near, far, big_one, first_one, second_one, kept_one[0]]
         + small_two
         + graph
-        + [src_row, dst_row]
-        + cargo,
+        + [src_row, dst_row, old_state, old_free],
         flops=10 * 10**9,
-        late=[6],
+        late=[5],
         kept=range(7 + KEPT),
-        smem=1,
-        scratch=[(atoms, D_ATOM)],
     )
     near, far, _ = sum_pair(table, owners)
     near, state_one, kept_two[0] = lax.optimization_barrier((near, state_one, kept_two[0]))

time: 141 us -> 137 us (0.972)
  starting transfers between devices: 58.6 us -> 53.7 us
    all_to_all x3 -> x2, starting transfers between devices: 17 us -> 9.8 us  [exchange(): return lax.all_to_all(pieces, 'shard', split_axis=0, concat_axis=0)]
    ppermute x36 -> x40, starting transfers between devices: 41.7 us -> 43.9 us  [moved(): return lax.ppermute(table, axis, [(i, i ^ step) for i in range(owners)])]
    ppermute x36 -> x40, waiting for transfers between devices: 23.7 us -> 24.5 us  [moved(): return lax.ppermute(table, axis, [(i, i ^ step) for i in range(owners)])]
    all_to_all x3 -> x2, waiting for transfers between devices: 4.97 us -> 4.93 us  [exchange(): return lax.all_to_all(pieces, 'shard', split_axis=0, concat_axis=0)]
  transfers between devices with their start and end apart: 39 -> 42, of which waited for: 16 -> 19; matrix products, arithmetic and copies ran while one was open for 1% -> 1% of each run, Pallas kernels for 26% -> 27%
where the time goes in v5:
time: 137 us; the launch traced here: 136 us
  starting transfers between devices  53.7 us (39%)
  Pallas kernels  50 us (36%)
  waiting for transfers between devices  29.4 us (21%)
    pallas_call x17, Pallas kernels, call(): pl.pallas_call(kernel, out_shape=outs, in_specs=[pl.BlockSpec(memory_spac...  44.1 us
    ppermute x40, starting transfers between devices, moved(): return lax.ppermute(table, axis, [(i, i ^ step) for i in range(owners)])  43.9 us
    ppermute x40, waiting for transfers between devices, moved(): return lax.ppermute(table, axis, [(i, i ^ step) for i in range(owners)])  24.5 us
    all_to_all x2, starting transfers between devices, exchange(): return lax.all_to_all(pieces, 'shard', split_axis=0, concat_axis=0)  9.8 us
    pallas_call x3, Pallas kernels, fetch(): pl.pallas_call(kernel, out_shape=[sds(x.shape, x.dtype) for x in arrays],...  5.89 us
    all_to_all x2, waiting for transfers between devices, exchange(): return lax.all_to_all(pieces, 'shard', split_axis=0, concat_axis=0)  4.93 us
  transfers between devices with their start and end apart: 42, of which 19 were waited for; matrix products, arithmetic and copies ran while one was open for 1% of the time, Pallas kernels for 27%

profile of v5, /device:TPU:0, one launch (start us, length us, event | category | flops | bytes accessed | tf_op | source)
XLA Modules:
  0.0 136.1 jit_solution(9367060504073571824)
XLA Ops:
  1.4 4.1 %collective-permute-start = (bf16[1,16,256]{2,1,0:T(8,128)(2,1)S(1)}, bf16[1,16,256]{2,1,0:T(8,128)(2,1)S(1)}, u32[]{:S(2)}, u32[]{:S(2)}) collective-permute-start(bf16[1,16,256]{2,1,0:T(8,128)(2,1)S(1)} %pack_first.1.refs_10_), channel_id=1, source_target_pairs={{0,4},{1,5},{2,6},{3,7},{4,0},{5,1},{6,2},{7,3},{8,12},{9,13},{10,... | collective-permute-start | bytes 24584 | tf_op jit(solution)/shard_map/ppermute | solution.py:865
  8.0 2.9 %collective-permute-start.3 = (bf16[2,16,256]{2,1,0:T(8,128)(2,1)S(1)}, bf16[2,16,256]{2,1,0:T(8,128)(2,1)S(1)}, u32[]{:S(2)}, u32[]{:S(2)}) collective-permute-start(bf16[2,16,256]{2,1,0:T(8,128)(2,1)S(1)} %constant_dynamic-update-slice_fusion), channel_id=1, source_target_pairs={{0,3},{1,2},{2,1},{3,0},{4,7},{5,6},{6,5},{7,4},{8,11},{9,10},{10,... | collective-permute-start | bytes 49160 | tf_op jit(solution)/shard_map/ppermute | solution.py:865
  11.6 1.9 %collective-permute-done.4.refs_2_ = bf16[1,144,256]{2,1,0:T(8,128)(2,1)S(1)} collective-permute-done((bf16[1,144,256]{2,1,0:T(8,128)(2,1)S(1)}, bf16[1,144,256]{2,1,0:T(8,128)(2,1)S(1)}, u32[]{:S(2)}, u32[]{:S(2)}) %collective-permute-start.4) | collective-permute-done | bytes 73760 | tf_op jit(solution)/shard_map/ppermute | solution.py:865
  13.5 1.7 %collective-permute-start.7 = (bf16[2,144,256]{2,1,0:T(8,128)(2,1)S(1)}, bf16[2,144,256]{2,1,0:T(8,128)(2,1)S(1)}, u32[]{:S(2)}, u32[]{:S(2)}) collective-permute-start(bf16[2,144,256]{2,1,0:T(8,128)(2,1)S(1)} %pad_maximum_fusion), channel_id=1, source_target_pairs={{0,3},{1,2},{2,1},{3,0},{4,7},{5,6},{6,5},{7,4},{8,11},{9,10},{10,... | collective-permute-start | bytes 442376 | tf_op jit(solution)/shard_map/ppermute | solution.py:865
  15.2 1.6 %collective-permute-start.6 = (bf16[2,144,256]{2,1,0:T(8,128)(2,1)S(1)}, bf16[2,144,256]{2,1,0:T(8,128)(2,1)S(1)}, u32[]{:S(2)}, u32[]{:S(2)}) collective-permute-start(bf16[2,144,256]{2,1,0:T(8,128)(2,1)S(1)} %pad_maximum_fusion), channel_id=1, source_target_pairs={{0,2},{1,3},{2,0},{3,1},{4,6},{5,7},{6,4},{7,5},{8,10},{9,11},{10,... | collective-permute-start | bytes 442376 | tf_op jit(solution)/shard_map/ppermute | solution.py:865
  17.1 6.1 %first_half.1 = (bf16[128,256]{1,0:T(8,128)(2,1)S(1)}, f32[128,1024]{1,0:T(8,128)}, bf16[128,1024]{1,0:T(8,128)(2,1)}, bf16[128,1024]{1,0:T(8,128)(2,1)}, bf16[6...) custom-call(s32[2]{0:T(128)S(1)} %pad_add_fusion.refs_0_, ...), custom_call_target="tpu_custom_call" | custom-call | flops 8000000000 | bytes 1048576 | tf_op jit(solution)/shard_map/first_half/pallas_call | solution.py:128
  23.3 1.7 %collective-permute-start.10 = (bf16[512,128]{1,0:T(8,128)(2,1)S(1)}, bf16[512,128]{1,0:T(8,128)(2,1)S(1)}, u32[]{:S(2)}, u32[]{:S(2)}) collective-permute-start(bf16[512,128]{1,0:T(8,128)(2,1)S(1)} %get-tuple-element.154), channel_id=1, source_target_pairs={{0,3},{1,2},{2,1},{3,0},{4,7},{5,6},{6,5},{7,4},{8,11},{9,10},{10,... | collective-permute-start | bytes 393224 | tf_op jit(solution)/shard_map/ppermute | solution.py:865
  25.0 1.6 %collective-permute-start.9 = (bf16[512,128]{1,0:T(8,128)(2,1)S(1)}, bf16[512,128]{1,0:T(8,128)(2,1)S(1)}, u32[]{:S(2)}, u32[]{:S(2)}) collective-permute-start(bf16[512,128]{1,0:T(8,128)(2,1)S(1)} %get-tuple-element.154), channel_id=1, source_target_pairs={{0,2},{1,3},{2,0},{3,1},{4,6},{5,7},{6,4},{7,5},{8,10},{9,11},{10,... | collective-permute-start | bytes 393224 | tf_op jit(solution)/shard_map/ppermute | solution.py:865
  32.7 2.2 %collective-permute-done.13.refs_4_ = bf16[128,384]{1,0:T(8,128)(2,1)S(1)} collective-permute-done((bf16[128,384]{1,0:T(8,128)(2,1)S(1)}, bf16[128,384]{1,0:T(8,128)(2,1)S(1)}, u32[]{:S(2)}, u32[]{:S(2)}) %collective-permute-start.13) | collective-permute-done | bytes 98336 | tf_op jit(solution)/shard_map/ppermute | solution.py:865
  36.3 2.8 %collective-permute-done.11.refs_1_ = bf16[512,128]{1,0:T(8,128)(2,1)S(1)} collective-permute-done((bf16[512,128]{1,0:T(8,128)(2,1)S(1)}, bf16[512,128]{1,0:T(8,128)(2,1)S(1)}, u32[]{:S(2)}, u32[]{:S(2)}) %collective-permute-start.11) | collective-permute-done | bytes 131104 | tf_op jit(solution)/shard_map/ppermute | solution.py:865
  39.1 7.6 %middle_half.1 = (bf16[512,128]{1,0:T(8,128)(2,1)}, bf16[512,256]{1,0:T(8,128)(2,1)}, bf16[512,256]{1,0:T(8,128)(2,1)}, f32[512,256]{1,0:T(8,128)}, bf16[512,256...) custom-call(bf16[512,128]{1,0:T(8,128)(2,1)S(1)} %add_convert_fusion, ...), custom_call_target="tpu_custom_call" | custom-call | flops 10000000000 | bytes 1048576 | tf_op jit(solution)/shard_map/middle_half/pallas_call | solution.py:128
  47.1 2.8 %collective-permute-start.16 = (bf16[512,128]{1,0:T(8,128)(2,1)S(1)}, bf16[512,128]{1,0:T(8,128)(2,1)S(1)}, u32[]{:S(2)}, u32[]{:S(2)}) collective-permute-start(bf16[512,128]{1,0:T(8,128)(2,1)S(1)} %get-tuple-element.175), channel_id=1, source_target_pairs={{0,2},{1,3},{2,0},{3,1},{4,6},{5,7},{6,4},{7,5},{8,10},{9,11},{10,... | collective-permute-start | bytes 393224 | tf_op jit(solution)/shard_map/ppermute | solution.py:865
  51.7 1.6 %collective-permute-done.17 = bf16[512,128]{1,0:T(8,128)(2,1)S(1)} collective-permute-done((bf16[512,128]{1,0:T(8,128)(2,1)S(1)}, bf16[512,128]{1,0:T(8,128)(2,1)S(1)}, u32[]{:S(2)}, u32[]{:S(2)}) %collective-permute-start.17) | collective-permute-done | bytes 131104 | tf_op jit(solution)/shard_map/ppermute | solution.py:865
  53.4 2.3 %collective-permute-done.16 = bf16[512,128]{1,0:T(8,128)(2,1)S(1)} collective-permute-done((bf16[512,128]{1,0:T(8,128)(2,1)S(1)}, bf16[512,128]{1,0:T(8,128)(2,1)S(1)}, u32[]{:S(2)}, u32[]{:S(2)}) %collective-permute-start.16) | collective-permute-done | bytes 131104 | tf_op jit(solution)/shard_map/ppermute | solution.py:865
  59.8 4.3 %collective-permute-done.18.refs_2_ = bf16[512,128]{1,0:T(8,128)(2,1)S(1)} collective-permute-done((bf16[512,128]{1,0:T(8,128)(2,1)S(1)}, bf16[512,128]{1,0:T(8,128)(2,1)S(1)}, u32[]{:S(2)}, u32[]{:S(2)}) %collective-permute-start.18) | collective-permute-done | bytes 131104 | tf_op jit(solution)/shard_map/ppermute | solution.py:865
  64.1 3.4 %turn.1 = (bf16[512,128]{1,0:T(8,128)(2,1)S(1)}, bf16[512,256]{1,0:T(8,128)(2,1)S(1)}, bf16[512,256]{1,0:T(8,128)(2,1)S(1)}, f32[128,1024]{1,0:T(8,128)S(1)}, bf...) custom-call(s32[2]{0:T(128)S(1)} %pad_add_fusion.refs_0_, ...), custom_call_target="tpu_custom_call" | custom-call | flops 2000000000 | bytes 1048576 | tf_op jit(solution)/shard_map/turn/pallas_call | solution.py:128
  67.6 3.2 %collective-permute-start.23 = (bf16[128,512]{1,0:T(8,128)(2,1)S(1)}, bf16[128,512]{1,0:T(8,128)(2,1)S(1)}, u32[]{:S(2)}, u32[]{:S(2)}) collective-permute-start(bf16[128,512]{1,0:T(8,128)(2,1)S(1)} %get-tuple-element.199), channel_id=1, source_target_pairs={{0,2},{1,3},{2,0},{3,1},{4,6},{5,7},{6,4},{7,5},{8,10},{9,11},{10,... | collective-permute-start | bytes 393224 | tf_op jit(solution)/shard_map/ppermute | solution.py:865
  71.9 2.1 %large_grads.1 = bf16[128,1280]{1,0:T(8,128)(2,1)} custom-call(bf16[512,256]{1,0:T(8,128)(2,1)S(1)} %get-tuple-element.190.refs_0_, bf16[512,256]{1,0:T(8,128)(2,1)S(1)} %get-tuple-element.191.refs_1_, bf16[128,1024]{1,0:T(8,128)(2,1)S(1)} %get-tuple-element.192.refs_2_, s32[1,1024]{1,0:T(1,128)S(1)} %bitcast.53, s32[1,1024]{1,0:T(1,128)S(1)} %bitcast.47, ...), custom_call_target="tpu_custom_call" | custom-call | flops 1000000000 | bytes 1048576 | tf_op jit(solution)/shard_map/large_grads/pallas_call | solution.py:128
  74.9 2.1 %collective-permute-done.23 = bf16[128,512]{1,0:T(8,128)(2,1)S(1)} collective-permute-done((bf16[128,512]{1,0:T(8,128)(2,1)S(1)}, bf16[128,512]{1,0:T(8,128)(2,1)S(1)}, u32[]{:S(2)}, u32[]{:S(2)}) %collective-permute-start.23) | collective-permute-done | bytes 131104 | tf_op jit(solution)/shard_map/ppermute | solution.py:865
  77.4 4.9 %all-to-all-start = ((bf16[8,16,1280]{2,1,0:T(8,128)(2,1)}), bf16[8,16,1280]{2,1,0:T(8,128)(2,1)S(1)}, u32[]{:S(2)}, u32[]{:S(2)}) async-start(bf16[8,16,1280]{2,1,0:T(8,128)(2,1)} %bitcast.15), calls=%async_computation | async-start | bytes 655360 | tf_op jit(solution)/shard_map/all_to_all | solution.py:842
  82.2 2.5 %fetch.4 = (f32[128,1024]{1,0:T(8,128)S(1)}, bf16[128,1024]{1,0:T(8,128)(2,1)S(1)}, bf16[128,1024]{1,0:T(8,128)(2,1)S(1)}, bf16[64,1024]{1,0:T(8,128)(2,1)S(1)},...) custom-call(f32[128,1024]{1,0:T(8,128)} %get-tuple-element.200.refs_, ...), custom_call_target="tpu_custom_call" | custom-call | flops 1000000000 | bytes 1048576 | tf_op jit(solution)/shard_map/fetch/pallas_call | solution.py:158
  85.5 7.1 %back_middle.1 = (bf16[128,256]{1,0:T(8,128)(2,1)S(1)}, bf16[128,512]{1,0:T(8,128)(2,1)S(1)}, bf16[512,256]{1,0:T(8,128)(2,1)S(1)}, bf16[512,256]{1,0:T(8,128)(2...) custom-call(s32[2]{0:T(128)S(1)} %pad_add_fusion.refs_0_, ...), custom_call_target="tpu_custom_call" | custom-call | flops 10000000000 | bytes 1048576 | tf_op jit(solution)/shard_map/back_middle/pallas_call | solution.py:128
  92.7 2.3 %collective-permute-start.28 = (bf16[128,512]{1,0:T(8,128)(2,1)S(1)}, bf16[128,512]{1,0:T(8,128)(2,1)S(1)}, u32[]{:S(2)}, u32[]{:S(2)}) collective-permute-start(bf16[128,512]{1,0:T(8,128)(2,1)S(1)} %get-tuple-element.246), channel_id=1, source_target_pairs={{0,3},{1,2},{2,1},{3,0},{4,7},{5,6},{6,5},{7,4},{8,11},{9,10},{10,... | collective-permute-start | bytes 393224 | tf_op jit(solution)/shard_map/ppermute | solution.py:865
  96.2 2.7 %large_pieces.1 = bf16[4,128,384]{2,1,0:T(8,128)(2,1)S(1)} custom-call(s32[2]{0:T(128)S(1)} %pad_add_fusion.refs_0_, bf16[512,256]{1,0:T(8,128)(2,1)S(1)} %get-tuple-element.238.refs_1_, bf16[512,256]{1,0:T(8,128)(2,1)S(1)} %get-tuple-element.239.refs_2_, bf16[128,1024]{1,0:T(8,128)(2,1)S(1)} %get-tuple-element.240.refs_3_, s32[1,1024]{1,0:T(1,128)S(1)} %bitcast.55, ...), custom_call_target="tpu_custom_call" | custom-call | flops 1000000000 | bytes 1048576 | tf_op jit(solution)/shard_map/large_pieces/pallas_call | solution.py:128
  101.4 2.3 %collective-permute-start.29 = (bf16[128,512]{1,0:T(8,128)(2,1)S(1)}, bf16[128,512]{1,0:T(8,128)(2,1)S(1)}, u32[]{:S(2)}, u32[]{:S(2)}) collective-permute-start(bf16[128,512]{1,0:T(8,128)(2,1)S(1)} %add_convert_fusion.refs_0_), channel_id=1, source_target_pairs={{0,4},{1,5},{2,6},{3,7},{4,0},{5,1},{6,2},{7,3},{8,12},{9,13},{10,... | collective-permute-start | bytes 393224 | tf_op jit(solution)/shard_map/ppermute | solution.py:865
  104.8 2.0 %collective-permute-start.34 = (bf16[2,64,256]{2,1,0:T(8,128)(2,1)S(1)}, bf16[2,64,256]{2,1,0:T(8,128)(2,1)S(1)}, u32[]{:S(2)}, u32[]{:S(2)}) collective-permute-start(bf16[2,64,256]{2,1,0:T(8,128)(2,1)S(1)} %get-tuple-element.284), channel_id=1, source_target_pairs={{0,2},{1,3},{2,0},{3,1},{4,6},{5,7},{6,4},{7,5},{8,10},{9,11},{10,... | collective-permute-start | bytes 196616 | tf_op jit(solution)/shard_map/ppermute | solution.py:865
  108.1 2.0 %fetch.5 = (f32[128,1024]{1,0:T(8,128)S(1)}, bf16[128,1024]{1,0:T(8,128)(2,1)S(1)}, bf16[128,1024]{1,0:T(8,128)(2,1)S(1)}, bf16[64,1024]{1,0:T(8,128)(2,1)S(1)},...) custom-call(f32[128,1024]{1,0:T(8,128)} %get-tuple-element.249.refs_, ...), custom_call_target="tpu_custom_call" | custom-call | flops 1000000000 | bytes 1048576 | tf_op jit(solution)/shard_map/fetch/pallas_call | solution.py:158
  110.7 5.4 %back_last.1 = (f32[128,1024]{1,0:T(8,128)S(1)}, bf16[128,640]{1,0:T(8,128)(2,1)}) custom-call(bf16[128,512]{1,0:T(8,128)(2,1)S(1)} %add_convert_fusion.refs_0_, bf16[128,512]{1,0:T(8,128)(2,1)S(1)} %collective-permute-done.29.refs_1_, f32[128,1024]{1,0:T(8,128)S(1)} %get-tuple-element.262.refs_2_, ...), custom_call_target="tpu_custom_call", output_to_operand_aliasing={{1}: (28, {})} | custom-call | flops 10000000000 | bytes 1048576 | tf_op jit(solution)/shard_map/back_last/pallas_call | solution.py:128
  116.1 4.9 %all-to-all-start.1 = ((bf16[8,16,640]{2,1,0:T(8,128)(2,1)}), bf16[8,16,640]{2,1,0:T(8,128)(2,1)S(1)}, u32[]{:S(2)}, u32[]{:S(2)}) async-start(bf16[8,16,640]{2,1,0:T(8,128)(2,1)} %bitcast.84), calls=%async_computation.1 | async-start | bytes 327680 | tf_op jit(solution)/shard_map/all_to_all | solution.py:842
  121.1 3.0 %collective-permute-start.36 = (bf16[64,256]{1,0:T(8,128)(2,1)S(1)}, bf16[64,256]{1,0:T(8,128)(2,1)S(1)}, u32[]{:S(2)}, u32[]{:S(2)}) collective-permute-start(bf16[64,256]{1,0:T(8,128)(2,1)S(1)} %slice_bitcast_fusion.4), channel_id=1, source_target_pairs={{0,4},{1,5},{2,6},{3,7},{4,0},{5,1},{6,2},{7,3},{8,12},{9,13},{10,... | collective-permute-start | bytes 98312 | tf_op jit(solution)/shard_map/ppermute | solution.py:865
  124.1 4.9 %all-to-all-done.1.refs_0_ = bf16[8,16,640]{2,1,0:T(8,128)(2,1)S(1)} async-done(((bf16[8,16,640]{2,1,0:T(8,128)(2,1)}), bf16[8,16,640]{2,1,0:T(8,128)(2,1)S(1)}, u32[]{:S(2)}, u32[]{:S(2)}) %all-to-all-start.1) | async-done | bytes 163872 | tf_op jit(solution)/shard_map/all_to_all | solution.py:842
  134.4 1.7 %adam.1 = (f32[16,3000]{1,0:T(8,128)}, f32[16,3000]{1,0:T(8,128)}, f32[16,3000]{1,0:T(8,128)}, f32[16,3000]{1,0:T(8,128)}, bf16[16,3000]{1,0:T(8,128)(2,1)}) custom-call(s32[2]{0:T(128)S(1)} %pad_add_fusion.refs_0_, f32[16,3000]{1,0:T(8,128)S(1)} %bitcast.41, f32[16,3000]{1,0:T(8,128)S(1)} %bitcast.42, f32[16,3000]{1,0:T(8,128)S(1)} %bitcast.43, ...), custom_call_target="tpu_custom_call" | custom-call | flops 100000000 | bytes 1048576 | tf_op jit(solution)/shard_map/adam/pallas_call | solution.py:128
  (122 shorter events, 33.2 us)
Async XLA Ops:
  1.4 6.6 %collective-permute-start = (bf16[1,16,256]{2,1,0:T(8,128)(2,1)S(1)}, bf16[1,16,256]{2,1,0:T(8,128)(2,1)S(1)}, u32[]{:S(2)}, u32[]{:S(2)}) collective-permute-start(bf16[1,16,256]{2,1,0:T(8,128)(2,1)S(1)} %pack_first.1.refs_10_), channel_id=1, source_target_pairs={{0,4},{1,5},{2,6},{3,7},{4,0},{5,1},{6,2},{7,3},{8,12},{9,13},{10,... | collective-permute-start | bytes 24584 | tf_op jit(solution)/shard_map/ppermute | solution.py:865
  7.2 6.3 %collective-permute-start.4 = (bf16[1,144,256]{2,1,0:T(8,128)(2,1)S(1)}, bf16[1,144,256]{2,1,0:T(8,128)(2,1)S(1)}, u32[]{:S(2)}, u32[]{:S(2)}) collective-permute-start(bf16[1,144,256]{2,1,0:T(8,128)(2,1)S(1)} %pack_cargo.1.refs_1_), channel_id=1, source_target_pairs={{0,4},{1,5},{2,6},{3,7},{4,0},{5,1},{6,2},{7,3},{8,12},{9,13},{10,... | collective-permute-start | bytes 221192 | tf_op jit(solution)/shard_map/ppermute | solution.py:865
  8.0 8.8 %collective-permute-start.3 = (bf16[2,16,256]{2,1,0:T(8,128)(2,1)S(1)}, bf16[2,16,256]{2,1,0:T(8,128)(2,1)S(1)}, u32[]{:S(2)}, u32[]{:S(2)}) collective-permute-start(bf16[2,16,256]{2,1,0:T(8,128)(2,1)S(1)} %constant_dynamic-update-slice_fusion), channel_id=1, source_target_pairs={{0,3},{1,2},{2,1},{3,0},{4,7},{5,6},{6,5},{7,4},{8,11},{9,10},{10,... | collective-permute-start | bytes 49160 | tf_op jit(solution)/shard_map/ppermute | solution.py:865
  10.9 6.2 %collective-permute-start.2 = (bf16[2,16,256]{2,1,0:T(8,128)(2,1)S(1)}, bf16[2,16,256]{2,1,0:T(8,128)(2,1)S(1)}, u32[]{:S(2)}, u32[]{:S(2)}) collective-permute-start(bf16[2,16,256]{2,1,0:T(8,128)(2,1)S(1)} %constant_dynamic-update-slice_fusion), channel_id=1, source_target_pairs={{0,2},{1,3},{2,0},{3,1},{4,6},{5,7},{6,4},{7,5},{8,10},{9,11},{10,... | collective-permute-start | bytes 49160 | tf_op jit(solution)/shard_map/ppermute | solution.py:865
  13.5 9.8 %collective-permute-start.7 = (bf16[2,144,256]{2,1,0:T(8,128)(2,1)S(1)}, bf16[2,144,256]{2,1,0:T(8,128)(2,1)S(1)}, u32[]{:S(2)}, u32[]{:S(2)}) collective-permute-start(bf16[2,144,256]{2,1,0:T(8,128)(2,1)S(1)} %pad_maximum_fusion), channel_id=1, source_target_pairs={{0,3},{1,2},{2,1},{3,0},{4,7},{5,6},{6,5},{7,4},{8,11},{9,10},{10,... | collective-permute-start | bytes 442376 | tf_op jit(solution)/shard_map/ppermute | solution.py:865
  15.2 8.1 %collective-permute-start.6 = (bf16[2,144,256]{2,1,0:T(8,128)(2,1)S(1)}, bf16[2,144,256]{2,1,0:T(8,128)(2,1)S(1)}, u32[]{:S(2)}, u32[]{:S(2)}) collective-permute-start(bf16[2,144,256]{2,1,0:T(8,128)(2,1)S(1)} %pad_maximum_fusion), channel_id=1, source_target_pairs={{0,2},{1,3},{2,0},{3,1},{4,6},{5,7},{6,4},{7,5},{8,10},{9,11},{10,... | collective-permute-start | bytes 442376 | tf_op jit(solution)/shard_map/ppermute | solution.py:865
  16.8 6.5 %collective-permute-start.5 = (bf16[2,144,256]{2,1,0:T(8,128)(2,1)S(1)}, bf16[2,144,256]{2,1,0:T(8,128)(2,1)S(1)}, u32[]{:S(2)}, u32[]{:S(2)}) collective-permute-start(bf16[2,144,256]{2,1,0:T(8,128)(2,1)S(1)} %pad_maximum_fusion), channel_id=1, source_target_pairs={{0,1},{1,0},{2,3},{3,2},{4,5},{5,4},{6,7},{7,6},{8,9},{9,8},{10,11... | collective-permute-start | bytes 442376 | tf_op jit(solution)/shard_map/ppermute | solution.py:865
  23.3 6.0 %collective-permute-start.10 = (bf16[512,128]{1,0:T(8,128)(2,1)S(1)}, bf16[512,128]{1,0:T(8,128)(2,1)S(1)}, u32[]{:S(2)}, u32[]{:S(2)}) collective-permute-start(bf16[512,128]{1,0:T(8,128)(2,1)S(1)} %get-tuple-element.154), channel_id=1, source_target_pairs={{0,3},{1,2},{2,1},{3,0},{4,7},{5,6},{6,5},{7,4},{8,11},{9,10},{10,... | collective-permute-start | bytes 393224 | tf_op jit(solution)/shard_map/ppermute | solution.py:865
  25.0 6.0 %collective-permute-start.9 = (bf16[512,128]{1,0:T(8,128)(2,1)S(1)}, bf16[512,128]{1,0:T(8,128)(2,1)S(1)}, u32[]{:S(2)}, u32[]{:S(2)}) collective-permute-start(bf16[512,128]{1,0:T(8,128)(2,1)S(1)} %get-tuple-element.154), channel_id=1, source_target_pairs={{0,2},{1,3},{2,0},{3,1},{4,6},{5,7},{6,4},{7,5},{8,10},{9,11},{10,... | collective-permute-start | bytes 393224 | tf_op jit(solution)/shard_map/ppermute | solution.py:865
  27.7 7.2 %collective-permute-start.13 = (bf16[128,384]{1,0:T(8,128)(2,1)S(1)}, bf16[128,384]{1,0:T(8,128)(2,1)S(1)}, u32[]{:S(2)}, u32[]{:S(2)}) collective-permute-start(bf16[128,384]{1,0:T(8,128)(2,1)S(1)} %get-tuple-element.161.refs_2_), channel_id=1, source_target_pairs={{0,16},{8,24},{16,0},{24,8},{1,17},{9,25},{17,1},{25,9},{2,18},{10... | collective-permute-start | bytes 294920 | tf_op jit(solution)/shard_map/ppermute | solution.py:865
  31.7 7.4 %collective-permute-start.11 = (bf16[512,128]{1,0:T(8,128)(2,1)S(1)}, bf16[512,128]{1,0:T(8,128)(2,1)S(1)}, u32[]{:S(2)}, u32[]{:S(2)}) collective-permute-start(bf16[512,128]{1,0:T(8,128)(2,1)S(1)} %add_convert_fusion.3.refs_0_), channel_id=1, source_target_pairs={{0,4},{1,5},{2,6},{3,7},{4,0},{5,1},{6,2},{7,3},{8,12},{9,13},{10,... | collective-permute-start | bytes 393224 | tf_op jit(solution)/shard_map/ppermute | solution.py:865
  46.7 6.7 %collective-permute-start.17 = (bf16[512,128]{1,0:T(8,128)(2,1)S(1)}, bf16[512,128]{1,0:T(8,128)(2,1)S(1)}, u32[]{:S(2)}, u32[]{:S(2)}) collective-permute-start(bf16[512,128]{1,0:T(8,128)(2,1)S(1)} %get-tuple-element.175), channel_id=1, source_target_pairs={{0,3},{1,2},{2,1},{3,0},{4,7},{5,6},{6,5},{7,4},{8,11},{9,10},{10,... | collective-permute-start | bytes 393224 | tf_op jit(solution)/shard_map/ppermute | solution.py:865
  47.1 8.6 %collective-permute-start.16 = (bf16[512,128]{1,0:T(8,128)(2,1)S(1)}, bf16[512,128]{1,0:T(8,128)(2,1)S(1)}, u32[]{:S(2)}, u32[]{:S(2)}) collective-permute-start(bf16[512,128]{1,0:T(8,128)(2,1)S(1)} %get-tuple-element.175), channel_id=1, source_target_pairs={{0,2},{1,3},{2,0},{3,1},{4,6},{5,7},{6,4},{7,5},{8,10},{9,11},{10,... | collective-permute-start | bytes 393224 | tf_op jit(solution)/shard_map/ppermute | solution.py:865
  50.2 6.7 %collective-permute-start.21 = (bf16[128,384]{1,0:T(8,128)(2,1)S(1)}, bf16[128,384]{1,0:T(8,128)(2,1)S(1)}, u32[]{:S(2)}, u32[]{:S(2)}) collective-permute-start(bf16[128,384]{1,0:T(8,128)(2,1)S(1)} %get-tuple-element.179.refs_1_), channel_id=1, source_target_pairs={{0,24},{8,16},{16,8},{24,0},{1,25},{9,17},{17,9},{25,1},{2,26},{10... | collective-permute-start | bytes 294920 | tf_op jit(solution)/shard_map/ppermute | solution.py:865
  50.3 7.2 %collective-permute-start.20 = (bf16[128,384]{1,0:T(8,128)(2,1)S(1)}, bf16[128,384]{1,0:T(8,128)(2,1)S(1)}, u32[]{:S(2)}, u32[]{:S(2)}) collective-permute-start(bf16[128,384]{1,0:T(8,128)(2,1)S(1)} %get-tuple-element.179.refs_1_), channel_id=1, source_target_pairs={{0,16},{8,24},{16,0},{24,8},{1,17},{9,25},{17,1},{25,9},{2,18},{10... | collective-permute-start | bytes 294920 | tf_op jit(solution)/shard_map/ppermute | solution.py:865
  55.8 8.3 %collective-permute-start.18 = (bf16[512,128]{1,0:T(8,128)(2,1)S(1)}, bf16[512,128]{1,0:T(8,128)(2,1)S(1)}, u32[]{:S(2)}, u32[]{:S(2)}) collective-permute-start(bf16[512,128]{1,0:T(8,128)(2,1)S(1)} %add_convert_fusion.2.refs_1_), channel_id=1, source_target_pairs={{0,4},{1,5},{2,6},{3,7},{4,0},{5,1},{6,2},{7,3},{8,12},{9,13},{10,... | collective-permute-start | bytes 393224 | tf_op jit(solution)/shard_map/ppermute | solution.py:865
  67.5 7.3 %collective-permute-start.24 = (bf16[128,512]{1,0:T(8,128)(2,1)S(1)}, bf16[128,512]{1,0:T(8,128)(2,1)S(1)}, u32[]{:S(2)}, u32[]{:S(2)}) collective-permute-start(bf16[128,512]{1,0:T(8,128)(2,1)S(1)} %get-tuple-element.199), channel_id=1, source_target_pairs={{0,3},{1,2},{2,1},{3,0},{4,7},{5,6},{6,5},{7,4},{8,11},{9,10},{10,... | collective-permute-start | bytes 393224 | tf_op jit(solution)/shard_map/ppermute | solution.py:865
  67.6 9.4 %collective-permute-start.23 = (bf16[128,512]{1,0:T(8,128)(2,1)S(1)}, bf16[128,512]{1,0:T(8,128)(2,1)S(1)}, u32[]{:S(2)}, u32[]{:S(2)}) collective-permute-start(bf16[128,512]{1,0:T(8,128)(2,1)S(1)} %get-tuple-element.199), channel_id=1, source_target_pairs={{0,2},{1,3},{2,0},{3,1},{4,6},{5,7},{6,4},{7,5},{8,10},{9,11},{10,... | collective-permute-start | bytes 393224 | tf_op jit(solution)/shard_map/ppermute | solution.py:865
  70.8 6.2 %collective-permute-start.22 = (bf16[128,512]{1,0:T(8,128)(2,1)S(1)}, bf16[128,512]{1,0:T(8,128)(2,1)S(1)}, u32[]{:S(2)}, u32[]{:S(2)}) collective-permute-start(bf16[128,512]{1,0:T(8,128)(2,1)S(1)} %get-tuple-element.199), channel_id=1, source_target_pairs={{0,1},{1,0},{2,3},{3,2},{4,5},{5,4},{6,7},{7,6},{8,9},{9,8},{10,11... | collective-permute-start | bytes 393224 | tf_op jit(solution)/shard_map/ppermute | solution.py:865
  77.1 8.4 %collective-permute-start.25 = (bf16[128,512]{1,0:T(8,128)(2,1)S(1)}, bf16[128,512]{1,0:T(8,128)(2,1)S(1)}, u32[]{:S(2)}, u32[]{:S(2)}) collective-permute-start(bf16[128,512]{1,0:T(8,128)(2,1)S(1)} %add_convert_fusion.1.refs_1_), channel_id=1, source_target_pairs={{0,4},{1,5},{2,6},{3,7},{4,0},{5,1},{6,2},{7,3},{8,12},{9,13},{10,... | collective-permute-start | bytes 393224 | tf_op jit(solution)/shard_map/ppermute | solution.py:865
  77.4 21.5 %all-to-all-start = ((bf16[8,16,1280]{2,1,0:T(8,128)(2,1)}), bf16[8,16,1280]{2,1,0:T(8,128)(2,1)S(1)}, u32[]{:S(2)}, u32[]{:S(2)}) async-start(bf16[8,16,1280]{2,1,0:T(8,128)(2,1)} %bitcast.15), calls=%async_computation | async-start | bytes 655360 | tf_op jit(solution)/shard_map/all_to_all | solution.py:842
  92.7 7.7 %collective-permute-start.28 = (bf16[128,512]{1,0:T(8,128)(2,1)S(1)}, bf16[128,512]{1,0:T(8,128)(2,1)S(1)}, u32[]{:S(2)}, u32[]{:S(2)}) collective-permute-start(bf16[128,512]{1,0:T(8,128)(2,1)S(1)} %get-tuple-element.246), channel_id=1, source_target_pairs={{0,3},{1,2},{2,1},{3,0},{4,7},{5,6},{6,5},{7,4},{8,11},{9,10},{10,... | collective-permute-start | bytes 393224 | tf_op jit(solution)/shard_map/ppermute | solution.py:865
  94.9 6.0 %collective-permute-start.27 = (bf16[128,512]{1,0:T(8,128)(2,1)S(1)}, bf16[128,512]{1,0:T(8,128)(2,1)S(1)}, u32[]{:S(2)}, u32[]{:S(2)}) collective-permute-start(bf16[128,512]{1,0:T(8,128)(2,1)S(1)} %get-tuple-element.246), channel_id=1, source_target_pairs={{0,2},{1,3},{2,0},{3,1},{4,6},{5,7},{6,4},{7,5},{8,10},{9,11},{10,... | collective-permute-start | bytes 393224 | tf_op jit(solution)/shard_map/ppermute | solution.py:865
  98.9 5.9 %collective-permute-start.32 = (bf16[128,384]{1,0:T(8,128)(2,1)S(1)}, bf16[128,384]{1,0:T(8,128)(2,1)S(1)}, u32[]{:S(2)}, u32[]{:S(2)}) collective-permute-start(bf16[128,384]{1,0:T(8,128)(2,1)S(1)} %get-tuple-element.293), channel_id=1, source_target_pairs={{0,24},{8,16},{16,8},{24,0},{1,25},{9,17},{17,9},{25,1},{2,26},{10... | collective-permute-start | bytes 294920 | tf_op jit(solution)/shard_map/ppermute | solution.py:865
  99.0 7.8 %collective-permute-start.31 = (bf16[128,384]{1,0:T(8,128)(2,1)S(1)}, bf16[128,384]{1,0:T(8,128)(2,1)S(1)}, u32[]{:S(2)}, u32[]{:S(2)}) collective-permute-start(bf16[128,384]{1,0:T(8,128)(2,1)S(1)} %get-tuple-element.294), channel_id=1, source_target_pairs={{0,16},{8,24},{16,0},{24,8},{1,17},{9,25},{17,1},{25,9},{2,18},{10... | collective-permute-start | bytes 294920 | tf_op jit(solution)/shard_map/ppermute | solution.py:865
  100.4 7.0 %collective-permute-start.30 = (bf16[128,384]{1,0:T(8,128)(2,1)S(1)}, bf16[128,384]{1,0:T(8,128)(2,1)S(1)}, u32[]{:S(2)}, u32[]{:S(2)}) collective-permute-start(bf16[128,384]{1,0:T(8,128)(2,1)S(1)} %get-tuple-element.295), channel_id=1, source_target_pairs={{0,8},{8,0},{16,24},{24,16},{1,9},{9,1},{17,25},{25,17},{2,10},{10... | collective-permute-start | bytes 294920 | tf_op jit(solution)/shard_map/ppermute | solution.py:865
  101.4 9.3 %collective-permute-start.29 = (bf16[128,512]{1,0:T(8,128)(2,1)S(1)}, bf16[128,512]{1,0:T(8,128)(2,1)S(1)}, u32[]{:S(2)}, u32[]{:S(2)}) collective-permute-start(bf16[128,512]{1,0:T(8,128)(2,1)S(1)} %add_convert_fusion.refs_0_), channel_id=1, source_target_pairs={{0,4},{1,5},{2,6},{3,7},{4,0},{5,1},{6,2},{7,3},{8,12},{9,13},{10,... | collective-permute-start | bytes 393224 | tf_op jit(solution)/shard_map/ppermute | solution.py:865
  103.6 17.4 %collective-permute-start.33 = (bf16[2,64,256]{2,1,0:T(8,128)(2,1)S(1)}, bf16[2,64,256]{2,1,0:T(8,128)(2,1)S(1)}, u32[]{:S(2)}, u32[]{:S(2)}) collective-permute-start(bf16[2,64,256]{2,1,0:T(8,128)(2,1)S(1)} %get-tuple-element.283), channel_id=1, source_target_pairs={{0,1},{1,0},{2,3},{3,2},{4,5},{5,4},{6,7},{7,6},{8,9},{9,8},{10,11... | collective-permute-start | bytes 196616 | tf_op jit(solution)/shard_map/ppermute | solution.py:865
  104.8 16.2 %collective-permute-start.34 = (bf16[2,64,256]{2,1,0:T(8,128)(2,1)S(1)}, bf16[2,64,256]{2,1,0:T(8,128)(2,1)S(1)}, u32[]{:S(2)}, u32[]{:S(2)}) collective-permute-start(bf16[2,64,256]{2,1,0:T(8,128)(2,1)S(1)} %get-tuple-element.284), channel_id=1, source_target_pairs={{0,2},{1,3},{2,0},{3,1},{4,6},{5,7},{6,4},{7,5},{8,10},{9,11},{10,... | collective-permute-start | bytes 196616 | tf_op jit(solution)/shard_map/ppermute | solution.py:865
  106.8 14.2 %collective-permute-start.35 = (bf16[2,64,256]{2,1,0:T(8,128)(2,1)S(1)}, bf16[2,64,256]{2,1,0:T(8,128)(2,1)S(1)}, u32[]{:S(2)}, u32[]{:S(2)}) collective-permute-start(bf16[2,64,256]{2,1,0:T(8,128)(2,1)S(1)} %get-tuple-element.285), channel_id=1, source_target_pairs={{0,3},{1,2},{2,1},{3,0},{4,7},{5,6},{6,5},{7,4},{8,11},{9,10},{10,... | collective-permute-start | bytes 196616 | tf_op jit(solution)/shard_map/ppermute | solution.py:865
  116.1 12.9 %all-to-all-start.1 = ((bf16[8,16,640]{2,1,0:T(8,128)(2,1)}), bf16[8,16,640]{2,1,0:T(8,128)(2,1)S(1)}, u32[]{:S(2)}, u32[]{:S(2)}) async-start(bf16[8,16,640]{2,1,0:T(8,128)(2,1)} %bitcast.84), calls=%async_computation.1 | async-start | bytes 327680 | tf_op jit(solution)/shard_map/all_to_all | solution.py:842
  121.1 9.9 %collective-permute-start.36 = (bf16[64,256]{1,0:T(8,128)(2,1)S(1)}, bf16[64,256]{1,0:T(8,128)(2,1)S(1)}, u32[]{:S(2)}, u32[]{:S(2)}) collective-permute-start(bf16[64,256]{1,0:T(8,128)(2,1)S(1)} %slice_bitcast_fusion.4), channel_id=1, source_target_pairs={{0,4},{1,5},{2,6},{3,7},{4,0},{5,1},{6,2},{7,3},{8,12},{9,13},{10,... | collective-permute-start | bytes 98312 | tf_op jit(solution)/shard_map/ppermute | solution.py:865
  (27 other events, 156.7 us)

commit v6 on v5

--- a/solution.py
+++ b/solution.py
@@ -809,32 +809,34 @@
     send(out_ref)
 
 
-def sum_parts(one, two, out_ref):
-    width = one.shape[2]
-    out_ref[:, :width] = low(total_of(one))
-    out_ref[:, width:] = low(total_of(two))
+def sum_parts(arrived, out_ref):
+    out_ref[...] = low(total_of(arrived))
 
 
 def adam(me, weights, first, second, *refs):
     *pieces, grad_ref, weights_ref, first_ref, second_ref, low_ref, hold = refs
     groups, _, lanes = hold.shape
-    total = sum_list(pieces)
-    for k, piece in enumerate(pieces):
-        hold[me[1] ^ k] = piece[:, PAD : PAD + lanes].astype(F32)
+    last, others = pieces[:groups], pieces[groups:]
+    small = sum_list([piece[:, :PAD] for piece in last])
+    for k, piece in enumerate(last):
+        hold[me[1] ^ k] = piece[:, PAD:].astype(F32)
     joint = jnp.concatenate([hold[g] for g in range(groups)], axis=1)
     grad = jnp.concatenate(
-        [total[:, :SMALL], joint[:, PAD:], joint[:, :SMALL], total[:, PAD + lanes :]], axis=1
+        [small[:, :SMALL], joint[:, PAD:], joint[:, :SMALL], sum_list(others)], axis=1
     )
     grad_ref[...] = grad
+    send(grad_ref)
     old = weights[...]
     new_first = beta_one * first[...] + (1.0 - beta_one) * grad
     new_second = beta_two * second[...] + (1.0 - beta_two) * grad * grad
     first_ref[...] = new_first
     second_ref[...] = new_second
+    send(first_ref, second_ref)
     first_hat = new_first / (1.0 - beta_one**adam_step)
     second_hat = new_second / (1.0 - beta_two**adam_step)
     new = old - learn_rate * (first_hat / (jnp.sqrt(second_hat) + epsilon) + decay_rate * old)
     weights_ref[...] = new
+    send(weights_ref)
     low_ref[...] = low(new)
 
 
@@ -1064,17 +1066,21 @@
         scratch=[pltpu.VMEM((D_EDGE, PAD), BF16), pltpu.SemaphoreType.DMA],
     )
     grad_edge = rows_first(grad_edge_t, F32)
+    grads_one, arrived_two = lax.optimization_barrier((grads_one, arrived_two))
     arrived_one = exchange(grads_one.reshape(owners, cols, PAD + lanes))
-    [owned] = call(
-        sum_parts, [sds((cols, PAD + lanes + BIG), BF16)], [arrived_one, arrived_two], flops=10**7
-    )
-    owned = [owned] + [moved(owned, k, groups, "group") for k in range(1, groups)]
+
+    def owned(arrived):
+        [total] = call(sum_parts, [sds(arrived.shape[1:], BF16)], [arrived], flops=10**7)
+        return everywhere(total)
+
+    pieces = owned(arrived_one) + owned(arrived_two)
     rows = weights.shape[0]
     results = call(
         adam,
         [sds((cols, rows), F32)] * 4 + [sds((cols, rows), BF16)],
-        [me, weights_t, jnp.transpose(first_moment), jnp.transpose(second_moment)] + owned,
+        [me, weights_t, jnp.transpose(first_moment), jnp.transpose(second_moment)] + pieces,
         flops=10**8,
+        kept=range(5),
         smem=1,
         scratch=[(groups, cols, lanes)],
     )

time: 137 us -> 136 us (level)
  waiting for transfers between devices: 29.4 us -> 26.8 us
  starting transfers between devices: 53.7 us -> 55.4 us
    ppermute x40 -> x43, starting transfers between devices: 43.9 us -> 45.7 us  [moved(): return lax.ppermute(table, axis, [(i, i ^ step) for i in range(owners)])]
    all_to_all x2, waiting for transfers between devices: 4.93 us -> 3.49 us  [exchange(): return lax.all_to_all(pieces, 'shard', split_axis=0, concat_axis=0)]
    ppermute x40 -> x43, waiting for transfers between devices: 24.5 us -> 23.3 us  [moved(): return lax.ppermute(table, axis, [(i, i ^ step) for i in range(owners)])]
    pallas_call x17 -> x18, Pallas kernels: 44.1 us -> 44.3 us  [call(): pl.pallas_call(kernel, out_shape=outs, in_specs=[pl.BlockSpec(memory_spac...]
  transfers between devices with their start and end apart: 42 -> 45, of which waited for: 19 -> 19; matrix products, arithmetic and copies ran while one was open for 1% -> 1% of each run, Pallas kernels for 27% -> 27%
where the time goes in v6:
time: 136 us; the launch traced here: 135 us
  starting transfers between devices  55.4 us (41%)
  Pallas kernels  50.2 us (37%)
  waiting for transfers between devices  26.8 us (20%)
    ppermute x43, starting transfers between devices, moved(): return lax.ppermute(table, axis, [(i, i ^ step) for i in range(owners)])  45.7 us
    pallas_call x18, Pallas kernels, call(): pl.pallas_call(kernel, out_shape=outs, in_specs=[pl.BlockSpec(memory_spac...  44.3 us
    ppermute x43, waiting for transfers between devices, moved(): return lax.ppermute(table, axis, [(i, i ^ step) for i in range(owners)])  23.3 us
    all_to_all x2, starting transfers between devices, exchange(): return lax.all_to_all(pieces, 'shard', split_axis=0, concat_axis=0)  9.63 us
    pallas_call x3, Pallas kernels, fetch(): pl.pallas_call(kernel, out_shape=[sds(x.shape, x.dtype) for x in arrays],...  5.89 us
    all_to_all x2, waiting for transfers between devices, exchange(): return lax.all_to_all(pieces, 'shard', split_axis=0, concat_axis=0)  3.49 us
  transfers between devices with their start and end apart: 45, of which 19 were waited for; matrix products, arithmetic and copies ran while one was open for 1% of the time, Pallas kernels for 27%

profile of v6, /device:TPU:0, one launch (start us, length us, event | category | flops | bytes accessed | tf_op | source)
XLA Modules:
  0.0 135.4 jit_solution(7524972906432791775)
XLA Ops:
  1.4 4.1 %collective-permute-start = (bf16[1,16,256]{2,1,0:T(8,128)(2,1)S(1)}, bf16[1,16,256]{2,1,0:T(8,128)(2,1)S(1)}, u32[]{:S(2)}, u32[]{:S(2)}) collective-permute-start(bf16[1,16,256]{2,1,0:T(8,128)(2,1)S(1)} %pack_first.1.refs_10_), channel_id=1, source_target_pairs={{0,4},{1,5},{2,6},{3,7},{4,0},{5,1},{6,2},{7,3},{8,12},{9,13},{10,... | collective-permute-start | bytes 24584 | tf_op jit(solution)/shard_map/ppermute | solution.py:867
  8.0 2.9 %collective-permute-start.3 = (bf16[2,16,256]{2,1,0:T(8,128)(2,1)S(1)}, bf16[2,16,256]{2,1,0:T(8,128)(2,1)S(1)}, u32[]{:S(2)}, u32[]{:S(2)}) collective-permute-start(bf16[2,16,256]{2,1,0:T(8,128)(2,1)S(1)} %constant_dynamic-update-slice_fusion), channel_id=1, source_target_pairs={{0,3},{1,2},{2,1},{3,0},{4,7},{5,6},{6,5},{7,4},{8,11},{9,10},{10,... | collective-permute-start | bytes 49160 | tf_op jit(solution)/shard_map/ppermute | solution.py:867
  11.6 1.9 %collective-permute-done.4.refs_2_ = bf16[1,144,256]{2,1,0:T(8,128)(2,1)S(1)} collective-permute-done((bf16[1,144,256]{2,1,0:T(8,128)(2,1)S(1)}, bf16[1,144,256]{2,1,0:T(8,128)(2,1)S(1)}, u32[]{:S(2)}, u32[]{:S(2)}) %collective-permute-start.4) | collective-permute-done | bytes 73760 | tf_op jit(solution)/shard_map/ppermute | solution.py:867
  13.5 1.7 %collective-permute-start.7 = (bf16[2,144,256]{2,1,0:T(8,128)(2,1)S(1)}, bf16[2,144,256]{2,1,0:T(8,128)(2,1)S(1)}, u32[]{:S(2)}, u32[]{:S(2)}) collective-permute-start(bf16[2,144,256]{2,1,0:T(8,128)(2,1)S(1)} %pad_maximum_fusion), channel_id=1, source_target_pairs={{0,3},{1,2},{2,1},{3,0},{4,7},{5,6},{6,5},{7,4},{8,11},{9,10},{10,... | collective-permute-start | bytes 442376 | tf_op jit(solution)/shard_map/ppermute | solution.py:867
  15.2 1.6 %collective-permute-start.6 = (bf16[2,144,256]{2,1,0:T(8,128)(2,1)S(1)}, bf16[2,144,256]{2,1,0:T(8,128)(2,1)S(1)}, u32[]{:S(2)}, u32[]{:S(2)}) collective-permute-start(bf16[2,144,256]{2,1,0:T(8,128)(2,1)S(1)} %pad_maximum_fusion), channel_id=1, source_target_pairs={{0,2},{1,3},{2,0},{3,1},{4,6},{5,7},{6,4},{7,5},{8,10},{9,11},{10,... | collective-permute-start | bytes 442376 | tf_op jit(solution)/shard_map/ppermute | solution.py:867
  17.1 6.1 %first_half.1 = (bf16[128,256]{1,0:T(8,128)(2,1)S(1)}, f32[128,1024]{1,0:T(8,128)}, bf16[128,1024]{1,0:T(8,128)(2,1)}, bf16[128,1024]{1,0:T(8,128)(2,1)}, bf16[6...) custom-call(s32[2]{0:T(128)S(1)} %pad_add_fusion.refs_0_, ...), custom_call_target="tpu_custom_call" | custom-call | flops 8000000000 | bytes 1048576 | tf_op jit(solution)/shard_map/first_half/pallas_call | solution.py:128
  23.3 1.7 %collective-permute-start.10 = (bf16[512,128]{1,0:T(8,128)(2,1)S(1)}, bf16[512,128]{1,0:T(8,128)(2,1)S(1)}, u32[]{:S(2)}, u32[]{:S(2)}) collective-permute-start(bf16[512,128]{1,0:T(8,128)(2,1)S(1)} %get-tuple-element.156), channel_id=1, source_target_pairs={{0,3},{1,2},{2,1},{3,0},{4,7},{5,6},{6,5},{7,4},{8,11},{9,10},{10,... | collective-permute-start | bytes 393224 | tf_op jit(solution)/shard_map/ppermute | solution.py:867
  25.0 1.6 %collective-permute-start.9 = (bf16[512,128]{1,0:T(8,128)(2,1)S(1)}, bf16[512,128]{1,0:T(8,128)(2,1)S(1)}, u32[]{:S(2)}, u32[]{:S(2)}) collective-permute-start(bf16[512,128]{1,0:T(8,128)(2,1)S(1)} %get-tuple-element.156), channel_id=1, source_target_pairs={{0,2},{1,3},{2,0},{3,1},{4,6},{5,7},{6,4},{7,5},{8,10},{9,11},{10,... | collective-permute-start | bytes 393224 | tf_op jit(solution)/shard_map/ppermute | solution.py:867
  32.7 2.2 %collective-permute-done.13.refs_4_ = bf16[128,384]{1,0:T(8,128)(2,1)S(1)} collective-permute-done((bf16[128,384]{1,0:T(8,128)(2,1)S(1)}, bf16[128,384]{1,0:T(8,128)(2,1)S(1)}, u32[]{:S(2)}, u32[]{:S(2)}) %collective-permute-start.13) | collective-permute-done | bytes 98336 | tf_op jit(solution)/shard_map/ppermute | solution.py:867
  36.3 2.8 %collective-permute-done.11.refs_1_ = bf16[512,128]{1,0:T(8,128)(2,1)S(1)} collective-permute-done((bf16[512,128]{1,0:T(8,128)(2,1)S(1)}, bf16[512,128]{1,0:T(8,128)(2,1)S(1)}, u32[]{:S(2)}, u32[]{:S(2)}) %collective-permute-start.11) | collective-permute-done | bytes 131104 | tf_op jit(solution)/shard_map/ppermute | solution.py:867
  39.1 7.6 %middle_half.1 = (bf16[512,128]{1,0:T(8,128)(2,1)}, bf16[512,256]{1,0:T(8,128)(2,1)}, bf16[512,256]{1,0:T(8,128)(2,1)}, f32[512,256]{1,0:T(8,128)}, bf16[512,256...) custom-call(bf16[512,128]{1,0:T(8,128)(2,1)S(1)} %add_convert_fusion, ...), custom_call_target="tpu_custom_call" | custom-call | flops 10000000000 | bytes 1048576 | tf_op jit(solution)/shard_map/middle_half/pallas_call | solution.py:128
  47.1 2.8 %collective-permute-start.16 = (bf16[512,128]{1,0:T(8,128)(2,1)S(1)}, bf16[512,128]{1,0:T(8,128)(2,1)S(1)}, u32[]{:S(2)}, u32[]{:S(2)}) collective-permute-start(bf16[512,128]{1,0:T(8,128)(2,1)S(1)} %get-tuple-element.177), channel_id=1, source_target_pairs={{0,2},{1,3},{2,0},{3,1},{4,6},{5,7},{6,4},{7,5},{8,10},{9,11},{10,... | collective-permute-start | bytes 393224 | tf_op jit(solution)/shard_map/ppermute | solution.py:867
  51.8 1.6 %collective-permute-done.17 = bf16[512,128]{1,0:T(8,128)(2,1)S(1)} collective-permute-done((bf16[512,128]{1,0:T(8,128)(2,1)S(1)}, bf16[512,128]{1,0:T(8,128)(2,1)S(1)}, u32[]{:S(2)}, u32[]{:S(2)}) %collective-permute-start.17) | collective-permute-done | bytes 131104 | tf_op jit(solution)/shard_map/ppermute | solution.py:867
  53.4 2.3 %collective-permute-done.16 = bf16[512,128]{1,0:T(8,128)(2,1)S(1)} collective-permute-done((bf16[512,128]{1,0:T(8,128)(2,1)S(1)}, bf16[512,128]{1,0:T(8,128)(2,1)S(1)}, u32[]{:S(2)}, u32[]{:S(2)}) %collective-permute-start.16) | collective-permute-done | bytes 131104 | tf_op jit(solution)/shard_map/ppermute | solution.py:867
  59.8 4.3 %collective-permute-done.18.refs_2_ = bf16[512,128]{1,0:T(8,128)(2,1)S(1)} collective-permute-done((bf16[512,128]{1,0:T(8,128)(2,1)S(1)}, bf16[512,128]{1,0:T(8,128)(2,1)S(1)}, u32[]{:S(2)}, u32[]{:S(2)}) %collective-permute-start.18) | collective-permute-done | bytes 131104 | tf_op jit(solution)/shard_map/ppermute | solution.py:867
  64.1 3.5 %turn.1 = (bf16[512,128]{1,0:T(8,128)(2,1)S(1)}, bf16[512,256]{1,0:T(8,128)(2,1)S(1)}, bf16[512,256]{1,0:T(8,128)(2,1)S(1)}, f32[128,1024]{1,0:T(8,128)S(1)}, bf...) custom-call(s32[2]{0:T(128)S(1)} %pad_add_fusion.refs_0_, ...), custom_call_target="tpu_custom_call" | custom-call | flops 2000000000 | bytes 1048576 | tf_op jit(solution)/shard_map/turn/pallas_call | solution.py:128
  67.7 3.1 %collective-permute-start.23 = (bf16[128,512]{1,0:T(8,128)(2,1)S(1)}, bf16[128,512]{1,0:T(8,128)(2,1)S(1)}, u32[]{:S(2)}, u32[]{:S(2)}) collective-permute-start(bf16[128,512]{1,0:T(8,128)(2,1)S(1)} %get-tuple-element.201), channel_id=1, source_target_pairs={{0,2},{1,3},{2,0},{3,1},{4,6},{5,7},{6,4},{7,5},{8,10},{9,11},{10,... | collective-permute-start | bytes 393224 | tf_op jit(solution)/shard_map/ppermute | solution.py:867
  72.0 2.1 %large_grads.1 = bf16[128,1280]{1,0:T(8,128)(2,1)} custom-call(bf16[512,256]{1,0:T(8,128)(2,1)S(1)} %get-tuple-element.192.refs_0_, bf16[512,256]{1,0:T(8,128)(2,1)S(1)} %get-tuple-element.193.refs_1_, bf16[128,1024]{1,0:T(8,128)(2,1)S(1)} %get-tuple-element.194.refs_2_, s32[1,1024]{1,0:T(1,128)S(1)} %bitcast.53, s32[1,1024]{1,0:T(1,128)S(1)} %bitcast.47, ...), custom_call_target="tpu_custom_call" | custom-call | flops 1000000000 | bytes 1048576 | tf_op jit(solution)/shard_map/large_grads/pallas_call | solution.py:128
  74.9 2.0 %collective-permute-done.23 = bf16[128,512]{1,0:T(8,128)(2,1)S(1)} collective-permute-done((bf16[128,512]{1,0:T(8,128)(2,1)S(1)}, bf16[128,512]{1,0:T(8,128)(2,1)S(1)}, u32[]{:S(2)}, u32[]{:S(2)}) %collective-permute-start.23) | collective-permute-done | bytes 131104 | tf_op jit(solution)/shard_map/ppermute | solution.py:867
  77.4 4.7 %all-to-all-start = ((bf16[8,16,1280]{2,1,0:T(8,128)(2,1)}), bf16[8,16,1280]{2,1,0:T(8,128)(2,1)S(1)}, u32[]{:S(2)}, u32[]{:S(2)}) async-start(bf16[8,16,1280]{2,1,0:T(8,128)(2,1)} %bitcast.15), calls=%async_computation | async-start | bytes 655360 | tf_op jit(solution)/shard_map/all_to_all | solution.py:844
  82.2 2.5 %fetch.4 = (f32[128,1024]{1,0:T(8,128)S(1)}, bf16[128,1024]{1,0:T(8,128)(2,1)S(1)}, bf16[128,1024]{1,0:T(8,128)(2,1)S(1)}, bf16[64,1024]{1,0:T(8,128)(2,1)S(1)},...) custom-call(f32[128,1024]{1,0:T(8,128)} %get-tuple-element.202.refs_, ...), custom_call_target="tpu_custom_call" | custom-call | flops 1000000000 | bytes 1048576 | tf_op jit(solution)/shard_map/fetch/pallas_call | solution.py:158
  85.5 7.2 %back_middle.1 = (bf16[128,256]{1,0:T(8,128)(2,1)S(1)}, bf16[128,512]{1,0:T(8,128)(2,1)S(1)}, bf16[512,256]{1,0:T(8,128)(2,1)S(1)}, bf16[512,256]{1,0:T(8,128)(2...) custom-call(s32[2]{0:T(128)S(1)} %pad_add_fusion.refs_0_, ...), custom_call_target="tpu_custom_call" | custom-call | flops 10000000000 | bytes 1048576 | tf_op jit(solution)/shard_map/back_middle/pallas_call | solution.py:128
  92.7 2.2 %collective-permute-start.28 = (bf16[128,512]{1,0:T(8,128)(2,1)S(1)}, bf16[128,512]{1,0:T(8,128)(2,1)S(1)}, u32[]{:S(2)}, u32[]{:S(2)}) collective-permute-start(bf16[128,512]{1,0:T(8,128)(2,1)S(1)} %get-tuple-element.248), channel_id=1, source_target_pairs={{0,3},{1,2},{2,1},{3,0},{4,7},{5,6},{6,5},{7,4},{8,11},{9,10},{10,... | collective-permute-start | bytes 393224 | tf_op jit(solution)/shard_map/ppermute | solution.py:867
  96.2 2.7 %large_pieces.1 = bf16[4,128,384]{2,1,0:T(8,128)(2,1)S(1)} custom-call(s32[2]{0:T(128)S(1)} %pad_add_fusion.refs_0_, bf16[512,256]{1,0:T(8,128)(2,1)S(1)} %get-tuple-element.240.refs_1_, bf16[512,256]{1,0:T(8,128)(2,1)S(1)} %get-tuple-element.241.refs_2_, bf16[128,1024]{1,0:T(8,128)(2,1)S(1)} %get-tuple-element.242.refs_3_, s32[1,1024]{1,0:T(1,128)S(1)} %bitcast.55, ...), custom_call_target="tpu_custom_call" | custom-call | flops 1000000000 | bytes 1048576 | tf_op jit(solution)/shard_map/large_pieces/pallas_call | solution.py:128
  101.4 2.8 %collective-permute-start.29 = (bf16[128,512]{1,0:T(8,128)(2,1)S(1)}, bf16[128,512]{1,0:T(8,128)(2,1)S(1)}, u32[]{:S(2)}, u32[]{:S(2)}) collective-permute-start(bf16[128,512]{1,0:T(8,128)(2,1)S(1)} %add_convert_fusion.refs_0_), channel_id=1, source_target_pairs={{0,4},{1,5},{2,6},{3,7},{4,0},{5,1},{6,2},{7,3},{8,12},{9,13},{10,... | collective-permute-start | bytes 393224 | tf_op jit(solution)/shard_map/ppermute | solution.py:867
  104.9 2.5 %collective-permute-start.34 = (bf16[2,64,256]{2,1,0:T(8,128)(2,1)S(1)}, bf16[2,64,256]{2,1,0:T(8,128)(2,1)S(1)}, u32[]{:S(2)}, u32[]{:S(2)}) collective-permute-start(bf16[2,64,256]{2,1,0:T(8,128)(2,1)S(1)} %get-tuple-element.286), channel_id=1, source_target_pairs={{0,2},{1,3},{2,0},{3,1},{4,6},{5,7},{6,4},{7,5},{8,10},{9,11},{10,... | collective-permute-start | bytes 196616 | tf_op jit(solution)/shard_map/ppermute | solution.py:867
  108.5 2.0 %fetch.5 = (f32[128,1024]{1,0:T(8,128)S(1)}, bf16[128,1024]{1,0:T(8,128)(2,1)S(1)}, bf16[128,1024]{1,0:T(8,128)(2,1)S(1)}, bf16[64,1024]{1,0:T(8,128)(2,1)S(1)},...) custom-call(f32[128,1024]{1,0:T(8,128)} %get-tuple-element.251.refs_, ...), custom_call_target="tpu_custom_call" | custom-call | flops 1000000000 | bytes 1048576 | tf_op jit(solution)/shard_map/fetch/pallas_call | solution.py:158
  110.8 5.4 %back_last.1 = (f32[128,1024]{1,0:T(8,128)S(1)}, bf16[128,640]{1,0:T(8,128)(2,1)}) custom-call(bf16[128,512]{1,0:T(8,128)(2,1)S(1)} %add_convert_fusion.refs_0_, bf16[128,512]{1,0:T(8,128)(2,1)S(1)} %collective-permute-done.29.refs_1_, f32[128,1024]{1,0:T(8,128)S(1)} %get-tuple-element.264.refs_2_, ...), custom_call_target="tpu_custom_call", output_to_operand_aliasing={{1}: (28, {})} | custom-call | flops 10000000000 | bytes 1048576 | tf_op jit(solution)/shard_map/back_last/pallas_call | solution.py:128
  116.2 4.9 %all-to-all-start.1 = ((bf16[8,16,640]{2,1,0:T(8,128)(2,1)}), bf16[8,16,640]{2,1,0:T(8,128)(2,1)S(1)}, u32[]{:S(2)}, u32[]{:S(2)}) async-start(bf16[8,16,640]{2,1,0:T(8,128)(2,1)} %bitcast.84), calls=%async_computation.1 | async-start | bytes 327680 | tf_op jit(solution)/shard_map/all_to_all | solution.py:844
  121.8 2.6 %collective-permute-start.36 = (bf16[64,256]{1,0:T(8,128)(2,1)S(1)}, bf16[64,256]{1,0:T(8,128)(2,1)S(1)}, u32[]{:S(2)}, u32[]{:S(2)}) collective-permute-start(bf16[64,256]{1,0:T(8,128)(2,1)S(1)} %slice_bitcast_fusion.4), channel_id=1, source_target_pairs={{0,4},{1,5},{2,6},{3,7},{4,0},{5,1},{6,2},{7,3},{8,12},{9,13},{10,... | collective-permute-start | bytes 98312 | tf_op jit(solution)/shard_map/ppermute | solution.py:867
  125.8 3.5 %all-to-all-done.1.refs_0_ = bf16[8,16,640]{2,1,0:T(8,128)(2,1)S(1)} async-done(((bf16[8,16,640]{2,1,0:T(8,128)(2,1)}), bf16[8,16,640]{2,1,0:T(8,128)(2,1)S(1)}, u32[]{:S(2)}, u32[]{:S(2)}) %all-to-all-start.1) | async-done | bytes 163872 | tf_op jit(solution)/shard_map/all_to_all | solution.py:844
  133.6 1.7 %adam.1 = (f32[16,3000]{1,0:T(8,128)}, f32[16,3000]{1,0:T(8,128)}, f32[16,3000]{1,0:T(8,128)}, f32[16,3000]{1,0:T(8,128)}, bf16[16,3000]{1,0:T(8,128)(2,1)}) custom-call(s32[2]{0:T(128)S(1)} %pad_add_fusion.refs_0_, f32[16,3000]{1,0:T(8,128)S(1)} %bitcast.41, f32[16,3000]{1,0:T(8,128)S(1)} %bitcast.42, f32[16,3000]{1,0:T(8,128)S(1)} %bitcast.43, ...), custom_call_target="tpu_custom_call" | custom-call | flops 100000000 | bytes 1048576 | tf_op jit(solution)/shard_map/adam/pallas_call | solution.py:128
  (129 shorter events, 33.4 us)
Async XLA Ops:
  1.4 6.6 %collective-permute-start = (bf16[1,16,256]{2,1,0:T(8,128)(2,1)S(1)}, bf16[1,16,256]{2,1,0:T(8,128)(2,1)S(1)}, u32[]{:S(2)}, u32[]{:S(2)}) collective-permute-start(bf16[1,16,256]{2,1,0:T(8,128)(2,1)S(1)} %pack_first.1.refs_10_), channel_id=1, source_target_pairs={{0,4},{1,5},{2,6},{3,7},{4,0},{5,1},{6,2},{7,3},{8,12},{9,13},{10,... | collective-permute-start | bytes 24584 | tf_op jit(solution)/shard_map/ppermute | solution.py:867
  7.2 6.3 %collective-permute-start.4 = (bf16[1,144,256]{2,1,0:T(8,128)(2,1)S(1)}, bf16[1,144,256]{2,1,0:T(8,128)(2,1)S(1)}, u32[]{:S(2)}, u32[]{:S(2)}) collective-permute-start(bf16[1,144,256]{2,1,0:T(8,128)(2,1)S(1)} %pack_cargo.1.refs_1_), channel_id=1, source_target_pairs={{0,4},{1,5},{2,6},{3,7},{4,0},{5,1},{6,2},{7,3},{8,12},{9,13},{10,... | collective-permute-start | bytes 221192 | tf_op jit(solution)/shard_map/ppermute | solution.py:867
  8.0 8.8 %collective-permute-start.3 = (bf16[2,16,256]{2,1,0:T(8,128)(2,1)S(1)}, bf16[2,16,256]{2,1,0:T(8,128)(2,1)S(1)}, u32[]{:S(2)}, u32[]{:S(2)}) collective-permute-start(bf16[2,16,256]{2,1,0:T(8,128)(2,1)S(1)} %constant_dynamic-update-slice_fusion), channel_id=1, source_target_pairs={{0,3},{1,2},{2,1},{3,0},{4,7},{5,6},{6,5},{7,4},{8,11},{9,10},{10,... | collective-permute-start | bytes 49160 | tf_op jit(solution)/shard_map/ppermute | solution.py:867
  10.9 6.2 %collective-permute-start.2 = (bf16[2,16,256]{2,1,0:T(8,128)(2,1)S(1)}, bf16[2,16,256]{2,1,0:T(8,128)(2,1)S(1)}, u32[]{:S(2)}, u32[]{:S(2)}) collective-permute-start(bf16[2,16,256]{2,1,0:T(8,128)(2,1)S(1)} %constant_dynamic-update-slice_fusion), channel_id=1, source_target_pairs={{0,2},{1,3},{2,0},{3,1},{4,6},{5,7},{6,4},{7,5},{8,10},{9,11},{10,... | collective-permute-start | bytes 49160 | tf_op jit(solution)/shard_map/ppermute | solution.py:867
  13.5 9.8 %collective-permute-start.7 = (bf16[2,144,256]{2,1,0:T(8,128)(2,1)S(1)}, bf16[2,144,256]{2,1,0:T(8,128)(2,1)S(1)}, u32[]{:S(2)}, u32[]{:S(2)}) collective-permute-start(bf16[2,144,256]{2,1,0:T(8,128)(2,1)S(1)} %pad_maximum_fusion), channel_id=1, source_target_pairs={{0,3},{1,2},{2,1},{3,0},{4,7},{5,6},{6,5},{7,4},{8,11},{9,10},{10,... | collective-permute-start | bytes 442376 | tf_op jit(solution)/shard_map/ppermute | solution.py:867
  15.2 8.1 %collective-permute-start.6 = (bf16[2,144,256]{2,1,0:T(8,128)(2,1)S(1)}, bf16[2,144,256]{2,1,0:T(8,128)(2,1)S(1)}, u32[]{:S(2)}, u32[]{:S(2)}) collective-permute-start(bf16[2,144,256]{2,1,0:T(8,128)(2,1)S(1)} %pad_maximum_fusion), channel_id=1, source_target_pairs={{0,2},{1,3},{2,0},{3,1},{4,6},{5,7},{6,4},{7,5},{8,10},{9,11},{10,... | collective-permute-start | bytes 442376 | tf_op jit(solution)/shard_map/ppermute | solution.py:867
  16.8 6.5 %collective-permute-start.5 = (bf16[2,144,256]{2,1,0:T(8,128)(2,1)S(1)}, bf16[2,144,256]{2,1,0:T(8,128)(2,1)S(1)}, u32[]{:S(2)}, u32[]{:S(2)}) collective-permute-start(bf16[2,144,256]{2,1,0:T(8,128)(2,1)S(1)} %pad_maximum_fusion), channel_id=1, source_target_pairs={{0,1},{1,0},{2,3},{3,2},{4,5},{5,4},{6,7},{7,6},{8,9},{9,8},{10,11... | collective-permute-start | bytes 442376 | tf_op jit(solution)/shard_map/ppermute | solution.py:867
  27.7 7.2 %collective-permute-start.13 = (bf16[128,384]{1,0:T(8,128)(2,1)S(1)}, bf16[128,384]{1,0:T(8,128)(2,1)S(1)}, u32[]{:S(2)}, u32[]{:S(2)}) collective-permute-start(bf16[128,384]{1,0:T(8,128)(2,1)S(1)} %get-tuple-element.163.refs_2_), channel_id=1, source_target_pairs={{0,16},{8,24},{16,0},{24,8},{1,17},{9,25},{17,1},{25,9},{2,18},{10... | collective-permute-start | bytes 294920 | tf_op jit(solution)/shard_map/ppermute | solution.py:867
  31.7 7.4 %collective-permute-start.11 = (bf16[512,128]{1,0:T(8,128)(2,1)S(1)}, bf16[512,128]{1,0:T(8,128)(2,1)S(1)}, u32[]{:S(2)}, u32[]{:S(2)}) collective-permute-start(bf16[512,128]{1,0:T(8,128)(2,1)S(1)} %add_convert_fusion.3.refs_0_), channel_id=1, source_target_pairs={{0,4},{1,5},{2,6},{3,7},{4,0},{5,1},{6,2},{7,3},{8,12},{9,13},{10,... | collective-permute-start | bytes 393224 | tf_op jit(solution)/shard_map/ppermute | solution.py:867
  46.7 6.7 %collective-permute-start.17 = (bf16[512,128]{1,0:T(8,128)(2,1)S(1)}, bf16[512,128]{1,0:T(8,128)(2,1)S(1)}, u32[]{:S(2)}, u32[]{:S(2)}) collective-permute-start(bf16[512,128]{1,0:T(8,128)(2,1)S(1)} %get-tuple-element.177), channel_id=1, source_target_pairs={{0,3},{1,2},{2,1},{3,0},{4,7},{5,6},{6,5},{7,4},{8,11},{9,10},{10,... | collective-permute-start | bytes 393224 | tf_op jit(solution)/shard_map/ppermute | solution.py:867
  47.1 8.6 %collective-permute-start.16 = (bf16[512,128]{1,0:T(8,128)(2,1)S(1)}, bf16[512,128]{1,0:T(8,128)(2,1)S(1)}, u32[]{:S(2)}, u32[]{:S(2)}) collective-permute-start(bf16[512,128]{1,0:T(8,128)(2,1)S(1)} %get-tuple-element.177), channel_id=1, source_target_pairs={{0,2},{1,3},{2,0},{3,1},{4,6},{5,7},{6,4},{7,5},{8,10},{9,11},{10,... | collective-permute-start | bytes 393224 | tf_op jit(solution)/shard_map/ppermute | solution.py:867
  50.3 6.7 %collective-permute-start.21 = (bf16[128,384]{1,0:T(8,128)(2,1)S(1)}, bf16[128,384]{1,0:T(8,128)(2,1)S(1)}, u32[]{:S(2)}, u32[]{:S(2)}) collective-permute-start(bf16[128,384]{1,0:T(8,128)(2,1)S(1)} %get-tuple-element.181.refs_1_), channel_id=1, source_target_pairs={{0,24},{8,16},{16,8},{24,0},{1,25},{9,17},{17,9},{25,1},{2,26},{10... | collective-permute-start | bytes 294920 | tf_op jit(solution)/shard_map/ppermute | solution.py:867
  50.3 7.2 %collective-permute-start.20 = (bf16[128,384]{1,0:T(8,128)(2,1)S(1)}, bf16[128,384]{1,0:T(8,128)(2,1)S(1)}, u32[]{:S(2)}, u32[]{:S(2)}) collective-permute-start(bf16[128,384]{1,0:T(8,128)(2,1)S(1)} %get-tuple-element.181.refs_1_), channel_id=1, source_target_pairs={{0,16},{8,24},{16,0},{24,8},{1,17},{9,25},{17,1},{25,9},{2,18},{10... | collective-permute-start | bytes 294920 | tf_op jit(solution)/shard_map/ppermute | solution.py:867
  55.8 8.3 %collective-permute-start.18 = (bf16[512,128]{1,0:T(8,128)(2,1)S(1)}, bf16[512,128]{1,0:T(8,128)(2,1)S(1)}, u32[]{:S(2)}, u32[]{:S(2)}) collective-permute-start(bf16[512,128]{1,0:T(8,128)(2,1)S(1)} %add_convert_fusion.2.refs_1_), channel_id=1, source_target_pairs={{0,4},{1,5},{2,6},{3,7},{4,0},{5,1},{6,2},{7,3},{8,12},{9,13},{10,... | collective-permute-start | bytes 393224 | tf_op jit(solution)/shard_map/ppermute | solution.py:867
  67.6 7.3 %collective-permute-start.24 = (bf16[128,512]{1,0:T(8,128)(2,1)S(1)}, bf16[128,512]{1,0:T(8,128)(2,1)S(1)}, u32[]{:S(2)}, u32[]{:S(2)}) collective-permute-start(bf16[128,512]{1,0:T(8,128)(2,1)S(1)} %get-tuple-element.201), channel_id=1, source_target_pairs={{0,3},{1,2},{2,1},{3,0},{4,7},{5,6},{6,5},{7,4},{8,11},{9,10},{10,... | collective-permute-start | bytes 393224 | tf_op jit(solution)/shard_map/ppermute | solution.py:867
  67.7 9.3 %collective-permute-start.23 = (bf16[128,512]{1,0:T(8,128)(2,1)S(1)}, bf16[128,512]{1,0:T(8,128)(2,1)S(1)}, u32[]{:S(2)}, u32[]{:S(2)}) collective-permute-start(bf16[128,512]{1,0:T(8,128)(2,1)S(1)} %get-tuple-element.201), channel_id=1, source_target_pairs={{0,2},{1,3},{2,0},{3,1},{4,6},{5,7},{6,4},{7,5},{8,10},{9,11},{10,... | collective-permute-start | bytes 393224 | tf_op jit(solution)/shard_map/ppermute | solution.py:867
  70.7 6.2 %collective-permute-start.22 = (bf16[128,512]{1,0:T(8,128)(2,1)S(1)}, bf16[128,512]{1,0:T(8,128)(2,1)S(1)}, u32[]{:S(2)}, u32[]{:S(2)}) collective-permute-start(bf16[128,512]{1,0:T(8,128)(2,1)S(1)} %get-tuple-element.201), channel_id=1, source_target_pairs={{0,1},{1,0},{2,3},{3,2},{4,5},{5,4},{6,7},{7,6},{8,9},{9,8},{10,11... | collective-permute-start | bytes 393224 | tf_op jit(solution)/shard_map/ppermute | solution.py:867
  77.0 8.5 %collective-permute-start.25 = (bf16[128,512]{1,0:T(8,128)(2,1)S(1)}, bf16[128,512]{1,0:T(8,128)(2,1)S(1)}, u32[]{:S(2)}, u32[]{:S(2)}) collective-permute-start(bf16[128,512]{1,0:T(8,128)(2,1)S(1)} %add_convert_fusion.1.refs_1_), channel_id=1, source_target_pairs={{0,4},{1,5},{2,6},{3,7},{4,0},{5,1},{6,2},{7,3},{8,12},{9,13},{10,... | collective-permute-start | bytes 393224 | tf_op jit(solution)/shard_map/ppermute | solution.py:867
  77.4 21.4 %all-to-all-start = ((bf16[8,16,1280]{2,1,0:T(8,128)(2,1)}), bf16[8,16,1280]{2,1,0:T(8,128)(2,1)S(1)}, u32[]{:S(2)}, u32[]{:S(2)}) async-start(bf16[8,16,1280]{2,1,0:T(8,128)(2,1)} %bitcast.15), calls=%async_computation | async-start | bytes 655360 | tf_op jit(solution)/shard_map/all_to_all | solution.py:844
  92.7 7.8 %collective-permute-start.28 = (bf16[128,512]{1,0:T(8,128)(2,1)S(1)}, bf16[128,512]{1,0:T(8,128)(2,1)S(1)}, u32[]{:S(2)}, u32[]{:S(2)}) collective-permute-start(bf16[128,512]{1,0:T(8,128)(2,1)S(1)} %get-tuple-element.248), channel_id=1, source_target_pairs={{0,3},{1,2},{2,1},{3,0},{4,7},{5,6},{6,5},{7,4},{8,11},{9,10},{10,... | collective-permute-start | bytes 393224 | tf_op jit(solution)/shard_map/ppermute | solution.py:867
  94.9 6.2 %collective-permute-start.27 = (bf16[128,512]{1,0:T(8,128)(2,1)S(1)}, bf16[128,512]{1,0:T(8,128)(2,1)S(1)}, u32[]{:S(2)}, u32[]{:S(2)}) collective-permute-start(bf16[128,512]{1,0:T(8,128)(2,1)S(1)} %get-tuple-element.248), channel_id=1, source_target_pairs={{0,2},{1,3},{2,0},{3,1},{4,6},{5,7},{6,4},{7,5},{8,10},{9,11},{10,... | collective-permute-start | bytes 393224 | tf_op jit(solution)/shard_map/ppermute | solution.py:867
  99.0 8.4 %collective-permute-start.31 = (bf16[128,384]{1,0:T(8,128)(2,1)S(1)}, bf16[128,384]{1,0:T(8,128)(2,1)S(1)}, u32[]{:S(2)}, u32[]{:S(2)}) collective-permute-start(bf16[128,384]{1,0:T(8,128)(2,1)S(1)} %get-tuple-element.298), channel_id=1, source_target_pairs={{0,16},{8,24},{16,0},{24,8},{1,17},{9,25},{17,1},{25,9},{2,18},{10... | collective-permute-start | bytes 294920 | tf_op jit(solution)/shard_map/ppermute | solution.py:867
  100.4 7.3 %collective-permute-start.30 = (bf16[128,384]{1,0:T(8,128)(2,1)S(1)}, bf16[128,384]{1,0:T(8,128)(2,1)S(1)}, u32[]{:S(2)}, u32[]{:S(2)}) collective-permute-start(bf16[128,384]{1,0:T(8,128)(2,1)S(1)} %get-tuple-element.299), channel_id=1, source_target_pairs={{0,8},{8,0},{16,24},{24,16},{1,9},{9,1},{17,25},{25,17},{2,10},{10... | collective-permute-start | bytes 294920 | tf_op jit(solution)/shard_map/ppermute | solution.py:867
  101.4 9.4 %collective-permute-start.29 = (bf16[128,512]{1,0:T(8,128)(2,1)S(1)}, bf16[128,512]{1,0:T(8,128)(2,1)S(1)}, u32[]{:S(2)}, u32[]{:S(2)}) collective-permute-start(bf16[128,512]{1,0:T(8,128)(2,1)S(1)} %add_convert_fusion.refs_0_), channel_id=1, source_target_pairs={{0,4},{1,5},{2,6},{3,7},{4,0},{5,1},{6,2},{7,3},{8,12},{9,13},{10,... | collective-permute-start | bytes 393224 | tf_op jit(solution)/shard_map/ppermute | solution.py:867
  104.2 16.9 %collective-permute-start.33 = (bf16[2,64,256]{2,1,0:T(8,128)(2,1)S(1)}, bf16[2,64,256]{2,1,0:T(8,128)(2,1)S(1)}, u32[]{:S(2)}, u32[]{:S(2)}) collective-permute-start(bf16[2,64,256]{2,1,0:T(8,128)(2,1)S(1)} %get-tuple-element.285), channel_id=1, source_target_pairs={{0,1},{1,0},{2,3},{3,2},{4,5},{5,4},{6,7},{7,6},{8,9},{9,8},{10,11... | collective-permute-start | bytes 196616 | tf_op jit(solution)/shard_map/ppermute | solution.py:867
  104.9 16.2 %collective-permute-start.34 = (bf16[2,64,256]{2,1,0:T(8,128)(2,1)S(1)}, bf16[2,64,256]{2,1,0:T(8,128)(2,1)S(1)}, u32[]{:S(2)}, u32[]{:S(2)}) collective-permute-start(bf16[2,64,256]{2,1,0:T(8,128)(2,1)S(1)} %get-tuple-element.286), channel_id=1, source_target_pairs={{0,2},{1,3},{2,0},{3,1},{4,6},{5,7},{6,4},{7,5},{8,10},{9,11},{10,... | collective-permute-start | bytes 196616 | tf_op jit(solution)/shard_map/ppermute | solution.py:867
  107.4 13.7 %collective-permute-start.35 = (bf16[2,64,256]{2,1,0:T(8,128)(2,1)S(1)}, bf16[2,64,256]{2,1,0:T(8,128)(2,1)S(1)}, u32[]{:S(2)}, u32[]{:S(2)}) collective-permute-start(bf16[2,64,256]{2,1,0:T(8,128)(2,1)S(1)} %get-tuple-element.287), channel_id=1, source_target_pairs={{0,3},{1,2},{2,1},{3,0},{4,7},{5,6},{6,5},{7,4},{8,11},{9,10},{10,... | collective-permute-start | bytes 196616 | tf_op jit(solution)/shard_map/ppermute | solution.py:867
  116.2 13.1 %all-to-all-start.1 = ((bf16[8,16,640]{2,1,0:T(8,128)(2,1)}), bf16[8,16,640]{2,1,0:T(8,128)(2,1)S(1)}, u32[]{:S(2)}, u32[]{:S(2)}) async-start(bf16[8,16,640]{2,1,0:T(8,128)(2,1)} %bitcast.84), calls=%async_computation.1 | async-start | bytes 327680 | tf_op jit(solution)/shard_map/all_to_all | solution.py:844
  121.3 9.6 %collective-permute-start.42 = (bf16[16,1280]{1,0:T(8,128)(2,1)S(1)}, bf16[16,1280]{1,0:T(8,128)(2,1)S(1)}, u32[]{:S(2)}, u32[]{:S(2)}) collective-permute-start(bf16[16,1280]{1,0:T(8,128)(2,1)S(1)} %sum_parts.3.refs_8_), channel_id=1, source_target_pairs={{0,24},{8,16},{16,8},{24,0},{1,25},{9,17},{17,9},{25,1},{2,26},{10... | collective-permute-start | bytes 122888 | tf_op jit(solution)/shard_map/ppermute | solution.py:867
  121.8 7.8 %collective-permute-start.36 = (bf16[64,256]{1,0:T(8,128)(2,1)S(1)}, bf16[64,256]{1,0:T(8,128)(2,1)S(1)}, u32[]{:S(2)}, u32[]{:S(2)}) collective-permute-start(bf16[64,256]{1,0:T(8,128)(2,1)S(1)} %slice_bitcast_fusion.4), channel_id=1, source_target_pairs={{0,4},{1,5},{2,6},{3,7},{4,0},{5,1},{6,2},{7,3},{8,12},{9,13},{10,... | collective-permute-start | bytes 98312 | tf_op jit(solution)/shard_map/ppermute | solution.py:867
  124.5 8.5 %collective-permute-start.41 = (bf16[16,1280]{1,0:T(8,128)(2,1)S(1)}, bf16[16,1280]{1,0:T(8,128)(2,1)S(1)}, u32[]{:S(2)}, u32[]{:S(2)}) collective-permute-start(bf16[16,1280]{1,0:T(8,128)(2,1)S(1)} %sum_parts.3.refs_8_), channel_id=1, source_target_pairs={{0,16},{8,24},{16,0},{24,8},{1,17},{9,25},{17,1},{25,9},{2,18},{10... | collective-permute-start | bytes 122888 | tf_op jit(solution)/shard_map/ppermute | solution.py:867
  125.6 7.3 %collective-permute-start.40 = (bf16[16,1280]{1,0:T(8,128)(2,1)S(1)}, bf16[16,1280]{1,0:T(8,128)(2,1)S(1)}, u32[]{:S(2)}, u32[]{:S(2)}) collective-permute-start(bf16[16,1280]{1,0:T(8,128)(2,1)S(1)} %sum_parts.3.refs_8_), channel_id=1, source_target_pairs={{0,8},{8,0},{16,24},{24,16},{1,9},{9,1},{17,25},{25,17},{2,10},{10... | collective-permute-start | bytes 122888 | tf_op jit(solution)/shard_map/ppermute | solution.py:867
  (30 other events, 168.1 us)

commit v7 on v6

--- a/solution.py
+++ b/solution.py
@@ -348,7 +348,9 @@
     out_ref[0] = low(padded(hold[...], ROWS, PAD))
 
 
-def pack_cargo(me, weights, state, fixed, out_ref, hold):
+def pack_cargo(
+    me, weights, state, fixed, dst_owner, dst_local, src_owner, src_local, out_ref, dst_ref, src_ref, hold
+):
     count = state.shape[0]
     free = (1 - fixed[...]).astype(F32)
     out_ref[0, :count] = state[...]
@@ -367,6 +369,8 @@
         for k in range(slots(width)):
             out_ref[0, base : base + ROWS] = low(mine[:, k * PAD : (k + 1) * PAD])
             base = base + ROWS
+    dst_ref[...] = dst_owner[...] * count + dst_local[...]
+    src_ref[...] = src_owner[...] * count + src_local[...]
 
 
 def order_of(owners):
@@ -899,18 +903,18 @@
     )
     pack, state = lax.optimization_barrier((pack, atom_state))
     pack = gathered(pack)
-    [cargo] = call(
+    cargo, dst_row, src_row = call(
         pack_cargo,
-        [sds((1, count + ROWS * (1 + 2 * slots(lanes)), D_ATOM), BF16)],
-        [me, weights_t, state, fixed_atoms.reshape(1, count)],
+        [sds((1, count + ROWS * (1 + 2 * slots(lanes)), D_ATOM), BF16)]
+        + [sds((1, edges), jnp.int32)] * 2,
+        [me, weights_t, state, fixed_atoms.reshape(1, count)]
+        + [x.reshape(1, edges) for x in (dst_owner, dst_local, src_owner, src_local)],
         flops=10**7,
-        late=[1, 2, 3],
+        late=range(1, 8),
         smem=1,
         scratch=[(groups, cols, lanes)],
     )
     cargo = gathered(cargo)
-    dst_row = (dst_owner[:, 0] * count + dst_local).reshape(1, edges)
-    src_row = (src_owner[:, 0] * count + src_local).reshape(1, edges)
     graph = [
         jnp.transpose(radial_basis),
         jnp.transpose(triplet_basis),

time: 136 us -> 135 us (level)
  transfers between devices with their start and end apart: 45 -> 45, of which waited for: 19 -> 20; matrix products, arithmetic and copies ran while one was open for 1% -> 1% of each run, Pallas kernels for 27% -> 27%
where the time goes in v7:
time: 135 us
  starting transfers between devices  54.2 us (40%)
  Pallas kernels  50.2 us (37%)
  waiting for transfers between devices  27.8 us (21%)
    ppermute x43, starting transfers between devices, moved(): return lax.ppermute(table, axis, [(i, i ^ step) for i in range(owners)])  45 us
    pallas_call x18, Pallas kernels, call(): pl.pallas_call(kernel, out_shape=outs, in_specs=[pl.BlockSpec(memory_spac...  44.3 us
    ppermute x43, waiting for transfers between devices, moved(): return lax.ppermute(table, axis, [(i, i ^ step) for i in range(owners)])  24.4 us
    all_to_all x2, starting transfers between devices, exchange(): return lax.all_to_all(pieces, 'shard', split_axis=0, concat_axis=0)  9.28 us
    pallas_call x3, Pallas kernels, fetch(): pl.pallas_call(kernel, out_shape=[sds(x.shape, x.dtype) for x in arrays],...  5.89 us
    all_to_all x2, waiting for transfers between devices, exchange(): return lax.all_to_all(pieces, 'shard', split_axis=0, concat_axis=0)  3.44 us
  transfers between devices with their start and end apart: 45, of which 20 were waited for; matrix products, arithmetic and copies ran while one was open for 1% of the time, Pallas kernels for 27%

profile of v7, /device:TPU:0, one launch (start us, length us, event | category | flops | bytes accessed | tf_op | source)
XLA Modules:
  0.0 134.7 jit_solution(16951805103962869443)
XLA Ops:
  1.4 4.1 %collective-permute-start = (bf16[1,16,256]{2,1,0:T(8,128)(2,1)S(1)}, bf16[1,16,256]{2,1,0:T(8,128)(2,1)S(1)}, u32[]{:S(2)}, u32[]{:S(2)}) collective-permute-start(bf16[1,16,256]{2,1,0:T(8,128)(2,1)S(1)} %pack_first.1.refs_10_), channel_id=1, source_target_pairs={{0,4},{1,5},{2,6},{3,7},{4,0},{5,1},{6,2},{7,3},{8,12},{9,13},{10,... | collective-permute-start | bytes 24584 | tf_op jit(solution)/shard_map/ppermute | solution.py:871
  5.6 1.7 %pack_cargo.1 = (bf16[1,144,256]{2,1,0:T(8,128)(2,1)S(1)}, s32[1,1024]{1,0:T(1,128)S(1)}, s32[1,1024]{1,0:T(1,128)S(1)}) custom-call(s32[2]{0:T(128)S(1)} %pad_add_fusion.refs_0_, f32[16,3000]{1,0:T(8,128)} %bitcast.40, bf16[64,256]{1,0:T(8,128)(2,1)} %refs_2_, s32[1,64]{1,0:T(1,128)} %bitcast.77, s32[1,1024]{1,0:T(1,128)} %bitcast.73, s32[1,1024]{1,0:T(1,128)} %bitcast.74, ...), custom_call_target="tpu_custom_call" | custom-call | flops 10000000 | bytes 1048576 | tf_op jit(solution)/shard_map/pack_cargo/pallas_call | solution.py:128
  7.4 2.9 %collective-permute-start.3 = (bf16[2,16,256]{2,1,0:T(8,128)(2,1)S(1)}, bf16[2,16,256]{2,1,0:T(8,128)(2,1)S(1)}, u32[]{:S(2)}, u32[]{:S(2)}) collective-permute-start(bf16[2,16,256]{2,1,0:T(8,128)(2,1)S(1)} %constant_dynamic-update-slice_fusion), channel_id=1, source_target_pairs={{0,3},{1,2},{2,1},{3,0},{4,7},{5,6},{6,5},{7,4},{8,11},{9,10},{10,... | collective-permute-start | bytes 49160 | tf_op jit(solution)/shard_map/ppermute | solution.py:871
  11.0 2.8 %collective-permute-done.4.refs_2_ = bf16[1,144,256]{2,1,0:T(8,128)(2,1)S(1)} collective-permute-done((bf16[1,144,256]{2,1,0:T(8,128)(2,1)S(1)}, bf16[1,144,256]{2,1,0:T(8,128)(2,1)S(1)}, u32[]{:S(2)}, u32[]{:S(2)}) %collective-permute-start.4) | collective-permute-done | bytes 73760 | tf_op jit(solution)/shard_map/ppermute | solution.py:871
  13.7 1.5 %collective-permute-start.7 = (bf16[2,144,256]{2,1,0:T(8,128)(2,1)S(1)}, bf16[2,144,256]{2,1,0:T(8,128)(2,1)S(1)}, u32[]{:S(2)}, u32[]{:S(2)}) collective-permute-start(bf16[2,144,256]{2,1,0:T(8,128)(2,1)S(1)} %constant_dynamic-update-slice_fusion.2), channel_id=1, source_target_pairs={{0,3},{1,2},{2,1},{3,0},{4,7},{5,6},{6,5},{7,4},{8,11},{9,10},{10,... | collective-permute-start | bytes 442376 | tf_op jit(solution)/shard_map/ppermute | solution.py:871
  17.3 6.1 %first_half.1 = (bf16[128,256]{1,0:T(8,128)(2,1)S(1)}, f32[128,1024]{1,0:T(8,128)}, bf16[128,1024]{1,0:T(8,128)(2,1)}, bf16[128,1024]{1,0:T(8,128)(2,1)}, bf16[6...) custom-call(s32[2]{0:T(128)S(1)} %pad_add_fusion.refs_0_, ...), custom_call_target="tpu_custom_call" | custom-call | flops 8000000000 | bytes 1048576 | tf_op jit(solution)/shard_map/first_half/pallas_call | solution.py:128
  23.5 1.6 %collective-permute-start.10 = (bf16[512,128]{1,0:T(8,128)(2,1)S(1)}, bf16[512,128]{1,0:T(8,128)(2,1)S(1)}, u32[]{:S(2)}, u32[]{:S(2)}) collective-permute-start(bf16[512,128]{1,0:T(8,128)(2,1)S(1)} %get-tuple-element.161), channel_id=1, source_target_pairs={{0,3},{1,2},{2,1},{3,0},{4,7},{5,6},{6,5},{7,4},{8,11},{9,10},{10,... | collective-permute-start | bytes 393224 | tf_op jit(solution)/shard_map/ppermute | solution.py:871
  27.9 1.6 %collective-permute-start.13 = (bf16[128,384]{1,0:T(8,128)(2,1)S(1)}, bf16[128,384]{1,0:T(8,128)(2,1)S(1)}, u32[]{:S(2)}, u32[]{:S(2)}) collective-permute-start(bf16[128,384]{1,0:T(8,128)(2,1)S(1)} %get-tuple-element.168.refs_2_), channel_id=1, source_target_pairs={{0,16},{8,24},{16,0},{24,8},{1,17},{9,25},{17,1},{25,9},{2,18},{10... | collective-permute-start | bytes 294920 | tf_op jit(solution)/shard_map/ppermute | solution.py:871
  32.9 2.2 %collective-permute-done.13.refs_4_ = bf16[128,384]{1,0:T(8,128)(2,1)S(1)} collective-permute-done((bf16[128,384]{1,0:T(8,128)(2,1)S(1)}, bf16[128,384]{1,0:T(8,128)(2,1)S(1)}, u32[]{:S(2)}, u32[]{:S(2)}) %collective-permute-start.13) | collective-permute-done | bytes 98336 | tf_op jit(solution)/shard_map/ppermute | solution.py:871
  36.4 2.8 %collective-permute-done.11.refs_1_ = bf16[512,128]{1,0:T(8,128)(2,1)S(1)} collective-permute-done((bf16[512,128]{1,0:T(8,128)(2,1)S(1)}, bf16[512,128]{1,0:T(8,128)(2,1)S(1)}, u32[]{:S(2)}, u32[]{:S(2)}) %collective-permute-start.11) | collective-permute-done | bytes 131104 | tf_op jit(solution)/shard_map/ppermute | solution.py:871
  39.2 7.6 %middle_half.1 = (bf16[512,128]{1,0:T(8,128)(2,1)}, bf16[512,256]{1,0:T(8,128)(2,1)}, bf16[512,256]{1,0:T(8,128)(2,1)}, f32[512,256]{1,0:T(8,128)}, bf16[512,256...) custom-call(bf16[512,128]{1,0:T(8,128)(2,1)S(1)} %add_convert_fusion, ...), custom_call_target="tpu_custom_call" | custom-call | flops 10000000000 | bytes 1048576 | tf_op jit(solution)/shard_map/middle_half/pallas_call | solution.py:128
  46.9 2.5 %collective-permute-start.16 = (bf16[512,128]{1,0:T(8,128)(2,1)S(1)}, bf16[512,128]{1,0:T(8,128)(2,1)S(1)}, u32[]{:S(2)}, u32[]{:S(2)}) collective-permute-start(bf16[512,128]{1,0:T(8,128)(2,1)S(1)} %get-tuple-element.183), channel_id=1, source_target_pairs={{0,2},{1,3},{2,0},{3,1},{4,6},{5,7},{6,4},{7,5},{8,10},{9,11},{10,... | collective-permute-start | bytes 393224 | tf_op jit(solution)/shard_map/ppermute | solution.py:871
  50.3 1.5 %collective-permute-start.20 = (bf16[128,384]{1,0:T(8,128)(2,1)S(1)}, bf16[128,384]{1,0:T(8,128)(2,1)S(1)}, u32[]{:S(2)}, u32[]{:S(2)}) collective-permute-start(bf16[128,384]{1,0:T(8,128)(2,1)S(1)} %get-tuple-element.187.refs_1_), channel_id=1, source_target_pairs={{0,16},{8,24},{16,0},{24,8},{1,17},{9,25},{17,1},{25,9},{2,18},{10... | collective-permute-start | bytes 294920 | tf_op jit(solution)/shard_map/ppermute | solution.py:871
  51.8 2.1 %collective-permute-done.17 = bf16[512,128]{1,0:T(8,128)(2,1)S(1)} collective-permute-done((bf16[512,128]{1,0:T(8,128)(2,1)S(1)}, bf16[512,128]{1,0:T(8,128)(2,1)S(1)}, u32[]{:S(2)}, u32[]{:S(2)}) %collective-permute-start.17) | collective-permute-done | bytes 131104 | tf_op jit(solution)/shard_map/ppermute | solution.py:871
  55.6 1.9 %collective-permute-done.20.refs_3_ = bf16[128,384]{1,0:T(8,128)(2,1)S(1)} collective-permute-done((bf16[128,384]{1,0:T(8,128)(2,1)S(1)}, bf16[128,384]{1,0:T(8,128)(2,1)S(1)}, u32[]{:S(2)}, u32[]{:S(2)}) %collective-permute-start.20) | collective-permute-done | bytes 98336 | tf_op jit(solution)/shard_map/ppermute | solution.py:871
  59.8 3.5 %collective-permute-done.18.refs_2_ = bf16[512,128]{1,0:T(8,128)(2,1)S(1)} collective-permute-done((bf16[512,128]{1,0:T(8,128)(2,1)S(1)}, bf16[512,128]{1,0:T(8,128)(2,1)S(1)}, u32[]{:S(2)}, u32[]{:S(2)}) %collective-permute-start.18) | collective-permute-done | bytes 131104 | tf_op jit(solution)/shard_map/ppermute | solution.py:871
  63.3 3.4 %turn.1 = (bf16[512,128]{1,0:T(8,128)(2,1)S(1)}, bf16[512,256]{1,0:T(8,128)(2,1)S(1)}, bf16[512,256]{1,0:T(8,128)(2,1)S(1)}, f32[128,1024]{1,0:T(8,128)S(1)}, bf...) custom-call(s32[2]{0:T(128)S(1)} %pad_add_fusion.refs_0_, ...), custom_call_target="tpu_custom_call" | custom-call | flops 2000000000 | bytes 1048576 | tf_op jit(solution)/shard_map/turn/pallas_call | solution.py:128
  66.9 2.4 %collective-permute-start.23 = (bf16[128,512]{1,0:T(8,128)(2,1)S(1)}, bf16[128,512]{1,0:T(8,128)(2,1)S(1)}, u32[]{:S(2)}, u32[]{:S(2)}) collective-permute-start(bf16[128,512]{1,0:T(8,128)(2,1)S(1)} %get-tuple-element.207), channel_id=1, source_target_pairs={{0,2},{1,3},{2,0},{3,1},{4,6},{5,7},{6,4},{7,5},{8,10},{9,11},{10,... | collective-permute-start | bytes 393224 | tf_op jit(solution)/shard_map/ppermute | solution.py:871
  71.2 2.1 %large_grads.1 = bf16[128,1280]{1,0:T(8,128)(2,1)} custom-call(bf16[512,256]{1,0:T(8,128)(2,1)S(1)} %get-tuple-element.198.refs_0_, bf16[512,256]{1,0:T(8,128)(2,1)S(1)} %get-tuple-element.199.refs_1_, bf16[128,1024]{1,0:T(8,128)(2,1)S(1)} %get-tuple-element.200.refs_2_, s32[1,1024]{1,0:T(1,128)S(1)} %get-tuple-element.180.refs_20_.refs_6_.refs_3_.refs_32_.refs_4_, ...), custom_call_target="tpu_custom_call" | custom-call | flops 1000000000 | bytes 1048576 | tf_op jit(solution)/shard_map/large_grads/pallas_call | solution.py:128
  76.2 4.4 %all-to-all-start = ((bf16[8,16,1280]{2,1,0:T(8,128)(2,1)}), bf16[8,16,1280]{2,1,0:T(8,128)(2,1)S(1)}, u32[]{:S(2)}, u32[]{:S(2)}) async-start(bf16[8,16,1280]{2,1,0:T(8,128)(2,1)} %bitcast.15), calls=%async_computation | async-start | bytes 655360 | tf_op jit(solution)/shard_map/all_to_all | solution.py:848
  80.6 2.5 %fetch.4 = (f32[128,1024]{1,0:T(8,128)S(1)}, bf16[128,1024]{1,0:T(8,128)(2,1)S(1)}, bf16[128,1024]{1,0:T(8,128)(2,1)S(1)}, bf16[64,1024]{1,0:T(8,128)(2,1)S(1)},...) custom-call(f32[128,1024]{1,0:T(8,128)} %get-tuple-element.208.refs_, ...), custom_call_target="tpu_custom_call" | custom-call | flops 1000000000 | bytes 1048576 | tf_op jit(solution)/shard_map/fetch/pallas_call | solution.py:158
  84.3 7.2 %back_middle.1 = (bf16[128,256]{1,0:T(8,128)(2,1)S(1)}, bf16[128,512]{1,0:T(8,128)(2,1)S(1)}, bf16[512,256]{1,0:T(8,128)(2,1)S(1)}, bf16[512,256]{1,0:T(8,128)(2...) custom-call(s32[2]{0:T(128)S(1)} %pad_add_fusion.refs_0_, ...), custom_call_target="tpu_custom_call" | custom-call | flops 10000000000 | bytes 1048576 | tf_op jit(solution)/shard_map/back_middle/pallas_call | solution.py:128
  91.5 1.9 %collective-permute-start.28 = (bf16[128,512]{1,0:T(8,128)(2,1)S(1)}, bf16[128,512]{1,0:T(8,128)(2,1)S(1)}, u32[]{:S(2)}, u32[]{:S(2)}) collective-permute-start(bf16[128,512]{1,0:T(8,128)(2,1)S(1)} %get-tuple-element.254), channel_id=1, source_target_pairs={{0,3},{1,2},{2,1},{3,0},{4,7},{5,6},{6,5},{7,4},{8,11},{9,10},{10,... | collective-permute-start | bytes 393224 | tf_op jit(solution)/shard_map/ppermute | solution.py:871
  95.0 2.7 %large_pieces.1 = bf16[4,128,384]{2,1,0:T(8,128)(2,1)S(1)} custom-call(s32[2]{0:T(128)S(1)} %pad_add_fusion.refs_0_, bf16[512,256]{1,0:T(8,128)(2,1)S(1)} %get-tuple-element.246.refs_1_, bf16[512,256]{1,0:T(8,128)(2,1)S(1)} %get-tuple-element.247.refs_2_, bf16[128,1024]{1,0:T(8,128)(2,1)S(1)} %get-tuple-element.248.refs_3_, ...), custom_call_target="tpu_custom_call" | custom-call | flops 1000000000 | bytes 1048576 | tf_op jit(solution)/shard_map/large_pieces/pallas_call | solution.py:128
  100.6 2.5 %collective-permute-start.29 = (bf16[128,512]{1,0:T(8,128)(2,1)S(1)}, bf16[128,512]{1,0:T(8,128)(2,1)S(1)}, u32[]{:S(2)}, u32[]{:S(2)}) collective-permute-start(bf16[128,512]{1,0:T(8,128)(2,1)S(1)} %add_convert_fusion.refs_0_), channel_id=1, source_target_pairs={{0,4},{1,5},{2,6},{3,7},{4,0},{5,1},{6,2},{7,3},{8,12},{9,13},{10,... | collective-permute-start | bytes 393224 | tf_op jit(solution)/shard_map/ppermute | solution.py:871
  104.6 1.7 %collective-permute-start.34 = (bf16[2,64,256]{2,1,0:T(8,128)(2,1)S(1)}, bf16[2,64,256]{2,1,0:T(8,128)(2,1)S(1)}, u32[]{:S(2)}, u32[]{:S(2)}) collective-permute-start(bf16[2,64,256]{2,1,0:T(8,128)(2,1)S(1)} %get-tuple-element.292), channel_id=1, source_target_pairs={{0,2},{1,3},{2,0},{3,1},{4,6},{5,7},{6,4},{7,5},{8,10},{9,11},{10,... | collective-permute-start | bytes 196616 | tf_op jit(solution)/shard_map/ppermute | solution.py:871
  108.0 2.0 %fetch.5 = (f32[128,1024]{1,0:T(8,128)S(1)}, bf16[128,1024]{1,0:T(8,128)(2,1)S(1)}, bf16[128,1024]{1,0:T(8,128)(2,1)S(1)}, bf16[64,1024]{1,0:T(8,128)(2,1)S(1)},...) custom-call(f32[128,1024]{1,0:T(8,128)} %get-tuple-element.257.refs_, ...), custom_call_target="tpu_custom_call" | custom-call | flops 1000000000 | bytes 1048576 | tf_op jit(solution)/shard_map/fetch/pallas_call | solution.py:158
  110.1 5.5 %back_last.1 = (f32[128,1024]{1,0:T(8,128)S(1)}, bf16[128,640]{1,0:T(8,128)(2,1)}) custom-call(bf16[128,512]{1,0:T(8,128)(2,1)S(1)} %add_convert_fusion.refs_0_, bf16[128,512]{1,0:T(8,128)(2,1)S(1)} %collective-permute-done.29.refs_1_, f32[128,1024]{1,0:T(8,128)S(1)} %get-tuple-element.270.refs_2_, ...), custom_call_target="tpu_custom_call", output_to_operand_aliasing={{1}: (28, {})} | custom-call | flops 10000000000 | bytes 1048576 | tf_op jit(solution)/shard_map/back_last/pallas_call | solution.py:128
  115.6 4.9 %all-to-all-start.1 = ((bf16[8,16,640]{2,1,0:T(8,128)(2,1)}), bf16[8,16,640]{2,1,0:T(8,128)(2,1)S(1)}, u32[]{:S(2)}, u32[]{:S(2)}) async-start(bf16[8,16,640]{2,1,0:T(8,128)(2,1)} %bitcast.72), calls=%async_computation.1 | async-start | bytes 327680 | tf_op jit(solution)/shard_map/all_to_all | solution.py:848
  120.7 3.0 %collective-permute-start.36 = (bf16[64,256]{1,0:T(8,128)(2,1)S(1)}, bf16[64,256]{1,0:T(8,128)(2,1)S(1)}, u32[]{:S(2)}, u32[]{:S(2)}) collective-permute-start(bf16[64,256]{1,0:T(8,128)(2,1)S(1)} %slice_bitcast_fusion.4), channel_id=1, source_target_pairs={{0,4},{1,5},{2,6},{3,7},{4,0},{5,1},{6,2},{7,3},{8,12},{9,13},{10,... | collective-permute-start | bytes 98312 | tf_op jit(solution)/shard_map/ppermute | solution.py:871
  125.1 3.4 %all-to-all-done.1.refs_0_ = bf16[8,16,640]{2,1,0:T(8,128)(2,1)S(1)} async-done(((bf16[8,16,640]{2,1,0:T(8,128)(2,1)}), bf16[8,16,640]{2,1,0:T(8,128)(2,1)S(1)}, u32[]{:S(2)}, u32[]{:S(2)}) %all-to-all-start.1) | async-done | bytes 163872 | tf_op jit(solution)/shard_map/all_to_all | solution.py:848
  132.8 1.7 %adam.1 = (f32[16,3000]{1,0:T(8,128)}, f32[16,3000]{1,0:T(8,128)}, f32[16,3000]{1,0:T(8,128)}, f32[16,3000]{1,0:T(8,128)}, bf16[16,3000]{1,0:T(8,128)(2,1)}) custom-call(s32[2]{0:T(128)S(1)} %pad_add_fusion.refs_0_, f32[16,3000]{1,0:T(8,128)S(1)} %bitcast.41, f32[16,3000]{1,0:T(8,128)S(1)} %bitcast.42, f32[16,3000]{1,0:T(8,128)S(1)} %bitcast.43, ...), custom_call_target="tpu_custom_call" | custom-call | flops 100000000 | bytes 1048576 | tf_op jit(solution)/shard_map/adam/pallas_call | solution.py:128
  (118 shorter events, 35.8 us)
Async XLA Ops:
  7.4 8.8 %collective-permute-start.3 = (bf16[2,16,256]{2,1,0:T(8,128)(2,1)S(1)}, bf16[2,16,256]{2,1,0:T(8,128)(2,1)S(1)}, u32[]{:S(2)}, u32[]{:S(2)}) collective-permute-start(bf16[2,16,256]{2,1,0:T(8,128)(2,1)S(1)} %constant_dynamic-update-slice_fusion), channel_id=1, source_target_pairs={{0,3},{1,2},{2,1},{3,0},{4,7},{5,6},{6,5},{7,4},{8,11},{9,10},{10,... | collective-permute-start | bytes 49160 | tf_op jit(solution)/shard_map/ppermute | solution.py:871
  10.3 6.9 %collective-permute-start.2 = (bf16[2,16,256]{2,1,0:T(8,128)(2,1)S(1)}, bf16[2,16,256]{2,1,0:T(8,128)(2,1)S(1)}, u32[]{:S(2)}, u32[]{:S(2)}) collective-permute-start(bf16[2,16,256]{2,1,0:T(8,128)(2,1)S(1)} %constant_dynamic-update-slice_fusion), channel_id=1, source_target_pairs={{0,2},{1,3},{2,0},{3,1},{4,6},{5,7},{6,4},{7,5},{8,10},{9,11},{10,... | collective-permute-start | bytes 49160 | tf_op jit(solution)/shard_map/ppermute | solution.py:871
  10.7 6.5 %collective-permute-start.1 = (bf16[2,16,256]{2,1,0:T(8,128)(2,1)S(1)}, bf16[2,16,256]{2,1,0:T(8,128)(2,1)S(1)}, u32[]{:S(2)}, u32[]{:S(2)}) collective-permute-start(bf16[2,16,256]{2,1,0:T(8,128)(2,1)S(1)} %constant_dynamic-update-slice_fusion), channel_id=1, source_target_pairs={{0,1},{1,0},{2,3},{3,2},{4,5},{5,4},{6,7},{7,6},{8,9},{9,8},{10,11... | collective-permute-start | bytes 49160 | tf_op jit(solution)/shard_map/ppermute | solution.py:871
  13.7 9.7 %collective-permute-start.7 = (bf16[2,144,256]{2,1,0:T(8,128)(2,1)S(1)}, bf16[2,144,256]{2,1,0:T(8,128)(2,1)S(1)}, u32[]{:S(2)}, u32[]{:S(2)}) collective-permute-start(bf16[2,144,256]{2,1,0:T(8,128)(2,1)S(1)} %constant_dynamic-update-slice_fusion.2), channel_id=1, source_target_pairs={{0,3},{1,2},{2,1},{3,0},{4,7},{5,6},{6,5},{7,4},{8,11},{9,10},{10,... | collective-permute-start | bytes 442376 | tf_op jit(solution)/shard_map/ppermute | solution.py:871
  15.2 8.2 %collective-permute-start.6 = (bf16[2,144,256]{2,1,0:T(8,128)(2,1)S(1)}, bf16[2,144,256]{2,1,0:T(8,128)(2,1)S(1)}, u32[]{:S(2)}, u32[]{:S(2)}) collective-permute-start(bf16[2,144,256]{2,1,0:T(8,128)(2,1)S(1)} %constant_dynamic-update-slice_fusion.2), channel_id=1, source_target_pairs={{0,2},{1,3},{2,0},{3,1},{4,6},{5,7},{6,4},{7,5},{8,10},{9,11},{10,... | collective-permute-start | bytes 442376 | tf_op jit(solution)/shard_map/ppermute | solution.py:871
  16.2 7.3 %collective-permute-start.5 = (bf16[2,144,256]{2,1,0:T(8,128)(2,1)S(1)}, bf16[2,144,256]{2,1,0:T(8,128)(2,1)S(1)}, u32[]{:S(2)}, u32[]{:S(2)}) collective-permute-start(bf16[2,144,256]{2,1,0:T(8,128)(2,1)S(1)} %constant_dynamic-update-slice_fusion.2), channel_id=1, source_target_pairs={{0,1},{1,0},{2,3},{3,2},{4,5},{5,4},{6,7},{7,6},{8,9},{9,8},{10,11... | collective-permute-start | bytes 442376 | tf_op jit(solution)/shard_map/ppermute | solution.py:871
  27.9 7.2 %collective-permute-start.13 = (bf16[128,384]{1,0:T(8,128)(2,1)S(1)}, bf16[128,384]{1,0:T(8,128)(2,1)S(1)}, u32[]{:S(2)}, u32[]{:S(2)}) collective-permute-start(bf16[128,384]{1,0:T(8,128)(2,1)S(1)} %get-tuple-element.168.refs_2_), channel_id=1, source_target_pairs={{0,16},{8,24},{16,0},{24,8},{1,17},{9,25},{17,1},{25,9},{2,18},{10... | collective-permute-start | bytes 294920 | tf_op jit(solution)/shard_map/ppermute | solution.py:871
  31.1 8.1 %collective-permute-start.11 = (bf16[512,128]{1,0:T(8,128)(2,1)S(1)}, bf16[512,128]{1,0:T(8,128)(2,1)S(1)}, u32[]{:S(2)}, u32[]{:S(2)}) collective-permute-start(bf16[512,128]{1,0:T(8,128)(2,1)S(1)} %add_convert_fusion.3.refs_0_), channel_id=1, source_target_pairs={{0,4},{1,5},{2,6},{3,7},{4,0},{5,1},{6,2},{7,3},{8,12},{9,13},{10,... | collective-permute-start | bytes 393224 | tf_op jit(solution)/shard_map/ppermute | solution.py:871
  46.8 7.2 %collective-permute-start.17 = (bf16[512,128]{1,0:T(8,128)(2,1)S(1)}, bf16[512,128]{1,0:T(8,128)(2,1)S(1)}, u32[]{:S(2)}, u32[]{:S(2)}) collective-permute-start(bf16[512,128]{1,0:T(8,128)(2,1)S(1)} %get-tuple-element.183), channel_id=1, source_target_pairs={{0,3},{1,2},{2,1},{3,0},{4,7},{5,6},{6,5},{7,4},{8,11},{9,10},{10,... | collective-permute-start | bytes 393224 | tf_op jit(solution)/shard_map/ppermute | solution.py:871
  46.9 8.2 %collective-permute-start.16 = (bf16[512,128]{1,0:T(8,128)(2,1)S(1)}, bf16[512,128]{1,0:T(8,128)(2,1)S(1)}, u32[]{:S(2)}, u32[]{:S(2)}) collective-permute-start(bf16[512,128]{1,0:T(8,128)(2,1)S(1)} %get-tuple-element.183), channel_id=1, source_target_pairs={{0,2},{1,3},{2,0},{3,1},{4,6},{5,7},{6,4},{7,5},{8,10},{9,11},{10,... | collective-permute-start | bytes 393224 | tf_op jit(solution)/shard_map/ppermute | solution.py:871
  50.3 7.2 %collective-permute-start.20 = (bf16[128,384]{1,0:T(8,128)(2,1)S(1)}, bf16[128,384]{1,0:T(8,128)(2,1)S(1)}, u32[]{:S(2)}, u32[]{:S(2)}) collective-permute-start(bf16[128,384]{1,0:T(8,128)(2,1)S(1)} %get-tuple-element.187.refs_1_), channel_id=1, source_target_pairs={{0,16},{8,24},{16,0},{24,8},{1,17},{9,25},{17,1},{25,9},{2,18},{10... | collective-permute-start | bytes 294920 | tf_op jit(solution)/shard_map/ppermute | solution.py:871
  55.4 7.9 %collective-permute-start.18 = (bf16[512,128]{1,0:T(8,128)(2,1)S(1)}, bf16[512,128]{1,0:T(8,128)(2,1)S(1)}, u32[]{:S(2)}, u32[]{:S(2)}) collective-permute-start(bf16[512,128]{1,0:T(8,128)(2,1)S(1)} %add_convert_fusion.2.refs_1_), channel_id=1, source_target_pairs={{0,4},{1,5},{2,6},{3,7},{4,0},{5,1},{6,2},{7,3},{8,12},{9,13},{10,... | collective-permute-start | bytes 393224 | tf_op jit(solution)/shard_map/ppermute | solution.py:871
  66.8 7.4 %collective-permute-start.24 = (bf16[128,512]{1,0:T(8,128)(2,1)S(1)}, bf16[128,512]{1,0:T(8,128)(2,1)S(1)}, u32[]{:S(2)}, u32[]{:S(2)}) collective-permute-start(bf16[128,512]{1,0:T(8,128)(2,1)S(1)} %get-tuple-element.207), channel_id=1, source_target_pairs={{0,3},{1,2},{2,1},{3,0},{4,7},{5,6},{6,5},{7,4},{8,11},{9,10},{10,... | collective-permute-start | bytes 393224 | tf_op jit(solution)/shard_map/ppermute | solution.py:871
  66.9 8.5 %collective-permute-start.23 = (bf16[128,512]{1,0:T(8,128)(2,1)S(1)}, bf16[128,512]{1,0:T(8,128)(2,1)S(1)}, u32[]{:S(2)}, u32[]{:S(2)}) collective-permute-start(bf16[128,512]{1,0:T(8,128)(2,1)S(1)} %get-tuple-element.207), channel_id=1, source_target_pairs={{0,2},{1,3},{2,0},{3,1},{4,6},{5,7},{6,4},{7,5},{8,10},{9,11},{10,... | collective-permute-start | bytes 393224 | tf_op jit(solution)/shard_map/ppermute | solution.py:871
  69.3 6.6 %collective-permute-start.22 = (bf16[128,512]{1,0:T(8,128)(2,1)S(1)}, bf16[128,512]{1,0:T(8,128)(2,1)S(1)}, u32[]{:S(2)}, u32[]{:S(2)}) collective-permute-start(bf16[128,512]{1,0:T(8,128)(2,1)S(1)} %get-tuple-element.207), channel_id=1, source_target_pairs={{0,1},{1,0},{2,3},{3,2},{4,5},{5,4},{6,7},{7,6},{8,9},{9,8},{10,11... | collective-permute-start | bytes 393224 | tf_op jit(solution)/shard_map/ppermute | solution.py:871
  75.9 8.4 %collective-permute-start.25 = (bf16[128,512]{1,0:T(8,128)(2,1)S(1)}, bf16[128,512]{1,0:T(8,128)(2,1)S(1)}, u32[]{:S(2)}, u32[]{:S(2)}) collective-permute-start(bf16[128,512]{1,0:T(8,128)(2,1)S(1)} %add_convert_fusion.1.refs_1_), channel_id=1, source_target_pairs={{0,4},{1,5},{2,6},{3,7},{4,0},{5,1},{6,2},{7,3},{8,12},{9,13},{10,... | collective-permute-start | bytes 393224 | tf_op jit(solution)/shard_map/ppermute | solution.py:871
  76.2 21.4 %all-to-all-start = ((bf16[8,16,1280]{2,1,0:T(8,128)(2,1)}), bf16[8,16,1280]{2,1,0:T(8,128)(2,1)S(1)}, u32[]{:S(2)}, u32[]{:S(2)}) async-start(bf16[8,16,1280]{2,1,0:T(8,128)(2,1)} %bitcast.15), calls=%async_computation | async-start | bytes 655360 | tf_op jit(solution)/shard_map/all_to_all | solution.py:848
  91.5 7.8 %collective-permute-start.28 = (bf16[128,512]{1,0:T(8,128)(2,1)S(1)}, bf16[128,512]{1,0:T(8,128)(2,1)S(1)}, u32[]{:S(2)}, u32[]{:S(2)}) collective-permute-start(bf16[128,512]{1,0:T(8,128)(2,1)S(1)} %get-tuple-element.254), channel_id=1, source_target_pairs={{0,3},{1,2},{2,1},{3,0},{4,7},{5,6},{6,5},{7,4},{8,11},{9,10},{10,... | collective-permute-start | bytes 393224 | tf_op jit(solution)/shard_map/ppermute | solution.py:871
  93.4 6.5 %collective-permute-start.27 = (bf16[128,512]{1,0:T(8,128)(2,1)S(1)}, bf16[128,512]{1,0:T(8,128)(2,1)S(1)}, u32[]{:S(2)}, u32[]{:S(2)}) collective-permute-start(bf16[128,512]{1,0:T(8,128)(2,1)S(1)} %get-tuple-element.254), channel_id=1, source_target_pairs={{0,2},{1,3},{2,0},{3,1},{4,6},{5,7},{6,4},{7,5},{8,10},{9,11},{10,... | collective-permute-start | bytes 393224 | tf_op jit(solution)/shard_map/ppermute | solution.py:871
  94.0 6.6 %collective-permute-start.26 = (bf16[128,512]{1,0:T(8,128)(2,1)S(1)}, bf16[128,512]{1,0:T(8,128)(2,1)S(1)}, u32[]{:S(2)}, u32[]{:S(2)}) collective-permute-start(bf16[128,512]{1,0:T(8,128)(2,1)S(1)} %get-tuple-element.254), channel_id=1, source_target_pairs={{0,1},{1,0},{2,3},{3,2},{4,5},{5,4},{6,7},{7,6},{8,9},{9,8},{10,11... | collective-permute-start | bytes 393224 | tf_op jit(solution)/shard_map/ppermute | solution.py:871
  97.7 6.9 %collective-permute-start.32 = (bf16[128,384]{1,0:T(8,128)(2,1)S(1)}, bf16[128,384]{1,0:T(8,128)(2,1)S(1)}, u32[]{:S(2)}, u32[]{:S(2)}) collective-permute-start(bf16[128,384]{1,0:T(8,128)(2,1)S(1)} %get-tuple-element.303), channel_id=1, source_target_pairs={{0,24},{8,16},{16,8},{24,0},{1,25},{9,17},{17,9},{25,1},{2,26},{10... | collective-permute-start | bytes 294920 | tf_op jit(solution)/shard_map/ppermute | solution.py:871
  97.8 8.5 %collective-permute-start.31 = (bf16[128,384]{1,0:T(8,128)(2,1)S(1)}, bf16[128,384]{1,0:T(8,128)(2,1)S(1)}, u32[]{:S(2)}, u32[]{:S(2)}) collective-permute-start(bf16[128,384]{1,0:T(8,128)(2,1)S(1)} %get-tuple-element.304), channel_id=1, source_target_pairs={{0,16},{8,24},{16,0},{24,8},{1,17},{9,25},{17,1},{25,9},{2,18},{10... | collective-permute-start | bytes 294920 | tf_op jit(solution)/shard_map/ppermute | solution.py:871
  99.3 8.1 %collective-permute-start.30 = (bf16[128,384]{1,0:T(8,128)(2,1)S(1)}, bf16[128,384]{1,0:T(8,128)(2,1)S(1)}, u32[]{:S(2)}, u32[]{:S(2)}) collective-permute-start(bf16[128,384]{1,0:T(8,128)(2,1)S(1)} %get-tuple-element.305), channel_id=1, source_target_pairs={{0,8},{8,0},{16,24},{24,16},{1,9},{9,1},{17,25},{25,17},{2,10},{10... | collective-permute-start | bytes 294920 | tf_op jit(solution)/shard_map/ppermute | solution.py:871
  100.6 9.5 %collective-permute-start.29 = (bf16[128,512]{1,0:T(8,128)(2,1)S(1)}, bf16[128,512]{1,0:T(8,128)(2,1)S(1)}, u32[]{:S(2)}, u32[]{:S(2)}) collective-permute-start(bf16[128,512]{1,0:T(8,128)(2,1)S(1)} %add_convert_fusion.refs_0_), channel_id=1, source_target_pairs={{0,4},{1,5},{2,6},{3,7},{4,0},{5,1},{6,2},{7,3},{8,12},{9,13},{10,... | collective-permute-start | bytes 393224 | tf_op jit(solution)/shard_map/ppermute | solution.py:871
  103.1 17.3 %collective-permute-start.33 = (bf16[2,64,256]{2,1,0:T(8,128)(2,1)S(1)}, bf16[2,64,256]{2,1,0:T(8,128)(2,1)S(1)}, u32[]{:S(2)}, u32[]{:S(2)}) collective-permute-start(bf16[2,64,256]{2,1,0:T(8,128)(2,1)S(1)} %get-tuple-element.291), channel_id=1, source_target_pairs={{0,1},{1,0},{2,3},{3,2},{4,5},{5,4},{6,7},{7,6},{8,9},{9,8},{10,11... | collective-permute-start | bytes 196616 | tf_op jit(solution)/shard_map/ppermute | solution.py:871
  104.6 15.9 %collective-permute-start.34 = (bf16[2,64,256]{2,1,0:T(8,128)(2,1)S(1)}, bf16[2,64,256]{2,1,0:T(8,128)(2,1)S(1)}, u32[]{:S(2)}, u32[]{:S(2)}) collective-permute-start(bf16[2,64,256]{2,1,0:T(8,128)(2,1)S(1)} %get-tuple-element.292), channel_id=1, source_target_pairs={{0,2},{1,3},{2,0},{3,1},{4,6},{5,7},{6,4},{7,5},{8,10},{9,11},{10,... | collective-permute-start | bytes 196616 | tf_op jit(solution)/shard_map/ppermute | solution.py:871
  106.3 14.1 %collective-permute-start.35 = (bf16[2,64,256]{2,1,0:T(8,128)(2,1)S(1)}, bf16[2,64,256]{2,1,0:T(8,128)(2,1)S(1)}, u32[]{:S(2)}, u32[]{:S(2)}) collective-permute-start(bf16[2,64,256]{2,1,0:T(8,128)(2,1)S(1)} %get-tuple-element.293), channel_id=1, source_target_pairs={{0,3},{1,2},{2,1},{3,0},{4,7},{5,6},{6,5},{7,4},{8,11},{9,10},{10,... | collective-permute-start | bytes 196616 | tf_op jit(solution)/shard_map/ppermute | solution.py:871
  115.6 13.0 %all-to-all-start.1 = ((bf16[8,16,640]{2,1,0:T(8,128)(2,1)}), bf16[8,16,640]{2,1,0:T(8,128)(2,1)S(1)}, u32[]{:S(2)}, u32[]{:S(2)}) async-start(bf16[8,16,640]{2,1,0:T(8,128)(2,1)} %bitcast.72), calls=%async_computation.1 | async-start | bytes 327680 | tf_op jit(solution)/shard_map/all_to_all | solution.py:848
  120.6 9.3 %collective-permute-start.42 = (bf16[16,1280]{1,0:T(8,128)(2,1)S(1)}, bf16[16,1280]{1,0:T(8,128)(2,1)S(1)}, u32[]{:S(2)}, u32[]{:S(2)}) collective-permute-start(bf16[16,1280]{1,0:T(8,128)(2,1)S(1)} %sum_parts.3.refs_8_), channel_id=1, source_target_pairs={{0,24},{8,16},{16,8},{24,0},{1,25},{9,17},{17,9},{25,1},{2,26},{10... | collective-permute-start | bytes 122888 | tf_op jit(solution)/shard_map/ppermute | solution.py:871
  120.7 8.3 %collective-permute-start.36 = (bf16[64,256]{1,0:T(8,128)(2,1)S(1)}, bf16[64,256]{1,0:T(8,128)(2,1)S(1)}, u32[]{:S(2)}, u32[]{:S(2)}) collective-permute-start(bf16[64,256]{1,0:T(8,128)(2,1)S(1)} %slice_bitcast_fusion.4), channel_id=1, source_target_pairs={{0,4},{1,5},{2,6},{3,7},{4,0},{5,1},{6,2},{7,3},{8,12},{9,13},{10,... | collective-permute-start | bytes 98312 | tf_op jit(solution)/shard_map/ppermute | solution.py:871
  123.6 8.5 %collective-permute-start.41 = (bf16[16,1280]{1,0:T(8,128)(2,1)S(1)}, bf16[16,1280]{1,0:T(8,128)(2,1)S(1)}, u32[]{:S(2)}, u32[]{:S(2)}) collective-permute-start(bf16[16,1280]{1,0:T(8,128)(2,1)S(1)} %sum_parts.3.refs_8_), channel_id=1, source_target_pairs={{0,16},{8,24},{16,0},{24,8},{1,17},{9,25},{17,1},{25,9},{2,18},{10... | collective-permute-start | bytes 122888 | tf_op jit(solution)/shard_map/ppermute | solution.py:871
  124.8 7.4 %collective-permute-start.40 = (bf16[16,1280]{1,0:T(8,128)(2,1)S(1)}, bf16[16,1280]{1,0:T(8,128)(2,1)S(1)}, u32[]{:S(2)}, u32[]{:S(2)}) collective-permute-start(bf16[16,1280]{1,0:T(8,128)(2,1)S(1)} %sum_parts.3.refs_8_), channel_id=1, source_target_pairs={{0,8},{8,0},{16,24},{24,16},{1,9},{9,1},{17,25},{25,17},{2,10},{10... | collective-permute-start | bytes 122888 | tf_op jit(solution)/shard_map/ppermute | solution.py:871
  (26 other events, 168.8 us)

commit v8 on v7

--- a/solution.py
+++ b/solution.py
@@ -472,7 +472,7 @@
     table = cut(low(act), width)
     total = jnp.zeros((FOLD, length), F32)
     items = in_ref.shape[1]
-    chunk = min(CHUNK, items)
+    chunk = min(CHUNK // 2, items)
     for start in range(0, items, chunk):
         cols = slice(start, start + chunk)
         in_high, in_low = high_low(in_ref[:, cols], length)
@@ -822,9 +822,14 @@
     groups, _, lanes = hold.shape
     last, others = pieces[:groups], pieces[groups:]
     small = sum_list([piece[:, :PAD] for piece in last])
-    for k, piece in enumerate(last):
-        hold[me[1] ^ k] = piece[:, PAD:].astype(F32)
-    joint = jnp.concatenate([hold[g] for g in range(groups)], axis=1)
+    parts = [piece[:, PAD:].astype(F32) for piece in last]
+    joint = []
+    for g in range(groups):
+        value = parts[0]
+        for k in range(1, groups):
+            value = jnp.where((me[1] ^ k) == g, parts[k], value)
+        joint.append(value)
+    joint = jnp.concatenate(joint, axis=1)
     grad = jnp.concatenate(
         [small[:, :SMALL], joint[:, PAD:], joint[:, :SMALL], sum_list(others)], axis=1
     )

time: 135 us -> 135 us (level)
  transfers between devices with their start and end apart: 45 -> 45, of which waited for: 20 -> 21; matrix products, arithmetic and copies ran while one was open for 1% -> 1% of each run, Pallas kernels for 27% -> 27%
where the time goes in v8:
time: 135 us
  starting transfers between devices  54.2 us (40%)
  Pallas kernels  50 us (37%)
  waiting for transfers between devices  28 us (21%)
    ppermute x43, starting transfers between devices, moved(): return lax.ppermute(table, axis, [(i, i ^ step) for i in range(owners)])  44.4 us
    pallas_call x18, Pallas kernels, call(): pl.pallas_call(kernel, out_shape=outs, in_specs=[pl.BlockSpec(memory_spac...  44.1 us
    ppermute x43, waiting for transfers between devices, moved(): return lax.ppermute(table, axis, [(i, i ^ step) for i in range(owners)])  24.6 us
    all_to_all x2, starting transfers between devices, exchange(): return lax.all_to_all(pieces, 'shard', split_axis=0, concat_axis=0)  9.77 us
    pallas_call x3, Pallas kernels, fetch(): pl.pallas_call(kernel, out_shape=[sds(x.shape, x.dtype) for x in arrays],...  5.89 us
    all_to_all x2, waiting for transfers between devices, exchange(): return lax.all_to_all(pieces, 'shard', split_axis=0, concat_axis=0)  3.44 us
  transfers between devices with their start and end apart: 45, of which 21 were waited for; matrix products, arithmetic and copies ran while one was open for 1% of the time, Pallas kernels for 27%

profile of v8, /device:TPU:0, one launch (start us, length us, event | category | flops | bytes accessed | tf_op | source)
XLA Modules:
  0.0 134.6 jit_solution(9795386735832550016)
XLA Ops:
  1.4 4.1 %collective-permute-start = (bf16[1,16,256]{2,1,0:T(8,128)(2,1)S(1)}, bf16[1,16,256]{2,1,0:T(8,128)(2,1)S(1)}, u32[]{:S(2)}, u32[]{:S(2)}) collective-permute-start(bf16[1,16,256]{2,1,0:T(8,128)(2,1)S(1)} %pack_first.1.refs_10_), channel_id=1, source_target_pairs={{0,4},{1,5},{2,6},{3,7},{4,0},{5,1},{6,2},{7,3},{8,12},{9,13},{10,... | collective-permute-start | bytes 24584 | tf_op jit(solution)/shard_map/ppermute | solution.py:876
  5.6 1.7 %pack_cargo.1 = (bf16[1,144,256]{2,1,0:T(8,128)(2,1)S(1)}, s32[1,1024]{1,0:T(1,128)S(1)}, s32[1,1024]{1,0:T(1,128)S(1)}) custom-call(s32[2]{0:T(128)S(1)} %pad_add_fusion.refs_0_, f32[16,3000]{1,0:T(8,128)} %bitcast.40, bf16[64,256]{1,0:T(8,128)(2,1)} %refs_2_, s32[1,64]{1,0:T(1,128)} %bitcast.77, s32[1,1024]{1,0:T(1,128)} %bitcast.73, s32[1,1024]{1,0:T(1,128)} %bitcast.74, ...), custom_call_target="tpu_custom_call" | custom-call | flops 10000000 | bytes 1048576 | tf_op jit(solution)/shard_map/pack_cargo/pallas_call | solution.py:128
  7.4 2.9 %collective-permute-start.3 = (bf16[2,16,256]{2,1,0:T(8,128)(2,1)S(1)}, bf16[2,16,256]{2,1,0:T(8,128)(2,1)S(1)}, u32[]{:S(2)}, u32[]{:S(2)}) collective-permute-start(bf16[2,16,256]{2,1,0:T(8,128)(2,1)S(1)} %constant_dynamic-update-slice_fusion), channel_id=1, source_target_pairs={{0,3},{1,2},{2,1},{3,0},{4,7},{5,6},{6,5},{7,4},{8,11},{9,10},{10,... | collective-permute-start | bytes 49160 | tf_op jit(solution)/shard_map/ppermute | solution.py:876
  11.0 2.8 %collective-permute-done.4.refs_2_ = bf16[1,144,256]{2,1,0:T(8,128)(2,1)S(1)} collective-permute-done((bf16[1,144,256]{2,1,0:T(8,128)(2,1)S(1)}, bf16[1,144,256]{2,1,0:T(8,128)(2,1)S(1)}, u32[]{:S(2)}, u32[]{:S(2)}) %collective-permute-start.4) | collective-permute-done | bytes 73760 | tf_op jit(solution)/shard_map/ppermute | solution.py:876
  13.7 1.5 %collective-permute-start.7 = (bf16[2,144,256]{2,1,0:T(8,128)(2,1)S(1)}, bf16[2,144,256]{2,1,0:T(8,128)(2,1)S(1)}, u32[]{:S(2)}, u32[]{:S(2)}) collective-permute-start(bf16[2,144,256]{2,1,0:T(8,128)(2,1)S(1)} %constant_dynamic-update-slice_fusion.2), channel_id=1, source_target_pairs={{0,3},{1,2},{2,1},{3,0},{4,7},{5,6},{6,5},{7,4},{8,11},{9,10},{10,... | collective-permute-start | bytes 442376 | tf_op jit(solution)/shard_map/ppermute | solution.py:876
  17.3 6.1 %first_half.1 = (bf16[128,256]{1,0:T(8,128)(2,1)S(1)}, f32[128,1024]{1,0:T(8,128)}, bf16[128,1024]{1,0:T(8,128)(2,1)}, bf16[128,1024]{1,0:T(8,128)(2,1)}, bf16[6...) custom-call(s32[2]{0:T(128)S(1)} %pad_add_fusion.refs_0_, ...), custom_call_target="tpu_custom_call" | custom-call | flops 8000000000 | bytes 1048576 | tf_op jit(solution)/shard_map/first_half/pallas_call | solution.py:128
  23.4 1.6 %collective-permute-start.10 = (bf16[512,128]{1,0:T(8,128)(2,1)S(1)}, bf16[512,128]{1,0:T(8,128)(2,1)S(1)}, u32[]{:S(2)}, u32[]{:S(2)}) collective-permute-start(bf16[512,128]{1,0:T(8,128)(2,1)S(1)} %get-tuple-element.161), channel_id=1, source_target_pairs={{0,3},{1,2},{2,1},{3,0},{4,7},{5,6},{6,5},{7,4},{8,11},{9,10},{10,... | collective-permute-start | bytes 393224 | tf_op jit(solution)/shard_map/ppermute | solution.py:876
  27.8 1.6 %collective-permute-start.13 = (bf16[128,384]{1,0:T(8,128)(2,1)S(1)}, bf16[128,384]{1,0:T(8,128)(2,1)S(1)}, u32[]{:S(2)}, u32[]{:S(2)}) collective-permute-start(bf16[128,384]{1,0:T(8,128)(2,1)S(1)} %get-tuple-element.168.refs_2_), channel_id=1, source_target_pairs={{0,16},{8,24},{16,0},{24,8},{1,17},{9,25},{17,1},{25,9},{2,18},{10... | collective-permute-start | bytes 294920 | tf_op jit(solution)/shard_map/ppermute | solution.py:876
  32.8 2.2 %collective-permute-done.13.refs_4_ = bf16[128,384]{1,0:T(8,128)(2,1)S(1)} collective-permute-done((bf16[128,384]{1,0:T(8,128)(2,1)S(1)}, bf16[128,384]{1,0:T(8,128)(2,1)S(1)}, u32[]{:S(2)}, u32[]{:S(2)}) %collective-permute-start.13) | collective-permute-done | bytes 98336 | tf_op jit(solution)/shard_map/ppermute | solution.py:876
  36.3 2.8 %collective-permute-done.11.refs_1_ = bf16[512,128]{1,0:T(8,128)(2,1)S(1)} collective-permute-done((bf16[512,128]{1,0:T(8,128)(2,1)S(1)}, bf16[512,128]{1,0:T(8,128)(2,1)S(1)}, u32[]{:S(2)}, u32[]{:S(2)}) %collective-permute-start.11) | collective-permute-done | bytes 131104 | tf_op jit(solution)/shard_map/ppermute | solution.py:876
  39.1 7.5 %middle_half.1 = (bf16[512,128]{1,0:T(8,128)(2,1)}, bf16[512,256]{1,0:T(8,128)(2,1)}, bf16[512,256]{1,0:T(8,128)(2,1)}, f32[512,256]{1,0:T(8,128)}, bf16[512,256...) custom-call(bf16[512,128]{1,0:T(8,128)(2,1)S(1)} %add_convert_fusion, ...), custom_call_target="tpu_custom_call" | custom-call | flops 10000000000 | bytes 1048576 | tf_op jit(solution)/shard_map/middle_half/pallas_call | solution.py:128
  46.7 2.5 %collective-permute-start.16 = (bf16[512,128]{1,0:T(8,128)(2,1)S(1)}, bf16[512,128]{1,0:T(8,128)(2,1)S(1)}, u32[]{:S(2)}, u32[]{:S(2)}) collective-permute-start(bf16[512,128]{1,0:T(8,128)(2,1)S(1)} %get-tuple-element.183), channel_id=1, source_target_pairs={{0,2},{1,3},{2,0},{3,1},{4,6},{5,7},{6,4},{7,5},{8,10},{9,11},{10,... | collective-permute-start | bytes 393224 | tf_op jit(solution)/shard_map/ppermute | solution.py:876
  50.2 1.5 %collective-permute-start.20 = (bf16[128,384]{1,0:T(8,128)(2,1)S(1)}, bf16[128,384]{1,0:T(8,128)(2,1)S(1)}, u32[]{:S(2)}, u32[]{:S(2)}) collective-permute-start(bf16[128,384]{1,0:T(8,128)(2,1)S(1)} %get-tuple-element.187.refs_1_), channel_id=1, source_target_pairs={{0,16},{8,24},{16,0},{24,8},{1,17},{9,25},{17,1},{25,9},{2,18},{10... | collective-permute-start | bytes 294920 | tf_op jit(solution)/shard_map/ppermute | solution.py:876
  51.7 2.1 %collective-permute-done.17 = bf16[512,128]{1,0:T(8,128)(2,1)S(1)} collective-permute-done((bf16[512,128]{1,0:T(8,128)(2,1)S(1)}, bf16[512,128]{1,0:T(8,128)(2,1)S(1)}, u32[]{:S(2)}, u32[]{:S(2)}) %collective-permute-start.17) | collective-permute-done | bytes 131104 | tf_op jit(solution)/shard_map/ppermute | solution.py:876
  55.5 1.9 %collective-permute-done.20.refs_3_ = bf16[128,384]{1,0:T(8,128)(2,1)S(1)} collective-permute-done((bf16[128,384]{1,0:T(8,128)(2,1)S(1)}, bf16[128,384]{1,0:T(8,128)(2,1)S(1)}, u32[]{:S(2)}, u32[]{:S(2)}) %collective-permute-start.20) | collective-permute-done | bytes 98336 | tf_op jit(solution)/shard_map/ppermute | solution.py:876
  59.7 3.5 %collective-permute-done.18.refs_2_ = bf16[512,128]{1,0:T(8,128)(2,1)S(1)} collective-permute-done((bf16[512,128]{1,0:T(8,128)(2,1)S(1)}, bf16[512,128]{1,0:T(8,128)(2,1)S(1)}, u32[]{:S(2)}, u32[]{:S(2)}) %collective-permute-start.18) | collective-permute-done | bytes 131104 | tf_op jit(solution)/shard_map/ppermute | solution.py:876
  63.2 3.4 %turn.1 = (bf16[512,128]{1,0:T(8,128)(2,1)S(1)}, bf16[512,256]{1,0:T(8,128)(2,1)S(1)}, bf16[512,256]{1,0:T(8,128)(2,1)S(1)}, f32[128,1024]{1,0:T(8,128)S(1)}, bf...) custom-call(s32[2]{0:T(128)S(1)} %pad_add_fusion.refs_0_, ...), custom_call_target="tpu_custom_call" | custom-call | flops 2000000000 | bytes 1048576 | tf_op jit(solution)/shard_map/turn/pallas_call | solution.py:128
  66.7 2.4 %collective-permute-start.23 = (bf16[128,512]{1,0:T(8,128)(2,1)S(1)}, bf16[128,512]{1,0:T(8,128)(2,1)S(1)}, u32[]{:S(2)}, u32[]{:S(2)}) collective-permute-start(bf16[128,512]{1,0:T(8,128)(2,1)S(1)} %get-tuple-element.207), channel_id=1, source_target_pairs={{0,2},{1,3},{2,0},{3,1},{4,6},{5,7},{6,4},{7,5},{8,10},{9,11},{10,... | collective-permute-start | bytes 393224 | tf_op jit(solution)/shard_map/ppermute | solution.py:876
  71.0 2.1 %large_grads.1 = bf16[128,1280]{1,0:T(8,128)(2,1)} custom-call(bf16[512,256]{1,0:T(8,128)(2,1)S(1)} %get-tuple-element.198.refs_0_, bf16[512,256]{1,0:T(8,128)(2,1)S(1)} %get-tuple-element.199.refs_1_, bf16[128,1024]{1,0:T(8,128)(2,1)S(1)} %get-tuple-element.200.refs_2_, s32[1,1024]{1,0:T(1,128)S(1)} %get-tuple-element.180.refs_20_.refs_6_.refs_3_.refs_32_.refs_4_, ...), custom_call_target="tpu_custom_call" | custom-call | flops 1000000000 | bytes 1048576 | tf_op jit(solution)/shard_map/large_grads/pallas_call | solution.py:128
  76.1 4.4 %all-to-all-start = ((bf16[8,16,1280]{2,1,0:T(8,128)(2,1)}), bf16[8,16,1280]{2,1,0:T(8,128)(2,1)S(1)}, u32[]{:S(2)}, u32[]{:S(2)}) async-start(bf16[8,16,1280]{2,1,0:T(8,128)(2,1)} %bitcast.15), calls=%async_computation | async-start | bytes 655360 | tf_op jit(solution)/shard_map/all_to_all | solution.py:853
  80.5 2.5 %fetch.4 = (f32[128,1024]{1,0:T(8,128)S(1)}, bf16[128,1024]{1,0:T(8,128)(2,1)S(1)}, bf16[128,1024]{1,0:T(8,128)(2,1)S(1)}, bf16[64,1024]{1,0:T(8,128)(2,1)S(1)},...) custom-call(f32[128,1024]{1,0:T(8,128)} %get-tuple-element.208.refs_, ...), custom_call_target="tpu_custom_call" | custom-call | flops 1000000000 | bytes 1048576 | tf_op jit(solution)/shard_map/fetch/pallas_call | solution.py:158
  84.1 7.2 %back_middle.1 = (bf16[128,256]{1,0:T(8,128)(2,1)S(1)}, bf16[128,512]{1,0:T(8,128)(2,1)S(1)}, bf16[512,256]{1,0:T(8,128)(2,1)S(1)}, bf16[512,256]{1,0:T(8,128)(2...) custom-call(s32[2]{0:T(128)S(1)} %pad_add_fusion.refs_0_, ...), custom_call_target="tpu_custom_call" | custom-call | flops 10000000000 | bytes 1048576 | tf_op jit(solution)/shard_map/back_middle/pallas_call | solution.py:128
  91.3 1.9 %collective-permute-start.28 = (bf16[128,512]{1,0:T(8,128)(2,1)S(1)}, bf16[128,512]{1,0:T(8,128)(2,1)S(1)}, u32[]{:S(2)}, u32[]{:S(2)}) collective-permute-start(bf16[128,512]{1,0:T(8,128)(2,1)S(1)} %get-tuple-element.254), channel_id=1, source_target_pairs={{0,3},{1,2},{2,1},{3,0},{4,7},{5,6},{6,5},{7,4},{8,11},{9,10},{10,... | collective-permute-start | bytes 393224 | tf_op jit(solution)/shard_map/ppermute | solution.py:876
  94.9 2.7 %large_pieces.1 = bf16[4,128,384]{2,1,0:T(8,128)(2,1)S(1)} custom-call(s32[2]{0:T(128)S(1)} %pad_add_fusion.refs_0_, bf16[512,256]{1,0:T(8,128)(2,1)S(1)} %get-tuple-element.246.refs_1_, bf16[512,256]{1,0:T(8,128)(2,1)S(1)} %get-tuple-element.247.refs_2_, bf16[128,1024]{1,0:T(8,128)(2,1)S(1)} %get-tuple-element.248.refs_3_, ...), custom_call_target="tpu_custom_call" | custom-call | flops 1000000000 | bytes 1048576 | tf_op jit(solution)/shard_map/large_pieces/pallas_call | solution.py:128
  100.5 2.1 %collective-permute-start.29 = (bf16[128,512]{1,0:T(8,128)(2,1)S(1)}, bf16[128,512]{1,0:T(8,128)(2,1)S(1)}, u32[]{:S(2)}, u32[]{:S(2)}) collective-permute-start(bf16[128,512]{1,0:T(8,128)(2,1)S(1)} %add_convert_fusion.refs_0_), channel_id=1, source_target_pairs={{0,4},{1,5},{2,6},{3,7},{4,0},{5,1},{6,2},{7,3},{8,12},{9,13},{10,... | collective-permute-start | bytes 393224 | tf_op jit(solution)/shard_map/ppermute | solution.py:876
  103.8 2.0 %collective-permute-start.34 = (bf16[2,64,256]{2,1,0:T(8,128)(2,1)S(1)}, bf16[2,64,256]{2,1,0:T(8,128)(2,1)S(1)}, u32[]{:S(2)}, u32[]{:S(2)}) collective-permute-start(bf16[2,64,256]{2,1,0:T(8,128)(2,1)S(1)} %get-tuple-element.292), channel_id=1, source_target_pairs={{0,2},{1,3},{2,0},{3,1},{4,6},{5,7},{6,4},{7,5},{8,10},{9,11},{10,... | collective-permute-start | bytes 196616 | tf_op jit(solution)/shard_map/ppermute | solution.py:876
  107.3 2.0 %fetch.5 = (f32[128,1024]{1,0:T(8,128)S(1)}, bf16[128,1024]{1,0:T(8,128)(2,1)S(1)}, bf16[128,1024]{1,0:T(8,128)(2,1)S(1)}, bf16[64,1024]{1,0:T(8,128)(2,1)S(1)},...) custom-call(f32[128,1024]{1,0:T(8,128)} %get-tuple-element.257.refs_, ...), custom_call_target="tpu_custom_call" | custom-call | flops 1000000000 | bytes 1048576 | tf_op jit(solution)/shard_map/fetch/pallas_call | solution.py:158
  109.4 5.4 %back_last.1 = (f32[128,1024]{1,0:T(8,128)S(1)}, bf16[128,640]{1,0:T(8,128)(2,1)}) custom-call(bf16[128,512]{1,0:T(8,128)(2,1)S(1)} %add_convert_fusion.refs_0_, bf16[128,512]{1,0:T(8,128)(2,1)S(1)} %collective-permute-done.29.refs_1_, f32[128,1024]{1,0:T(8,128)S(1)} %get-tuple-element.270.refs_2_, ...), custom_call_target="tpu_custom_call", output_to_operand_aliasing={{1}: (28, {})} | custom-call | flops 10000000000 | bytes 1048576 | tf_op jit(solution)/shard_map/back_last/pallas_call | solution.py:128
  114.9 5.3 %all-to-all-start.1 = ((bf16[8,16,640]{2,1,0:T(8,128)(2,1)}), bf16[8,16,640]{2,1,0:T(8,128)(2,1)S(1)}, u32[]{:S(2)}, u32[]{:S(2)}) async-start(bf16[8,16,640]{2,1,0:T(8,128)(2,1)} %bitcast.72), calls=%async_computation.1 | async-start | bytes 327680 | tf_op jit(solution)/shard_map/all_to_all | solution.py:853
  120.5 2.9 %collective-permute-start.36 = (bf16[64,256]{1,0:T(8,128)(2,1)S(1)}, bf16[64,256]{1,0:T(8,128)(2,1)S(1)}, u32[]{:S(2)}, u32[]{:S(2)}) collective-permute-start(bf16[64,256]{1,0:T(8,128)(2,1)S(1)} %slice_bitcast_fusion.4), channel_id=1, source_target_pairs={{0,4},{1,5},{2,6},{3,7},{4,0},{5,1},{6,2},{7,3},{8,12},{9,13},{10,... | collective-permute-start | bytes 98312 | tf_op jit(solution)/shard_map/ppermute | solution.py:876
  124.9 3.4 %all-to-all-done.1.refs_0_ = bf16[8,16,640]{2,1,0:T(8,128)(2,1)S(1)} async-done(((bf16[8,16,640]{2,1,0:T(8,128)(2,1)}), bf16[8,16,640]{2,1,0:T(8,128)(2,1)S(1)}, u32[]{:S(2)}, u32[]{:S(2)}) %all-to-all-start.1) | async-done | bytes 163872 | tf_op jit(solution)/shard_map/all_to_all | solution.py:853
  132.7 1.7 %adam.1 = (f32[16,3000]{1,0:T(8,128)}, f32[16,3000]{1,0:T(8,128)}, f32[16,3000]{1,0:T(8,128)}, f32[16,3000]{1,0:T(8,128)}, bf16[16,3000]{1,0:T(8,128)(2,1)}) custom-call(s32[2]{0:T(128)S(1)} %pad_add_fusion.refs_0_, f32[16,3000]{1,0:T(8,128)S(1)} %bitcast.41, f32[16,3000]{1,0:T(8,128)S(1)} %bitcast.42, f32[16,3000]{1,0:T(8,128)S(1)} %bitcast.43, ...), custom_call_target="tpu_custom_call" | custom-call | flops 100000000 | bytes 1048576 | tf_op jit(solution)/shard_map/adam/pallas_call | solution.py:128
  (118 shorter events, 35.6 us)
Async XLA Ops:
  7.2 6.5 %collective-permute-start.4 = (bf16[1,144,256]{2,1,0:T(8,128)(2,1)S(1)}, bf16[1,144,256]{2,1,0:T(8,128)(2,1)S(1)}, u32[]{:S(2)}, u32[]{:S(2)}) collective-permute-start(bf16[1,144,256]{2,1,0:T(8,128)(2,1)S(1)} %get-tuple-element.163.refs_1_), channel_id=1, source_target_pairs={{0,4},{1,5},{2,6},{3,7},{4,0},{5,1},{6,2},{7,3},{8,12},{9,13},{10,... | collective-permute-start | bytes 221192 | tf_op jit(solution)/shard_map/ppermute | solution.py:876
  7.4 8.8 %collective-permute-start.3 = (bf16[2,16,256]{2,1,0:T(8,128)(2,1)S(1)}, bf16[2,16,256]{2,1,0:T(8,128)(2,1)S(1)}, u32[]{:S(2)}, u32[]{:S(2)}) collective-permute-start(bf16[2,16,256]{2,1,0:T(8,128)(2,1)S(1)} %constant_dynamic-update-slice_fusion), channel_id=1, source_target_pairs={{0,3},{1,2},{2,1},{3,0},{4,7},{5,6},{6,5},{7,4},{8,11},{9,10},{10,... | collective-permute-start | bytes 49160 | tf_op jit(solution)/shard_map/ppermute | solution.py:876
  10.3 6.9 %collective-permute-start.2 = (bf16[2,16,256]{2,1,0:T(8,128)(2,1)S(1)}, bf16[2,16,256]{2,1,0:T(8,128)(2,1)S(1)}, u32[]{:S(2)}, u32[]{:S(2)}) collective-permute-start(bf16[2,16,256]{2,1,0:T(8,128)(2,1)S(1)} %constant_dynamic-update-slice_fusion), channel_id=1, source_target_pairs={{0,2},{1,3},{2,0},{3,1},{4,6},{5,7},{6,4},{7,5},{8,10},{9,11},{10,... | collective-permute-start | bytes 49160 | tf_op jit(solution)/shard_map/ppermute | solution.py:876
  10.7 6.5 %collective-permute-start.1 = (bf16[2,16,256]{2,1,0:T(8,128)(2,1)S(1)}, bf16[2,16,256]{2,1,0:T(8,128)(2,1)S(1)}, u32[]{:S(2)}, u32[]{:S(2)}) collective-permute-start(bf16[2,16,256]{2,1,0:T(8,128)(2,1)S(1)} %constant_dynamic-update-slice_fusion), channel_id=1, source_target_pairs={{0,1},{1,0},{2,3},{3,2},{4,5},{5,4},{6,7},{7,6},{8,9},{9,8},{10,11... | collective-permute-start | bytes 49160 | tf_op jit(solution)/shard_map/ppermute | solution.py:876
  13.7 9.6 %collective-permute-start.7 = (bf16[2,144,256]{2,1,0:T(8,128)(2,1)S(1)}, bf16[2,144,256]{2,1,0:T(8,128)(2,1)S(1)}, u32[]{:S(2)}, u32[]{:S(2)}) collective-permute-start(bf16[2,144,256]{2,1,0:T(8,128)(2,1)S(1)} %constant_dynamic-update-slice_fusion.2), channel_id=1, source_target_pairs={{0,3},{1,2},{2,1},{3,0},{4,7},{5,6},{6,5},{7,4},{8,11},{9,10},{10,... | collective-permute-start | bytes 442376 | tf_op jit(solution)/shard_map/ppermute | solution.py:876
  15.2 8.1 %collective-permute-start.6 = (bf16[2,144,256]{2,1,0:T(8,128)(2,1)S(1)}, bf16[2,144,256]{2,1,0:T(8,128)(2,1)S(1)}, u32[]{:S(2)}, u32[]{:S(2)}) collective-permute-start(bf16[2,144,256]{2,1,0:T(8,128)(2,1)S(1)} %constant_dynamic-update-slice_fusion.2), channel_id=1, source_target_pairs={{0,2},{1,3},{2,0},{3,1},{4,6},{5,7},{6,4},{7,5},{8,10},{9,11},{10,... | collective-permute-start | bytes 442376 | tf_op jit(solution)/shard_map/ppermute | solution.py:876
  16.2 7.2 %collective-permute-start.5 = (bf16[2,144,256]{2,1,0:T(8,128)(2,1)S(1)}, bf16[2,144,256]{2,1,0:T(8,128)(2,1)S(1)}, u32[]{:S(2)}, u32[]{:S(2)}) collective-permute-start(bf16[2,144,256]{2,1,0:T(8,128)(2,1)S(1)} %constant_dynamic-update-slice_fusion.2), channel_id=1, source_target_pairs={{0,1},{1,0},{2,3},{3,2},{4,5},{5,4},{6,7},{7,6},{8,9},{9,8},{10,11... | collective-permute-start | bytes 442376 | tf_op jit(solution)/shard_map/ppermute | solution.py:876
  27.8 7.2 %collective-permute-start.13 = (bf16[128,384]{1,0:T(8,128)(2,1)S(1)}, bf16[128,384]{1,0:T(8,128)(2,1)S(1)}, u32[]{:S(2)}, u32[]{:S(2)}) collective-permute-start(bf16[128,384]{1,0:T(8,128)(2,1)S(1)} %get-tuple-element.168.refs_2_), channel_id=1, source_target_pairs={{0,16},{8,24},{16,0},{24,8},{1,17},{9,25},{17,1},{25,9},{2,18},{10... | collective-permute-start | bytes 294920 | tf_op jit(solution)/shard_map/ppermute | solution.py:876
  31.0 8.1 %collective-permute-start.11 = (bf16[512,128]{1,0:T(8,128)(2,1)S(1)}, bf16[512,128]{1,0:T(8,128)(2,1)S(1)}, u32[]{:S(2)}, u32[]{:S(2)}) collective-permute-start(bf16[512,128]{1,0:T(8,128)(2,1)S(1)} %add_convert_fusion.3.refs_0_), channel_id=1, source_target_pairs={{0,4},{1,5},{2,6},{3,7},{4,0},{5,1},{6,2},{7,3},{8,12},{9,13},{10,... | collective-permute-start | bytes 393224 | tf_op jit(solution)/shard_map/ppermute | solution.py:876
  46.6 7.2 %collective-permute-start.17 = (bf16[512,128]{1,0:T(8,128)(2,1)S(1)}, bf16[512,128]{1,0:T(8,128)(2,1)S(1)}, u32[]{:S(2)}, u32[]{:S(2)}) collective-permute-start(bf16[512,128]{1,0:T(8,128)(2,1)S(1)} %get-tuple-element.183), channel_id=1, source_target_pairs={{0,3},{1,2},{2,1},{3,0},{4,7},{5,6},{6,5},{7,4},{8,11},{9,10},{10,... | collective-permute-start | bytes 393224 | tf_op jit(solution)/shard_map/ppermute | solution.py:876
  46.7 8.2 %collective-permute-start.16 = (bf16[512,128]{1,0:T(8,128)(2,1)S(1)}, bf16[512,128]{1,0:T(8,128)(2,1)S(1)}, u32[]{:S(2)}, u32[]{:S(2)}) collective-permute-start(bf16[512,128]{1,0:T(8,128)(2,1)S(1)} %get-tuple-element.183), channel_id=1, source_target_pairs={{0,2},{1,3},{2,0},{3,1},{4,6},{5,7},{6,4},{7,5},{8,10},{9,11},{10,... | collective-permute-start | bytes 393224 | tf_op jit(solution)/shard_map/ppermute | solution.py:876
  50.2 7.2 %collective-permute-start.20 = (bf16[128,384]{1,0:T(8,128)(2,1)S(1)}, bf16[128,384]{1,0:T(8,128)(2,1)S(1)}, u32[]{:S(2)}, u32[]{:S(2)}) collective-permute-start(bf16[128,384]{1,0:T(8,128)(2,1)S(1)} %get-tuple-element.187.refs_1_), channel_id=1, source_target_pairs={{0,16},{8,24},{16,0},{24,8},{1,17},{9,25},{17,1},{25,9},{2,18},{10... | collective-permute-start | bytes 294920 | tf_op jit(solution)/shard_map/ppermute | solution.py:876
  55.2 7.9 %collective-permute-start.18 = (bf16[512,128]{1,0:T(8,128)(2,1)S(1)}, bf16[512,128]{1,0:T(8,128)(2,1)S(1)}, u32[]{:S(2)}, u32[]{:S(2)}) collective-permute-start(bf16[512,128]{1,0:T(8,128)(2,1)S(1)} %add_convert_fusion.2.refs_1_), channel_id=1, source_target_pairs={{0,4},{1,5},{2,6},{3,7},{4,0},{5,1},{6,2},{7,3},{8,12},{9,13},{10,... | collective-permute-start | bytes 393224 | tf_op jit(solution)/shard_map/ppermute | solution.py:876
  66.6 7.4 %collective-permute-start.24 = (bf16[128,512]{1,0:T(8,128)(2,1)S(1)}, bf16[128,512]{1,0:T(8,128)(2,1)S(1)}, u32[]{:S(2)}, u32[]{:S(2)}) collective-permute-start(bf16[128,512]{1,0:T(8,128)(2,1)S(1)} %get-tuple-element.207), channel_id=1, source_target_pairs={{0,3},{1,2},{2,1},{3,0},{4,7},{5,6},{6,5},{7,4},{8,11},{9,10},{10,... | collective-permute-start | bytes 393224 | tf_op jit(solution)/shard_map/ppermute | solution.py:876
  66.7 8.5 %collective-permute-start.23 = (bf16[128,512]{1,0:T(8,128)(2,1)S(1)}, bf16[128,512]{1,0:T(8,128)(2,1)S(1)}, u32[]{:S(2)}, u32[]{:S(2)}) collective-permute-start(bf16[128,512]{1,0:T(8,128)(2,1)S(1)} %get-tuple-element.207), channel_id=1, source_target_pairs={{0,2},{1,3},{2,0},{3,1},{4,6},{5,7},{6,4},{7,5},{8,10},{9,11},{10,... | collective-permute-start | bytes 393224 | tf_op jit(solution)/shard_map/ppermute | solution.py:876
  69.1 6.6 %collective-permute-start.22 = (bf16[128,512]{1,0:T(8,128)(2,1)S(1)}, bf16[128,512]{1,0:T(8,128)(2,1)S(1)}, u32[]{:S(2)}, u32[]{:S(2)}) collective-permute-start(bf16[128,512]{1,0:T(8,128)(2,1)S(1)} %get-tuple-element.207), channel_id=1, source_target_pairs={{0,1},{1,0},{2,3},{3,2},{4,5},{5,4},{6,7},{7,6},{8,9},{9,8},{10,11... | collective-permute-start | bytes 393224 | tf_op jit(solution)/shard_map/ppermute | solution.py:876
  75.7 8.4 %collective-permute-start.25 = (bf16[128,512]{1,0:T(8,128)(2,1)S(1)}, bf16[128,512]{1,0:T(8,128)(2,1)S(1)}, u32[]{:S(2)}, u32[]{:S(2)}) collective-permute-start(bf16[128,512]{1,0:T(8,128)(2,1)S(1)} %add_convert_fusion.1.refs_1_), channel_id=1, source_target_pairs={{0,4},{1,5},{2,6},{3,7},{4,0},{5,1},{6,2},{7,3},{8,12},{9,13},{10,... | collective-permute-start | bytes 393224 | tf_op jit(solution)/shard_map/ppermute | solution.py:876
  76.1 21.5 %all-to-all-start = ((bf16[8,16,1280]{2,1,0:T(8,128)(2,1)}), bf16[8,16,1280]{2,1,0:T(8,128)(2,1)S(1)}, u32[]{:S(2)}, u32[]{:S(2)}) async-start(bf16[8,16,1280]{2,1,0:T(8,128)(2,1)} %bitcast.15), calls=%async_computation | async-start | bytes 655360 | tf_op jit(solution)/shard_map/all_to_all | solution.py:853
  91.3 7.8 %collective-permute-start.28 = (bf16[128,512]{1,0:T(8,128)(2,1)S(1)}, bf16[128,512]{1,0:T(8,128)(2,1)S(1)}, u32[]{:S(2)}, u32[]{:S(2)}) collective-permute-start(bf16[128,512]{1,0:T(8,128)(2,1)S(1)} %get-tuple-element.254), channel_id=1, source_target_pairs={{0,3},{1,2},{2,1},{3,0},{4,7},{5,6},{6,5},{7,4},{8,11},{9,10},{10,... | collective-permute-start | bytes 393224 | tf_op jit(solution)/shard_map/ppermute | solution.py:876
  93.2 6.5 %collective-permute-start.27 = (bf16[128,512]{1,0:T(8,128)(2,1)S(1)}, bf16[128,512]{1,0:T(8,128)(2,1)S(1)}, u32[]{:S(2)}, u32[]{:S(2)}) collective-permute-start(bf16[128,512]{1,0:T(8,128)(2,1)S(1)} %get-tuple-element.254), channel_id=1, source_target_pairs={{0,2},{1,3},{2,0},{3,1},{4,6},{5,7},{6,4},{7,5},{8,10},{9,11},{10,... | collective-permute-start | bytes 393224 | tf_op jit(solution)/shard_map/ppermute | solution.py:876
  93.8 6.6 %collective-permute-start.26 = (bf16[128,512]{1,0:T(8,128)(2,1)S(1)}, bf16[128,512]{1,0:T(8,128)(2,1)S(1)}, u32[]{:S(2)}, u32[]{:S(2)}) collective-permute-start(bf16[128,512]{1,0:T(8,128)(2,1)S(1)} %get-tuple-element.254), channel_id=1, source_target_pairs={{0,1},{1,0},{2,3},{3,2},{4,5},{5,4},{6,7},{7,6},{8,9},{9,8},{10,11... | collective-permute-start | bytes 393224 | tf_op jit(solution)/shard_map/ppermute | solution.py:876
  97.7 8.2 %collective-permute-start.31 = (bf16[128,384]{1,0:T(8,128)(2,1)S(1)}, bf16[128,384]{1,0:T(8,128)(2,1)S(1)}, u32[]{:S(2)}, u32[]{:S(2)}) collective-permute-start(bf16[128,384]{1,0:T(8,128)(2,1)S(1)} %get-tuple-element.304), channel_id=1, source_target_pairs={{0,16},{8,24},{16,0},{24,8},{1,17},{9,25},{17,1},{25,9},{2,18},{10... | collective-permute-start | bytes 294920 | tf_op jit(solution)/shard_map/ppermute | solution.py:876
  99.1 7.5 %collective-permute-start.30 = (bf16[128,384]{1,0:T(8,128)(2,1)S(1)}, bf16[128,384]{1,0:T(8,128)(2,1)S(1)}, u32[]{:S(2)}, u32[]{:S(2)}) collective-permute-start(bf16[128,384]{1,0:T(8,128)(2,1)S(1)} %get-tuple-element.305), channel_id=1, source_target_pairs={{0,8},{8,0},{16,24},{24,16},{1,9},{9,1},{17,25},{25,17},{2,10},{10... | collective-permute-start | bytes 294920 | tf_op jit(solution)/shard_map/ppermute | solution.py:876
  100.5 9.0 %collective-permute-start.29 = (bf16[128,512]{1,0:T(8,128)(2,1)S(1)}, bf16[128,512]{1,0:T(8,128)(2,1)S(1)}, u32[]{:S(2)}, u32[]{:S(2)}) collective-permute-start(bf16[128,512]{1,0:T(8,128)(2,1)S(1)} %add_convert_fusion.refs_0_), channel_id=1, source_target_pairs={{0,4},{1,5},{2,6},{3,7},{4,0},{5,1},{6,2},{7,3},{8,12},{9,13},{10,... | collective-permute-start | bytes 393224 | tf_op jit(solution)/shard_map/ppermute | solution.py:876
  102.6 17.7 %collective-permute-start.33 = (bf16[2,64,256]{2,1,0:T(8,128)(2,1)S(1)}, bf16[2,64,256]{2,1,0:T(8,128)(2,1)S(1)}, u32[]{:S(2)}, u32[]{:S(2)}) collective-permute-start(bf16[2,64,256]{2,1,0:T(8,128)(2,1)S(1)} %get-tuple-element.291), channel_id=1, source_target_pairs={{0,1},{1,0},{2,3},{3,2},{4,5},{5,4},{6,7},{7,6},{8,9},{9,8},{10,11... | collective-permute-start | bytes 196616 | tf_op jit(solution)/shard_map/ppermute | solution.py:876
  103.8 16.4 %collective-permute-start.34 = (bf16[2,64,256]{2,1,0:T(8,128)(2,1)S(1)}, bf16[2,64,256]{2,1,0:T(8,128)(2,1)S(1)}, u32[]{:S(2)}, u32[]{:S(2)}) collective-permute-start(bf16[2,64,256]{2,1,0:T(8,128)(2,1)S(1)} %get-tuple-element.292), channel_id=1, source_target_pairs={{0,2},{1,3},{2,0},{3,1},{4,6},{5,7},{6,4},{7,5},{8,10},{9,11},{10,... | collective-permute-start | bytes 196616 | tf_op jit(solution)/shard_map/ppermute | solution.py:876
  105.9 14.4 %collective-permute-start.35 = (bf16[2,64,256]{2,1,0:T(8,128)(2,1)S(1)}, bf16[2,64,256]{2,1,0:T(8,128)(2,1)S(1)}, u32[]{:S(2)}, u32[]{:S(2)}) collective-permute-start(bf16[2,64,256]{2,1,0:T(8,128)(2,1)S(1)} %get-tuple-element.293), channel_id=1, source_target_pairs={{0,3},{1,2},{2,1},{3,0},{4,7},{5,6},{6,5},{7,4},{8,11},{9,10},{10,... | collective-permute-start | bytes 196616 | tf_op jit(solution)/shard_map/ppermute | solution.py:876
  114.9 13.5 %all-to-all-start.1 = ((bf16[8,16,640]{2,1,0:T(8,128)(2,1)}), bf16[8,16,640]{2,1,0:T(8,128)(2,1)S(1)}, u32[]{:S(2)}, u32[]{:S(2)}) async-start(bf16[8,16,640]{2,1,0:T(8,128)(2,1)} %bitcast.72), calls=%async_computation.1 | async-start | bytes 327680 | tf_op jit(solution)/shard_map/all_to_all | solution.py:853
  120.3 9.4 %collective-permute-start.42 = (bf16[16,1280]{1,0:T(8,128)(2,1)S(1)}, bf16[16,1280]{1,0:T(8,128)(2,1)S(1)}, u32[]{:S(2)}, u32[]{:S(2)}) collective-permute-start(bf16[16,1280]{1,0:T(8,128)(2,1)S(1)} %sum_parts.3.refs_8_), channel_id=1, source_target_pairs={{0,24},{8,16},{16,8},{24,0},{1,25},{9,17},{17,9},{25,1},{2,26},{10... | collective-permute-start | bytes 122888 | tf_op jit(solution)/shard_map/ppermute | solution.py:876
  120.5 8.2 %collective-permute-start.36 = (bf16[64,256]{1,0:T(8,128)(2,1)S(1)}, bf16[64,256]{1,0:T(8,128)(2,1)S(1)}, u32[]{:S(2)}, u32[]{:S(2)}) collective-permute-start(bf16[64,256]{1,0:T(8,128)(2,1)S(1)} %slice_bitcast_fusion.4), channel_id=1, source_target_pairs={{0,4},{1,5},{2,6},{3,7},{4,0},{5,1},{6,2},{7,3},{8,12},{9,13},{10,... | collective-permute-start | bytes 98312 | tf_op jit(solution)/shard_map/ppermute | solution.py:876
  123.4 8.5 %collective-permute-start.41 = (bf16[16,1280]{1,0:T(8,128)(2,1)S(1)}, bf16[16,1280]{1,0:T(8,128)(2,1)S(1)}, u32[]{:S(2)}, u32[]{:S(2)}) collective-permute-start(bf16[16,1280]{1,0:T(8,128)(2,1)S(1)} %sum_parts.3.refs_8_), channel_id=1, source_target_pairs={{0,16},{8,24},{16,0},{24,8},{1,17},{9,25},{17,1},{25,9},{2,18},{10... | collective-permute-start | bytes 122888 | tf_op jit(solution)/shard_map/ppermute | solution.py:876
  124.7 7.3 %collective-permute-start.40 = (bf16[16,1280]{1,0:T(8,128)(2,1)S(1)}, bf16[16,1280]{1,0:T(8,128)(2,1)S(1)}, u32[]{:S(2)}, u32[]{:S(2)}) collective-permute-start(bf16[16,1280]{1,0:T(8,128)(2,1)S(1)} %sum_parts.3.refs_8_), channel_id=1, source_target_pairs={{0,8},{8,0},{16,24},{24,16},{1,9},{9,1},{17,25},{25,17},{2,10},{10... | collective-permute-start | bytes 122888 | tf_op jit(solution)/shard_map/ppermute | solution.py:876
  (26 other events, 169.0 us)
